TPU v7x, 32 devices: a whole 2x2x4 slice. The times are simulated.
32 devices in a mesh: clip: 8 (over y, x, core), tm: 4 (over z).
Axes of the slice: x: 2, y: 2, z: 4, core: 2. Of those that a mesh axis runs over, the one named last changes fastest.
Arguments:
- tokens: bfloat16 [2, 16, 2048, 1024], P(None, 'tm', 'clip'), may hold values from -6 to 6
- segments: int32 [2, 2048], P(None, 'clip'), may hold values from 0 to 3, as said below
- assignment: int32 [2, 32], P(None, 'clip'), may hold values from 0 to 31, as said below
- actions: int32 [2, 32, 16], P(None, None, 'tm'), may hold values from 0 to 7
- norm_gain: bfloat16 [3, 1024], P(None, 'clip'), may hold values from 0.099609375 to 1.8984375
- norm_bias: bfloat16 [3, 1024], P(None, 'clip'), may hold values from -1.75 to 1.75
- space_in_weight: bfloat16 [1024, 3072], P('clip'), may hold values from -0.1875 to 0.1875
- space_out_weight: bfloat16 [1024, 1024], P('clip'), may hold values from -1.5 to 1.5
- time_in_weight: bfloat16 [1024, 3072], P('clip'), may hold values from -0.1875 to 0.1875
- time_out_weight: bfloat16 [1024, 1024], P('clip'), may hold values from -0.5 to 0.5
- hidden_weight: bfloat16 [1024, 4096], P('clip'), may hold values from -0.1875 to 0.1875
- hidden_bias: bfloat16 [4096], P('clip'), may hold values from -3 to 3
- output_weight: bfloat16 [4096, 1024], P('clip'), may hold values from -0.09375 to 0.09375
- output_bias: bfloat16 [1024], P('clip'), may hold values from -3 to 3
- action_table: bfloat16 [8, 1024], P(None, 'clip'), may hold values from -3 to 3
- out_grad: float32 [2, 16, 2048, 1024], P(None, 'tm', 'clip'), may hold values from -6 to 6
Outputs:
- block_out: bfloat16 [2, 16, 2048, 1024], P(None, 'tm', 'clip')
- tokens_grad: float32 [2, 16, 2048, 1024], P(None, 'tm', 'clip')
- norm_gain_grad: float32 [3, 1024], P(None, 'clip')
- norm_bias_grad: float32 [3, 1024], P(None, 'clip')
- space_in_grad: float32 [1024, 3072], P('clip')
- space_out_grad: float32 [1024, 1024], P('clip')
- time_in_grad: float32 [1024, 3072], P('clip')
- time_out_grad: float32 [1024, 1024], P('clip')
- hidden_grad: float32 [1024, 4096], P('clip')
- hidden_bias_grad: float32 [4096], P('clip')
- output_grad: float32 [4096, 1024], P('clip')
- output_bias_grad: float32 [1024], P('clip')
- action_table_grad: float32 [8, 1024], P(None, 'clip')
Inputs may be any that keep to these rules, and one draw needn't show every extreme that they name: `segments`: on every clip index and micro-batch the 256 positions hold first some clips of 256 positions, then clips of 64 positions, numbered upward from 0 in that order; every frame uses the same numbering. `assignment`: each row is a permutation of the 32 clip numbers; numbers of local clips that a clip index does not use are read by nobody.
All inputs are finite; a program needn't handle non-finite values.
Results may differ from a plain program's by a relative error of at most 0.018.
Values may be sent and summed in bfloat16 or wider, within the bound.
No kernel may reach another device: no remote copies, remote signals or barrier semaphores. Data moves between devices by JAX's collectives and lax.ppermute only.
A program may use at most 512 MiB of HBM per device.

v0:
```python
import jax
import jax.numpy as jnp
from jax import lax
from jax.sharding import PartitionSpec as P

HEADS = 16


norm_eps = 1e-05
masked_fill = -1e30
space_forms = ("bqhe,bkhe->bhqk", "bhqk,bkhe->bqhe", "bhqk,bqhe->bkhe")
time_forms = ("qbhe,kbhe->bhqk", "bhqk,kbhe->qbhe", "bhqk,qbhe->kbhe")


def layer_norm(values, norm_gains, shifts):
    centered = values - jnp.mean(values, axis=-1, keepdims=True)
    spread = jnp.mean(centered * centered, axis=-1, keepdims=True)
    return centered * lax.rsqrt(spread + norm_eps) * norm_gains + shifts


def norm_back(values, norm_gains, shifts, grad_values):
    _, pullback = jax.vjp(layer_norm, values, norm_gains, shifts)
    return pullback(grad_values)


def gelu_tanh(values):
    return jax.nn.gelu(values, approximate=True)


def project(left, right):
    return jnp.einsum("fsd,de->fse", left, right, preferred_element_type=jnp.float32)


def project_back(left, right):
    return jnp.einsum("fse,de->fsd", left, right, preferred_element_type=jnp.float32)


def weight_grad(left, right):
    return jnp.einsum("fsd,fse->de", left, right, preferred_element_type=jnp.float32)


def split_heads(packed, model_width):
    shape_lead = packed.shape[:-1]
    return tuple(
        (
            packed[..., part_index * model_width : (part_index + 1) * model_width].reshape(
                shape_lead + (HEADS, model_width // HEADS)
            )
            for part_index in range(3)
        )
    )


def join_heads(portions):
    return jnp.concatenate(
        [portion.reshape(portion.shape[:-2] + (-1,)) for portion in portions], axis=-1
    )


def attend(queries, key_rows, value_rows, allowed, forms):
    score_scale = queries.shape[-1] ** (-0.5)
    raw_scores = (
        jnp.einsum(forms[0], queries, key_rows, preferred_element_type=jnp.float32) * score_scale
    )
    scores = jnp.where(allowed, raw_scores, masked_fill)
    row_top = jnp.max(scores, axis=-1, keepdims=True)
    log_total = row_top + jnp.log(jnp.sum(jnp.exp(scores - row_top), axis=-1, keepdims=True))
    attn_probs = jnp.exp(scores - log_total).astype(jnp.bfloat16)
    mixed = jnp.einsum(forms[1], attn_probs, value_rows, preferred_element_type=jnp.float32)
    return (mixed.astype(jnp.bfloat16), log_total)


def attend_back(queries, key_rows, value_rows, allowed, log_total, grad_mixed, forms):
    score_scale = queries.shape[-1] ** (-0.5)
    raw_scores = (
        jnp.einsum(forms[0], queries, key_rows, preferred_element_type=jnp.float32) * score_scale
    )
    scores = jnp.where(allowed, raw_scores, masked_fill)
    attn_probs = jnp.exp(scores - log_total)
    grad_prob = jnp.einsum(forms[0], grad_mixed, value_rows, preferred_element_type=jnp.float32)
    grad_score = (
        attn_probs * (grad_prob - jnp.sum(attn_probs * grad_prob, axis=-1, keepdims=True))
    ).astype(jnp.bfloat16)
    grad_query = (
        jnp.einsum(forms[1], grad_score, key_rows, preferred_element_type=jnp.float32) * score_scale
    )
    grad_key = (
        jnp.einsum(forms[2], grad_score, queries, preferred_element_type=jnp.float32) * score_scale
    )
    grad_value = jnp.einsum(
        forms[2], attn_probs.astype(jnp.bfloat16), grad_mixed, preferred_element_type=jnp.float32
    )
    return (grad_query, grad_key, grad_value)


def frame_actions(labels, owners, action_rows, action_count):
    segment_hit = labels[:, None] == jnp.arange(owners.shape[0])[None, :]
    clip_of = jnp.sum(jnp.where(segment_hit, owners[None, :], 0), axis=1)
    clip_hit = clip_of[:, None] == jnp.arange(action_rows.shape[0])[None, :]
    chosen = jnp.sum(jnp.where(clip_hit[:, :, None], action_rows[None, :, :], 0), axis=1)
    action_hit = jnp.transpose(chosen)[:, :, None] == jnp.arange(action_count)[None, None, :]
    return action_hit.astype(jnp.float32)


def one_batch(frame_tokens, labels, owners, action_rows, gathered, grad_out):
    (
        gain_rows,
        shift_rows,
        space_in_full,
        space_out_full,
        time_in_full,
        time_out_full,
        hidden_full,
        hidden_bias_full,
        output_full,
        output_bias_full,
        table_full,
    ) = gathered
    frames_here, slot_count, model_width = frame_tokens.shape
    gain_rows = gain_rows.astype(jnp.float32)
    shift_rows = shift_rows.astype(jnp.float32)
    action_hot = frame_actions(labels, owners, action_rows, table_full.shape[0])
    embedded = frame_tokens.astype(jnp.float32) + jnp.einsum(
        "fsa,ad->fsd", action_hot, table_full.astype(jnp.float32), precision=lax.Precision.HIGHEST
    )
    norm_one = layer_norm(embedded, gain_rows[0], shift_rows[0]).astype(jnp.bfloat16)
    space_packed = project(norm_one, space_in_full).astype(jnp.bfloat16)
    space_query, space_key, space_value = split_heads(space_packed, model_width)
    space_mask = (labels[:, None] == labels[None, :])[None, None]
    space_mixed, space_total = attend(space_query, space_key, space_value, space_mask, space_forms)
    space_flat = space_mixed.reshape(frames_here, slot_count, model_width)
    after_space = embedded + project(space_flat, space_out_full)
    norm_two = layer_norm(after_space, gain_rows[1], shift_rows[1]).astype(jnp.bfloat16)
    time_packed = project(norm_two, time_in_full).astype(jnp.bfloat16)
    frames_all = frames_here * lax.axis_size("tm")
    block_width = slot_count // 4
    own_frames = lax.axis_index("tm") * frames_here + jnp.arange(frames_here)
    time_mask = (own_frames[:, None] >= jnp.arange(frames_all)[None, :])[None, None]
    time_query = split_heads(time_packed, model_width)[0]
    kept_keys, block_mixes, block_totals = ([], [], [])
    for block_index in range(4):
        row_start = block_index * block_width
        block_cols = time_packed[:, row_start : row_start + block_width]
        key_all, value_all = (
            lax.all_gather(
                block_cols[..., model_width : 2 * model_width], "tm", axis=0, tiled=True
            ),
            lax.all_gather(block_cols[..., 2 * model_width :], "tm", axis=0, tiled=True),
        )
        key_heads = key_all.reshape(frames_all, block_width, HEADS, -1)
        value_heads = value_all.reshape(frames_all, block_width, HEADS, -1)
        kept_keys.append((key_heads, value_heads))
        block_mixed, block_total = attend(
            time_query[:, row_start : row_start + block_width],
            key_heads,
            value_heads,
            time_mask,
            time_forms,
        )
        block_mixes.append(block_mixed)
        block_totals.append(block_total)
    time_flat = jnp.concatenate(block_mixes, axis=1).reshape(frames_here, slot_count, model_width)
    after_time = after_space + project(time_flat, time_out_full)
    norm_three = layer_norm(after_time, gain_rows[2], shift_rows[2]).astype(jnp.bfloat16)
    pre_act = project(norm_three, hidden_full) + hidden_bias_full.astype(jnp.float32)
    activation = gelu_tanh(pre_act).astype(jnp.bfloat16)
    block_result = (
        after_time + project(activation, output_full) + output_bias_full.astype(jnp.float32)
    ).astype(jnp.bfloat16)
    grad_branch = grad_out.astype(jnp.bfloat16)
    output_grad = weight_grad(activation, grad_branch)
    output_bias_grad = jnp.sum(grad_branch.astype(jnp.float32), axis=(0, 1))
    grad_activation = project_back(grad_branch, output_full)
    _, gelu_pull = jax.vjp(gelu_tanh, pre_act)
    grad_pre = gelu_pull(grad_activation)[0].astype(jnp.bfloat16)
    hidden_grad = weight_grad(norm_three, grad_pre)
    hidden_bias_grad = jnp.sum(grad_pre.astype(jnp.float32), axis=(0, 1))
    grad_norm_three = project_back(grad_pre, hidden_full)
    back_three, gain_three, shift_three = norm_back(
        after_time, gain_rows[2], shift_rows[2], grad_norm_three
    )
    grad_after_time = grad_out + back_three
    grad_time_branch = grad_after_time.astype(jnp.bfloat16)
    time_out_grad = weight_grad(time_flat, grad_time_branch)
    grad_time_flat = project_back(grad_time_branch, time_out_full).astype(jnp.bfloat16)
    packed_pieces = []
    for block_index in range(4):
        row_start = block_index * block_width
        key_heads, value_heads = kept_keys[block_index]
        grad_block = grad_time_flat[:, row_start : row_start + block_width].reshape(
            frames_here, block_width, HEADS, -1
        )
        grad_query, grad_key, grad_value = attend_back(
            time_query[:, row_start : row_start + block_width],
            key_heads,
            value_heads,
            time_mask,
            block_totals[block_index],
            grad_block,
            time_forms,
        )
        key_summed, value_summed = (
            lax.psum_scatter(
                grad_key.reshape(frames_all, block_width, model_width).astype(jnp.bfloat16),
                "tm",
                scatter_dimension=0,
                tiled=True,
            ).astype(jnp.float32),
            lax.psum_scatter(
                grad_value.reshape(frames_all, block_width, model_width).astype(jnp.bfloat16),
                "tm",
                scatter_dimension=0,
                tiled=True,
            ).astype(jnp.float32),
        )
        packed_pieces.append(
            jnp.concatenate(
                [
                    grad_query.reshape(frames_here, block_width, model_width),
                    key_summed,
                    value_summed,
                ],
                axis=-1,
            ).astype(jnp.bfloat16)
        )
    grad_time_packed = jnp.concatenate(packed_pieces, axis=1)
    time_in_grad = weight_grad(norm_two, grad_time_packed)
    grad_norm_two = project_back(grad_time_packed, time_in_full)
    back_two, gain_two, shift_two = norm_back(
        after_space, gain_rows[1], shift_rows[1], grad_norm_two
    )
    grad_after_space = grad_after_time + back_two
    grad_space_branch = grad_after_space.astype(jnp.bfloat16)
    space_out_grad = weight_grad(space_flat, grad_space_branch)
    grad_space_flat = project_back(grad_space_branch, space_out_full).astype(jnp.bfloat16)
    grad_space_heads = grad_space_flat.reshape(frames_here, slot_count, HEADS, -1)
    space_grads = attend_back(
        space_query, space_key, space_value, space_mask, space_total, grad_space_heads, space_forms
    )
    grad_space_packed = join_heads(space_grads).astype(jnp.bfloat16)
    space_in_grad = weight_grad(norm_one, grad_space_packed)
    grad_norm_one = project_back(grad_space_packed, space_in_full)
    back_one, gain_one, shift_one = norm_back(embedded, gain_rows[0], shift_rows[0], grad_norm_one)
    start_grad = grad_after_space + back_one
    table_grad = jnp.einsum("fsa,fsd->ad", action_hot, start_grad, precision=lax.Precision.HIGHEST)
    gain_grads = jnp.stack([gain_one, gain_two, gain_three])
    shift_grads = jnp.stack([shift_one, shift_two, shift_three])
    return (
        block_result,
        start_grad,
        (
            gain_grads,
            shift_grads,
            space_in_grad,
            space_out_grad,
            time_in_grad,
            time_out_grad,
            hidden_grad,
            hidden_bias_grad,
            output_grad,
            output_bias_grad,
            table_grad,
        ),
    )


def local(
    tokens,
    segments,
    assignment,
    actions,
    norm_gain,
    norm_bias,
    space_in_weight,
    space_out_weight,
    time_in_weight,
    time_out_weight,
    hidden_weight,
    hidden_bias,
    output_weight,
    output_bias,
    action_table,
    out_grad,
):
    outputs, input_grads, grad_sums = ([], [], None)
    weight_shards = (
        norm_gain,
        norm_bias,
        space_in_weight,
        space_out_weight,
        time_in_weight,
        time_out_weight,
        hidden_weight,
        hidden_bias,
        output_weight,
        output_bias,
        action_table,
    )
    for micro_step in range(tokens.shape[0]):
        gathered = (
            lax.all_gather(weight_shards[0], "clip", axis=1, tiled=True),
            lax.all_gather(weight_shards[1], "clip", axis=1, tiled=True),
            lax.all_gather(weight_shards[2], "clip", axis=0, tiled=True),
            lax.all_gather(weight_shards[3], "clip", axis=0, tiled=True),
            lax.all_gather(weight_shards[4], "clip", axis=0, tiled=True),
            lax.all_gather(weight_shards[5], "clip", axis=0, tiled=True),
            lax.all_gather(weight_shards[6], "clip", axis=0, tiled=True),
            lax.all_gather(weight_shards[7], "clip", axis=0, tiled=True),
            lax.all_gather(weight_shards[8], "clip", axis=0, tiled=True),
            lax.all_gather(weight_shards[9], "clip", axis=0, tiled=True),
            lax.all_gather(weight_shards[10], "clip", axis=1, tiled=True),
        )
        block_result, start_grad, batch_grads = one_batch(
            tokens[micro_step],
            segments[micro_step],
            assignment[micro_step],
            actions[micro_step],
            gathered,
            out_grad[micro_step],
        )
        outputs.append(block_result)
        input_grads.append(start_grad)
        if grad_sums is None:
            grad_sums = batch_grads
        else:
            grad_sums = tuple((running + addend for running, addend in zip(grad_sums, batch_grads)))
    (
        gain_sum,
        shift_sum,
        space_in_sum,
        space_out_sum,
        time_in_sum,
        time_out_sum,
        hidden_sum,
        hidden_bias_sum,
        output_sum,
        output_bias_sum,
        table_sum,
    ) = grad_sums
    clip_grads = (
        lax.psum_scatter(
            gain_sum.astype(jnp.bfloat16), "clip", scatter_dimension=1, tiled=True
        ).astype(jnp.float32),
        lax.psum_scatter(
            shift_sum.astype(jnp.bfloat16), "clip", scatter_dimension=1, tiled=True
        ).astype(jnp.float32),
        lax.psum_scatter(
            space_in_sum.astype(jnp.bfloat16), "clip", scatter_dimension=0, tiled=True
        ).astype(jnp.float32),
        lax.psum_scatter(
            space_out_sum.astype(jnp.bfloat16), "clip", scatter_dimension=0, tiled=True
        ).astype(jnp.float32),
        lax.psum_scatter(
            time_in_sum.astype(jnp.bfloat16), "clip", scatter_dimension=0, tiled=True
        ).astype(jnp.float32),
        lax.psum_scatter(
            time_out_sum.astype(jnp.bfloat16), "clip", scatter_dimension=0, tiled=True
        ).astype(jnp.float32),
        lax.psum_scatter(
            hidden_sum.astype(jnp.bfloat16), "clip", scatter_dimension=0, tiled=True
        ).astype(jnp.float32),
        lax.psum_scatter(
            hidden_bias_sum.astype(jnp.bfloat16), "clip", scatter_dimension=0, tiled=True
        ).astype(jnp.float32),
        lax.psum_scatter(
            output_sum.astype(jnp.bfloat16), "clip", scatter_dimension=0, tiled=True
        ).astype(jnp.float32),
        lax.psum_scatter(
            output_bias_sum.astype(jnp.bfloat16), "clip", scatter_dimension=0, tiled=True
        ).astype(jnp.float32),
        lax.psum_scatter(
            table_sum.astype(jnp.bfloat16), "clip", scatter_dimension=1, tiled=True
        ).astype(jnp.float32),
    )
    (
        gain_part,
        shift_part,
        space_in_part,
        space_out_part,
        time_in_part,
        time_out_part,
        hidden_part,
        hidden_bias_part,
        output_part,
        output_bias_part,
        table_part,
    ) = clip_grads
    final_grads = (
        lax.psum(gain_part.astype(jnp.bfloat16), "tm").astype(jnp.float32),
        lax.psum(shift_part.astype(jnp.bfloat16), "tm").astype(jnp.float32),
        lax.psum(space_in_part.astype(jnp.bfloat16), "tm").astype(jnp.float32),
        lax.psum(space_out_part.astype(jnp.bfloat16), "tm").astype(jnp.float32),
        lax.psum(time_in_part.astype(jnp.bfloat16), "tm").astype(jnp.float32),
        lax.psum(time_out_part.astype(jnp.bfloat16), "tm").astype(jnp.float32),
        lax.psum(hidden_part.astype(jnp.bfloat16), "tm").astype(jnp.float32),
        lax.psum(hidden_bias_part.astype(jnp.bfloat16), "tm").astype(jnp.float32),
        lax.psum(output_part.astype(jnp.bfloat16), "tm").astype(jnp.float32),
        lax.psum(output_bias_part.astype(jnp.bfloat16), "tm").astype(jnp.float32),
        lax.psum(table_part.astype(jnp.bfloat16), "tm").astype(jnp.float32),
    )
    return (
        jnp.stack(outputs),
        jnp.stack(input_grads),
        final_grads[0],
        final_grads[1],
        final_grads[2],
        final_grads[3],
        final_grads[4],
        final_grads[5],
        final_grads[6],
        final_grads[7],
        final_grads[8],
        final_grads[9],
        final_grads[10],
    )


def solution(mesh):
    return jax.shard_map(
        local,
        mesh=mesh,
        in_specs=(
            P(None, "tm", "clip", None),
            P(None, "clip"),
            P(None, "clip"),
            P(None, None, "tm"),
            P(None, "clip"),
            P(None, "clip"),
            P("clip", None),
            P("clip", None),
            P("clip", None),
            P("clip", None),
            P("clip", None),
            P("clip"),
            P("clip", None),
            P("clip"),
            P(None, "clip"),
            P(None, "tm", "clip", None),
        ),
        out_specs=(
            P(None, "tm", "clip", None),
            P(None, "tm", "clip", None),
            P(None, "clip"),
            P(None, "clip"),
            P("clip", None),
            P("clip", None),
            P("clip", None),
            P("clip", None),
            P("clip", None),
            P("clip"),
            P("clip", None),
            P("clip"),
            P(None, "clip"),
        ),
        check_vma=False,
    )
```

profile of v0, /device:TPU:0, one launch (start us, length us, event | category | flops | bytes accessed | tf_op | source)
XLA Modules:
  0.0 2590.7 jit_solution(12840591736738419927)
XLA Ops:
  45.7 12.5 all-gather.25.cloned.1.call-done
  113.4 19.2 fusion.403
  351.8 29.6 %all-gather.65.cloned.1.call-done = bf16[16,64,1024]{2,1,0:T(8,128)(2,1)} async-done(((bf16[4,64,1024]{2,1,0:T(8,128)(2,1)}), bf16[16,64,1024]{2,1,0:T(8,128)(2,1)}) %all-gather.65.cloned.1.call-update) | async-done | bytes 2097168 | tf_op jit(solution)/shard_map/all_gather | solution.py:148
  395.6 32.1 %all-gather.61.cloned.1.call-done = bf16[16,64,1024]{2,1,0:T(8,128)(2,1)} async-done(((bf16[4,64,1024]{2,1,0:T(8,128)(2,1)}), bf16[16,64,1024]{2,1,0:T(8,128)(2,1)}) %all-gather.61.cloned.1.call-update) | async-done | bytes 2097168 | tf_op jit(solution)/shard_map/all_gather | solution.py:148
  441.7 32.1 %all-gather.57.cloned.1.call-done = bf16[16,64,1024]{2,1,0:T(8,128)(2,1)} async-done(((bf16[4,64,1024]{2,1,0:T(8,128)(2,1)}), bf16[16,64,1024]{2,1,0:T(8,128)(2,1)}) %all-gather.57.cloned.1.call-update) | async-done | bytes 2097168 | tf_op jit(solution)/shard_map/all_gather | solution.py:148
  487.9 32.1 %all-gather.53.cloned.1.call-done = bf16[16,64,1024]{2,1,0:T(8,128)(2,1)} async-done(((bf16[4,64,1024]{2,1,0:T(8,128)(2,1)}), bf16[16,64,1024]{2,1,0:T(8,128)(2,1)}) %all-gather.53.cloned.1.call-update) | async-done | bytes 2097168 | tf_op jit(solution)/shard_map/all_gather | solution.py:148
  544.0 22.3 all-gather.43.cloned.1.call-done
  572.8 39.8 %all-gather.45.cloned.1.call-done = bf16[16,64,1024]{2,1,0:T(8,128)(2,1)} async-done(((bf16[4,64,1024]{2,1,0:T(8,128)(2,1)}), bf16[16,64,1024]{2,1,0:T(8,128)(2,1)}) %all-gather.45.cloned.1.call-update) | async-done | bytes 2097168 | tf_op jit(solution)/shard_map/all_gather | solution.py:145
  619.0 39.7 %all-gather.39.cloned.1.call-done = bf16[16,64,1024]{2,1,0:T(8,128)(2,1)} async-done(((bf16[4,64,1024]{2,1,0:T(8,128)(2,1)}), bf16[16,64,1024]{2,1,0:T(8,128)(2,1)}) %all-gather.39.cloned.1.call-update) | async-done | bytes 2097168 | tf_op jit(solution)/shard_map/all_gather | solution.py:148
  665.1 39.7 %all-gather.41.cloned.1.call-done = bf16[16,64,1024]{2,1,0:T(8,128)(2,1)} async-done(((bf16[4,64,1024]{2,1,0:T(8,128)(2,1)}), bf16[16,64,1024]{2,1,0:T(8,128)(2,1)}) %all-gather.41.cloned.1.call-update) | async-done | bytes 2097168 | tf_op jit(solution)/shard_map/all_gather | solution.py:145
  711.2 39.7 %all-gather.35.cloned.1.call-done = bf16[16,64,1024]{2,1,0:T(8,128)(2,1)} async-done(((bf16[4,64,1024]{2,1,0:T(8,128)(2,1)}), bf16[16,64,1024]{2,1,0:T(8,128)(2,1)}) %all-gather.35.cloned.1.call-update) | async-done | bytes 2097168 | tf_op jit(solution)/shard_map/all_gather | solution.py:148
  757.6 39.4 %all-gather.37.cloned.1.call-done = bf16[16,64,1024]{2,1,0:T(8,128)(2,1)} async-done(((bf16[4,64,1024]{2,1,0:T(8,128)(2,1)}), bf16[16,64,1024]{2,1,0:T(8,128)(2,1)}) %all-gather.37.cloned.1.call-update) | async-done | bytes 2097168 | tf_op jit(solution)/shard_map/all_gather | solution.py:145
  803.4 39.7 %all-gather.31.cloned.1.call-done = bf16[16,64,1024]{2,1,0:T(8,128)(2,1)} async-done(((bf16[4,64,1024]{2,1,0:T(8,128)(2,1)}), bf16[16,64,1024]{2,1,0:T(8,128)(2,1)}) %all-gather.31.cloned.1.call-update) | async-done | bytes 2097168 | tf_op jit(solution)/shard_map/all_gather | solution.py:148
  849.5 39.8 %all-gather.33.cloned.1.call-done = bf16[16,64,1024]{2,1,0:T(8,128)(2,1)} async-done(((bf16[4,64,1024]{2,1,0:T(8,128)(2,1)}), bf16[16,64,1024]{2,1,0:T(8,128)(2,1)}) %all-gather.33.cloned.1.call-update) | async-done | bytes 2097168 | tf_op jit(solution)/shard_map/all_gather | solution.py:145
  974.1 16.4 fusion.34
  990.5 12.1 fusion.36
  1002.6 27.8 %all-gather.51.cloned.1.call-done = bf16[4096,1024]{1,0:T(8,128)(2,1)} async-done(((bf16[512,1024]{1,0:T(8,128)(2,1)}), bf16[4096,1024]{1,0:T(8,128)(2,1)}) %all-gather.51.cloned.1.call-update) | async-done | bytes 8388624 | tf_op jit(solution)/shard_map/all_gather | solution.py:309
  1030.4 27.1 %convert_reduce_fusion = (f32[4096]{0:T(1024)}, bf16[4,256,4096]{2,1,0:T(8,128)(2,1)}) fusion(f32[4,256,4096]{2,1,0:T(8,128)} %fusion.34, f32[4096]{0:T(1024)S(1)} %bitcast.511, bf16[4096,1024]{1,0:T(8,128)(2,1)} %all-gather.51.cloned.1.call-done, f32[2,4,256,1024]{3,2,1,0:T(8,128)} %param.31), kind=kOutput, calls=%fused_computation.22 | convolution fusion | flops 8686399488 | bytes 35684352 | tf_op jit(solution)/shard_map/fse,de->fsd/dot_general | solution.py:35
  1057.5 15.1 fusion.30
  1072.6 27.2 %convert_reduce_fusion.1 = (f32[4096]{0:T(1024)}, bf16[4,256,4096]{2,1,0:T(8,128)(2,1)}) fusion(f32[4,256,4096]{2,1,0:T(8,128)} %fusion.36, f32[4096]{0:T(1024)S(1)} %bitcast.512, bf16[4096,1024]{1,0:T(8,128)(2,1)} %all-gather.51.cloned.1.call-done, f32[2,4,256,1024]{3,2,1,0:T(8,128)} %param.31), kind=kOutput, calls=%fused_computation.23 | convolution fusion | flops 8686399488 | bytes 35684352 | tf_op jit(solution)/shard_map/fse,de->fsd/dot_general | solution.py:35
  1099.8 19.5 fusion.388
  1125.7 14.2 convert_reduce_fusion.2
  1571.6 45.6 %reduce-scatter.44.cloned.1.call-done = bf16[4,64,1024]{2,1,0:T(8,128)(2,1)} async-done(((bf16[16,64,1024]{2,1,0:T(8,128)(2,1)}), bf16[4,64,1024]{2,1,0:T(8,128)(2,1)}) %reduce-scatter.44.cloned.1.call-update) | async-done | bytes 524304 | tf_op jit(solution)/shard_map/reduce_scatter | solution.py:203
  1617.2 45.4 %reduce-scatter.42.cloned.1.call-done = bf16[4,64,1024]{2,1,0:T(8,128)(2,1)} async-done(((bf16[16,64,1024]{2,1,0:T(8,128)(2,1)}), bf16[4,64,1024]{2,1,0:T(8,128)(2,1)}) %reduce-scatter.42.cloned.1.call-update) | async-done | bytes 524304 | tf_op jit(solution)/shard_map/reduce_scatter | solution.py:209
  1662.6 45.6 %reduce-scatter.40.cloned.1.call-done = bf16[4,64,1024]{2,1,0:T(8,128)(2,1)} async-done(((bf16[16,64,1024]{2,1,0:T(8,128)(2,1)}), bf16[4,64,1024]{2,1,0:T(8,128)(2,1)}) %reduce-scatter.40.cloned.1.call-update) | async-done | bytes 524304 | tf_op jit(solution)/shard_map/reduce_scatter | solution.py:203
  1708.2 45.5 %reduce-scatter.38.cloned.1.call-done = bf16[4,64,1024]{2,1,0:T(8,128)(2,1)} async-done(((bf16[16,64,1024]{2,1,0:T(8,128)(2,1)}), bf16[4,64,1024]{2,1,0:T(8,128)(2,1)}) %reduce-scatter.38.cloned.1.call-update) | async-done | bytes 524304 | tf_op jit(solution)/shard_map/reduce_scatter | solution.py:209
  1753.7 45.5 %reduce-scatter.36.cloned.1.call-done = bf16[4,64,1024]{2,1,0:T(8,128)(2,1)} async-done(((bf16[16,64,1024]{2,1,0:T(8,128)(2,1)}), bf16[4,64,1024]{2,1,0:T(8,128)(2,1)}) %reduce-scatter.36.cloned.1.call-update) | async-done | bytes 524304 | tf_op jit(solution)/shard_map/reduce_scatter | solution.py:203
  1799.2 45.4 %reduce-scatter.34.cloned.1.call-done = bf16[4,64,1024]{2,1,0:T(8,128)(2,1)} async-done(((bf16[16,64,1024]{2,1,0:T(8,128)(2,1)}), bf16[4,64,1024]{2,1,0:T(8,128)(2,1)}) %reduce-scatter.34.cloned.1.call-update) | async-done | bytes 524304 | tf_op jit(solution)/shard_map/reduce_scatter | solution.py:209
  1844.5 45.6 %reduce-scatter.32.cloned.1.call-done = bf16[4,64,1024]{2,1,0:T(8,128)(2,1)} async-done(((bf16[16,64,1024]{2,1,0:T(8,128)(2,1)}), bf16[4,64,1024]{2,1,0:T(8,128)(2,1)}) %reduce-scatter.32.cloned.1.call-update) | async-done | bytes 524304 | tf_op jit(solution)/shard_map/reduce_scatter | solution.py:203
  1890.2 15.9 multiply_reduce_fusion.6
  1924.5 16.7 fusion.341
  1941.2 18.1 fusion.15
  1960.0 20.8 fusion.384
  1980.8 23.3 fusion.14
  2040.1 12.5 multiply_convert_fusion
  2097.4 12.7 multiply_reduce_fusion.1
  2110.0 13.1 multiply_convert_fusion.1
  2142.1 15.8 fusion.144
  2157.9 17.1 fusion.19
  2175.7 21.1 fusion.340
  2196.8 22.2 fusion.18
  2231.0 14.9 fusion.387
  2256.6 15.1 add_add_fusion.8
  2302.0 17.4 fusion.192
  2319.5 23.4 all-reduce.2
  2343.0 17.5 fusion.189
  2377.2 36.3 %reduce-scatter.80.cloned.1.call-done = bf16[128,8]{1,0:T(8,128)(2,1)} async-done(((bf16[1024,8]{1,0:T(8,128)(2,1)}), bf16[128,8]{1,0:T(8,128)(2,1)}) %reduce-scatter.80.cloned.1.call-update) | async-done | bytes 2064
  2429.2 144.0 %all-reduce.7.cloned.1.call-done = (bf16[128,3072]{1,0:T(8,128)(2,1)}, bf16[128,1024]{1,0:T(8,128)(2,1)}, bf16[128,3072]{1,0:T(8,128)(2,1)}, bf16[128,1024]{1,0:...) async-done(((bf16[128,3072]{1,0:T(8,128)(2,1)}, bf16[128,1024]{1,0:T(8,128)(2,1)}, bf16[128,3072]{1,0:T(8,128)(2,1)}, bf16[128,1024]{1,0:T(8,128)(2,1)}, ...) | async-done | bytes 4194320 | tf_op jit(solution)/shard_map/psum | solution.py:391
  (868 shorter events, 1158.3 us)
Async XLA Ops:
  7.2 51.0 %all-gather.25.cloned.1.call-start = ((), (), s32[]{:S(2)}) async-start(), calls=%async_computation.25 | async-start | bytes 7077888 | tf_op jit(solution)/shard_map/all_gather | solution.py:303
  7.9 105.5 %all-gather.27.cloned.1.call-start = ((), (), s32[]{:S(2)}) async-start(), calls=%async_computation.26 | async-start | bytes 2359296 | tf_op jit(solution)/shard_map/all_gather | solution.py:304
  8.7 127.1 %all-gather.29.cloned.1.call-start = ((), (), s32[]{:S(2)}) async-start(), calls=%async_computation.27 | async-start | bytes 7077888 | tf_op jit(solution)/shard_map/all_gather | solution.py:305
  9.4 275.6 %all-gather.67.cloned.1.call-start = ((), (), s32[]{:S(2)}) async-start(), calls=%async_computation.46 | async-start | bytes 2621440 | tf_op jit(solution)/shard_map/all_gather | solution.py:145
  150.1 152.1 %all-gather.63.cloned.1.call-start = ((), (), s32[]{:S(2)}) async-start(), calls=%async_computation.44 | async-start | bytes 2621440 | tf_op jit(solution)/shard_map/all_gather | solution.py:145
  150.7 168.2 %all-gather.59.cloned.1.call-start = ((), (), s32[]{:S(2)}) async-start(), calls=%async_computation.42 | async-start | bytes 2621440 | tf_op jit(solution)/shard_map/all_gather | solution.py:145
  151.2 184.6 %all-gather.55.cloned.1.call-start = ((), (), s32[]{:S(2)}) async-start(), calls=%async_computation.40 | async-start | bytes 2621440 | tf_op jit(solution)/shard_map/all_gather | solution.py:145
  152.0 229.5 %all-gather.65.cloned.1.call-start = ((), (), s32[]{:S(2)}) async-start(), calls=%async_computation.45 | async-start | bytes 2621440 | tf_op jit(solution)/shard_map/all_gather | solution.py:148
  152.7 275.0 %all-gather.61.cloned.1.call-start = ((), (), s32[]{:S(2)}) async-start(), calls=%async_computation.43 | async-start | bytes 2621440 | tf_op jit(solution)/shard_map/all_gather | solution.py:148
  153.5 320.3 %all-gather.57.cloned.1.call-start = ((), (), s32[]{:S(2)}) async-start(), calls=%async_computation.41 | async-start | bytes 2621440 | tf_op jit(solution)/shard_map/all_gather | solution.py:148
  159.2 360.9 %all-gather.53.cloned.1.call-start = ((), (), s32[]{:S(2)}) async-start(), calls=%async_computation.39 | async-start | bytes 2621440 | tf_op jit(solution)/shard_map/all_gather | solution.py:148
  203.0 363.3 %all-gather.43.cloned.1.call-start = ((), (), s32[]{:S(2)}) async-start(), calls=%async_computation.34 | async-start | bytes 2621440 | tf_op jit(solution)/shard_map/all_gather | solution.py:148
  229.4 383.2 %all-gather.45.cloned.1.call-start = ((), (), s32[]{:S(2)}) async-start(), calls=%async_computation.35 | async-start | bytes 2621440 | tf_op jit(solution)/shard_map/all_gather | solution.py:145
  230.2 428.5 %all-gather.39.cloned.1.call-start = ((), (), s32[]{:S(2)}) async-start(), calls=%async_computation.32 | async-start | bytes 2621440 | tf_op jit(solution)/shard_map/all_gather | solution.py:148
  230.7 474.0 %all-gather.41.cloned.1.call-start = ((), (), s32[]{:S(2)}) async-start(), calls=%async_computation.33 | async-start | bytes 2621440 | tf_op jit(solution)/shard_map/all_gather | solution.py:145
  231.3 519.6 %all-gather.35.cloned.1.call-start = ((), (), s32[]{:S(2)}) async-start(), calls=%async_computation.30 | async-start | bytes 2621440 | tf_op jit(solution)/shard_map/all_gather | solution.py:148
  231.9 565.1 %all-gather.37.cloned.1.call-start = ((), (), s32[]{:S(2)}) async-start(), calls=%async_computation.31 | async-start | bytes 2621440 | tf_op jit(solution)/shard_map/all_gather | solution.py:145
  232.5 610.6 %all-gather.31.cloned.1.call-start = ((), (), s32[]{:S(2)}) async-start(), calls=%async_computation.28 | async-start | bytes 2621440 | tf_op jit(solution)/shard_map/all_gather | solution.py:148
  233.1 656.3 %all-gather.33.cloned.1.call-start = ((), (), s32[]{:S(2)}) async-start(), calls=%async_computation.29 | async-start | bytes 2621440 | tf_op jit(solution)/shard_map/all_gather | solution.py:145
  233.8 715.6 %all-gather.47.cloned.1.call-start = ((), (), s32[]{:S(2)}) async-start(), calls=%async_computation.36 | async-start | bytes 2359296 | tf_op jit(solution)/shard_map/all_gather | solution.py:306
  234.4 739.6 %all-gather.49.cloned.1.call-start = ((), (), s32[]{:S(2)}) async-start(), calls=%async_computation.37 | async-start | bytes 9437184 | tf_op jit(solution)/shard_map/all_gather | solution.py:307
  235.1 795.2 %all-gather.51.cloned.1.call-start = ((), (), s32[]{:S(2)}) async-start(), calls=%async_computation.38 | async-start | bytes 9437184 | tf_op jit(solution)/shard_map/all_gather | solution.py:309
  235.9 1320.3 %reduce-scatter.62.cloned.1.call-start = ((), (), s32[]{:S(2)}) async-start(), calls=%async_computation.62 | async-start | bytes 2621440 | tf_op jit(solution)/shard_map/reduce_scatter | solution.py:209
  1163.6 392.6 %reduce-scatter.60.cloned.1.call-start = ((), (), s32[]{:S(2)}) async-start(), calls=%async_computation.61 | async-start | bytes 2621440 | tf_op jit(solution)/shard_map/reduce_scatter | solution.py:203
  1185.8 370.5 %reduce-scatter.58.cloned.1.call-start = ((), (), s32[]{:S(2)}) async-start(), calls=%async_computation.60 | async-start | bytes 2621440 | tf_op jit(solution)/shard_map/reduce_scatter | solution.py:209
  1204.7 351.6 %reduce-scatter.56.cloned.1.call-start = ((), (), s32[]{:S(2)}) async-start(), calls=%async_computation.59 | async-start | bytes 2621440 | tf_op jit(solution)/shard_map/reduce_scatter | solution.py:203
  1227.9 328.4 %reduce-scatter.54.cloned.1.call-start = ((), (), s32[]{:S(2)}) async-start(), calls=%async_computation.58 | async-start | bytes 2621440 | tf_op jit(solution)/shard_map/reduce_scatter | solution.py:209
  1247.3 309.0 %reduce-scatter.52.cloned.1.call-start = ((), (), s32[]{:S(2)}) async-start(), calls=%async_computation.57 | async-start | bytes 2621440 | tf_op jit(solution)/shard_map/reduce_scatter | solution.py:203
  1270.4 285.9 %reduce-scatter.50.cloned.1.call-start = ((), (), s32[]{:S(2)}) async-start(), calls=%async_computation.56 | async-start | bytes 2621440 | tf_op jit(solution)/shard_map/reduce_scatter | solution.py:209
  1289.5 266.9 %reduce-scatter.48.cloned.1.call-start = ((), (), s32[]{:S(2)}) async-start(), calls=%async_computation.55 | async-start | bytes 2621440 | tf_op jit(solution)/shard_map/reduce_scatter | solution.py:203
  1312.7 258.9 %reduce-scatter.46.cloned.1.call-start = ((), (), s32[]{:S(2)}) async-start(), calls=%async_computation.54 | async-start | bytes 2621440 | tf_op jit(solution)/shard_map/reduce_scatter | solution.py:209
  1338.1 279.1 %reduce-scatter.44.cloned.1.call-start = ((), (), s32[]{:S(2)}) async-start(), calls=%async_computation.53 | async-start | bytes 2621440 | tf_op jit(solution)/shard_map/reduce_scatter | solution.py:203
  1361.2 301.4 %reduce-scatter.42.cloned.1.call-start = ((), (), s32[]{:S(2)}) async-start(), calls=%async_computation.52 | async-start | bytes 2621440 | tf_op jit(solution)/shard_map/reduce_scatter | solution.py:209
  1380.3 327.9 %reduce-scatter.40.cloned.1.call-start = ((), (), s32[]{:S(2)}) async-start(), calls=%async_computation.51 | async-start | bytes 2621440 | tf_op jit(solution)/shard_map/reduce_scatter | solution.py:203
  1403.6 350.2 %reduce-scatter.38.cloned.1.call-start = ((), (), s32[]{:S(2)}) async-start(), calls=%async_computation.50 | async-start | bytes 2621440 | tf_op jit(solution)/shard_map/reduce_scatter | solution.py:209
  1423.0 376.2 %reduce-scatter.36.cloned.1.call-start = ((), (), s32[]{:S(2)}) async-start(), calls=%async_computation.49 | async-start | bytes 2621440 | tf_op jit(solution)/shard_map/reduce_scatter | solution.py:203
  1446.4 398.2 %reduce-scatter.34.cloned.1.call-start = ((), (), s32[]{:S(2)}) async-start(), calls=%async_computation.48 | async-start | bytes 2621440 | tf_op jit(solution)/shard_map/reduce_scatter | solution.py:209
  1465.5 424.6 %reduce-scatter.32.cloned.1.call-start = ((), (), s32[]{:S(2)}) async-start(), calls=%async_computation.47 | async-start | bytes 2621440 | tf_op jit(solution)/shard_map/reduce_scatter | solution.py:203
  1494.8 797.0 %reduce-scatter.70.cloned.1.call-start = ((), (), s32[]{:S(2)}) async-start(), calls=%async_computation.66 | async-start | bytes 2359296 | tf_op jit(solution)/shard_map/reduce_scatter | solution.py:356
  1556.2 735.7 %reduce-scatter.66.cloned.1.call-start = ((), (), s32[]{:S(2)}) async-start(), calls=%async_computation.64 | async-start | bytes 2359296 | tf_op jit(solution)/shard_map/reduce_scatter | solution.py:350
  1924.0 367.9 %reduce-scatter.72.cloned.1.call-start = ((), (), s32[]{:S(2)}) async-start(), calls=%async_computation.67 | async-start | bytes 9437184 | tf_op jit(solution)/shard_map/reduce_scatter | solution.py:359
  1959.3 332.6 %reduce-scatter.74.cloned.1.call-start = ((), (), s32[]{:S(2)}) async-start(), calls=%async_computation.68 | async-start | bytes 9437184 | tf_op jit(solution)/shard_map/reduce_scatter | solution.py:365
  2004.2 287.7 %reduce-scatter.64.cloned.1.call-start = ((), (), s32[]{:S(2)}) async-start(), calls=%async_computation.63 | async-start | bytes 7077888 | tf_op jit(solution)/shard_map/reduce_scatter | solution.py:347
  2175.1 126.9 %reduce-scatter.68.cloned.1.call-start = ((), (), s32[]{:S(2)}) async-start(), calls=%async_computation.65 | async-start | bytes 7077888 | tf_op jit(solution)/shard_map/reduce_scatter | solution.py:353
  2219.0 150.7 %reduce-scatter.76.cloned.1.call-start = ((), (), s32[]{:S(2)}) async-start(), calls=%async_computation.69 | async-start | bytes 294912
  2275.1 101.3 %reduce-scatter.78.cloned.1.call-start = ((), (), s32[]{:S(2)}) async-start(), calls=%async_computation.70 | async-start | bytes 294912
  2276.2 137.3 %reduce-scatter.80.cloned.1.call-start = ((), (), s32[]{:S(2)}) async-start(), calls=%async_computation.71 | async-start | bytes 294912
  2281.1 292.0 %all-reduce.7.cloned.1.call-start = ((), (), s32[]{:S(2)}) async-start(), calls=%async_computation.72 | async-start | bytes 8388608 | tf_op jit(solution)/shard_map/psum | solution.py:391
  (222 other events, 6923.2 us)
Sparse Core Ops, SparseCore 0:
  9.9 48.2 all-gather.24
  60.1 27.8 all-gather.26
  89.9 45.5 all-gather.28
  150.2 45.9 all-gather.66
  197.6 44.6 all-gather.62
  243.7 44.6 all-gather.58
  290.5 44.6 all-gather.54
  336.8 44.6 all-gather.64
  383.0 44.6 all-gather.60
  429.1 44.6 all-gather.56
  475.4 44.6 all-gather.52
  521.5 44.7 all-gather.42
  567.9 44.6 all-gather.44
  614.0 44.6 all-gather.38
  660.1 44.6 all-gather.40
  706.2 44.6 all-gather.34
  752.3 44.6 all-gather.36
  798.4 44.6 all-gather.30
  844.7 44.6 all-gather.32
  891.1 26.5 all-gather.46
  919.6 54.3 all-gather.48
  975.9 54.3 all-gather.50
  1163.7 43.8 reduce-scatter.61
  1209.9 43.1 reduce-scatter.59
  1255.4 43.1 reduce-scatter.57
  1300.9 43.1 reduce-scatter.55
  1346.2 43.1 reduce-scatter.53
  1391.8 43.2 reduce-scatter.51
  1437.4 43.1 reduce-scatter.49
  1482.9 43.1 reduce-scatter.47
  1528.4 43.1 reduce-scatter.45
  1574.0 43.1 reduce-scatter.43
  1619.4 43.1 reduce-scatter.41
  1665.0 43.1 reduce-scatter.39
  1710.5 43.1 reduce-scatter.37
  1756.0 43.1 reduce-scatter.35
  1801.3 43.1 reduce-scatter.33
  1846.9 43.1 reduce-scatter.31
  1893.3 40.5 reduce-scatter.69
  1937.5 41.2 reduce-scatter.65
  1982.2 71.2 reduce-scatter.71
  2057.4 71.2 reduce-scatter.73
  2175.1 61.2 reduce-scatter.63
  2240.1 61.7 reduce-scatter.67
  2305.4 33.5 reduce-scatter.75
  2342.7 33.6 reduce-scatter.77
  2379.8 33.6 reduce-scatter.79
  2416.4 156.7 all-reduce.6
where the time goes:
time: 2600 us; the launch traced here: 2590 us
  waiting for transfers between devices  1010 us (39%)
  matrix products  838 us (32%)
  local copies, waits for them, and re-layouts  464 us (18%)
  other arithmetic  175 us (7%)
  blocking collectives  80.4 us (3%)
    all_gather x8, waiting for transfers between devices, one_batch(): lax.all_gather(block_cols[..., 2 * model_width:], 'tm', axis=0, tiled=True)  267 us
    reduce_scatter x8, waiting for transfers between devices, one_batch(): lax.psum_scatter(grad_key.reshape(frames_all, block_width, model_width).a...  182 us
    dot_general x12, matrix products, weight_grad(): jnp.einsum('fsd,fse->de', left, right, preferred_element_type=jnp.float32)  170 us
    dot_general x12, matrix products, project_back(): jnp.einsum('fse,de->fsd', left, right, preferred_element_type=jnp.float32)  163 us
    all_gather x8, waiting for transfers between devices, one_batch(): lax.all_gather(block_cols[..., model_width:2 * model_width], 'tm', axis=0...  159 us
    psum x1, waiting for transfers between devices, local(): lax.psum(space_in_part.astype(jnp.bfloat16), 'tm').astype(jnp.float32)  144 us
    reduce_scatter x8, waiting for transfers between devices, one_batch(): lax.psum_scatter(grad_value.reshape(frames_all, block_width, model_width)...  140 us
    dot_general x12, matrix products, project(): jnp.einsum('fsd,de->fse', left, right, preferred_element_type=jnp.float32)  132 us
  transfers between devices with their start and end apart: 48, of which 27 were waited for; matrix products, arithmetic and copies ran while one was open for 49% of the time, Pallas kernels for 0%

commit v1 on v0

v1 whole, which is shorter than its diff:
```python
import functools

import jax
import jax.numpy as jnp
from jax import lax
from jax.experimental import pallas as pl
from jax.experimental.pallas import tpu as pltpu
from jax.sharding import PartitionSpec as P

HEADS = 16
HEAD = 64
EPS = 1e-05
MASKED = -1e30
ROWS = 256
CHUNK = 1024
VMEM_LIMIT = 62 * 1024 * 1024

bf16 = jnp.bfloat16
f32 = jnp.float32

NN = (((1,), (0,)), ((), ()))
NT = (((1,), (1,)), ((), ()))
TN = (((0,), (0,)), ((), ()))


def dot(left, right, form=NN):
    return lax.dot_general(left, right, form, preferred_element_type=f32)


def standardize(values):
    centered = values - jnp.mean(values, axis=-1, keepdims=True)
    rate = lax.rsqrt(jnp.mean(centered * centered, axis=-1, keepdims=True) + EPS)
    return centered * rate, rate


def norm_back(hat, rate, gain, grad):
    scaled = grad * gain
    return rate * (
        scaled
        - jnp.mean(scaled, axis=-1, keepdims=True)
        - hat * jnp.mean(scaled * hat, axis=-1, keepdims=True)
    )


def add_row(ref, row, first):
    @pl.when(first)
    def _():
        ref[...] = row

    @pl.when(jnp.logical_not(first))
    def _():
        ref[...] += row


def column_sum(values):
    return jnp.sum(values, axis=0, keepdims=True)


def pair_slices(pair):
    lane = pair * 128
    return slice(lane, lane + 128), slice(1024 + lane, 1024 + lane + 128), slice(2048 + lane, 2048 + lane + 128)


def attend(qkv_ref, key_mask, query_mask, mixed_t, lse_ref):
    blank = jnp.zeros((HEAD, ROWS), bf16)
    for pair in range(HEADS // 2):
        q_at, k_at, v_at = pair_slices(pair)
        q_t = (qkv_ref[:, q_at] * jnp.asarray(HEAD**-0.5, bf16)).T
        v_t = qkv_ref[:, v_at].T
        keys = jnp.concatenate([qkv_ref[:, k_at], key_mask], axis=1)
        for part in range(2):
            head = pair * 2 + part
            half = slice(part * HEAD, (part + 1) * HEAD)
            parts = [q_t[half], blank] if part == 0 else [blank, q_t[half]]
            scores = dot(keys, jnp.concatenate(parts + [query_mask], axis=0))
            top = jnp.max(scores, axis=0, keepdims=True)
            raised = jnp.exp(scores - top)
            total = jnp.sum(raised, axis=0, keepdims=True)
            mixed = dot(v_t[half], raised.astype(bf16))
            mixed_t[head * HEAD : (head + 1) * HEAD, :] = (mixed * (1.0 / total)).astype(bf16)
            lse_ref[head : head + 1, :] = top + jnp.log(total)


def attend_back(qkv_ref, key_mask, query_mask, lse_ref, grad_ref, grad_t, mixed_t, out_ref, query_t):
    blank = jnp.zeros((HEAD, ROWS), bf16)
    scale = jnp.asarray(HEAD**-0.5, bf16)
    low_half = lax.broadcasted_iota(jnp.int32, (ROWS, 128), 1) < HEAD
    for pair in range(HEADS // 2):
        q_at, k_at, v_at = pair_slices(pair)
        queries = qkv_ref[:, q_at] * scale
        keys = qkv_ref[:, k_at]
        values = qkv_ref[:, v_at]
        grads = grad_ref[:, q_at]
        q_t = queries.T
        k_t = (keys * scale).T
        keys_masked = jnp.concatenate([keys, key_mask], axis=1)
        grad_keys = grad_values = None
        for part in range(2):
            head = pair * 2 + part
            half = slice(part * HEAD, (part + 1) * HEAD)
            at = slice(head * HEAD, (head + 1) * HEAD)
            parts = [q_t[half], blank] if part == 0 else [blank, q_t[half]]
            scores = dot(keys_masked, jnp.concatenate(parts + [query_mask], axis=0))
            probs = jnp.exp(scores - lse_ref[head : head + 1, :])
            head_grad = grad_t[at, :]
            grad_parts = [head_grad, blank] if part == 0 else [blank, head_grad]
            grad_probs = dot(values, jnp.concatenate(grad_parts, axis=0))
            along = jnp.sum(head_grad.astype(f32) * mixed_t[at, :].astype(f32), axis=0, keepdims=True)
            grad_scores = (probs * (grad_probs - along)).astype(bf16)
            keep = low_half if part == 0 else jnp.logical_not(low_half)
            zero = jnp.zeros_like(queries)
            gv = dot(probs.astype(bf16), jnp.where(keep, grads, zero))
            gk = dot(grad_scores, jnp.where(keep, queries, zero))
            grad_values = gv if grad_values is None else grad_values + gv
            grad_keys = gk if grad_keys is None else grad_keys + gk
            query_t[at, :] = dot(k_t[half], grad_scores).astype(bf16)
        out_ref[:, k_at] = grad_keys.astype(bf16)
        out_ref[:, v_at] = grad_values.astype(bf16)
    for quarter in range(4):
        at = slice(quarter * 256, (quarter + 1) * 256)
        out_ref[:, at] = query_t[at, :].T


def block_of(weights, index):
    own = 1024 // weights.shape[0]
    return weights[:, index * own : (index + 1) * own, :].reshape(1024, 1024)


def piece_at(place, step, count, rows):
    return pl.ds(pl.multiple_of(lax.rem(place[0] + step, count) * rows, rows), rows)


def stacked(refs):
    parts = [ref[...].reshape(-1, ref.shape[-1]) for ref in refs]
    return parts[0] if len(parts) == 1 else jnp.concatenate(parts, axis=0)


def unstack(refs, values):
    rows = values.shape[0] // len(refs)
    for index, ref in enumerate(refs):
        ref[...] = values[index * rows : (index + 1) * rows].reshape(ref.shape)


def space_forward(
    place, tok, hot, kmask, qmask, gain, bias, table, weights,
    norm_out, qkv_out, mix_out, lse_out, *rest,
):
    after_out, (mixed_t, after) = rest[:-2], rest[-2:]
    embedded = tok[...].astype(f32) + dot(hot[...], table[...])
    hat, _ = standardize(embedded)
    normed = (hat * gain[0:1, :] + bias[0:1, :]).astype(bf16)
    norm_out[...] = normed
    for part in range(3):
        qkv_out[:, part * 1024 : (part + 1) * 1024] = dot(normed, block_of(weights, part)).astype(bf16)
    attend(qkv_out, kmask[...], qmask[...], mixed_t, lse_out)
    mixed = mixed_t[...].T
    mix_out[...] = mixed
    after[...] = (embedded + dot(mixed, block_of(weights, 3))).astype(bf16)
    count = len(after_out)
    for step in range(count):
        after_out[step][...] = after[piece_at(place, step, count, ROWS // count), :]


def grad_into_norm(gqkv, weights):
    total = None
    for part in range(3):
        piece = dot(gqkv[:, part * 1024 : (part + 1) * 1024], block_of(weights, part), NT)
        total = piece if total is None else total + piece
    return total


def space_backward(count, *refs):
    grads, refs = refs[:count], refs[count:]
    (
        place, tok, hot, kmask, qmask, gain, table, weights, qkv, mix, lse,
        gqkv_out, gas_out, tok_out, gain_out, bias_out, table_out, grad_t, mixed_t, query_t, grad_rows,
    ) = refs
    first = pl.program_id(0) == 0
    for step in range(count):
        gas_out[piece_at(place, step, count, ROWS // count), :] = grads[step][...]
    upstream = gas_out[...]
    mixed_t[...] = mix[...].T
    grad_rows[...] = dot(upstream, block_of(weights, 3), NT).astype(bf16)
    grad_t[...] = grad_rows[...].T
    attend_back(qkv, kmask[...], qmask[...], lse, grad_rows, grad_t, mixed_t, gqkv_out, query_t)
    grad_norm = grad_into_norm(gqkv_out, weights)
    embedded = tok[...].astype(f32) + dot(hot[...], table[...])
    hat, rate = standardize(embedded)
    add_row(gain_out, column_sum(grad_norm * hat), first)
    add_row(bias_out, column_sum(grad_norm), first)
    total = upstream.astype(f32) + norm_back(hat, rate, gain[0:1, :], grad_norm)
    tok_out[...] = total
    add_row(table_out, dot(hot[...], total.astype(bf16), TN), first)


def time_forward(count, *refs):
    x, refs = refs[:count], refs[count:]
    kmask, qmask, gain, bias, weights, norm_out, qkv_out, mix_out, lse_out, after_out, mixed_t = refs
    after_space = stacked(x).astype(f32)
    hat, _ = standardize(after_space)
    normed = (hat * gain[1:2, :] + bias[1:2, :]).astype(bf16)
    norm_out[...] = normed
    for part in range(3):
        qkv_out[:, part * 1024 : (part + 1) * 1024] = dot(normed, block_of(weights, part)).astype(bf16)
    attend(qkv_out, kmask[...], qmask[...], mixed_t, lse_out)
    mixed = mixed_t[...].T
    mix_out[...] = mixed
    after_out[...] = after_space + dot(mixed, block_of(weights, 3))


def feed_forward(count, *refs):
    grad, refs = refs[:count], refs[count:]
    x, gain, bias, hidden_bias, out_bias, weights = refs[:6]
    norm_out, act_out, gpre_out, gat_out, branch_out, gain_out, bias_out, hb_out, ob_out = refs[6:15]
    block_out = refs[15:]
    first = pl.program_id(0) == 0
    after_time = x[...]
    hat, rate = standardize(after_time)
    normed = (hat * gain[2:3, :] + bias[2:3, :]).astype(bf16)
    norm_out[...] = normed
    branch = stacked(grad)
    branch_out[...] = branch
    clips = weights.shape[0]
    own = 1024 // clips
    per_chunk = clips // 4
    result = None
    grad_norm = None
    for chunk in range(4):
        at = slice(chunk * 1024, (chunk + 1) * 1024)
        w_hidden = block_of(weights, chunk)
        w_down = weights[chunk * per_chunk : (chunk + 1) * per_chunk, 4 * own :, :].reshape(1024, 1024)
        u = dot(normed, w_hidden) + hidden_bias[0:1, at]
        c0 = 0.7978845608028654
        square = u * u
        t = jnp.tanh(u * (c0 + (c0 * 0.044715) * square))
        half_plus = 0.5 + 0.5 * t
        act = (u * half_plus).astype(bf16)
        act_out[:, at] = act
        down = dot(act, w_down)
        result = down if result is None else result + down
        slope = half_plus + (0.5 * u) * (1.0 - t * t) * (c0 + (3.0 * c0 * 0.044715) * square)
        gpre = (dot(branch, w_down, NT) * slope).astype(bf16)
        gpre_out[:, at] = gpre
        back = dot(gpre, w_hidden, NT)
        grad_norm = back if grad_norm is None else grad_norm + back
    block = (after_time + result + out_bias[0:1, :]).astype(bf16)
    unstack(block_out, block)
    upstream = branch.astype(f32)
    gat_out[...] = (upstream + norm_back(hat, rate, gain[2:3, :], grad_norm)).astype(bf16)
    add_row(gain_out, column_sum(grad_norm * hat), first)
    add_row(bias_out, column_sum(grad_norm), first)
    add_row(ob_out, column_sum(upstream), first)
    add_row(hb_out, column_sum(gpre_out[...].astype(f32)), first)


def time_backward(count, *refs):
    x, refs = refs[:count], refs[count:]
    gat, kmask, qmask, gain, weights, qkv, mix, lse, gqkv_out, gain_out, bias_out = refs[:11]
    gas_out = refs[11 : 11 + count]
    grad_t, mixed_t, query_t, grad_rows = refs[11 + count :]
    first = pl.program_id(0) == 0
    upstream = gat[...]
    mixed_t[...] = mix[...].T
    grad_rows[...] = dot(upstream, block_of(weights, 3), NT).astype(bf16)
    grad_t[...] = grad_rows[...].T
    attend_back(qkv, kmask[...], qmask[...], lse, grad_rows, grad_t, mixed_t, gqkv_out, query_t)
    grad_norm = grad_into_norm(gqkv_out, weights)
    hat, rate = standardize(stacked(x).astype(f32))
    add_row(gain_out, column_sum(grad_norm * hat), first)
    add_row(bias_out, column_sum(grad_norm), first)
    total = upstream.astype(f32) + norm_back(hat, rate, gain[1:2, :], grad_norm)
    unstack(gas_out, total.astype(bf16))


def assemble(count, *refs):
    place, parts, out = refs[0], refs[1:-1], refs[-1]
    for micro in range(out.shape[0]):
        for step in range(count):
            out[micro, piece_at(place, step, count, ROWS // count), :] = parts[micro * count + step][...]


def rows_of(ref):
    value = ref[...]
    return value.reshape(-1, value.shape[-1])


def weight_kernel(pairs, micros, own, by_rows, has_small, *refs):
    out = refs[-1]
    offset = 0
    for pair in range(pairs):
        base = pair * 2 * micros
        total = None
        for index in range(micros):
            piece = dot(rows_of(refs[base + index]), rows_of(refs[base + micros + index]), TN)
            total = piece if total is None else total + piece
        total = total.astype(bf16)
        if by_rows:
            out[0] = total
            continue
        for block in range(total.shape[1] // 1024):
            for shard in range(out.shape[0]):
                out[shard, offset : offset + own, :] = total[
                    shard * own : (shard + 1) * own, block * 1024 : (block + 1) * 1024
                ]
            offset += own
    if has_small:
        out[:, offset:, :] = refs[pairs * 2 * micros][...]


def params():
    return pltpu.CompilerParams(vmem_limit_bytes=VMEM_LIMIT)


def ordered_call(kernel, behind, in_specs, **options):
    count = len(behind)

    def body(*refs):
        kernel(*refs[count:])

    aliases = options.pop("input_output_aliases", {})
    call = pl.pallas_call(
        body,
        in_specs=[pl.BlockSpec(memory_space=pl.ANY)] * count + in_specs,
        input_output_aliases={count + k: v for k, v in aliases.items()},
        compiler_params=params(),
        **options,
    )
    return lambda *operands: call(*behind, *operands)


def whole(shape):
    rank = len(shape)
    return pl.BlockSpec(shape, lambda i: (0,) * rank, pipeline_mode=pl.Buffered(1))


def total_spec(shape):
    rank = len(shape)
    return pl.BlockSpec(shape, lambda i: (0,) * rank)


def step_spec(shape):
    rank = len(shape)
    return pl.BlockSpec((None,) + shape, lambda i: (i,) + (0,) * rank)


def micro_spec(micro, shape):
    rank = len(shape)
    return pl.BlockSpec((None, None) + shape, lambda i: (micro, i) + (0,) * rank)


def shape_of(shape, kind):
    return jax.ShapeDtypeStruct(shape, kind)


def smem():
    return pl.BlockSpec(memory_space=pltpu.SMEM)


def call_space_forward(behind, micro, place, tok, hot, kmask, qmask, gain, bias, table, weights, count):
    _, frames, slots, width = tok.shape
    per = slots // count
    return ordered_call(
        space_forward,
        behind,
        grid=(frames,),
        in_specs=[smem(), micro_spec(micro, (slots, width)), step_spec(hot.shape[1:])]
        + [whole(a.shape) for a in (kmask, qmask, gain, bias, table, weights)],
        out_specs=[
            step_spec((slots, width)), step_spec((slots, 3 * width)), step_spec((slots, width)),
            step_spec((HEADS, slots)),
        ]
        + [step_spec((per, width))] * count,
        out_shape=[
            shape_of((frames, slots, width), bf16), shape_of((frames, slots, 3 * width), bf16),
            shape_of((frames, slots, width), bf16), shape_of((frames, HEADS, slots), f32),
        ]
        + [shape_of((frames, per, width), bf16)] * count,
        scratch_shapes=[pltpu.VMEM((width, ROWS), bf16), pltpu.VMEM((ROWS, width), bf16)],
        name="space_forward",
    )(place, tok, hot, kmask, qmask, gain, bias, table, weights)


def back_scratch(width):
    return [
        pltpu.VMEM((width, ROWS), bf16), pltpu.VMEM((width, ROWS), bf16),
        pltpu.VMEM((width, ROWS), bf16), pltpu.VMEM((ROWS, width), bf16),
    ]


def call_space_backward(
    behind, micro, grads, place, tok, hot, kmask, qmask, gain, table, weights, qkv, mix, lse, buffer
):
    micros, frames, slots, width = tok.shape
    count = len(grads)
    row = shape_of((1, width), f32)
    operands = list(grads) + [place, tok, hot, kmask, qmask, gain, table, weights, qkv, mix, lse]
    specs = (
        [step_spec((slots // count, width))] * count
        + [smem(), micro_spec(micro, (slots, width)), step_spec(hot.shape[1:])]
        + [whole(a.shape) for a in (kmask, qmask, gain, table, weights)]
        + [step_spec((slots, 3 * width)), step_spec((slots, width)), step_spec((HEADS, slots))]
    )
    before = len(operands)
    kernel = functools.partial(space_backward, count)
    aliases = {}
    if buffer is not None:
        aliases = {before: 2}
        operands.append(buffer)
        specs.append(pl.BlockSpec(memory_space=pl.ANY))
        kernel = lambda *refs: space_backward(count, *refs[:before], *refs[before + 1 :])
    return ordered_call(
        kernel,
        behind,
        grid=(frames,),
        in_specs=specs,
        out_specs=[
            step_spec((slots, 3 * width)), step_spec((slots, width)), micro_spec(micro, (slots, width)),
            total_spec((1, width)), total_spec((1, width)), total_spec((hot.shape[2], width)),
        ],
        out_shape=[
            shape_of((frames, slots, 3 * width), bf16), shape_of((frames, slots, width), bf16),
            shape_of((micros, frames, slots, width), f32), row, row, shape_of((hot.shape[2], width), f32),
        ],
        scratch_shapes=back_scratch(width),
        input_output_aliases=aliases,
        name="space_backward",
    )(*operands)


def group_spec(array, count):
    frames, _, width = array.shape
    return pl.BlockSpec((frames, ROWS // (frames * count), width), lambda i: (0, i, 0))


def call_time_forward(behind, x, kmask, qmask, gain, bias, weights):
    count = len(x)
    frames, slots, width = x[0].shape
    groups = slots * frames * count // ROWS
    return ordered_call(
        functools.partial(time_forward, count),
        behind,
        grid=(groups,),
        in_specs=[group_spec(a, count) for a in x] + [whole(a.shape) for a in (kmask, qmask, gain, bias, weights)],
        out_specs=[
            step_spec((ROWS, width)), step_spec((ROWS, 3 * width)), step_spec((ROWS, width)),
            step_spec((HEADS, ROWS)), step_spec((ROWS, width)),
        ],
        out_shape=[
            shape_of((groups, ROWS, width), bf16), shape_of((groups, ROWS, 3 * width), bf16),
            shape_of((groups, ROWS, width), bf16), shape_of((groups, HEADS, ROWS), f32),
            shape_of((groups, ROWS, width), f32),
        ],
        scratch_shapes=[pltpu.VMEM((width, ROWS), bf16)],
        name="time_forward",
    )(*x, kmask, qmask, gain, bias, weights)


def call_feed_forward(behind, grad, x, gain, bias, hidden_bias, out_bias, weights):
    count = len(grad)
    groups, _, width = x.shape
    ff = hidden_bias.shape[1]
    row = shape_of((1, width), f32)
    rows = lambda cols: shape_of((groups, ROWS, cols), bf16)
    return ordered_call(
        functools.partial(feed_forward, count),
        behind,
        grid=(groups,),
        in_specs=[group_spec(a, count) for a in grad]
        + [step_spec((ROWS, width))]
        + [whole(a.shape) for a in (gain, bias, hidden_bias, out_bias, weights)],
        out_specs=[
            step_spec((ROWS, width)), step_spec((ROWS, ff)), step_spec((ROWS, ff)),
            step_spec((ROWS, width)), step_spec((ROWS, width)),
            total_spec((1, width)), total_spec((1, width)), total_spec((1, ff)), total_spec((1, width)),
        ]
        + [group_spec(a, count) for a in grad],
        out_shape=[rows(width), rows(ff), rows(ff), rows(width), rows(width), row, row, shape_of((1, ff), f32), row]
        + [shape_of(a.shape, bf16) for a in grad],
        name="feed_forward",
    )(*grad, x, gain, bias, hidden_bias, out_bias, weights)


def call_time_backward(behind, x, gat, kmask, qmask, gain, weights, qkv, mix, lse):
    count = len(x)
    groups, _, width = gat.shape
    row = shape_of((1, width), f32)
    return ordered_call(
        functools.partial(time_backward, count),
        behind,
        grid=(groups,),
        in_specs=[group_spec(a, count) for a in x]
        + [step_spec((ROWS, width))]
        + [whole(a.shape) for a in (kmask, qmask, gain, weights)]
        + [step_spec((ROWS, 3 * width)), step_spec((ROWS, width)), step_spec((HEADS, ROWS))],
        out_specs=[step_spec((ROWS, 3 * width)), total_spec((1, width)), total_spec((1, width))]
        + [group_spec(a, count) for a in x],
        out_shape=[shape_of((groups, ROWS, 3 * width), bf16), row, row] + [shape_of(a.shape, bf16) for a in x],
        scratch_shapes=back_scratch(width),
        name="time_backward",
    )(*x, gat, kmask, qmask, gain, weights, qkv, mix, lse)


def call_assemble(place, parts):
    micros, count = len(parts), len(parts[0])
    frames, per, width = parts[0][0].shape
    flat = [p for pieces in parts for p in pieces]
    return ordered_call(
        functools.partial(assemble, count),
        [],
        grid=(frames,),
        in_specs=[smem()] + [step_spec((per, width))] * len(flat),
        out_specs=pl.BlockSpec((micros, None, per * count, width), lambda i: (0, i, 0, 0)),
        out_shape=shape_of((micros, frames, per * count, width), bf16),
        name="assemble",
    )(place, *flat)


def weight_grad(behind, pairs, clips, rows, name, small=None, buffer=None, down_at=None):
    own = 1024 // clips
    block = 256
    width = pairs[0][0][0].shape[-1]
    by_rows = down_at is not None

    def left_spec(a):
        rank = a.ndim
        return pl.BlockSpec(a.shape[:-1] + (block,), lambda i: (0,) * (rank - 1) + (i,))

    operands, specs = [], []
    cols = 0
    for lefts, rights in pairs:
        operands += list(lefts) + list(rights)
        specs += [left_spec(a) for a in lefts] + [whole(a.shape) for a in rights]
        cols += rights[0].shape[-1]
    shards = block // own
    if small is not None:
        operands.append(small)
        specs.append(pl.BlockSpec((shards,) + small.shape[1:], lambda i: (i, 0, 0)))
    aliases = {}
    if buffer is not None:
        aliases = {len(operands): 0}
        operands.append(buffer)
        specs.append(pl.BlockSpec(memory_space=pl.ANY))
    if by_rows:
        steps = width // clips // block
        out_spec = pl.BlockSpec((1, block, 1024), lambda i: (i // steps, down_at // block + i % steps, 0))
    else:
        out_rows = cols // 1024 * own + (0 if small is None else small.shape[1])
        out_spec = pl.BlockSpec((shards, out_rows, 1024), lambda i: (i, 0, 0))
    return ordered_call(
        functools.partial(weight_kernel, len(pairs), len(pairs[0][0]), own, by_rows, small is not None),
        behind,
        grid=(width // block,),
        in_specs=specs,
        out_specs=out_spec,
        out_shape=shape_of((clips, rows, 1024), bf16),
        input_output_aliases=aliases,
        name=name,
    )(*operands)


def one_hot(index, count, kind=bf16):
    return (index[..., None] == jnp.arange(count)).astype(kind)


def space_masks(labels):
    keys = one_hot(labels, 128)
    queries = jnp.where(labels[None, :] == jnp.arange(128)[:, None], 0.0, MASKED)
    queries = jnp.where(jnp.arange(128)[:, None] < 8, queries, 0.0).astype(bf16)
    return keys, queries


def time_masks(frames, count, me):
    per = ROWS // frames
    row = jnp.arange(ROWS)
    held = frames // count
    frame = jnp.mod(me - row // (held * per), count) * held + row // per % held
    place = row % per
    lane = jnp.arange(128)
    keys = ((lane[None, :] == place[:, None]) | (lane[None, :] == per + frame[:, None])).astype(bf16)
    other = (lane[:, None] < per) & (lane[:, None] != place[None, :])
    later = (lane[:, None] >= per) & (lane[:, None] < per + frames) & (lane[:, None] - per > frame[None, :])
    queries = jnp.where(other | later, MASKED, 0.0).astype(bf16)
    return keys, queries


def action_rows(labels, owners, actions):
    clip_of = jnp.sum(jnp.where(labels[:, None] == jnp.arange(owners.shape[0]), owners[None, :], 0), axis=1)
    hit = clip_of[:, None] == jnp.arange(actions.shape[0])
    chosen = jnp.sum(jnp.where(hit[:, :, None], actions[None], 0), axis=1)
    return jnp.transpose(chosen)


def exchange(values):
    return lax.all_to_all(values, "tm", 0, 0, tiled=True)


def gather(shards):
    own = shards[0].shape[0]
    parts = []
    for shard in shards:
        rows, cols = shard.shape
        parts += [shard[:, at : at + 1024] for at in range(0, cols, 1024)]
    return lax.all_gather(jnp.concatenate(parts, axis=0), "clip", axis=0, tiled=False)


def reduce_clip(total):
    return lax.psum_scatter(total, "clip", scatter_dimension=0, tiled=False)


def shift(values, step):
    count = lax.axis_size("tm")
    return lax.ppermute(values, "tm", [(k, (k + step) % count) for k in range(count)])


def sum_half(part):
    count = lax.axis_size("tm")
    rows = part.shape[0] // count
    me = lax.axis_index("tm")
    piece = lambda step: lax.dynamic_slice_in_dim(part, lax.rem(me + step, count) * rows, rows, axis=0)
    total = piece(0).astype(f32)
    for received in [shift(piece(step), step) for step in range(1, count)]:
        total = total + received.astype(f32)
    return total.astype(bf16)


def share_half(mine):
    count = lax.axis_size("tm")
    rows = mine.shape[0]
    me = lax.axis_index("tm")
    whole_rows = jnp.zeros((count * rows, mine.shape[1]), mine.dtype)
    for step, held in enumerate([mine] + [shift(mine, step) for step in range(1, count)]):
        at = lax.rem(me + count - step, count) * rows
        whole_rows = lax.dynamic_update_slice_in_dim(whole_rows, held, at, axis=0)
    return whole_rows


def mark(values):
    return values.reshape(-1, values.shape[-1])[:8, :128]


def together(*lists):
    flat = lax.optimization_barrier([a for arrays in lists for a in arrays])
    out = []
    for arrays in lists:
        out.append(list(flat[: len(arrays)]))
        flat = flat[len(arrays) :]
    return out


def columns(rows, own, first, count):
    return jnp.concatenate([rows[(first + c) * own : (first + c + 1) * own] for c in range(count)], axis=1).astype(f32)


def local(
    tokens, segments, assignment, actions, norm_gain, norm_bias,
    space_in, space_out, time_in, time_out, hidden, hidden_bias, down, out_bias,
    action_table, out_grad,
):
    micros, frames_here, slots, width = tokens.shape
    pieces = lax.axis_size("tm")
    clips = lax.axis_size("clip")
    frames = frames_here * pieces
    per = slots // pieces
    own = norm_gain.shape[1]
    nact = action_table.shape[0]
    micro = range(micros)
    hb_rows = hidden_bias.shape[0] // own
    small_rows = 6 + nact + hb_rows + 1

    small = jnp.concatenate(
        [norm_gain, norm_bias, action_table, hidden_bias.reshape(-1, own), out_bias.reshape(-1, own)], axis=0
    )
    small_all = lax.all_gather(small, "clip", axis=0, tiled=False)
    w_space = gather([space_in, space_out])
    w_time = gather([time_in, time_out])
    w_ff = gather([hidden, down])

    rows_by = lambda start, count: jnp.transpose(small_all[:, start : start + count], (1, 0, 2)).reshape(count, width)
    gain = rows_by(0, 3).astype(f32)
    bias = rows_by(3, 3).astype(f32)
    table = jnp.pad(rows_by(6, nact), ((0, 128 - nact), (0, 0)))
    hb_all = small_all[:, 6 + nact : 6 + nact + hb_rows].reshape(1, -1).astype(f32)
    ob_all = small_all[:, 6 + nact + hb_rows :].reshape(1, -1).astype(f32)

    me = lax.axis_index("tm").astype(jnp.int32)
    place = me.reshape(1)
    tmasks = time_masks(frames, pieces, me)
    hots = [one_hot(action_rows(segments[m], assignment[m], actions[m]), 128) for m in micro]
    smasks = [space_masks(segments[m]) for m in micro]

    pick = lambda parts, index: [parts[m][index] for m in micro]
    outward = lambda parts: [parts[0]] + [
        lax.ppermute(parts[d], "tm", [(k, (k + d) % pieces) for k in range(pieces)]) for d in range(1, pieces)
    ]
    inward = lambda parts: [parts[0]] + [
        lax.ppermute(parts[d], "tm", [(k, (k - d) % pieces) for k in range(pieces)]) for d in range(1, pieces)
    ]
    marks = lambda parts: [mark(a) for a in parts[1:]]
    rounded = lambda values, d: lax.dynamic_slice_in_dim(values, (me + d) % pieces * per, per, axis=1).astype(bf16)
    sent = [[rounded(out_grad[m], d) for d in range(pieces)] for m in micro]

    branch = [outward(sent[0])]
    forward, after, middle, ahead, pieces_out, back, gas, last = [], [], [], [], [], [], [], []
    behind = []
    for m in micro:
        forward.append(
            call_space_forward(behind, m, place, tokens, hots[m], *smasks[m], gain, bias, table, w_space, pieces)
        )
        after.append(outward(forward[m][4:]))
        behind = [forward[m][3]] + marks(branch[0])
    for m in micro:
        middle.append(list(call_time_forward(behind, after[m], *tmasks, gain, bias, w_time)))
        behind = [middle[m][3]]
    for m in micro[1:]:
        late, (middle[-1][4],) = together(sent[m], [middle[-1][4]])
        branch.append(outward(late))
    for m in micro:
        ahead.append(call_feed_forward(behind, branch[m], middle[m][4], gain, bias, hb_all, ob_all, w_ff))
        pieces_out.append(inward(ahead[m][9:]))
        behind = [ahead[m][5]]
    behind += marks(pieces_out[0])
    ff_grad = weight_grad(behind, [(pick(ahead, 1), pick(ahead, 4))], clips, 8 * own, "down_grad", down_at=4 * own)
    ff_grad = weight_grad([], [(pick(ahead, 0), pick(ahead, 2))], clips, 8 * own, "hidden_grad", buffer=ff_grad)
    (ff_grad,), pieces_out[-1] = together([ff_grad], pieces_out[-1])
    ff_part = reduce_clip(ff_grad)
    behind = [ff_grad]
    for m in micro:
        back.append(
            call_time_backward(
                behind, after[m], ahead[m][3], *tmasks, gain, w_time, middle[m][1], middle[m][2], middle[m][3]
            )
        )
        gas.append(inward(back[m][3:]))
        behind = [back[m][1]]
    time_grad = weight_grad(
        behind, [(pick(middle, 0), pick(back, 0)), (pick(middle, 2), pick(ahead, 3))], clips, 4 * own, "time_grad"
    )
    (time_grad,), gas[0] = together([time_grad], gas[0])
    time_part = reduce_clip(time_grad)
    behind = [time_grad]
    grad_buffer = None
    for m in micro:
        last.append(
            list(
                call_space_backward(
                    behind, m, gas[m], place, tokens, hots[m], *smasks[m], gain, table, w_space,
                    forward[m][1], forward[m][2], forward[m][3], grad_buffer,
                )
            )
        )
        grad_buffer = last[m][2]
        behind = []
        if m == 0:
            (ff_part,), (last[m][3],) = together([ff_part], [last[m][3]])
            ff_half = sum_half(ff_part)
            behind = [mark(ff_part)]

    total = lambda values: functools.reduce(jnp.add, values)
    gain_grad = jnp.concatenate([total(pick(last, 3)), total(pick(back, 1)), total(pick(ahead, 5))])
    bias_grad = jnp.concatenate([total(pick(last, 4)), total(pick(back, 2)), total(pick(ahead, 6))])
    table_grad = total(pick(last, 5))[:nact]
    hb_grad = total(pick(ahead, 7))
    ob_grad = total(pick(ahead, 8))
    split = lambda a: jnp.transpose(a.reshape(a.shape[0], clips, own), (1, 0, 2))
    small_grads = jnp.concatenate(
        [
            split(gain_grad), split(bias_grad), split(table_grad),
            hb_grad.reshape(clips, hb_rows, own), ob_grad.reshape(clips, 1, own),
        ],
        axis=1,
    ).astype(bf16).reshape(clips, -1)
    extra = 8 * pieces - 4 * own % (8 * pieces)
    small_grads = jnp.pad(small_grads, ((0, 0), (0, extra * 1024 - small_grads.shape[1]))).reshape(clips, extra, 1024)
    space_grad = weight_grad(
        [mark(ff_half)], [(pick(forward, 0), pick(last, 0)), (pick(forward, 2), pick(last, 1))],
        clips, 4 * own + extra, "space_grad", small=small_grads,
    )

    ff_sum = lax.psum(ff_part, "tm")
    (ff_half,), (space_grad,) = together([ff_half], [space_grad])
    space_part = reduce_clip(space_grad)
    ff_sum = share_half(ff_half)
    (time_part,), (ff_half,) = together([time_part], [ff_half])
    time_sum = share_half(sum_half(time_part))
    early = (
        call_assemble(place, pieces_out),
        columns(time_sum, own, 0, 3),
        columns(time_sum, own, 3, 1),
        columns(ff_sum, own, 0, 4),
        ff_sum[4 * own :].astype(f32),
    )
    space_part, *early = lax.optimization_barrier((space_part,) + early)
    space_sum = share_half(sum_half(space_part))
    mine = space_sum[4 * own :].reshape(-1)[: small_rows * own].reshape(small_rows, own).astype(f32)
    return (
        early[0],
        grad_buffer,
        mine[0:3],
        mine[3:6],
        columns(space_sum, own, 0, 3),
        columns(space_sum, own, 3, 1),
        early[1],
        early[2],
        early[3],
        mine[6 + nact : 6 + nact + hb_rows].reshape(-1),
        early[4],
        mine[6 + nact + hb_rows :].reshape(-1),
        mine[6 : 6 + nact],
    )


def solution(mesh):
    rows = P("clip", None)
    cols = P(None, "clip")
    line = P("clip")
    wide = P(None, "tm", "clip", None)
    return jax.shard_map(
        local,
        mesh=mesh,
        in_specs=(
            wide, cols, cols, P(None, None, "tm"), cols, cols,
            rows, rows, rows, rows, rows, line, rows, line, cols, wide,
        ),
        out_specs=(wide, wide, cols, cols, rows, rows, rows, rows, rows, line, rows, line, cols),
        check_vma=False,
    )
```

time: 2600 us -> 811 us (0.31)
  waiting for transfers between devices: 1010 us -> 111 us
  matrix products: 838 us -> 0 us
  Pallas kernels: 0 us -> 496 us
  local copies, waits for them, and re-layouts: 464 us -> 32.4 us
  other arithmetic: 175 us -> 25.5 us
  starting transfers between devices: 7.61 us -> 110 us
  blocking collectives: 80.4 us -> 9.17 us
    dot_general x100 -> x0, matrix products: 838 us -> none  [the longest x12 170 us: weight_grad(): jnp.einsum('fsd,fse->de', left, right, preferred_element_type=jnp.float32)]
    pallas_call x0 -> x15, Pallas kernels: none -> 496 us  [ordered_call(): return lambda *operands: call(*behind, *operands)]
    all_gather x22 -> x3, waiting for transfers between devices: 476 us -> 24.9 us  [gather(): lax.all_gather(jnp.concatenate(parts, axis=0), 'clip', axis=0, tiled=False)]
    reduce_scatter x22 -> x3, waiting for transfers between devices: 332 us -> 0.04 us  [reduce_clip(): return lax.psum_scatter(total, 'clip', scatter_dimension=0, tiled=False)]
    reshape x38 -> x3, local copies, waits for them, and re-layouts: 161 us -> 1.1 us  [the longest x1 0.58 us: local(): mine[6 + nact:6 + nact + hb_rows].reshape(-1)]
    convert_element_type x34 -> x2, local copies, waits for them, and re-layouts: 161 us -> 2.81 us  [local(): lax.dynamic_slice_in_dim(values, (me + d) % pieces * per, per, axis=1)]
    psum x1 -> x0, waiting for transfers between devices: 144 us -> none  [local(): lax.psum(space_in_part.astype(jnp.bfloat16), 'tm').astype(jnp.float32)]
    ppermute x0 -> x42, starting transfers between devices: none -> 109 us  [the longest x18 49 us: shift(): lax.ppermute(values, 'tm', [(k, (k + step) % count) for k in range(count)])]
  transfers between devices with their start and end apart: 48 -> 48, of which waited for: 27 -> 11; matrix products, arithmetic and copies ran while one was open for 49% -> 5% of each run, Pallas kernels for 0% -> 62%
where the time goes in v1:
time: 811 us; the launch traced here: 799 us
  Pallas kernels  496 us (61%)
  waiting for transfers between devices  111 us (14%)
  starting transfers between devices  110 us (14%)
  local copies, waits for them, and re-layouts  32.4 us (4%)
  other arithmetic  25.5 us (3%)
  between operations  15.6 us (2%)
  blocking collectives  9.17 us (1%)
    pallas_call x15, Pallas kernels, ordered_call(): return lambda *operands: call(*behind, *operands)  496 us
    ppermute x18, waiting for transfers between devices, shift(): lax.ppermute(values, 'tm', [(k, (k + step) % count) for k in range(count)])  85.8 us
    ppermute x18, starting transfers between devices, shift(): lax.ppermute(values, 'tm', [(k, (k + step) % count) for k in range(count)])  49 us
    ppermute x12, starting transfers between devices, local(): lax.ppermute(parts[d], 'tm', [(k, (k + d) % pieces) for k in range(pieces)])  41.5 us
    all_gather x3, waiting for transfers between devices, gather(): lax.all_gather(jnp.concatenate(parts, axis=0), 'clip', axis=0, tiled=False)  24.9 us
    ppermute x12, starting transfers between devices, local(): lax.ppermute(parts[d], 'tm', [(k, (k - d) % pieces) for k in range(pieces)])  18.8 us
  transfers between devices with their start and end apart: 48, of which 11 were waited for; matrix products, arithmetic and copies ran while one was open for 5% of the time, Pallas kernels for 62%

profile of v1, /device:TPU:0, one launch (start us, length us, event | category | flops | bytes accessed | tf_op | source)
XLA Modules:
  0.0 798.9 jit_solution(11140389222424187858)
XLA Ops:
  8.5 2.0 pad_maximum_fusion
  14.8 4.1 fusion.26
  20.5 3.0 collective-permute-start
  23.5 2.6 collective-permute-start.1
  27.7 9.2 %all-gather.4 = bf16[8,19,128]{2,1,0:T(8,128)(2,1)S(1)} all-gather(bf16[1,19,128]{2,1,0:T(8,128)(2,1)S(1)} %bitcast.126), channel_id=2, replica_groups=mesh['clip'=8,'tm'=4] {'clip'}, dimensions={0}, use_global_device_ids=true | all-gather | bytes 43776 | tf_op jit(solution)/shard_map/all_gather | solution.py:673
  43.0 24.9 %all-gather.9.cloned.1.call-done = bf16[4096,1024]{1,0:T(8,128)(2,1)} async-done(((bf16[512,1024]{1,0:T(8,128)(2,1)}), bf16[4096,1024]{1,0:T(8,128)(2,1)}) %all-gather.9.cloned.1.call-update) | async-done | bytes 8388624 | tf_op jit(solution)/shard_map/all_gather | solution.py:603
  68.0 34.9 %space_forward.2 = (bf16[4,256,1024]{2,1,0:T(8,128)(2,1)}, bf16[4,256,3072]{2,1,0:T(8,128)(2,1)}, bf16[4,256,1024]{2,1,0:T(8,128)(2,1)}, f32[4,16,256]{2,1,0:T(8...) custom-call(s32[1]{0:T(128)} %bitcast.refs_0_.refs_4_.refs_5_, ...), custom_call_target="tpu_custom_call" | custom-call | tf_op jit(solution)/shard_map/space_forward/pallas_call | solution.py:328
  108.5 2.4 collective-permute-start.4
  112.5 35.0 %space_forward.3 = (bf16[4,256,1024]{2,1,0:T(8,128)(2,1)}, bf16[4,256,3072]{2,1,0:T(8,128)(2,1)}, bf16[4,256,1024]{2,1,0:T(8,128)(2,1)}, f32[4,16,256]{2,1,0:T(8...) custom-call(f32[4,16,256]{2,1,0:T(8,128)} %get-tuple-element.117.ref, ...), custom_call_target="tpu_custom_call" | custom-call | tf_op jit(solution)/shard_map/space_forward/pallas_call | solution.py:328
  148.7 3.1 collective-permute-start.8
  154.3 34.1 %time_forward.2 = (bf16[4,256,1024]{2,1,0:T(8,128)(2,1)}, bf16[4,256,3072]{2,1,0:T(8,128)(2,1)}, bf16[4,256,1024]{2,1,0:T(8,128)(2,1)}, f32[4,16,256]{2,1,0:T(8,128)}, f32[4,256,1024]{2,1,0:T(8,128)}) custom-call(f32[4,16,256]{2,1,0:T(8,128)} %get-tuple-element.118.refs_0_.refs_15_, bf16[8,128]{1,0:T(8,128)(2,1)} %slice.227.refs_1_, ...), custom_call_target="tpu_custom_call" | custom-call | tf_op jit(solution)/shard_map/time_forward/pallas_call | solution.py:328
  188.5 34.1 %time_forward.3 = (bf16[4,256,1024]{2,1,0:T(8,128)(2,1)}, bf16[4,256,3072]{2,1,0:T(8,128)(2,1)}, bf16[4,256,1024]{2,1,0:T(8,128)(2,1)}, f32[4,16,256]{2,1,0:T(8,128)}, f32[4,256,1024]{2,1,0:T(8,128)}) custom-call(f32[4,16,256]{2,1,0:T(8,128)} %get-tuple-element.123.refs_0_.refs_12_, bf16[4,64,1024]{2,1,0:T(8,128)(2,1)} %get-tuple-element.124.refs_1_, ...), custom_call_target="tpu_custom_call" | custom-call | tf_op jit(solution)/shard_map/time_forward/pallas_call | solution.py:328
  222.6 20.7 %collective-permute-start.10 = (bf16[4,64,1024]{2,1,0:T(8,128)(2,1)}, bf16[4,64,1024]{2,1,0:T(8,128)(2,1)S(1)}, u32[]{:S(2)}, u32[]{:S(2)}) collective-permute-start(bf16[4,64,1024]{2,1,0:T(8,128)(2,1)} %get-tuple-element.135), channel_id=1, source_target_pairs={{0,2},{1,3},{2,0},{3,1},{4,6},{5,7},{6,4},{7,5},{8,10},{9,11},{10,... | collective-permute-start | bytes 1572872 | tf_op jit(solution)/shard_map/ppermute | solution.py:693
  243.9 3.8 collective-permute-start.11
  247.9 53.2 %feed_forward.2 = (bf16[4,256,1024]{2,1,0:T(8,128)(2,1)}, bf16[4,256,4096]{2,1,0:T(8,128)(2,1)}, bf16[4,256,4096]{2,1,0:T(8,128)(2,1)}, bf16[4,256,1024]{2,1,0:T...) custom-call(f32[4,16,256]{2,1,0:T(8,128)} %get-tuple-element.128.ref, ...), custom_call_target="tpu_custom_call" | custom-call | tf_op jit(solution)/shard_map/feed_forward/pallas_call | solution.py:328
  301.1 3.8 collective-permute-start.12
  306.6 53.2 %feed_forward.3 = (bf16[4,256,1024]{2,1,0:T(8,128)(2,1)}, bf16[4,256,4096]{2,1,0:T(8,128)(2,1)}, bf16[4,256,4096]{2,1,0:T(8,128)(2,1)}, bf16[4,256,1024]{2,1,0:T...) custom-call(f32[1,1024]{1,0:T(1,128)} %get-tuple-element.131.refs_0_, ...), custom_call_target="tpu_custom_call" | custom-call | tf_op jit(solution)/shard_map/feed_forward/pallas_call | solution.py:328
  359.7 3.2 collective-permute-start.15
  366.3 25.0 %down_grad.1.refs_4_ = bf16[8,1024,1024]{2,1,0:T(8,128)(2,1)} custom-call(f32[1,1024]{1,0:T(1,128)} %get-tuple-element.141.refs_0_, bf16[8,128]{1,0:T(8,128)(2,1)} %slice.232.refs_1_, bf16[8,128]{1,0:T(8,128)(2,1)} %slice.233.refs_2_, bf16[8,128]{1,0:T(8,128)(2,1)} %slice.234.refs_3_, bf16[4,256,4096]{2,1,0:T(8,128)(2,1)} %get-tuple-element.145.refs_4_, ...), custom_call_target="tpu_custom_call" | custom-call | tf_op jit(solution)/shard_map/down_grad/pallas_call | solution.py:328
  391.3 25.7 %hidden_grad.1.refs_0_ = bf16[8,1024,1024]{2,1,0:T(8,128)(2,1)} custom-call(bf16[4,256,1024]{2,1,0:T(8,128)(2,1)} %get-tuple-element.130.refs_0_, bf16[4,256,1024]{2,1,0:T(8,128)(2,1)} %get-tuple-element.138.refs_1_, bf16[4,256,4096]{2,1,0:T(8,128)(2,1)} %get-tuple-element.139.refs_2_, ...), custom_call_target="tpu_custom_call", output_to_operand_aliasing={{}: (4, {})} | custom-call | tf_op jit(solution)/shard_map/hidden_grad/pallas_call | solution.py:328
  417.1 33.8 %time_backward.2 = (bf16[4,256,3072]{2,1,0:T(8,128)(2,1)}, f32[1,1024]{1,0:T(1,128)}, f32[1,1024]{1,0:T(1,128)}, bf16[4,64,1024]{2,1,0:T(8,128)(2,1)}, bf16[4,64...) custom-call(bf16[8,1024,1024]{2,1,0:T(8,128)(2,1)} %hidden_grad.1.refs_0_, ...), custom_call_target="tpu_custom_call" | custom-call | tf_op jit(solution)/shard_map/time_backward/pallas_call | solution.py:328
  450.9 3.8 collective-permute-start.18
  455.5 33.8 %time_backward.3 = (bf16[4,256,3072]{2,1,0:T(8,128)(2,1)}, f32[1,1024]{1,0:T(1,128)}, f32[1,1024]{1,0:T(1,128)}, bf16[4,64,1024]{2,1,0:T(8,128)(2,1)}, bf16[4,64...) custom-call(f32[1,1024]{1,0:T(1,128)} %get-tuple-element.157.refs_0_, ...), custom_call_target="tpu_custom_call" | custom-call | tf_op jit(solution)/shard_map/time_backward/pallas_call | solution.py:328
  489.3 26.5 %time_grad.1.refs_0_ = bf16[8,512,1024]{2,1,0:T(8,128)(2,1)} custom-call(f32[1,1024]{1,0:T(1,128)} %get-tuple-element.161.refs_0_, bf16[4,256,1024]{2,1,0:T(8,128)(2,1)} %get-tuple-element.162.refs_1_, bf16[4,256,1024]{2,1,0:T(8,128)(2,1)} %get-tuple-element.163.refs_2_, bf16[4,256,3072]{2,1,0:T(8,128)(2,1)} %get-tuple-element.164.refs_3_, ...), custom_call_target="tpu_custom_call" | custom-call | tf_op jit(solution)/shard_map/time_grad/pallas_call | solution.py:328
  517.2 3.2 collective-permute-start.24
  522.0 37.5 %space_backward.2 = (bf16[4,256,3072]{2,1,0:T(8,128)(2,1)}, bf16[4,256,1024]{2,1,0:T(8,128)(2,1)}, f32[2,4,256,1024]{3,2,1,0:T(8,128)}, f32[1,1024]{1,0:T(1,128)...) custom-call(bf16[8,512,1024]{2,1,0:T(8,128)(2,1)} %time_grad.1.refs_0_, bf16[4,64,1024]{2,1,0:T(8,128)(2,1)} %get-tuple-element.171.refs_1_, ...), custom_call_target="tpu_custom_call" | custom-call | tf_op jit(solution)/shard_map/space_backward/pallas_call | solution.py:328
  560.8 2.7 constant_dynamic-slice_fusion.8
  563.6 2.1 collective-permute-start.21
  565.7 2.0 collective-permute-start.22
  569.3 37.6 %space_backward.3 = (bf16[4,256,3072]{2,1,0:T(8,128)(2,1)}, bf16[4,256,1024]{2,1,0:T(8,128)(2,1)}, f32[2,4,256,1024]{3,2,1,0:T(8,128)}, f32[1,1024]{1,0:T(1,128)...) custom-call(bf16[8,128]{1,0:T(8,128)(2,1)} %slice.201.refs_0_, ...), custom_call_target="tpu_custom_call", output_to_operand_aliasing={{2}: (16, {})} | custom-call | tf_op jit(solution)/shard_map/space_backward/pallas_call | solution.py:328
  610.3 1.9 add_convert_fusion
  612.7 26.5 %space_grad.1 = bf16[8,544,1024]{2,1,0:T(8,128)(2,1)} custom-call(bf16[8,128]{1,0:T(8,128)(2,1)} %slice.235.refs_0_, bf16[4,256,1024]{2,1,0:T(8,128)(2,1)} %get-tuple-element.179.refs_1_, bf16[4,256,1024]{2,1,0:T(8,128)(2,1)} %get-tuple-element.180.refs_2_, bf16[4,256,3072]{2,1,0:T(8,128)(2,1)} %get-tuple-element.181.refs_3_, ...), custom_call_target="tpu_custom_call" | custom-call | tf_op jit(solution)/shard_map/space_grad/pallas_call | solution.py:328
  644.9 6.7 collective-permute-done.27
  651.6 6.7 collective-permute-done.28
  660.4 6.4 collective-permute-start.30
  666.8 2.7 collective-permute-start.31
  669.5 4.8 assemble.1
  674.7 3.5 collective-permute-start.32
  680.2 26.9 %collective-permute-done.31 = bf16[128,1024]{1,0:T(8,128)(2,1)S(1)} collective-permute-done((bf16[128,1024]{1,0:T(8,128)(2,1)}, bf16[128,1024]{1,0:T(8,128)(2,1)S(1)}, u32[]{:S(2)}, u32[]{:S(2)}) %collective-permute-start.31) | collective-permute-done | bytes 262176 | tf_op jit(solution)/shard_map/ppermute | solution.py:612
  709.9 8.4 %collective-permute-done.34 = bf16[256,1024]{1,0:T(8,128)(2,1)S(1)} collective-permute-done((bf16[256,1024]{1,0:T(8,128)(2,1)S(1)}, bf16[256,1024]{1,0:T(8,128)(2,1)S(1)}, u32[]{:S(2)}, u32[]{:S(2)}) %collective-permute-start.34) | collective-permute-done | bytes 524320 | tf_op jit(solution)/shard_map/ppermute | solution.py:612
  718.3 2.7 collective-permute-done.35
  725.4 14.6 %collective-permute-start.36 = (bf16[136,1024]{1,0:T(8,128)(2,1)S(1)}, bf16[136,1024]{1,0:T(8,128)(2,1)S(1)}, u32[]{:S(2)}, u32[]{:S(2)}) collective-permute-start(bf16[136,1024]{1,0:T(8,128)(2,1)S(1)} %get-tuple-element.246), channel_id=1, source_target_pairs={{0,1},{1,2},{2,3},{3,0},{4,5},{5,6},{6,7},{7,4},{8,9},{9,10},{10,1... | collective-permute-start | bytes 835592 | tf_op jit(solution)/shard_map/ppermute | solution.py:612
  740.0 2.7 collective-permute-start.37
  742.7 7.1 collective-permute-done.36
  749.9 10.7 %collective-permute-done.37 = bf16[136,1024]{1,0:T(8,128)(2,1)S(1)} collective-permute-done((bf16[136,1024]{1,0:T(8,128)(2,1)S(1)}, bf16[136,1024]{1,0:T(8,128)(2,1)S(1)}, u32[]{:S(2)}, u32[]{:S(2)}) %collective-permute-start.37) | collective-permute-done | bytes 278560 | tf_op jit(solution)/shard_map/ppermute | solution.py:612
  761.8 6.5 collective-permute-start.39
  770.8 5.4 collective-permute-done.39
  776.2 10.7 %collective-permute-done.40 = bf16[136,1024]{1,0:T(8,128)(2,1)S(1)} collective-permute-done((bf16[136,1024]{1,0:T(8,128)(2,1)S(1)}, bf16[136,1024]{1,0:T(8,128)(2,1)S(1)}, u32[]{:S(2)}, u32[]{:S(2)}) %collective-permute-start.40) | collective-permute-done | bytes 278560 | tf_op jit(solution)/shard_map/ppermute | solution.py:612
  (249 shorter events, 67.1 us)
Async XLA Ops:
  7.2 60.8 %all-gather.9.cloned.1.call-start = ((), (), s32[]{:S(2)}) async-start(), calls=%async_computation.6 | async-start | bytes 9437184 | tf_op jit(solution)/shard_map/all_gather | solution.py:603
  10.5 142.8 %all-gather.11.cloned.1.call-start = ((), (), s32[]{:S(2)}) async-start(), calls=%async_computation.7 | async-start | bytes 9437184 | tf_op jit(solution)/shard_map/all_gather | solution.py:603
  11.7 236.2 %all-gather.13.cloned.1.call-start = ((), (), s32[]{:S(2)}) async-start(), calls=%async_computation.8 | async-start | bytes 18874368 | tf_op jit(solution)/shard_map/all_gather | solution.py:603
  14.7 544.8 %reduce-scatter.4.cloned.1.call-start = ((), (), s32[]{:S(2)}) async-start(), calls=%async_computation.3 | async-start | bytes 18874368 | tf_op jit(solution)/shard_map/reduce_scatter | solution.py:607
  20.5 85.6 %collective-permute-start = (bf16[4,64,1024]{2,1,0:T(8,128)(2,1)}, bf16[4,64,1024]{2,1,0:T(8,128)(2,1)S(1)}, u32[]{:S(2)}, u32[]{:S(2)}) collective-permute-start(bf16[4,64,1024]{2,1,0:T(8,128)(2,1)} %get-tuple-element.241), channel_id=1, source_target_pairs={{0,1},{1,2},{2,3},{3,0},{4,5},{5,6},{6,7},{7,4},{8,9},{9,10},{10,1... | collective-permute-start | bytes 1572872 | tf_op jit(solution)/shard_map/ppermute | solution.py:693
  23.5 83.2 %collective-permute-start.1 = (bf16[4,64,1024]{2,1,0:T(8,128)(2,1)}, bf16[4,64,1024]{2,1,0:T(8,128)(2,1)S(1)}, u32[]{:S(2)}, u32[]{:S(2)}) collective-permute-start(bf16[4,64,1024]{2,1,0:T(8,128)(2,1)} %get-tuple-element.240), channel_id=1, source_target_pairs={{0,2},{1,3},{2,0},{3,1},{4,6},{5,7},{6,4},{7,5},{8,10},{9,11},{10,... | collective-permute-start | bytes 1572872 | tf_op jit(solution)/shard_map/ppermute | solution.py:693
  26.1 81.2 %collective-permute-start.2 = (bf16[4,64,1024]{2,1,0:T(8,128)(2,1)}, bf16[4,64,1024]{2,1,0:T(8,128)(2,1)}, u32[]{:S(2)}, u32[]{:S(2)}) collective-permute-start(bf16[4,64,1024]{2,1,0:T(8,128)(2,1)} %get-tuple-element.239), channel_id=1, source_target_pairs={{0,3},{1,0},{2,1},{3,2},{4,7},{5,4},{6,5},{7,6},{8,11},{9,8},{10,9... | collective-permute-start | bytes 1572872 | tf_op jit(solution)/shard_map/ppermute | solution.py:693
  102.9 45.9 %collective-permute-start.3 = (bf16[4,64,1024]{2,1,0:T(8,128)(2,1)}, bf16[4,64,1024]{2,1,0:T(8,128)(2,1)S(1)}, u32[]{:S(2)}, u32[]{:S(2)}) collective-permute-start(bf16[4,64,1024]{2,1,0:T(8,128)(2,1)} %get-tuple-element.120), channel_id=1, source_target_pairs={{0,1},{1,2},{2,3},{3,0},{4,5},{5,6},{6,7},{7,4},{8,9},{9,10},{10,1... | collective-permute-start | bytes 1572872 | tf_op jit(solution)/shard_map/ppermute | solution.py:693
  108.5 44.9 %collective-permute-start.4 = (bf16[4,64,1024]{2,1,0:T(8,128)(2,1)}, bf16[4,64,1024]{2,1,0:T(8,128)(2,1)S(1)}, u32[]{:S(2)}, u32[]{:S(2)}) collective-permute-start(bf16[4,64,1024]{2,1,0:T(8,128)(2,1)} %get-tuple-element.121), channel_id=1, source_target_pairs={{0,2},{1,3},{2,0},{3,1},{4,6},{5,7},{6,4},{7,5},{8,10},{9,11},{10,... | collective-permute-start | bytes 1572872 | tf_op jit(solution)/shard_map/ppermute | solution.py:693
  110.9 42.4 %collective-permute-start.5 = (bf16[4,64,1024]{2,1,0:T(8,128)(2,1)}, bf16[4,64,1024]{2,1,0:T(8,128)(2,1)S(1)}, u32[]{:S(2)}, u32[]{:S(2)}) collective-permute-start(bf16[4,64,1024]{2,1,0:T(8,128)(2,1)} %get-tuple-element.122), channel_id=1, source_target_pairs={{0,3},{1,0},{2,1},{3,2},{4,7},{5,4},{6,5},{7,6},{8,11},{9,8},{10,9... | collective-permute-start | bytes 1572872 | tf_op jit(solution)/shard_map/ppermute | solution.py:693
  147.5 41.0 %collective-permute-start.6 = (bf16[4,64,1024]{2,1,0:T(8,128)(2,1)}, bf16[4,64,1024]{2,1,0:T(8,128)(2,1)}, u32[]{:S(2)}, u32[]{:S(2)}) collective-permute-start(bf16[4,64,1024]{2,1,0:T(8,128)(2,1)} %get-tuple-element.125), channel_id=1, source_target_pairs={{0,1},{1,2},{2,3},{3,0},{4,5},{5,6},{6,7},{7,4},{8,9},{9,10},{10,1... | collective-permute-start | bytes 1572872 | tf_op jit(solution)/shard_map/ppermute | solution.py:693
  148.2 40.2 %collective-permute-start.7 = (bf16[4,64,1024]{2,1,0:T(8,128)(2,1)}, bf16[4,64,1024]{2,1,0:T(8,128)(2,1)}, u32[]{:S(2)}, u32[]{:S(2)}) collective-permute-start(bf16[4,64,1024]{2,1,0:T(8,128)(2,1)} %get-tuple-element.126), channel_id=1, source_target_pairs={{0,2},{1,3},{2,0},{3,1},{4,6},{5,7},{6,4},{7,5},{8,10},{9,11},{10,... | collective-permute-start | bytes 1572872 | tf_op jit(solution)/shard_map/ppermute | solution.py:693
  148.7 39.7 %collective-permute-start.8 = (bf16[4,64,1024]{2,1,0:T(8,128)(2,1)}, bf16[4,64,1024]{2,1,0:T(8,128)(2,1)}, u32[]{:S(2)}, u32[]{:S(2)}) collective-permute-start(bf16[4,64,1024]{2,1,0:T(8,128)(2,1)} %get-tuple-element.127), channel_id=1, source_target_pairs={{0,3},{1,0},{2,1},{3,2},{4,7},{5,4},{6,5},{7,6},{8,11},{9,8},{10,9... | collective-permute-start | bytes 1572872 | tf_op jit(solution)/shard_map/ppermute | solution.py:693
  222.6 82.3 %collective-permute-start.10 = (bf16[4,64,1024]{2,1,0:T(8,128)(2,1)}, bf16[4,64,1024]{2,1,0:T(8,128)(2,1)S(1)}, u32[]{:S(2)}, u32[]{:S(2)}) collective-permute-start(bf16[4,64,1024]{2,1,0:T(8,128)(2,1)} %get-tuple-element.135), channel_id=1, source_target_pairs={{0,2},{1,3},{2,0},{3,1},{4,6},{5,7},{6,4},{7,5},{8,10},{9,11},{10,... | collective-permute-start | bytes 1572872 | tf_op jit(solution)/shard_map/ppermute | solution.py:693
  243.9 62.6 %collective-permute-start.11 = (bf16[4,64,1024]{2,1,0:T(8,128)(2,1)}, bf16[4,64,1024]{2,1,0:T(8,128)(2,1)}, u32[]{:S(2)}, u32[]{:S(2)}) collective-permute-start(bf16[4,64,1024]{2,1,0:T(8,128)(2,1)} %get-tuple-element.136), channel_id=1, source_target_pairs={{0,3},{1,0},{2,1},{3,2},{4,7},{5,4},{6,5},{7,6},{8,11},{9,8},{10,9... | collective-permute-start | bytes 1572872 | tf_op jit(solution)/shard_map/ppermute | solution.py:693
  247.7 58.8 %collective-permute-start.9 = (bf16[4,64,1024]{2,1,0:T(8,128)(2,1)}, bf16[4,64,1024]{2,1,0:T(8,128)(2,1)}, u32[]{:S(2)}, u32[]{:S(2)}) collective-permute-start(bf16[4,64,1024]{2,1,0:T(8,128)(2,1)} %get-tuple-element.134), channel_id=1, source_target_pairs={{0,1},{1,2},{2,3},{3,0},{4,5},{5,6},{6,7},{7,4},{8,9},{9,10},{10,1... | collective-permute-start | bytes 1572872 | tf_op jit(solution)/shard_map/ppermute | solution.py:693
  301.1 63.0 %collective-permute-start.12 = (bf16[4,64,1024]{2,1,0:T(8,128)(2,1)}, bf16[4,64,1024]{2,1,0:T(8,128)(2,1)S(1)}, u32[]{:S(2)}, u32[]{:S(2)}) collective-permute-start(bf16[4,64,1024]{2,1,0:T(8,128)(2,1)} %get-tuple-element.142), channel_id=1, source_target_pairs={{0,3},{1,0},{2,1},{3,2},{4,7},{5,4},{6,5},{7,6},{8,11},{9,8},{10,9... | collective-permute-start | bytes 1572872 | tf_op jit(solution)/shard_map/ppermute | solution.py:696
  304.9 60.2 %collective-permute-start.13 = (bf16[4,64,1024]{2,1,0:T(8,128)(2,1)}, bf16[4,64,1024]{2,1,0:T(8,128)(2,1)S(1)}, u32[]{:S(2)}, u32[]{:S(2)}) collective-permute-start(bf16[4,64,1024]{2,1,0:T(8,128)(2,1)} %get-tuple-element.143), channel_id=1, source_target_pairs={{0,2},{1,3},{2,0},{3,1},{4,6},{5,7},{6,4},{7,5},{8,10},{9,11},{10,... | collective-permute-start | bytes 1572872 | tf_op jit(solution)/shard_map/ppermute | solution.py:696
  305.7 60.0 %collective-permute-start.14 = (bf16[4,64,1024]{2,1,0:T(8,128)(2,1)}, bf16[4,64,1024]{2,1,0:T(8,128)(2,1)S(1)}, u32[]{:S(2)}, u32[]{:S(2)}) collective-permute-start(bf16[4,64,1024]{2,1,0:T(8,128)(2,1)} %get-tuple-element.144), channel_id=1, source_target_pairs={{0,1},{1,2},{2,3},{3,0},{4,5},{5,6},{6,7},{7,4},{8,9},{9,10},{10,1... | collective-permute-start | bytes 1572872 | tf_op jit(solution)/shard_map/ppermute | solution.py:696
  359.7 57.3 %collective-permute-start.15 = (bf16[4,64,1024]{2,1,0:T(8,128)(2,1)}, bf16[4,64,1024]{2,1,0:T(8,128)(2,1)}, u32[]{:S(2)}, u32[]{:S(2)}) collective-permute-start(bf16[4,64,1024]{2,1,0:T(8,128)(2,1)} %get-tuple-element.150), channel_id=1, source_target_pairs={{0,3},{1,0},{2,1},{3,2},{4,7},{5,4},{6,5},{7,6},{8,11},{9,8},{10,9... | collective-permute-start | bytes 1572872 | tf_op jit(solution)/shard_map/ppermute | solution.py:696
  363.0 54.1 %collective-permute-start.16 = (bf16[4,64,1024]{2,1,0:T(8,128)(2,1)}, bf16[4,64,1024]{2,1,0:T(8,128)(2,1)}, u32[]{:S(2)}, u32[]{:S(2)}) collective-permute-start(bf16[4,64,1024]{2,1,0:T(8,128)(2,1)} %get-tuple-element.151), channel_id=1, source_target_pairs={{0,2},{1,3},{2,0},{3,1},{4,6},{5,7},{6,4},{7,5},{8,10},{9,11},{10,... | collective-permute-start | bytes 1572872 | tf_op jit(solution)/shard_map/ppermute | solution.py:696
  364.1 52.9 %collective-permute-start.17 = (bf16[4,64,1024]{2,1,0:T(8,128)(2,1)}, bf16[4,64,1024]{2,1,0:T(8,128)(2,1)}, u32[]{:S(2)}, u32[]{:S(2)}) collective-permute-start(bf16[4,64,1024]{2,1,0:T(8,128)(2,1)} %get-tuple-element.152), channel_id=1, source_target_pairs={{0,1},{1,2},{2,3},{3,0},{4,5},{5,6},{6,7},{7,4},{8,9},{9,10},{10,1... | collective-permute-start | bytes 1572872 | tf_op jit(solution)/shard_map/ppermute | solution.py:696
  417.1 222.2 %reduce-scatter.8.cloned.1.call-start = ((), (), s32[]{:S(2)}) async-start(), calls=%async_computation.5 | async-start | bytes 9437184 | tf_op jit(solution)/shard_map/reduce_scatter | solution.py:607
  450.9 64.9 %collective-permute-start.18 = (bf16[4,64,1024]{2,1,0:T(8,128)(2,1)}, bf16[4,64,1024]{2,1,0:T(8,128)(2,1)S(1)}, u32[]{:S(2)}, u32[]{:S(2)}) collective-permute-start(bf16[4,64,1024]{2,1,0:T(8,128)(2,1)} %get-tuple-element.167), channel_id=1, source_target_pairs={{0,3},{1,0},{2,1},{3,2},{4,7},{5,4},{6,5},{7,6},{8,11},{9,8},{10,9... | collective-permute-start | bytes 1572872 | tf_op jit(solution)/shard_map/ppermute | solution.py:696
  454.8 61.1 %collective-permute-start.19 = (bf16[4,64,1024]{2,1,0:T(8,128)(2,1)}, bf16[4,64,1024]{2,1,0:T(8,128)(2,1)S(1)}, u32[]{:S(2)}, u32[]{:S(2)}) collective-permute-start(bf16[4,64,1024]{2,1,0:T(8,128)(2,1)} %get-tuple-element.168), channel_id=1, source_target_pairs={{0,2},{1,3},{2,0},{3,1},{4,6},{5,7},{6,4},{7,5},{8,10},{9,11},{10,... | collective-permute-start | bytes 1572872 | tf_op jit(solution)/shard_map/ppermute | solution.py:696
  454.8 61.1 %collective-permute-start.20 = (bf16[4,64,1024]{2,1,0:T(8,128)(2,1)}, bf16[4,64,1024]{2,1,0:T(8,128)(2,1)S(1)}, u32[]{:S(2)}, u32[]{:S(2)}) collective-permute-start(bf16[4,64,1024]{2,1,0:T(8,128)(2,1)} %get-tuple-element.169), channel_id=1, source_target_pairs={{0,1},{1,2},{2,3},{3,0},{4,5},{5,6},{6,7},{7,4},{8,9},{9,10},{10,1... | collective-permute-start | bytes 1572872 | tf_op jit(solution)/shard_map/ppermute | solution.py:696
  517.0 207.2 %reduce-scatter.6.cloned.1.call-start = ((), (), s32[]{:S(2)}) async-start(), calls=%async_computation.4 | async-start | bytes 10027008 | tf_op jit(solution)/shard_map/reduce_scatter | solution.py:607
  517.2 50.5 %collective-permute-start.24 = (bf16[4,64,1024]{2,1,0:T(8,128)(2,1)}, bf16[4,64,1024]{2,1,0:T(8,128)(2,1)S(1)}, u32[]{:S(2)}, u32[]{:S(2)}) collective-permute-start(bf16[4,64,1024]{2,1,0:T(8,128)(2,1)} %get-tuple-element.183), channel_id=1, source_target_pairs={{0,3},{1,0},{2,1},{3,2},{4,7},{5,4},{6,5},{7,6},{8,11},{9,8},{10,9... | collective-permute-start | bytes 1572872 | tf_op jit(solution)/shard_map/ppermute | solution.py:696
  520.4 47.9 %collective-permute-start.25 = (bf16[4,64,1024]{2,1,0:T(8,128)(2,1)}, bf16[4,64,1024]{2,1,0:T(8,128)(2,1)S(1)}, u32[]{:S(2)}, u32[]{:S(2)}) collective-permute-start(bf16[4,64,1024]{2,1,0:T(8,128)(2,1)} %get-tuple-element.184), channel_id=1, source_target_pairs={{0,2},{1,3},{2,0},{3,1},{4,6},{5,7},{6,4},{7,5},{8,10},{9,11},{10,... | collective-permute-start | bytes 1572872 | tf_op jit(solution)/shard_map/ppermute | solution.py:696
  521.7 46.6 %collective-permute-start.26 = (bf16[4,64,1024]{2,1,0:T(8,128)(2,1)}, bf16[4,64,1024]{2,1,0:T(8,128)(2,1)S(1)}, u32[]{:S(2)}, u32[]{:S(2)}) collective-permute-start(bf16[4,64,1024]{2,1,0:T(8,128)(2,1)} %get-tuple-element.185), channel_id=1, source_target_pairs={{0,1},{1,2},{2,3},{3,0},{4,5},{5,6},{6,7},{7,4},{8,9},{9,10},{10,1... | collective-permute-start | bytes 1572872 | tf_op jit(solution)/shard_map/ppermute | solution.py:696
  563.6 46.7 %collective-permute-start.21 = (bf16[256,1024]{1,0:T(8,128)(2,1)}, bf16[256,1024]{1,0:T(8,128)(2,1)}, u32[]{:S(2)}, u32[]{:S(2)}) collective-permute-start(bf16[256,1024]{1,0:T(8,128)(2,1)} %get-tuple-element.231), channel_id=1, source_target_pairs={{0,1},{1,2},{2,3},{3,0},{4,5},{5,6},{6,7},{7,4},{8,9},{9,10},{10,1... | collective-permute-start | bytes 1572872 | tf_op jit(solution)/shard_map/ppermute | solution.py:612
  565.7 44.5 %collective-permute-start.22 = (bf16[256,1024]{1,0:T(8,128)(2,1)}, bf16[256,1024]{1,0:T(8,128)(2,1)}, u32[]{:S(2)}, u32[]{:S(2)}) collective-permute-start(bf16[256,1024]{1,0:T(8,128)(2,1)} %get-tuple-element.233), channel_id=1, source_target_pairs={{0,2},{1,3},{2,0},{3,1},{4,6},{5,7},{6,4},{7,5},{8,10},{9,11},{10,... | collective-permute-start | bytes 1572872 | tf_op jit(solution)/shard_map/ppermute | solution.py:612
  567.7 42.5 %collective-permute-start.23 = (bf16[256,1024]{1,0:T(8,128)(2,1)}, bf16[256,1024]{1,0:T(8,128)(2,1)}, u32[]{:S(2)}, u32[]{:S(2)}) collective-permute-start(bf16[256,1024]{1,0:T(8,128)(2,1)} %get-tuple-element.232), channel_id=1, source_target_pairs={{0,3},{1,0},{2,1},{3,2},{4,7},{5,4},{6,5},{7,6},{8,11},{9,8},{10,9... | collective-permute-start | bytes 1572872 | tf_op jit(solution)/shard_map/ppermute | solution.py:612
  640.5 11.2 %collective-permute-start.27 = (bf16[128,1024]{1,0:T(8,128)(2,1)S(1)}, bf16[128,1024]{1,0:T(8,128)(2,1)S(1)}, u32[]{:S(2)}, u32[]{:S(2)}) collective-permute-start(bf16[128,1024]{1,0:T(8,128)(2,1)S(1)} %get-tuple-element.253), channel_id=1, source_target_pairs={{0,1},{1,2},{2,3},{3,0},{4,5},{5,6},{6,7},{7,4},{8,9},{9,10},{10,1... | collective-permute-start | bytes 786440 | tf_op jit(solution)/shard_map/ppermute | solution.py:612
  642.3 16.1 %collective-permute-start.28 = (bf16[128,1024]{1,0:T(8,128)(2,1)S(1)}, bf16[128,1024]{1,0:T(8,128)(2,1)S(1)}, u32[]{:S(2)}, u32[]{:S(2)}) collective-permute-start(bf16[128,1024]{1,0:T(8,128)(2,1)S(1)} %get-tuple-element.255), channel_id=1, source_target_pairs={{0,2},{1,3},{2,0},{3,1},{4,6},{5,7},{6,4},{7,5},{8,10},{9,11},{10,... | collective-permute-start | bytes 786440 | tf_op jit(solution)/shard_map/ppermute | solution.py:612
  643.3 15.1 %collective-permute-start.29 = (bf16[128,1024]{1,0:T(8,128)(2,1)S(1)}, bf16[128,1024]{1,0:T(8,128)(2,1)S(1)}, u32[]{:S(2)}, u32[]{:S(2)}) collective-permute-start(bf16[128,1024]{1,0:T(8,128)(2,1)S(1)} %get-tuple-element.254), channel_id=1, source_target_pairs={{0,3},{1,0},{2,1},{3,2},{4,7},{5,4},{6,5},{7,6},{8,11},{9,8},{10,9... | collective-permute-start | bytes 786440 | tf_op jit(solution)/shard_map/ppermute | solution.py:612
  660.4 18.1 %collective-permute-start.30 = (bf16[128,1024]{1,0:T(8,128)(2,1)}, bf16[128,1024]{1,0:T(8,128)(2,1)}, u32[]{:S(2)}, u32[]{:S(2)}) collective-permute-start(bf16[128,1024]{1,0:T(8,128)(2,1)} %get-tuple-element.224), channel_id=1, source_target_pairs={{0,1},{1,2},{2,3},{3,0},{4,5},{5,6},{6,7},{7,4},{8,9},{9,10},{10,1... | collective-permute-start | bytes 786440 | tf_op jit(solution)/shard_map/ppermute | solution.py:612
  666.8 40.3 %collective-permute-start.31 = (bf16[128,1024]{1,0:T(8,128)(2,1)}, bf16[128,1024]{1,0:T(8,128)(2,1)S(1)}, u32[]{:S(2)}, u32[]{:S(2)}) collective-permute-start(bf16[128,1024]{1,0:T(8,128)(2,1)} %get-tuple-element.224), channel_id=1, source_target_pairs={{0,2},{1,3},{2,0},{3,1},{4,6},{5,7},{6,4},{7,5},{8,10},{9,11},{10,... | collective-permute-start | bytes 786440 | tf_op jit(solution)/shard_map/ppermute | solution.py:612
  674.3 35.5 %collective-permute-start.33 = (bf16[256,1024]{1,0:T(8,128)(2,1)S(1)}, bf16[256,1024]{1,0:T(8,128)(2,1)S(1)}, u32[]{:S(2)}, u32[]{:S(2)}) collective-permute-start(bf16[256,1024]{1,0:T(8,128)(2,1)S(1)} %add_convert_fusion), channel_id=1, source_target_pairs={{0,1},{1,2},{2,3},{3,0},{4,5},{5,6},{6,7},{7,4},{8,9},{9,10},{10,1... | collective-permute-start | bytes 1572872 | tf_op jit(solution)/shard_map/ppermute | solution.py:612
  674.4 43.9 %collective-permute-start.34 = (bf16[256,1024]{1,0:T(8,128)(2,1)S(1)}, bf16[256,1024]{1,0:T(8,128)(2,1)S(1)}, u32[]{:S(2)}, u32[]{:S(2)}) collective-permute-start(bf16[256,1024]{1,0:T(8,128)(2,1)S(1)} %add_convert_fusion), channel_id=1, source_target_pairs={{0,2},{1,3},{2,0},{3,1},{4,6},{5,7},{6,4},{7,5},{8,10},{9,11},{10,... | collective-permute-start | bytes 1572872 | tf_op jit(solution)/shard_map/ppermute | solution.py:612
  674.7 32.9 %collective-permute-start.32 = (bf16[128,1024]{1,0:T(8,128)(2,1)}, bf16[128,1024]{1,0:T(8,128)(2,1)S(1)}, u32[]{:S(2)}, u32[]{:S(2)}) collective-permute-start(bf16[128,1024]{1,0:T(8,128)(2,1)} %get-tuple-element.224), channel_id=1, source_target_pairs={{0,3},{1,0},{2,1},{3,2},{4,7},{5,4},{6,5},{7,6},{8,11},{9,8},{10,9... | collective-permute-start | bytes 786440 | tf_op jit(solution)/shard_map/ppermute | solution.py:612
  678.4 42.6 %collective-permute-start.35 = (bf16[256,1024]{1,0:T(8,128)(2,1)S(1)}, bf16[256,1024]{1,0:T(8,128)(2,1)S(1)}, u32[]{:S(2)}, u32[]{:S(2)}) collective-permute-start(bf16[256,1024]{1,0:T(8,128)(2,1)S(1)} %add_convert_fusion), channel_id=1, source_target_pairs={{0,3},{1,0},{2,1},{3,2},{4,7},{5,4},{6,5},{7,6},{8,11},{9,8},{10,9... | collective-permute-start | bytes 1572872 | tf_op jit(solution)/shard_map/ppermute | solution.py:612
  725.4 24.4 %collective-permute-start.36 = (bf16[136,1024]{1,0:T(8,128)(2,1)S(1)}, bf16[136,1024]{1,0:T(8,128)(2,1)S(1)}, u32[]{:S(2)}, u32[]{:S(2)}) collective-permute-start(bf16[136,1024]{1,0:T(8,128)(2,1)S(1)} %get-tuple-element.246), channel_id=1, source_target_pairs={{0,1},{1,2},{2,3},{3,0},{4,5},{5,6},{6,7},{7,4},{8,9},{9,10},{10,1... | collective-permute-start | bytes 835592 | tf_op jit(solution)/shard_map/ppermute | solution.py:612
  740.0 20.5 %collective-permute-start.37 = (bf16[136,1024]{1,0:T(8,128)(2,1)S(1)}, bf16[136,1024]{1,0:T(8,128)(2,1)S(1)}, u32[]{:S(2)}, u32[]{:S(2)}) collective-permute-start(bf16[136,1024]{1,0:T(8,128)(2,1)S(1)} %get-tuple-element.248), channel_id=1, source_target_pairs={{0,2},{1,3},{2,0},{3,1},{4,6},{5,7},{6,4},{7,5},{8,10},{9,11},{10,... | collective-permute-start | bytes 835592 | tf_op jit(solution)/shard_map/ppermute | solution.py:612
  742.7 17.8 %collective-permute-start.38 = (bf16[136,1024]{1,0:T(8,128)(2,1)S(1)}, bf16[136,1024]{1,0:T(8,128)(2,1)S(1)}, u32[]{:S(2)}, u32[]{:S(2)}) collective-permute-start(bf16[136,1024]{1,0:T(8,128)(2,1)S(1)} %get-tuple-element.247), channel_id=1, source_target_pairs={{0,3},{1,0},{2,1},{3,2},{4,7},{5,4},{6,5},{7,6},{8,11},{9,8},{10,9... | collective-permute-start | bytes 835592 | tf_op jit(solution)/shard_map/ppermute | solution.py:612
  761.8 14.3 %collective-permute-start.39 = (bf16[136,1024]{1,0:T(8,128)(2,1)S(1)}, bf16[136,1024]{1,0:T(8,128)(2,1)S(1)}, u32[]{:S(2)}, u32[]{:S(2)}) collective-permute-start(bf16[136,1024]{1,0:T(8,128)(2,1)S(1)} %get-tuple-element.222), channel_id=1, source_target_pairs={{0,1},{1,2},{2,3},{3,0},{4,5},{5,6},{6,7},{7,4},{8,9},{9,10},{10,1... | collective-permute-start | bytes 835592 | tf_op jit(solution)/shard_map/ppermute | solution.py:612
  768.3 18.6 %collective-permute-start.40 = (bf16[136,1024]{1,0:T(8,128)(2,1)S(1)}, bf16[136,1024]{1,0:T(8,128)(2,1)S(1)}, u32[]{:S(2)}, u32[]{:S(2)}) collective-permute-start(bf16[136,1024]{1,0:T(8,128)(2,1)S(1)} %get-tuple-element.222), channel_id=1, source_target_pairs={{0,2},{1,3},{2,0},{3,1},{4,6},{5,7},{6,4},{7,5},{8,10},{9,11},{10,... | collective-permute-start | bytes 835592 | tf_op jit(solution)/shard_map/ppermute | solution.py:612
  769.1 17.9 %collective-permute-start.41 = (bf16[136,1024]{1,0:T(8,128)(2,1)S(1)}, bf16[136,1024]{1,0:T(8,128)(2,1)S(1)}, u32[]{:S(2)}, u32[]{:S(2)}) collective-permute-start(bf16[136,1024]{1,0:T(8,128)(2,1)S(1)} %get-tuple-element.222), channel_id=1, source_target_pairs={{0,3},{1,0},{2,1},{3,2},{4,7},{5,4},{6,5},{7,6},{8,11},{9,8},{10,9... | collective-permute-start | bytes 835592 | tf_op jit(solution)/shard_map/ppermute | solution.py:612
  (41 other events, 313.7 us)
Sparse Core Ops, SparseCore 0:
  10.7 57.2 all-gather.8
  70.4 54.3 all-gather.10
  127.3 89.8 all-gather.12
  417.2 116.4 reduce-scatter.3
  537.0 71.2 reduce-scatter.7
  639.4 72.7 reduce-scatter.5

commit v2 on v1

--- a/solution.py
+++ b/solution.py
@@ -12,7 +12,8 @@
 EPS = 1e-05
 MASKED = -1e30
 ROWS = 256
-CHUNK = 1024
+FF_CHUNK = 1024
+FF_GROUPS = 1
 VMEM_LIMIT = 62 * 1024 * 1024
 
 bf16 = jnp.bfloat16
@@ -63,59 +64,83 @@
 
 def attend(qkv_ref, key_mask, query_mask, mixed_t, lse_ref):
     blank = jnp.zeros((HEAD, ROWS), bf16)
-    for pair in range(HEADS // 2):
+    scale = jnp.asarray(HEAD**-0.5, bf16)
+
+    def scores_of(pair):
         q_at, k_at, v_at = pair_slices(pair)
-        q_t = (qkv_ref[:, q_at] * jnp.asarray(HEAD**-0.5, bf16)).T
-        v_t = qkv_ref[:, v_at].T
+        q_t = (qkv_ref[:, q_at] * scale).T
         keys = jnp.concatenate([qkv_ref[:, k_at], key_mask], axis=1)
+        first = jnp.concatenate([q_t[:HEAD], blank, query_mask], axis=0)
+        second = jnp.concatenate([blank, q_t[HEAD:], query_mask], axis=0)
+        return dot(keys, jnp.concatenate([first, second], axis=1))
+
+    def finish(pair, scores):
+        v_t = qkv_ref[:, pair_slices(pair)[2]].T
+        top = jnp.max(scores, axis=0, keepdims=True)
+        raised = jnp.exp(scores - top)
+        total = jnp.sum(raised, axis=0, keepdims=True)
+        weights = raised.astype(bf16)
+        lse = top + jnp.log(total)
+        rate = 1.0 / total
         for part in range(2):
             head = pair * 2 + part
-            half = slice(part * HEAD, (part + 1) * HEAD)
-            parts = [q_t[half], blank] if part == 0 else [blank, q_t[half]]
-            scores = dot(keys, jnp.concatenate(parts + [query_mask], axis=0))
-            top = jnp.max(scores, axis=0, keepdims=True)
-            raised = jnp.exp(scores - top)
-            total = jnp.sum(raised, axis=0, keepdims=True)
-            mixed = dot(v_t[half], raised.astype(bf16))
-            mixed_t[head * HEAD : (head + 1) * HEAD, :] = (mixed * (1.0 / total)).astype(bf16)
-            lse_ref[head : head + 1, :] = top + jnp.log(total)
+            at = slice(part * ROWS, (part + 1) * ROWS)
+            mixed = dot(v_t[part * HEAD : (part + 1) * HEAD], weights[:, at])
+            mixed_t[head * HEAD : (head + 1) * HEAD, :] = (mixed * rate[:, at]).astype(bf16)
+            lse_ref[head : head + 1, :] = lse[:, at]
+
+    queue = [scores_of(0), scores_of(1)]
+    for pair in range(HEADS // 2):
+        if pair + 2 < HEADS // 2:
+            queue.append(scores_of(pair + 2))
+        finish(pair, queue.pop(0))
 
 
 def attend_back(qkv_ref, key_mask, query_mask, lse_ref, grad_ref, grad_t, mixed_t, out_ref, query_t):
     blank = jnp.zeros((HEAD, ROWS), bf16)
     scale = jnp.asarray(HEAD**-0.5, bf16)
     low_half = lax.broadcasted_iota(jnp.int32, (ROWS, 128), 1) < HEAD
+    zero = jnp.zeros((ROWS, 128), bf16)
+
+    def both(top, bottom, extra):
+        first = jnp.concatenate([top, blank] + extra, axis=0)
+        second = jnp.concatenate([blank, bottom] + extra, axis=0)
+        return jnp.concatenate([first, second], axis=1)
+
+    def halves(values):
+        return jnp.concatenate([jnp.where(low_half, values, zero), jnp.where(low_half, zero, values)], axis=0)
+
+    def start(pair):
+        q_at, k_at, v_at = pair_slices(pair)
+        q_t = (qkv_ref[:, q_at] * scale).T
+        keys = jnp.concatenate([qkv_ref[:, k_at], key_mask], axis=1)
+        scores = dot(keys, both(q_t[:HEAD], q_t[HEAD:], [query_mask]))
+        pair_t = grad_t[q_at, :]
+        grad_probs = dot(qkv_ref[:, v_at], both(pair_t[:HEAD], pair_t[HEAD:], []))
+        return scores, grad_probs
+
+    def finish(pair, scores, grad_probs):
+        q_at, k_at, v_at = pair_slices(pair)
+        head = pair * 2
+        lse = jnp.concatenate([lse_ref[head : head + 1, :], lse_ref[head + 1 : head + 2, :]], axis=1)
+        product = grad_t[q_at, :].astype(f32) * mixed_t[q_at, :].astype(f32)
+        along = jnp.concatenate([column_sum(product[:HEAD]), column_sum(product[HEAD:])], axis=1)
+        probs = jnp.exp(scores - lse)
+        grad_scores = (probs * (grad_probs - along)).astype(bf16)
+        out_ref[:, v_at] = dot(probs.astype(bf16), halves(grad_ref[:, q_at])).astype(bf16)
+        out_ref[:, k_at] = dot(grad_scores, halves(qkv_ref[:, q_at] * scale)).astype(bf16)
+        k_t = (qkv_ref[:, k_at] * scale).T
+        for part in range(2):
+            at = slice((head + part) * HEAD, (head + part + 1) * HEAD)
+            columns_at = slice(part * ROWS, (part + 1) * ROWS)
+            query_t[at, :] = dot(k_t[part * HEAD : (part + 1) * HEAD], grad_scores[:, columns_at]).astype(bf16)
+
+    ahead = start(0)
     for pair in range(HEADS // 2):
-        q_at, k_at, v_at = pair_slices(pair)
-        queries = qkv_ref[:, q_at] * scale
-        keys = qkv_ref[:, k_at]
-        values = qkv_ref[:, v_at]
-        grads = grad_ref[:, q_at]
-        q_t = queries.T
-        k_t = (keys * scale).T
-        keys_masked = jnp.concatenate([keys, key_mask], axis=1)
-        grad_keys = grad_values = None
-        for part in range(2):
-            head = pair * 2 + part
-            half = slice(part * HEAD, (part + 1) * HEAD)
-            at = slice(head * HEAD, (head + 1) * HEAD)
-            parts = [q_t[half], blank] if part == 0 else [blank, q_t[half]]
-            scores = dot(keys_masked, jnp.concatenate(parts + [query_mask], axis=0))
-            probs = jnp.exp(scores - lse_ref[head : head + 1, :])
-            head_grad = grad_t[at, :]
-            grad_parts = [head_grad, blank] if part == 0 else [blank, head_grad]
-            grad_probs = dot(values, jnp.concatenate(grad_parts, axis=0))
-            along = jnp.sum(head_grad.astype(f32) * mixed_t[at, :].astype(f32), axis=0, keepdims=True)
-            grad_scores = (probs * (grad_probs - along)).astype(bf16)
-            keep = low_half if part == 0 else jnp.logical_not(low_half)
-            zero = jnp.zeros_like(queries)
-            gv = dot(probs.astype(bf16), jnp.where(keep, grads, zero))
-            gk = dot(grad_scores, jnp.where(keep, queries, zero))
-            grad_values = gv if grad_values is None else grad_values + gv
-            grad_keys = gk if grad_keys is None else grad_keys + gk
-            query_t[at, :] = dot(k_t[half], grad_scores).astype(bf16)
-        out_ref[:, k_at] = grad_keys.astype(bf16)
-        out_ref[:, v_at] = grad_values.astype(bf16)
+        held = ahead
+        if pair + 1 < HEADS // 2:
+            ahead = start(pair + 1)
+        finish(pair, *held)
     for quarter in range(4):
         at = slice(quarter * 256, (quarter + 1) * 256)
         out_ref[:, at] = query_t[at, :].T
@@ -130,15 +155,20 @@
     return pl.ds(pl.multiple_of(lax.rem(place[0] + step, count) * rows, rows), rows)
 
 
-def stacked(refs):
-    parts = [ref[...].reshape(-1, ref.shape[-1]) for ref in refs]
+def stacked(refs, groups=1):
+    per = refs[0].shape[1] // groups
+    width = refs[0].shape[-1]
+    parts = [ref[:, g * per : (g + 1) * per, :].reshape(-1, width) for g in range(groups) for ref in refs]
     return parts[0] if len(parts) == 1 else jnp.concatenate(parts, axis=0)
 
 
-def unstack(refs, values):
-    rows = values.shape[0] // len(refs)
-    for index, ref in enumerate(refs):
-        ref[...] = values[index * rows : (index + 1) * rows].reshape(ref.shape)
+def unstack(refs, values, groups=1):
+    per = refs[0].shape[1] // groups
+    rows = values.shape[0] // (len(refs) * groups)
+    for g in range(groups):
+        for index, ref in enumerate(refs):
+            at = (g * len(refs) + index) * rows
+            ref[:, g * per : (g + 1) * per, :] = values[at : at + rows].reshape(ref.shape[0], per, ref.shape[2])
 
 
 def space_forward(
@@ -214,43 +244,65 @@
     norm_out, act_out, gpre_out, gat_out, branch_out, gain_out, bias_out, hb_out, ob_out = refs[6:15]
     block_out = refs[15:]
     first = pl.program_id(0) == 0
-    after_time = x[...]
+    clips = weights.shape[0]
+    own = 1024 // clips
+    groups = x.shape[0]
+    width = x.shape[2]
+    size = FF_CHUNK
+    chunks = 4096 // size
+    half = 1024 // size
+    share = size * clips // 4096
+    branch = stacked(grad, groups)
+    branch_out[...] = branch.reshape(branch_out.shape)
+
+    def down_of(chunk):
+        if share:
+            return weights[chunk * share : (chunk + 1) * share, 4 * own :, :].reshape(size, 1024)
+        return None
+
+    def hidden_of(chunk):
+        block, column = chunk // half, chunk % half
+        return weights[:, block * own : (block + 1) * own, column * size : (column + 1) * size].reshape(1024, size)
+
+    part_at = lambda chunk: slice(chunk * size, (chunk + 1) * size)
+    back_act = dot(branch, down_of(0), NT)
+    after_time = x[...].reshape(groups * ROWS, width)
     hat, rate = standardize(after_time)
     normed = (hat * gain[2:3, :] + bias[2:3, :]).astype(bf16)
-    norm_out[...] = normed
-    branch = stacked(grad)
-    branch_out[...] = branch
-    clips = weights.shape[0]
-    own = 1024 // clips
-    per_chunk = clips // 4
+    norm_out[...] = normed.reshape(norm_out.shape)
+    pre = dot(normed, hidden_of(0)) + hidden_bias[0:1, part_at(0)]
     result = None
     grad_norm = None
-    for chunk in range(4):
-        at = slice(chunk * 1024, (chunk + 1) * 1024)
-        w_hidden = block_of(weights, chunk)
-        w_down = weights[chunk * per_chunk : (chunk + 1) * per_chunk, 4 * own :, :].reshape(1024, 1024)
-        u = dot(normed, w_hidden) + hidden_bias[0:1, at]
+    bias_sums = []
+    for chunk in range(chunks):
+        at = part_at(chunk)
+        u, grad_act = pre, back_act
+        if chunk + 1 < chunks:
+            pre = dot(normed, hidden_of(chunk + 1)) + hidden_bias[0:1, part_at(chunk + 1)]
+            back_act = dot(branch, down_of(chunk + 1), NT)
         c0 = 0.7978845608028654
         square = u * u
         t = jnp.tanh(u * (c0 + (c0 * 0.044715) * square))
         half_plus = 0.5 + 0.5 * t
         act = (u * half_plus).astype(bf16)
-        act_out[:, at] = act
-        down = dot(act, w_down)
+        act_out[:, :, at] = act.reshape(groups, ROWS, size)
+        slope = half_plus + (0.5 * u) * (1.0 - t * t) * (c0 + (3.0 * c0 * 0.044715) * square)
+        gpre = (grad_act * slope).astype(bf16)
+        gpre_out[:, :, at] = gpre.reshape(groups, ROWS, size)
+        bias_sums.append(column_sum(gpre.astype(f32)))
+        down = dot(act, down_of(chunk))
         result = down if result is None else result + down
-        slope = half_plus + (0.5 * u) * (1.0 - t * t) * (c0 + (3.0 * c0 * 0.044715) * square)
-        gpre = (dot(branch, w_down, NT) * slope).astype(bf16)
-        gpre_out[:, at] = gpre
-        back = dot(gpre, w_hidden, NT)
+        back = dot(gpre, hidden_of(chunk), NT)
         grad_norm = back if grad_norm is None else grad_norm + back
     block = (after_time + result + out_bias[0:1, :]).astype(bf16)
-    unstack(block_out, block)
+    unstack(block_out, block, groups)
     upstream = branch.astype(f32)
-    gat_out[...] = (upstream + norm_back(hat, rate, gain[2:3, :], grad_norm)).astype(bf16)
+    gat = (upstream + norm_back(hat, rate, gain[2:3, :], grad_norm)).astype(bf16)
+    gat_out[...] = gat.reshape(gat_out.shape)
     add_row(gain_out, column_sum(grad_norm * hat), first)
     add_row(bias_out, column_sum(grad_norm), first)
     add_row(ob_out, column_sum(upstream), first)
-    add_row(hb_out, column_sum(gpre_out[...].astype(f32)), first)
+    add_row(hb_out, jnp.concatenate(bias_sums, axis=1), first)
 
 
 def time_backward(count, *refs):
@@ -295,7 +347,7 @@
             total = piece if total is None else total + piece
         total = total.astype(bf16)
         if by_rows:
-            out[0] = total
+            out[...] = total.reshape(out.shape)
             continue
         for block in range(total.shape[1] // 1024):
             for shard in range(out.shape[0]):
@@ -459,21 +511,25 @@
     count = len(grad)
     groups, _, width = x.shape
     ff = hidden_bias.shape[1]
+    each = FF_GROUPS if groups % FF_GROUPS == 0 else 1
     row = shape_of((1, width), f32)
     rows = lambda cols: shape_of((groups, ROWS, cols), bf16)
+    spec = lambda cols: pl.BlockSpec((each, ROWS, cols), lambda i: (i, 0, 0))
+    grad_spec = lambda a: pl.BlockSpec(
+        (a.shape[0], each * ROWS // (a.shape[0] * count), width), lambda i: (0, i, 0)
+    )
     return ordered_call(
         functools.partial(feed_forward, count),
         behind,
-        grid=(groups,),
-        in_specs=[group_spec(a, count) for a in grad]
-        + [step_spec((ROWS, width))]
+        grid=(groups // each,),
+        in_specs=[grad_spec(a) for a in grad]
+        + [spec(width)]
         + [whole(a.shape) for a in (gain, bias, hidden_bias, out_bias, weights)],
         out_specs=[
-            step_spec((ROWS, width)), step_spec((ROWS, ff)), step_spec((ROWS, ff)),
-            step_spec((ROWS, width)), step_spec((ROWS, width)),
+            spec(width), spec(ff), spec(ff), spec(width), spec(width),
             total_spec((1, width)), total_spec((1, width)), total_spec((1, ff)), total_spec((1, width)),
         ]
-        + [group_spec(a, count) for a in grad],
+        + [grad_spec(a) for a in grad],
         out_shape=[rows(width), rows(ff), rows(ff), rows(width), rows(width), row, row, shape_of((1, ff), f32), row]
         + [shape_of(a.shape, bf16) for a in grad],
         name="feed_forward",
@@ -515,9 +571,9 @@
     )(place, *flat)
 
 
-def weight_grad(behind, pairs, clips, rows, name, small=None, buffer=None, down_at=None):
+def weight_grad(behind, pairs, clips, rows, name, small=None, down_at=None):
     own = 1024 // clips
-    block = 256
+    block = 256 if down_at is None else 512
     width = pairs[0][0][0].shape[-1]
     by_rows = down_at is not None
 
@@ -535,14 +591,9 @@
     if small is not None:
         operands.append(small)
         specs.append(pl.BlockSpec((shards,) + small.shape[1:], lambda i: (i, 0, 0)))
-    aliases = {}
-    if buffer is not None:
-        aliases = {len(operands): 0}
-        operands.append(buffer)
-        specs.append(pl.BlockSpec(memory_space=pl.ANY))
     if by_rows:
-        steps = width // clips // block
-        out_spec = pl.BlockSpec((1, block, 1024), lambda i: (i // steps, down_at // block + i % steps, 0))
+        per = width // clips
+        out_spec = pl.BlockSpec((block // per, per, 1024), lambda i: (i, down_at // per, 0))
     else:
         out_rows = cols // 1024 * own + (0 if small is None else small.shape[1])
         out_spec = pl.BlockSpec((shards, out_rows, 1024), lambda i: (i, 0, 0))
@@ -552,6 +603,64 @@
         grid=(width // block,),
         in_specs=specs,
         out_specs=out_spec,
+        out_shape=shape_of((clips, rows, 1024), bf16),
+        name=name,
+    )(*operands)
+
+
+def column_kernel(starts, micros, *refs):
+    out = refs[-1]
+    step = pl.program_id(0)
+    for pair, (start, end) in enumerate(starts):
+        lefts = refs[pair * 2 * micros : pair * 2 * micros + micros]
+        rights = refs[pair * 2 * micros + micros : (pair + 1) * 2 * micros]
+
+        def fill():
+            total = None
+            for left, right in zip(lefts, rights):
+                piece = dot(rows_of(left), rows_of(right), TN)
+                total = piece if total is None else total + piece
+            out[...] = total.astype(bf16).reshape(out.shape)
+
+        if len(starts) == 1:
+            fill()
+        else:
+            pl.when(jnp.logical_and(step >= start, step < end))(fill)
+
+
+def weight_columns(behind, pairs, clips, rows, name, buffer=None):
+    own = 1024 // clips
+    block = 512
+    operands, specs, starts = [], [], []
+    step = 0
+    for lefts, rights in pairs:
+        count = rights[0].shape[-1] // block
+
+        def right_spec(a, start=step, last=count - 1):
+            rank = a.ndim
+            return pl.BlockSpec(
+                a.shape[:-1] + (block,), lambda i: (0,) * (rank - 1) + (jnp.clip(i - start, 0, last),)
+            )
+
+        operands += list(lefts) + list(rights)
+        specs += [whole(a.shape) for a in lefts] + [right_spec(a) for a in rights]
+        starts.append((step, step + count))
+        step += count
+    kernel = functools.partial(column_kernel, starts, len(pairs[0][0]))
+    aliases = {}
+    if buffer is not None:
+        before = len(operands)
+        aliases = {before: 0}
+        operands.append(buffer)
+        specs.append(pl.BlockSpec(memory_space=pl.ANY))
+        inner = kernel
+        kernel = lambda *refs: inner(*refs[:before], *refs[before + 1 :])
+    return ordered_call(
+        kernel,
+        behind,
+        grid=(step,),
+        in_specs=specs,
+        out_specs=pl.BlockSpec((clips, own, block), lambda i: (0, i // 2, i % 2)),
         out_shape=shape_of((clips, rows, 1024), bf16),
         input_output_aliases=aliases,
         name=name,
@@ -720,7 +829,7 @@
         behind = [ahead[m][5]]
     behind += marks(pieces_out[0])
     ff_grad = weight_grad(behind, [(pick(ahead, 1), pick(ahead, 4))], clips, 8 * own, "down_grad", down_at=4 * own)
-    ff_grad = weight_grad([], [(pick(ahead, 0), pick(ahead, 2))], clips, 8 * own, "hidden_grad", buffer=ff_grad)
+    ff_grad = weight_columns([], [(pick(ahead, 0), pick(ahead, 2))], clips, 8 * own, "hidden_grad", buffer=ff_grad)
     (ff_grad,), pieces_out[-1] = together([ff_grad], pieces_out[-1])
     ff_part = reduce_clip(ff_grad)
     behind = [ff_grad]
@@ -732,7 +841,7 @@
         )
         gas.append(inward(back[m][3:]))
         behind = [back[m][1]]
-    time_grad = weight_grad(
+    time_grad = weight_columns(
         behind, [(pick(middle, 0), pick(back, 0)), (pick(middle, 2), pick(ahead, 3))], clips, 4 * own, "time_grad"
     )
     (time_grad,), gas[0] = together([time_grad], gas[0])

time: 811 us -> 772 us (0.952)
  Pallas kernels: 496 us -> 422 us
  waiting for transfers between devices: 111 us -> 153 us
    pallas_call x15, Pallas kernels: 496 us -> 422 us  [ordered_call(): return lambda *operands: call(*behind, *operands)]
    ppermute x12, waiting for transfers between devices: 0.03 us -> 26 us  [local(): lax.ppermute(parts[d], 'tm', [(k, (k - d) % pieces) for k in range(pieces)])]
    ppermute x12, waiting for transfers between devices: 0.03 us -> 22.7 us  [local(): lax.ppermute(parts[d], 'tm', [(k, (k + d) % pieces) for k in range(pieces)])]
    ppermute x18, waiting for transfers between devices: 85.8 us -> 73.2 us  [shift(): lax.ppermute(values, 'tm', [(k, (k + step) % count) for k in range(count)])]
    ppermute x12, starting transfers between devices: 41.5 us -> 31.6 us  [local(): lax.ppermute(parts[d], 'tm', [(k, (k + d) % pieces) for k in range(pieces)])]
  transfers between devices with their start and end apart: 48 -> 48, of which waited for: 11 -> 14; matrix products, arithmetic and copies ran while one was open for 5% -> 6% of each run, Pallas kernels for 62% -> 55%
where the time goes in v2:
time: 772 us; the launch traced here: 762 us
  Pallas kernels  422 us (55%)
  waiting for transfers between devices  153 us (20%)
  starting transfers between devices  105 us (14%)
  local copies, waits for them, and re-layouts  32.5 us (4%)
  other arithmetic  25.5 us (3%)
  between operations  15.3 us (2%)
  blocking collectives  9.17 us (1%)
    pallas_call x15, Pallas kernels, ordered_call(): return lambda *operands: call(*behind, *operands)  422 us
    ppermute x18, waiting for transfers between devices, shift(): lax.ppermute(values, 'tm', [(k, (k + step) % count) for k in range(count)])  73.2 us
    ppermute x18, starting transfers between devices, shift(): lax.ppermute(values, 'tm', [(k, (k + step) % count) for k in range(count)])  54.8 us
    ppermute x12, starting transfers between devices, local(): lax.ppermute(parts[d], 'tm', [(k, (k + d) % pieces) for k in range(pieces)])  31.6 us
    all_gather x3, waiting for transfers between devices, gather(): lax.all_gather(jnp.concatenate(parts, axis=0), 'clip', axis=0, tiled=False)  30.5 us
    ppermute x12, waiting for transfers between devices, local(): lax.ppermute(parts[d], 'tm', [(k, (k - d) % pieces) for k in range(pieces)])  26 us
    ppermute x12, waiting for transfers between devices, local(): lax.ppermute(parts[d], 'tm', [(k, (k + d) % pieces) for k in range(pieces)])  22.7 us
    ppermute x12, starting transfers between devices, local(): lax.ppermute(parts[d], 'tm', [(k, (k - d) % pieces) for k in range(pieces)])  18.4 us
  transfers between devices with their start and end apart: 48, of which 14 were waited for; matrix products, arithmetic and copies ran while one was open for 6% of the time, Pallas kernels for 55%

profile of v2, /device:TPU:0, one launch (start us, length us, event | category | flops | bytes accessed | tf_op | source)
XLA Modules:
  0.0 761.7 jit_solution(10385310306380115052)
XLA Ops:
  14.8 4.1 fusion.26
  20.5 3.0 collective-permute-start
  23.5 2.6 collective-permute-start.1
  27.7 9.2 %all-gather.4 = bf16[8,19,128]{2,1,0:T(8,128)(2,1)S(1)} all-gather(bf16[1,19,128]{2,1,0:T(8,128)(2,1)S(1)} %bitcast.126), channel_id=2, replica_groups=mesh['clip'=8,'tm'=4] {'clip'}, dimensions={0}, use_global_device_ids=true | all-gather | bytes 43776 | tf_op jit(solution)/shard_map/all_gather | solution.py:782
  43.0 24.9 %all-gather.9.cloned.1.call-done = bf16[4096,1024]{1,0:T(8,128)(2,1)} async-done(((bf16[512,1024]{1,0:T(8,128)(2,1)}), bf16[4096,1024]{1,0:T(8,128)(2,1)}) %all-gather.9.cloned.1.call-update) | async-done | bytes 8388624 | tf_op jit(solution)/shard_map/all_gather | solution.py:712
  68.0 22.6 %space_forward.2 = (bf16[4,256,1024]{2,1,0:T(8,128)(2,1)}, bf16[4,256,3072]{2,1,0:T(8,128)(2,1)}, bf16[4,256,1024]{2,1,0:T(8,128)(2,1)}, f32[4,16,256]{2,1,0:T(8...) custom-call(s32[1]{0:T(128)} %bitcast.refs_0_.refs_4_.refs_5_, ...), custom_call_target="tpu_custom_call" | custom-call | tf_op jit(solution)/shard_map/space_forward/pallas_call | solution.py:380
  100.1 22.7 %space_forward.3 = (bf16[4,256,1024]{2,1,0:T(8,128)(2,1)}, bf16[4,256,3072]{2,1,0:T(8,128)(2,1)}, bf16[4,256,1024]{2,1,0:T(8,128)(2,1)}, f32[4,16,256]{2,1,0:T(8...) custom-call(f32[4,16,256]{2,1,0:T(8,128)} %get-tuple-element.117.ref, ...), custom_call_target="tpu_custom_call" | custom-call | tf_op jit(solution)/shard_map/space_forward/pallas_call | solution.py:380
  129.0 22.3 %collective-permute-done.4.refs_6_.refs_3_ = bf16[4,64,1024]{2,1,0:T(8,128)(2,1)S(1)} collective-permute-done((bf16[4,64,1024]{2,1,0:T(8,128)(2,1)}, bf16[4,64,1024]{2,1,0:T(8,128)(2,1)S(1)}, u32[]{:S(2)}, u32[]{:S(2)}) %collective-permute-start.4) | collective-permute-done | bytes 524320 | tf_op jit(solution)/shard_map/ppermute | solution.py:802
  152.3 21.8 %time_forward.2 = (bf16[4,256,1024]{2,1,0:T(8,128)(2,1)}, bf16[4,256,3072]{2,1,0:T(8,128)(2,1)}, bf16[4,256,1024]{2,1,0:T(8,128)(2,1)}, f32[4,16,256]{2,1,0:T(8,128)}, f32[4,256,1024]{2,1,0:T(8,128)}) custom-call(f32[4,16,256]{2,1,0:T(8,128)} %get-tuple-element.118.refs_0_.refs_15_, bf16[8,128]{1,0:T(8,128)(2,1)} %slice.227.refs_1_, ...), custom_call_target="tpu_custom_call" | custom-call | tf_op jit(solution)/shard_map/time_forward/pallas_call | solution.py:380
  174.4 21.9 %time_forward.3 = (bf16[4,256,1024]{2,1,0:T(8,128)(2,1)}, bf16[4,256,3072]{2,1,0:T(8,128)(2,1)}, bf16[4,256,1024]{2,1,0:T(8,128)(2,1)}, f32[4,16,256]{2,1,0:T(8,128)}, f32[4,256,1024]{2,1,0:T(8,128)}) custom-call(f32[4,16,256]{2,1,0:T(8,128)} %get-tuple-element.123.refs_0_.refs_12_, bf16[4,64,1024]{2,1,0:T(8,128)(2,1)} %get-tuple-element.124.refs_1_, ...), custom_call_target="tpu_custom_call" | custom-call | tf_op jit(solution)/shard_map/time_forward/pallas_call | solution.py:380
  196.4 10.9 %collective-permute-start.10 = (bf16[4,64,1024]{2,1,0:T(8,128)(2,1)}, bf16[4,64,1024]{2,1,0:T(8,128)(2,1)S(1)}, u32[]{:S(2)}, u32[]{:S(2)}) collective-permute-start(bf16[4,64,1024]{2,1,0:T(8,128)(2,1)} %get-tuple-element.135), channel_id=1, source_target_pairs={{0,2},{1,3},{2,0},{3,1},{4,6},{5,7},{6,4},{7,5},{8,10},{9,11},{10,... | collective-permute-start | bytes 1572872 | tf_op jit(solution)/shard_map/ppermute | solution.py:802
  207.8 3.4 collective-permute-start.11
  211.6 5.6 all-gather.13.cloned.1.call-done
  217.2 50.8 %feed_forward.2 = (bf16[4,256,1024]{2,1,0:T(8,128)(2,1)}, bf16[4,256,4096]{2,1,0:T(8,128)(2,1)}, bf16[4,256,4096]{2,1,0:T(8,128)(2,1)}, bf16[4,256,1024]{2,1,0:T...) custom-call(f32[4,16,256]{2,1,0:T(8,128)} %get-tuple-element.128.ref, ...), custom_call_target="tpu_custom_call" | custom-call | tf_op jit(solution)/shard_map/feed_forward/pallas_call | solution.py:380
  268.0 3.4 collective-permute-start.12
  273.5 50.8 %feed_forward.3 = (bf16[4,256,1024]{2,1,0:T(8,128)(2,1)}, bf16[4,256,4096]{2,1,0:T(8,128)(2,1)}, bf16[4,256,4096]{2,1,0:T(8,128)(2,1)}, bf16[4,256,1024]{2,1,0:T...) custom-call(f32[1,1024]{1,0:T(1,128)} %get-tuple-element.131.refs_0_, ...), custom_call_target="tpu_custom_call" | custom-call | tf_op jit(solution)/shard_map/feed_forward/pallas_call | solution.py:380
  324.3 2.8 collective-permute-start.15
  330.3 22.9 %down_grad.1.refs_4_ = bf16[8,1024,1024]{2,1,0:T(8,128)(2,1)} custom-call(f32[1,1024]{1,0:T(1,128)} %get-tuple-element.141.refs_0_, bf16[8,128]{1,0:T(8,128)(2,1)} %slice.232.refs_1_, bf16[8,128]{1,0:T(8,128)(2,1)} %slice.233.refs_2_, bf16[8,128]{1,0:T(8,128)(2,1)} %slice.234.refs_3_, bf16[4,256,4096]{2,1,0:T(8,128)(2,1)} %get-tuple-element.145.refs_4_, ...), custom_call_target="tpu_custom_call" | custom-call | tf_op jit(solution)/shard_map/down_grad/pallas_call | solution.py:380
  353.2 23.2 %hidden_grad.1.refs_0_ = bf16[8,1024,1024]{2,1,0:T(8,128)(2,1)} custom-call(bf16[4,256,1024]{2,1,0:T(8,128)(2,1)} %get-tuple-element.130.refs_0_, bf16[4,256,1024]{2,1,0:T(8,128)(2,1)} %get-tuple-element.138.refs_1_, bf16[4,256,4096]{2,1,0:T(8,128)(2,1)} %get-tuple-element.139.refs_2_, ...), custom_call_target="tpu_custom_call", output_to_operand_aliasing={{}: (4, {})} | custom-call | tf_op jit(solution)/shard_map/hidden_grad/pallas_call | solution.py:380
  376.5 30.0 %time_backward.2 = (bf16[4,256,3072]{2,1,0:T(8,128)(2,1)}, f32[1,1024]{1,0:T(1,128)}, f32[1,1024]{1,0:T(1,128)}, bf16[4,64,1024]{2,1,0:T(8,128)(2,1)}, bf16[4,64...) custom-call(bf16[8,1024,1024]{2,1,0:T(8,128)(2,1)} %hidden_grad.1.refs_0_, ...), custom_call_target="tpu_custom_call" | custom-call | tf_op jit(solution)/shard_map/time_backward/pallas_call | solution.py:380
  406.5 3.8 collective-permute-start.18
  411.2 30.6 %time_backward.3 = (bf16[4,256,3072]{2,1,0:T(8,128)(2,1)}, f32[1,1024]{1,0:T(1,128)}, f32[1,1024]{1,0:T(1,128)}, bf16[4,64,1024]{2,1,0:T(8,128)(2,1)}, bf16[4,64...) custom-call(f32[1,1024]{1,0:T(1,128)} %get-tuple-element.157.refs_0_, ...), custom_call_target="tpu_custom_call" | custom-call | tf_op jit(solution)/shard_map/time_backward/pallas_call | solution.py:380
  441.8 26.0 %time_grad.1.refs_0_ = bf16[8,512,1024]{2,1,0:T(8,128)(2,1)} custom-call(f32[1,1024]{1,0:T(1,128)} %get-tuple-element.161.refs_0_, bf16[4,256,1024]{2,1,0:T(8,128)(2,1)} %get-tuple-element.162.refs_1_, bf16[4,256,1024]{2,1,0:T(8,128)(2,1)} %get-tuple-element.163.refs_2_, bf16[4,256,3072]{2,1,0:T(8,128)(2,1)} %get-tuple-element.164.refs_3_, ...), custom_call_target="tpu_custom_call" | custom-call | tf_op jit(solution)/shard_map/time_grad/pallas_call | solution.py:380
  469.2 3.3 collective-permute-start.24
  474.2 33.5 %space_backward.2 = (bf16[4,256,3072]{2,1,0:T(8,128)(2,1)}, bf16[4,256,1024]{2,1,0:T(8,128)(2,1)}, f32[2,4,256,1024]{3,2,1,0:T(8,128)}, f32[1,1024]{1,0:T(1,128)...) custom-call(bf16[8,512,1024]{2,1,0:T(8,128)(2,1)} %time_grad.1.refs_0_, bf16[4,64,1024]{2,1,0:T(8,128)(2,1)} %get-tuple-element.171.refs_1_, ...), custom_call_target="tpu_custom_call" | custom-call | tf_op jit(solution)/shard_map/space_backward/pallas_call | solution.py:380
  509.0 2.9 constant_dynamic-slice_fusion.8
  511.9 2.5 collective-permute-start.21
  516.9 26.0 %collective-permute-done.25.refs_3_ = bf16[4,64,1024]{2,1,0:T(8,128)(2,1)S(1)} collective-permute-done((bf16[4,64,1024]{2,1,0:T(8,128)(2,1)}, bf16[4,64,1024]{2,1,0:T(8,128)(2,1)S(1)}, u32[]{:S(2)}, u32[]{:S(2)}) %collective-permute-start.25) | collective-permute-done | bytes 524320 | tf_op jit(solution)/shard_map/ppermute | solution.py:805
  543.9 33.3 %space_backward.3 = (bf16[4,256,3072]{2,1,0:T(8,128)(2,1)}, bf16[4,256,1024]{2,1,0:T(8,128)(2,1)}, f32[2,4,256,1024]{3,2,1,0:T(8,128)}, f32[1,1024]{1,0:T(1,128)...) custom-call(bf16[8,128]{1,0:T(8,128)(2,1)} %slice.201.refs_0_, ...), custom_call_target="tpu_custom_call", output_to_operand_aliasing={{2}: (16, {})} | custom-call | tf_op jit(solution)/shard_map/space_backward/pallas_call | solution.py:380
  583.0 26.5 %space_grad.1 = bf16[8,544,1024]{2,1,0:T(8,128)(2,1)} custom-call(bf16[8,128]{1,0:T(8,128)(2,1)} %slice.235.refs_0_, bf16[4,256,1024]{2,1,0:T(8,128)(2,1)} %get-tuple-element.179.refs_1_, bf16[4,256,1024]{2,1,0:T(8,128)(2,1)} %get-tuple-element.180.refs_2_, bf16[4,256,3072]{2,1,0:T(8,128)(2,1)} %get-tuple-element.181.refs_3_, ...), custom_call_target="tpu_custom_call" | custom-call | tf_op jit(solution)/shard_map/space_grad/pallas_call | solution.py:380
  610.9 3.7 collective-permute-start.29
  614.7 4.5 collective-permute-done.27
  619.2 23.9 %collective-permute-done.28 = bf16[128,1024]{1,0:T(8,128)(2,1)S(1)} collective-permute-done((bf16[128,1024]{1,0:T(8,128)(2,1)S(1)}, bf16[128,1024]{1,0:T(8,128)(2,1)S(1)}, u32[]{:S(2)}, u32[]{:S(2)}) %collective-permute-start.28) | collective-permute-done | bytes 262176 | tf_op jit(solution)/shard_map/ppermute | solution.py:721
  645.1 6.2 collective-permute-start.30
  651.3 4.8 assemble.1
  656.0 3.0 collective-permute-start.34
  659.0 2.9 collective-permute-start.32
  663.2 12.0 %collective-permute-done.31 = bf16[128,1024]{1,0:T(8,128)(2,1)S(1)} collective-permute-done((bf16[128,1024]{1,0:T(8,128)(2,1)}, bf16[128,1024]{1,0:T(8,128)(2,1)S(1)}, u32[]{:S(2)}, u32[]{:S(2)}) %collective-permute-start.31) | collective-permute-done | bytes 262176 | tf_op jit(solution)/shard_map/ppermute | solution.py:721
  677.6 8.4 %collective-permute-done.34 = bf16[256,1024]{1,0:T(8,128)(2,1)S(1)} collective-permute-done((bf16[256,1024]{1,0:T(8,128)(2,1)S(1)}, bf16[256,1024]{1,0:T(8,128)(2,1)S(1)}, u32[]{:S(2)}, u32[]{:S(2)}) %collective-permute-start.34) | collective-permute-done | bytes 524320 | tf_op jit(solution)/shard_map/ppermute | solution.py:721
  690.5 21.8 %collective-permute-start.36 = (bf16[136,1024]{1,0:T(8,128)(2,1)S(1)}, bf16[136,1024]{1,0:T(8,128)(2,1)S(1)}, u32[]{:S(2)}, u32[]{:S(2)}) collective-permute-start(bf16[136,1024]{1,0:T(8,128)(2,1)S(1)} %get-tuple-element.246), channel_id=1, source_target_pairs={{0,1},{1,2},{2,3},{3,0},{4,5},{5,6},{6,7},{7,4},{8,9},{9,10},{10,1... | collective-permute-start | bytes 835592 | tf_op jit(solution)/shard_map/ppermute | solution.py:721
  712.3 2.4 collective-permute-start.38
  714.7 4.7 collective-permute-done.36
  719.4 6.9 collective-permute-done.37
  726.3 2.9 collective-permute-done.38
  730.5 6.3 collective-permute-start.39
  736.7 3.4 collective-permute-start.40
  740.1 4.1 collective-permute-done.39
  744.2 5.8 collective-permute-done.40
  (249 shorter events, 71.4 us)
Async XLA Ops:
  7.2 60.8 %all-gather.9.cloned.1.call-start = ((), (), s32[]{:S(2)}) async-start(), calls=%async_computation.6 | async-start | bytes 9437184 | tf_op jit(solution)/shard_map/all_gather | solution.py:712
  10.5 118.4 %all-gather.11.cloned.1.call-start = ((), (), s32[]{:S(2)}) async-start(), calls=%async_computation.7 | async-start | bytes 9437184 | tf_op jit(solution)/shard_map/all_gather | solution.py:712
  11.7 205.5 %all-gather.13.cloned.1.call-start = ((), (), s32[]{:S(2)}) async-start(), calls=%async_computation.8 | async-start | bytes 18874368 | tf_op jit(solution)/shard_map/all_gather | solution.py:712
  14.7 493.0 %reduce-scatter.4.cloned.1.call-start = ((), (), s32[]{:S(2)}) async-start(), calls=%async_computation.3 | async-start | bytes 18874368 | tf_op jit(solution)/shard_map/reduce_scatter | solution.py:716
  20.5 73.3 %collective-permute-start = (bf16[4,64,1024]{2,1,0:T(8,128)(2,1)}, bf16[4,64,1024]{2,1,0:T(8,128)(2,1)S(1)}, u32[]{:S(2)}, u32[]{:S(2)}) collective-permute-start(bf16[4,64,1024]{2,1,0:T(8,128)(2,1)} %get-tuple-element.241), channel_id=1, source_target_pairs={{0,1},{1,2},{2,3},{3,0},{4,5},{5,6},{6,7},{7,4},{8,9},{9,10},{10,1... | collective-permute-start | bytes 1572872 | tf_op jit(solution)/shard_map/ppermute | solution.py:802
  23.5 70.9 %collective-permute-start.1 = (bf16[4,64,1024]{2,1,0:T(8,128)(2,1)}, bf16[4,64,1024]{2,1,0:T(8,128)(2,1)S(1)}, u32[]{:S(2)}, u32[]{:S(2)}) collective-permute-start(bf16[4,64,1024]{2,1,0:T(8,128)(2,1)} %get-tuple-element.240), channel_id=1, source_target_pairs={{0,2},{1,3},{2,0},{3,1},{4,6},{5,7},{6,4},{7,5},{8,10},{9,11},{10,... | collective-permute-start | bytes 1572872 | tf_op jit(solution)/shard_map/ppermute | solution.py:802
  26.1 68.9 %collective-permute-start.2 = (bf16[4,64,1024]{2,1,0:T(8,128)(2,1)}, bf16[4,64,1024]{2,1,0:T(8,128)(2,1)}, u32[]{:S(2)}, u32[]{:S(2)}) collective-permute-start(bf16[4,64,1024]{2,1,0:T(8,128)(2,1)} %get-tuple-element.239), channel_id=1, source_target_pairs={{0,3},{1,0},{2,1},{3,2},{4,7},{5,4},{6,5},{7,6},{8,11},{9,8},{10,9... | collective-permute-start | bytes 1572872 | tf_op jit(solution)/shard_map/ppermute | solution.py:802
  90.6 34.7 %collective-permute-start.3 = (bf16[4,64,1024]{2,1,0:T(8,128)(2,1)}, bf16[4,64,1024]{2,1,0:T(8,128)(2,1)S(1)}, u32[]{:S(2)}, u32[]{:S(2)}) collective-permute-start(bf16[4,64,1024]{2,1,0:T(8,128)(2,1)} %get-tuple-element.120), channel_id=1, source_target_pairs={{0,1},{1,2},{2,3},{3,0},{4,5},{5,6},{6,7},{7,4},{8,9},{9,10},{10,1... | collective-permute-start | bytes 1572872 | tf_op jit(solution)/shard_map/ppermute | solution.py:802
  96.2 55.1 %collective-permute-start.4 = (bf16[4,64,1024]{2,1,0:T(8,128)(2,1)}, bf16[4,64,1024]{2,1,0:T(8,128)(2,1)S(1)}, u32[]{:S(2)}, u32[]{:S(2)}) collective-permute-start(bf16[4,64,1024]{2,1,0:T(8,128)(2,1)} %get-tuple-element.121), channel_id=1, source_target_pairs={{0,2},{1,3},{2,0},{3,1},{4,6},{5,7},{6,4},{7,5},{8,10},{9,11},{10,... | collective-permute-start | bytes 1572872 | tf_op jit(solution)/shard_map/ppermute | solution.py:802
  98.7 52.6 %collective-permute-start.5 = (bf16[4,64,1024]{2,1,0:T(8,128)(2,1)}, bf16[4,64,1024]{2,1,0:T(8,128)(2,1)S(1)}, u32[]{:S(2)}, u32[]{:S(2)}) collective-permute-start(bf16[4,64,1024]{2,1,0:T(8,128)(2,1)} %get-tuple-element.122), channel_id=1, source_target_pairs={{0,3},{1,0},{2,1},{3,2},{4,7},{5,4},{6,5},{7,6},{8,11},{9,8},{10,9... | collective-permute-start | bytes 1572872 | tf_op jit(solution)/shard_map/ppermute | solution.py:802
  122.8 51.3 %collective-permute-start.6 = (bf16[4,64,1024]{2,1,0:T(8,128)(2,1)}, bf16[4,64,1024]{2,1,0:T(8,128)(2,1)}, u32[]{:S(2)}, u32[]{:S(2)}) collective-permute-start(bf16[4,64,1024]{2,1,0:T(8,128)(2,1)} %get-tuple-element.125), channel_id=1, source_target_pairs={{0,1},{1,2},{2,3},{3,0},{4,5},{5,6},{6,7},{7,4},{8,9},{9,10},{10,1... | collective-permute-start | bytes 1572872 | tf_op jit(solution)/shard_map/ppermute | solution.py:802
  123.5 51.0 %collective-permute-start.7 = (bf16[4,64,1024]{2,1,0:T(8,128)(2,1)}, bf16[4,64,1024]{2,1,0:T(8,128)(2,1)}, u32[]{:S(2)}, u32[]{:S(2)}) collective-permute-start(bf16[4,64,1024]{2,1,0:T(8,128)(2,1)} %get-tuple-element.126), channel_id=1, source_target_pairs={{0,2},{1,3},{2,0},{3,1},{4,6},{5,7},{6,4},{7,5},{8,10},{9,11},{10,... | collective-permute-start | bytes 1572872 | tf_op jit(solution)/shard_map/ppermute | solution.py:802
  125.3 49.1 %collective-permute-start.8 = (bf16[4,64,1024]{2,1,0:T(8,128)(2,1)}, bf16[4,64,1024]{2,1,0:T(8,128)(2,1)}, u32[]{:S(2)}, u32[]{:S(2)}) collective-permute-start(bf16[4,64,1024]{2,1,0:T(8,128)(2,1)} %get-tuple-element.127), channel_id=1, source_target_pairs={{0,3},{1,0},{2,1},{3,2},{4,7},{5,4},{6,5},{7,6},{8,11},{9,8},{10,9... | collective-permute-start | bytes 1572872 | tf_op jit(solution)/shard_map/ppermute | solution.py:802
  196.4 75.0 %collective-permute-start.10 = (bf16[4,64,1024]{2,1,0:T(8,128)(2,1)}, bf16[4,64,1024]{2,1,0:T(8,128)(2,1)S(1)}, u32[]{:S(2)}, u32[]{:S(2)}) collective-permute-start(bf16[4,64,1024]{2,1,0:T(8,128)(2,1)} %get-tuple-element.135), channel_id=1, source_target_pairs={{0,2},{1,3},{2,0},{3,1},{4,6},{5,7},{6,4},{7,5},{8,10},{9,11},{10,... | collective-permute-start | bytes 1572872 | tf_op jit(solution)/shard_map/ppermute | solution.py:802
  207.8 65.6 %collective-permute-start.11 = (bf16[4,64,1024]{2,1,0:T(8,128)(2,1)}, bf16[4,64,1024]{2,1,0:T(8,128)(2,1)}, u32[]{:S(2)}, u32[]{:S(2)}) collective-permute-start(bf16[4,64,1024]{2,1,0:T(8,128)(2,1)} %get-tuple-element.136), channel_id=1, source_target_pairs={{0,3},{1,0},{2,1},{3,2},{4,7},{5,4},{6,5},{7,6},{8,11},{9,8},{10,9... | collective-permute-start | bytes 1572872 | tf_op jit(solution)/shard_map/ppermute | solution.py:802
  211.2 62.2 %collective-permute-start.9 = (bf16[4,64,1024]{2,1,0:T(8,128)(2,1)}, bf16[4,64,1024]{2,1,0:T(8,128)(2,1)}, u32[]{:S(2)}, u32[]{:S(2)}) collective-permute-start(bf16[4,64,1024]{2,1,0:T(8,128)(2,1)} %get-tuple-element.134), channel_id=1, source_target_pairs={{0,1},{1,2},{2,3},{3,0},{4,5},{5,6},{6,7},{7,4},{8,9},{9,10},{10,1... | collective-permute-start | bytes 1572872 | tf_op jit(solution)/shard_map/ppermute | solution.py:802
  268.0 60.2 %collective-permute-start.12 = (bf16[4,64,1024]{2,1,0:T(8,128)(2,1)}, bf16[4,64,1024]{2,1,0:T(8,128)(2,1)S(1)}, u32[]{:S(2)}, u32[]{:S(2)}) collective-permute-start(bf16[4,64,1024]{2,1,0:T(8,128)(2,1)} %get-tuple-element.142), channel_id=1, source_target_pairs={{0,3},{1,0},{2,1},{3,2},{4,7},{5,4},{6,5},{7,6},{8,11},{9,8},{10,9... | collective-permute-start | bytes 1572872 | tf_op jit(solution)/shard_map/ppermute | solution.py:805
  271.4 57.6 %collective-permute-start.13 = (bf16[4,64,1024]{2,1,0:T(8,128)(2,1)}, bf16[4,64,1024]{2,1,0:T(8,128)(2,1)S(1)}, u32[]{:S(2)}, u32[]{:S(2)}) collective-permute-start(bf16[4,64,1024]{2,1,0:T(8,128)(2,1)} %get-tuple-element.143), channel_id=1, source_target_pairs={{0,2},{1,3},{2,0},{3,1},{4,6},{5,7},{6,4},{7,5},{8,10},{9,11},{10,... | collective-permute-start | bytes 1572872 | tf_op jit(solution)/shard_map/ppermute | solution.py:805
  272.2 57.5 %collective-permute-start.14 = (bf16[4,64,1024]{2,1,0:T(8,128)(2,1)}, bf16[4,64,1024]{2,1,0:T(8,128)(2,1)S(1)}, u32[]{:S(2)}, u32[]{:S(2)}) collective-permute-start(bf16[4,64,1024]{2,1,0:T(8,128)(2,1)} %get-tuple-element.144), channel_id=1, source_target_pairs={{0,1},{1,2},{2,3},{3,0},{4,5},{5,6},{6,7},{7,4},{8,9},{9,10},{10,1... | collective-permute-start | bytes 1572872 | tf_op jit(solution)/shard_map/ppermute | solution.py:805
  324.3 52.1 %collective-permute-start.15 = (bf16[4,64,1024]{2,1,0:T(8,128)(2,1)}, bf16[4,64,1024]{2,1,0:T(8,128)(2,1)}, u32[]{:S(2)}, u32[]{:S(2)}) collective-permute-start(bf16[4,64,1024]{2,1,0:T(8,128)(2,1)} %get-tuple-element.150), channel_id=1, source_target_pairs={{0,3},{1,0},{2,1},{3,2},{4,7},{5,4},{6,5},{7,6},{8,11},{9,8},{10,9... | collective-permute-start | bytes 1572872 | tf_op jit(solution)/shard_map/ppermute | solution.py:805
  327.1 49.3 %collective-permute-start.16 = (bf16[4,64,1024]{2,1,0:T(8,128)(2,1)}, bf16[4,64,1024]{2,1,0:T(8,128)(2,1)}, u32[]{:S(2)}, u32[]{:S(2)}) collective-permute-start(bf16[4,64,1024]{2,1,0:T(8,128)(2,1)} %get-tuple-element.151), channel_id=1, source_target_pairs={{0,2},{1,3},{2,0},{3,1},{4,6},{5,7},{6,4},{7,5},{8,10},{9,11},{10,... | collective-permute-start | bytes 1572872 | tf_op jit(solution)/shard_map/ppermute | solution.py:805
  328.2 48.2 %collective-permute-start.17 = (bf16[4,64,1024]{2,1,0:T(8,128)(2,1)}, bf16[4,64,1024]{2,1,0:T(8,128)(2,1)}, u32[]{:S(2)}, u32[]{:S(2)}) collective-permute-start(bf16[4,64,1024]{2,1,0:T(8,128)(2,1)} %get-tuple-element.152), channel_id=1, source_target_pairs={{0,1},{1,2},{2,3},{3,0},{4,5},{5,6},{6,7},{7,4},{8,9},{9,10},{10,1... | collective-permute-start | bytes 1572872 | tf_op jit(solution)/shard_map/ppermute | solution.py:805
  376.5 233.1 %reduce-scatter.8.cloned.1.call-start = ((), (), s32[]{:S(2)}) async-start(), calls=%async_computation.5 | async-start | bytes 9437184 | tf_op jit(solution)/shard_map/reduce_scatter | solution.py:716
  406.5 61.4 %collective-permute-start.18 = (bf16[4,64,1024]{2,1,0:T(8,128)(2,1)}, bf16[4,64,1024]{2,1,0:T(8,128)(2,1)S(1)}, u32[]{:S(2)}, u32[]{:S(2)}) collective-permute-start(bf16[4,64,1024]{2,1,0:T(8,128)(2,1)} %get-tuple-element.167), channel_id=1, source_target_pairs={{0,3},{1,0},{2,1},{3,2},{4,7},{5,4},{6,5},{7,6},{8,11},{9,8},{10,9... | collective-permute-start | bytes 1572872 | tf_op jit(solution)/shard_map/ppermute | solution.py:805
  410.3 57.5 %collective-permute-start.19 = (bf16[4,64,1024]{2,1,0:T(8,128)(2,1)}, bf16[4,64,1024]{2,1,0:T(8,128)(2,1)S(1)}, u32[]{:S(2)}, u32[]{:S(2)}) collective-permute-start(bf16[4,64,1024]{2,1,0:T(8,128)(2,1)} %get-tuple-element.168), channel_id=1, source_target_pairs={{0,2},{1,3},{2,0},{3,1},{4,6},{5,7},{6,4},{7,5},{8,10},{9,11},{10,... | collective-permute-start | bytes 1572872 | tf_op jit(solution)/shard_map/ppermute | solution.py:805
  410.3 57.6 %collective-permute-start.20 = (bf16[4,64,1024]{2,1,0:T(8,128)(2,1)}, bf16[4,64,1024]{2,1,0:T(8,128)(2,1)S(1)}, u32[]{:S(2)}, u32[]{:S(2)}) collective-permute-start(bf16[4,64,1024]{2,1,0:T(8,128)(2,1)} %get-tuple-element.169), channel_id=1, source_target_pairs={{0,1},{1,2},{2,3},{3,0},{4,5},{5,6},{6,7},{7,4},{8,9},{9,10},{10,1... | collective-permute-start | bytes 1572872 | tf_op jit(solution)/shard_map/ppermute | solution.py:805
  469.0 220.3 %reduce-scatter.6.cloned.1.call-start = ((), (), s32[]{:S(2)}) async-start(), calls=%async_computation.4 | async-start | bytes 10027008 | tf_op jit(solution)/shard_map/reduce_scatter | solution.py:716
  469.2 47.1 %collective-permute-start.24 = (bf16[4,64,1024]{2,1,0:T(8,128)(2,1)}, bf16[4,64,1024]{2,1,0:T(8,128)(2,1)S(1)}, u32[]{:S(2)}, u32[]{:S(2)}) collective-permute-start(bf16[4,64,1024]{2,1,0:T(8,128)(2,1)} %get-tuple-element.183), channel_id=1, source_target_pairs={{0,3},{1,0},{2,1},{3,2},{4,7},{5,4},{6,5},{7,6},{8,11},{9,8},{10,9... | collective-permute-start | bytes 1572872 | tf_op jit(solution)/shard_map/ppermute | solution.py:805
  472.5 70.4 %collective-permute-start.25 = (bf16[4,64,1024]{2,1,0:T(8,128)(2,1)}, bf16[4,64,1024]{2,1,0:T(8,128)(2,1)S(1)}, u32[]{:S(2)}, u32[]{:S(2)}) collective-permute-start(bf16[4,64,1024]{2,1,0:T(8,128)(2,1)} %get-tuple-element.184), channel_id=1, source_target_pairs={{0,2},{1,3},{2,0},{3,1},{4,6},{5,7},{6,4},{7,5},{8,10},{9,11},{10,... | collective-permute-start | bytes 1572872 | tf_op jit(solution)/shard_map/ppermute | solution.py:805
  473.6 69.3 %collective-permute-start.26 = (bf16[4,64,1024]{2,1,0:T(8,128)(2,1)}, bf16[4,64,1024]{2,1,0:T(8,128)(2,1)S(1)}, u32[]{:S(2)}, u32[]{:S(2)}) collective-permute-start(bf16[4,64,1024]{2,1,0:T(8,128)(2,1)} %get-tuple-element.185), channel_id=1, source_target_pairs={{0,1},{1,2},{2,3},{3,0},{4,5},{5,6},{6,7},{7,4},{8,9},{9,10},{10,1... | collective-permute-start | bytes 1572872 | tf_op jit(solution)/shard_map/ppermute | solution.py:805
  511.9 68.7 %collective-permute-start.21 = (bf16[256,1024]{1,0:T(8,128)(2,1)}, bf16[256,1024]{1,0:T(8,128)(2,1)}, u32[]{:S(2)}, u32[]{:S(2)}) collective-permute-start(bf16[256,1024]{1,0:T(8,128)(2,1)} %get-tuple-element.231), channel_id=1, source_target_pairs={{0,1},{1,2},{2,3},{3,0},{4,5},{5,6},{6,7},{7,4},{8,9},{9,10},{10,1... | collective-permute-start | bytes 1572872 | tf_op jit(solution)/shard_map/ppermute | solution.py:721
  514.4 66.2 %collective-permute-start.22 = (bf16[256,1024]{1,0:T(8,128)(2,1)}, bf16[256,1024]{1,0:T(8,128)(2,1)}, u32[]{:S(2)}, u32[]{:S(2)}) collective-permute-start(bf16[256,1024]{1,0:T(8,128)(2,1)} %get-tuple-element.233), channel_id=1, source_target_pairs={{0,2},{1,3},{2,0},{3,1},{4,6},{5,7},{6,4},{7,5},{8,10},{9,11},{10,... | collective-permute-start | bytes 1572872 | tf_op jit(solution)/shard_map/ppermute | solution.py:721
  516.3 64.3 %collective-permute-start.23 = (bf16[256,1024]{1,0:T(8,128)(2,1)}, bf16[256,1024]{1,0:T(8,128)(2,1)}, u32[]{:S(2)}, u32[]{:S(2)}) collective-permute-start(bf16[256,1024]{1,0:T(8,128)(2,1)} %get-tuple-element.232), channel_id=1, source_target_pairs={{0,3},{1,0},{2,1},{3,2},{4,7},{5,4},{6,5},{7,6},{8,11},{9,8},{10,9... | collective-permute-start | bytes 1572872 | tf_op jit(solution)/shard_map/ppermute | solution.py:721
  610.8 8.4 %collective-permute-start.27 = (bf16[128,1024]{1,0:T(8,128)(2,1)S(1)}, bf16[128,1024]{1,0:T(8,128)(2,1)S(1)}, u32[]{:S(2)}, u32[]{:S(2)}) collective-permute-start(bf16[128,1024]{1,0:T(8,128)(2,1)S(1)} %get-tuple-element.253), channel_id=1, source_target_pairs={{0,1},{1,2},{2,3},{3,0},{4,5},{5,6},{6,7},{7,4},{8,9},{9,10},{10,1... | collective-permute-start | bytes 786440 | tf_op jit(solution)/shard_map/ppermute | solution.py:721
  610.9 32.3 %collective-permute-start.28 = (bf16[128,1024]{1,0:T(8,128)(2,1)S(1)}, bf16[128,1024]{1,0:T(8,128)(2,1)S(1)}, u32[]{:S(2)}, u32[]{:S(2)}) collective-permute-start(bf16[128,1024]{1,0:T(8,128)(2,1)S(1)} %get-tuple-element.255), channel_id=1, source_target_pairs={{0,2},{1,3},{2,0},{3,1},{4,6},{5,7},{6,4},{7,5},{8,10},{9,11},{10,... | collective-permute-start | bytes 786440 | tf_op jit(solution)/shard_map/ppermute | solution.py:721
  610.9 32.2 %collective-permute-start.29 = (bf16[128,1024]{1,0:T(8,128)(2,1)S(1)}, bf16[128,1024]{1,0:T(8,128)(2,1)S(1)}, u32[]{:S(2)}, u32[]{:S(2)}) collective-permute-start(bf16[128,1024]{1,0:T(8,128)(2,1)S(1)} %get-tuple-element.254), channel_id=1, source_target_pairs={{0,3},{1,0},{2,1},{3,2},{4,7},{5,4},{6,5},{7,6},{8,11},{9,8},{10,9... | collective-permute-start | bytes 786440 | tf_op jit(solution)/shard_map/ppermute | solution.py:721
  645.1 17.1 %collective-permute-start.30 = (bf16[128,1024]{1,0:T(8,128)(2,1)}, bf16[128,1024]{1,0:T(8,128)(2,1)}, u32[]{:S(2)}, u32[]{:S(2)}) collective-permute-start(bf16[128,1024]{1,0:T(8,128)(2,1)} %get-tuple-element.224), channel_id=1, source_target_pairs={{0,1},{1,2},{2,3},{3,0},{4,5},{5,6},{6,7},{7,4},{8,9},{9,10},{10,1... | collective-permute-start | bytes 786440 | tf_op jit(solution)/shard_map/ppermute | solution.py:721
  651.3 24.0 %collective-permute-start.31 = (bf16[128,1024]{1,0:T(8,128)(2,1)}, bf16[128,1024]{1,0:T(8,128)(2,1)S(1)}, u32[]{:S(2)}, u32[]{:S(2)}) collective-permute-start(bf16[128,1024]{1,0:T(8,128)(2,1)} %get-tuple-element.224), channel_id=1, source_target_pairs={{0,2},{1,3},{2,0},{3,1},{4,6},{5,7},{6,4},{7,5},{8,10},{9,11},{10,... | collective-permute-start | bytes 786440 | tf_op jit(solution)/shard_map/ppermute | solution.py:721
  656.0 21.5 %collective-permute-start.33 = (bf16[256,1024]{1,0:T(8,128)(2,1)S(1)}, bf16[256,1024]{1,0:T(8,128)(2,1)S(1)}, u32[]{:S(2)}, u32[]{:S(2)}) collective-permute-start(bf16[256,1024]{1,0:T(8,128)(2,1)S(1)} %add_convert_fusion), channel_id=1, source_target_pairs={{0,1},{1,2},{2,3},{3,0},{4,5},{5,6},{6,7},{7,4},{8,9},{9,10},{10,1... | collective-permute-start | bytes 1572872 | tf_op jit(solution)/shard_map/ppermute | solution.py:721
  656.0 30.0 %collective-permute-start.34 = (bf16[256,1024]{1,0:T(8,128)(2,1)S(1)}, bf16[256,1024]{1,0:T(8,128)(2,1)S(1)}, u32[]{:S(2)}, u32[]{:S(2)}) collective-permute-start(bf16[256,1024]{1,0:T(8,128)(2,1)S(1)} %add_convert_fusion), channel_id=1, source_target_pairs={{0,2},{1,3},{2,0},{3,1},{4,6},{5,7},{6,4},{7,5},{8,10},{9,11},{10,... | collective-permute-start | bytes 1572872 | tf_op jit(solution)/shard_map/ppermute | solution.py:721
  659.0 16.2 %collective-permute-start.32 = (bf16[128,1024]{1,0:T(8,128)(2,1)}, bf16[128,1024]{1,0:T(8,128)(2,1)S(1)}, u32[]{:S(2)}, u32[]{:S(2)}) collective-permute-start(bf16[128,1024]{1,0:T(8,128)(2,1)} %get-tuple-element.224), channel_id=1, source_target_pairs={{0,3},{1,0},{2,1},{3,2},{4,7},{5,4},{6,5},{7,6},{8,11},{9,8},{10,9... | collective-permute-start | bytes 786440 | tf_op jit(solution)/shard_map/ppermute | solution.py:721
  662.2 23.9 %collective-permute-start.35 = (bf16[256,1024]{1,0:T(8,128)(2,1)S(1)}, bf16[256,1024]{1,0:T(8,128)(2,1)S(1)}, u32[]{:S(2)}, u32[]{:S(2)}) collective-permute-start(bf16[256,1024]{1,0:T(8,128)(2,1)S(1)} %add_convert_fusion), channel_id=1, source_target_pairs={{0,3},{1,0},{2,1},{3,2},{4,7},{5,4},{6,5},{7,6},{8,11},{9,8},{10,9... | collective-permute-start | bytes 1572872 | tf_op jit(solution)/shard_map/ppermute | solution.py:721
  690.5 28.9 %collective-permute-start.36 = (bf16[136,1024]{1,0:T(8,128)(2,1)S(1)}, bf16[136,1024]{1,0:T(8,128)(2,1)S(1)}, u32[]{:S(2)}, u32[]{:S(2)}) collective-permute-start(bf16[136,1024]{1,0:T(8,128)(2,1)S(1)} %get-tuple-element.246), channel_id=1, source_target_pairs={{0,1},{1,2},{2,3},{3,0},{4,5},{5,6},{6,7},{7,4},{8,9},{9,10},{10,1... | collective-permute-start | bytes 835592 | tf_op jit(solution)/shard_map/ppermute | solution.py:721
  712.3 14.0 %collective-permute-start.37 = (bf16[136,1024]{1,0:T(8,128)(2,1)S(1)}, bf16[136,1024]{1,0:T(8,128)(2,1)S(1)}, u32[]{:S(2)}, u32[]{:S(2)}) collective-permute-start(bf16[136,1024]{1,0:T(8,128)(2,1)S(1)} %get-tuple-element.248), channel_id=1, source_target_pairs={{0,2},{1,3},{2,0},{3,1},{4,6},{5,7},{6,4},{7,5},{8,10},{9,11},{10,... | collective-permute-start | bytes 835592 | tf_op jit(solution)/shard_map/ppermute | solution.py:721
  712.3 16.9 %collective-permute-start.38 = (bf16[136,1024]{1,0:T(8,128)(2,1)S(1)}, bf16[136,1024]{1,0:T(8,128)(2,1)S(1)}, u32[]{:S(2)}, u32[]{:S(2)}) collective-permute-start(bf16[136,1024]{1,0:T(8,128)(2,1)S(1)} %get-tuple-element.247), channel_id=1, source_target_pairs={{0,3},{1,0},{2,1},{3,2},{4,7},{5,4},{6,5},{7,6},{8,11},{9,8},{10,9... | collective-permute-start | bytes 835592 | tf_op jit(solution)/shard_map/ppermute | solution.py:721
  730.5 13.8 %collective-permute-start.39 = (bf16[136,1024]{1,0:T(8,128)(2,1)S(1)}, bf16[136,1024]{1,0:T(8,128)(2,1)S(1)}, u32[]{:S(2)}, u32[]{:S(2)}) collective-permute-start(bf16[136,1024]{1,0:T(8,128)(2,1)S(1)} %get-tuple-element.222), channel_id=1, source_target_pairs={{0,1},{1,2},{2,3},{3,0},{4,5},{5,6},{6,7},{7,4},{8,9},{9,10},{10,1... | collective-permute-start | bytes 835592 | tf_op jit(solution)/shard_map/ppermute | solution.py:721
  736.7 13.3 %collective-permute-start.40 = (bf16[136,1024]{1,0:T(8,128)(2,1)S(1)}, bf16[136,1024]{1,0:T(8,128)(2,1)S(1)}, u32[]{:S(2)}, u32[]{:S(2)}) collective-permute-start(bf16[136,1024]{1,0:T(8,128)(2,1)S(1)} %get-tuple-element.222), channel_id=1, source_target_pairs={{0,2},{1,3},{2,0},{3,1},{4,6},{5,7},{6,4},{7,5},{8,10},{9,11},{10,... | collective-permute-start | bytes 835592 | tf_op jit(solution)/shard_map/ppermute | solution.py:721
  740.1 10.0 %collective-permute-start.41 = (bf16[136,1024]{1,0:T(8,128)(2,1)S(1)}, bf16[136,1024]{1,0:T(8,128)(2,1)S(1)}, u32[]{:S(2)}, u32[]{:S(2)}) collective-permute-start(bf16[136,1024]{1,0:T(8,128)(2,1)S(1)} %get-tuple-element.222), channel_id=1, source_target_pairs={{0,3},{1,0},{2,1},{3,2},{4,7},{5,4},{6,5},{7,6},{8,11},{9,8},{10,9... | collective-permute-start | bytes 835592 | tf_op jit(solution)/shard_map/ppermute | solution.py:721
  (41 other events, 346.7 us)
Sparse Core Ops, SparseCore 0:
  10.7 57.2 all-gather.8
  70.4 54.3 all-gather.10
  127.3 89.8 all-gather.12
  376.6 116.4 reduce-scatter.3
  496.3 71.3 reduce-scatter.7
  609.7 70.9 reduce-scatter.5

commit v3 on v2

--- a/solution.py
+++ b/solution.py
@@ -841,12 +841,6 @@
         )
         gas.append(inward(back[m][3:]))
         behind = [back[m][1]]
-    time_grad = weight_columns(
-        behind, [(pick(middle, 0), pick(back, 0)), (pick(middle, 2), pick(ahead, 3))], clips, 4 * own, "time_grad"
-    )
-    (time_grad,), gas[0] = together([time_grad], gas[0])
-    time_part = reduce_clip(time_grad)
-    behind = [time_grad]
     grad_buffer = None
     for m in micro:
         last.append(
@@ -858,11 +852,16 @@
             )
         )
         grad_buffer = last[m][2]
-        behind = []
         if m == 0:
-            (ff_part,), (last[m][3],) = together([ff_part], [last[m][3]])
+            time_grad = weight_columns(
+                [last[m][3]], [(pick(middle, 0), pick(back, 0)), (pick(middle, 2), pick(ahead, 3))],
+                clips, 4 * own, "time_grad",
+            )
+            (time_grad,), gas[-1] = together([time_grad], gas[-1])
+            time_part = reduce_clip(time_grad)
+            (ff_part,), (last[m][4],) = together([ff_part], [last[m][4]])
             ff_half = sum_half(ff_part)
-            behind = [mark(ff_part)]
+            behind = [mark(time_grad[0]), mark(ff_part)]
 
     total = lambda values: functools.reduce(jnp.add, values)
     gain_grad = jnp.concatenate([total(pick(last, 3)), total(pick(back, 1)), total(pick(ahead, 5))])

time: 772 us -> 790 us (1.023)
  waiting for transfers between devices: 153 us -> 173 us
    ppermute x18, waiting for transfers between devices: 73.2 us -> 87.1 us  [shift(): lax.ppermute(values, 'tm', [(k, (k + step) % count) for k in range(count)])]
  transfers between devices with their start and end apart: 48 -> 48, of which waited for: 14 -> 16; matrix products, arithmetic and copies ran while one was open for 6% -> 6% of each run, Pallas kernels for 55% -> 54%
where the time goes in v3:
time: 790 us; the launch traced here: 777 us
  Pallas kernels  423 us (54%)
  waiting for transfers between devices  173 us (22%)
  starting transfers between devices  98.6 us (12%)
  local copies, waits for them, and re-layouts  33 us (4%)
  other arithmetic  25.6 us (3%)
  between operations  15.2 us (2%)
  blocking collectives  9.16 us (1%)
    pallas_call x15, Pallas kernels, ordered_call(): return lambda *operands: call(*behind, *operands)  423 us
    ppermute x18, waiting for transfers between devices, shift(): lax.ppermute(values, 'tm', [(k, (k + step) % count) for k in range(count)])  87.1 us
    ppermute x18, starting transfers between devices, shift(): lax.ppermute(values, 'tm', [(k, (k + step) % count) for k in range(count)])  48.3 us
    ppermute x12, waiting for transfers between devices, local(): lax.ppermute(parts[d], 'tm', [(k, (k - d) % pieces) for k in range(pieces)])  32 us
    ppermute x12, starting transfers between devices, local(): lax.ppermute(parts[d], 'tm', [(k, (k + d) % pieces) for k in range(pieces)])  31.6 us
    all_gather x3, waiting for transfers between devices, gather(): lax.all_gather(jnp.concatenate(parts, axis=0), 'clip', axis=0, tiled=False)  30.5 us
    ppermute x12, waiting for transfers between devices, local(): lax.ppermute(parts[d], 'tm', [(k, (k + d) % pieces) for k in range(pieces)])  22.7 us
    ppermute x12, starting transfers between devices, local(): lax.ppermute(parts[d], 'tm', [(k, (k - d) % pieces) for k in range(pieces)])  18.5 us
  transfers between devices with their start and end apart: 48, of which 16 were waited for; matrix products, arithmetic and copies ran while one was open for 6% of the time, Pallas kernels for 54%

profile of v3, /device:TPU:0, one launch (start us, length us, event | category | flops | bytes accessed | tf_op | source)
XLA Modules:
  0.0 776.9 jit_solution(571570204640751466)
XLA Ops:
  14.8 4.1 fusion.26
  20.5 3.0 collective-permute-start
  23.5 2.6 collective-permute-start.1
  27.7 9.2 %all-gather.4 = bf16[8,19,128]{2,1,0:T(8,128)(2,1)S(1)} all-gather(bf16[1,19,128]{2,1,0:T(8,128)(2,1)S(1)} %bitcast.128), channel_id=2, replica_groups=mesh['clip'=8,'tm'=4] {'clip'}, dimensions={0}, use_global_device_ids=true | all-gather | bytes 43776 | tf_op jit(solution)/shard_map/all_gather | solution.py:782
  43.0 24.9 %all-gather.9.cloned.1.call-done = bf16[4096,1024]{1,0:T(8,128)(2,1)} async-done(((bf16[512,1024]{1,0:T(8,128)(2,1)}), bf16[4096,1024]{1,0:T(8,128)(2,1)}) %all-gather.9.cloned.1.call-update) | async-done | bytes 8388624 | tf_op jit(solution)/shard_map/all_gather | solution.py:712
  68.0 22.6 %space_forward.2 = (bf16[4,256,1024]{2,1,0:T(8,128)(2,1)}, bf16[4,256,3072]{2,1,0:T(8,128)(2,1)}, bf16[4,256,1024]{2,1,0:T(8,128)(2,1)}, f32[4,16,256]{2,1,0:T(8...) custom-call(s32[1]{0:T(128)} %bitcast.refs_0_.refs_4_.refs_5_.refs_6, ...), custom_call_target="tpu_custom_call" | custom-call | tf_op jit(solution)/shard_map/space_forward/pallas_call | solution.py:380
  96.2 2.4 collective-permute-start.4
  100.1 22.7 %space_forward.3 = (bf16[4,256,1024]{2,1,0:T(8,128)(2,1)}, bf16[4,256,3072]{2,1,0:T(8,128)(2,1)}, bf16[4,256,1024]{2,1,0:T(8,128)(2,1)}, f32[4,16,256]{2,1,0:T(8...) custom-call(f32[4,16,256]{2,1,0:T(8,128)} %get-tuple-element.117.ref, ...), custom_call_target="tpu_custom_call" | custom-call | tf_op jit(solution)/shard_map/space_forward/pallas_call | solution.py:380
  129.0 22.3 %collective-permute-done.4.refs_6_.refs_3_ = bf16[4,64,1024]{2,1,0:T(8,128)(2,1)S(1)} collective-permute-done((bf16[4,64,1024]{2,1,0:T(8,128)(2,1)}, bf16[4,64,1024]{2,1,0:T(8,128)(2,1)S(1)}, u32[]{:S(2)}, u32[]{:S(2)}) %collective-permute-start.4) | collective-permute-done | bytes 524320 | tf_op jit(solution)/shard_map/ppermute | solution.py:802
  152.2 21.8 %time_forward.2 = (bf16[4,256,1024]{2,1,0:T(8,128)(2,1)}, bf16[4,256,3072]{2,1,0:T(8,128)(2,1)}, bf16[4,256,1024]{2,1,0:T(8,128)(2,1)}, f32[4,16,256]{2,1,0:T(8,128)}, f32[4,256,1024]{2,1,0:T(8,128)}) custom-call(f32[4,16,256]{2,1,0:T(8,128)} %get-tuple-element.118.refs_0_.refs_16_, bf16[8,128]{1,0:T(8,128)(2,1)} %slice.235.refs_1_, ...), custom_call_target="tpu_custom_call" | custom-call | tf_op jit(solution)/shard_map/time_forward/pallas_call | solution.py:380
  174.4 21.9 %time_forward.3 = (bf16[4,256,1024]{2,1,0:T(8,128)(2,1)}, bf16[4,256,3072]{2,1,0:T(8,128)(2,1)}, bf16[4,256,1024]{2,1,0:T(8,128)(2,1)}, f32[4,16,256]{2,1,0:T(8,128)}, f32[4,256,1024]{2,1,0:T(8,128)}) custom-call(f32[4,16,256]{2,1,0:T(8,128)} %get-tuple-element.123.refs_0_.refs_12_, bf16[4,64,1024]{2,1,0:T(8,128)(2,1)} %get-tuple-element.124.refs_1_, ...), custom_call_target="tpu_custom_call" | custom-call | tf_op jit(solution)/shard_map/time_forward/pallas_call | solution.py:380
  196.4 10.9 %collective-permute-start.10 = (bf16[4,64,1024]{2,1,0:T(8,128)(2,1)}, bf16[4,64,1024]{2,1,0:T(8,128)(2,1)S(1)}, u32[]{:S(2)}, u32[]{:S(2)}) collective-permute-start(bf16[4,64,1024]{2,1,0:T(8,128)(2,1)} %get-tuple-element.135), channel_id=1, source_target_pairs={{0,2},{1,3},{2,0},{3,1},{4,6},{5,7},{6,4},{7,5},{8,10},{9,11},{10,... | collective-permute-start | bytes 1572872 | tf_op jit(solution)/shard_map/ppermute | solution.py:802
  207.8 3.4 collective-permute-start.11
  211.6 5.6 all-gather.13.cloned.1.call-done
  217.2 50.8 %feed_forward.2 = (bf16[4,256,1024]{2,1,0:T(8,128)(2,1)}, bf16[4,256,4096]{2,1,0:T(8,128)(2,1)}, bf16[4,256,4096]{2,1,0:T(8,128)(2,1)}, bf16[4,256,1024]{2,1,0:T...) custom-call(f32[4,16,256]{2,1,0:T(8,128)} %get-tuple-element.128.ref, ...), custom_call_target="tpu_custom_call" | custom-call | tf_op jit(solution)/shard_map/feed_forward/pallas_call | solution.py:380
  268.0 3.4 collective-permute-start.12
  273.5 50.8 %feed_forward.3 = (bf16[4,256,1024]{2,1,0:T(8,128)(2,1)}, bf16[4,256,4096]{2,1,0:T(8,128)(2,1)}, bf16[4,256,4096]{2,1,0:T(8,128)(2,1)}, bf16[4,256,1024]{2,1,0:T...) custom-call(f32[1,1024]{1,0:T(1,128)} %get-tuple-element.131.refs_0_, ...), custom_call_target="tpu_custom_call" | custom-call | tf_op jit(solution)/shard_map/feed_forward/pallas_call | solution.py:380
  324.3 2.8 collective-permute-start.15
  330.3 22.9 %down_grad.1.refs_4_ = bf16[8,1024,1024]{2,1,0:T(8,128)(2,1)} custom-call(f32[1,1024]{1,0:T(1,128)} %get-tuple-element.141.refs_0_, bf16[8,128]{1,0:T(8,128)(2,1)} %slice.240.refs_1_, bf16[8,128]{1,0:T(8,128)(2,1)} %slice.241.refs_2_, bf16[8,128]{1,0:T(8,128)(2,1)} %slice.242.refs_3_, bf16[4,256,4096]{2,1,0:T(8,128)(2,1)} %get-tuple-element.145.refs_4_, ...), custom_call_target="tpu_custom_call" | custom-call | tf_op jit(solution)/shard_map/down_grad/pallas_call | solution.py:380
  353.2 23.2 %hidden_grad.1.refs_0_ = bf16[8,1024,1024]{2,1,0:T(8,128)(2,1)} custom-call(bf16[4,256,1024]{2,1,0:T(8,128)(2,1)} %get-tuple-element.130.refs_0_, bf16[4,256,1024]{2,1,0:T(8,128)(2,1)} %get-tuple-element.138.refs_1_, bf16[4,256,4096]{2,1,0:T(8,128)(2,1)} %get-tuple-element.139.refs_2_, ...), custom_call_target="tpu_custom_call", output_to_operand_aliasing={{}: (4, {})} | custom-call | tf_op jit(solution)/shard_map/hidden_grad/pallas_call | solution.py:380
  376.5 29.9 %time_backward.2 = (bf16[4,256,3072]{2,1,0:T(8,128)(2,1)}, f32[1,1024]{1,0:T(1,128)}, f32[1,1024]{1,0:T(1,128)}, bf16[4,64,1024]{2,1,0:T(8,128)(2,1)}, bf16[4,64...) custom-call(bf16[8,1024,1024]{2,1,0:T(8,128)(2,1)} %hidden_grad.1.refs_0_, ...), custom_call_target="tpu_custom_call" | custom-call | tf_op jit(solution)/shard_map/time_backward/pallas_call | solution.py:380
  406.5 3.8 collective-permute-start.18
  410.9 30.6 %time_backward.3 = (bf16[4,256,3072]{2,1,0:T(8,128)(2,1)}, f32[1,1024]{1,0:T(1,128)}, f32[1,1024]{1,0:T(1,128)}, bf16[4,64,1024]{2,1,0:T(8,128)(2,1)}, bf16[4,64...) custom-call(f32[1,1024]{1,0:T(1,128)} %get-tuple-element.157.refs_0_, ...), custom_call_target="tpu_custom_call" | custom-call | tf_op jit(solution)/shard_map/time_backward/pallas_call | solution.py:380
  441.6 3.2 collective-permute-start.24
  447.6 32.0 %collective-permute-done.19.refs_3_ = bf16[4,64,1024]{2,1,0:T(8,128)(2,1)} collective-permute-done((bf16[4,64,1024]{2,1,0:T(8,128)(2,1)}, bf16[4,64,1024]{2,1,0:T(8,128)(2,1)}, u32[]{:S(2)}, u32[]{:S(2)}) %collective-permute-start.19) | collective-permute-done | bytes 524320 | tf_op jit(solution)/shard_map/ppermute | solution.py:805
  479.6 33.4 %space_backward.2 = (bf16[4,256,3072]{2,1,0:T(8,128)(2,1)}, bf16[4,256,1024]{2,1,0:T(8,128)(2,1)}, f32[2,4,256,1024]{3,2,1,0:T(8,128)}, f32[1,1024]{1,0:T(1,128)...) custom-call(f32[1,1024]{1,0:T(1,128)} %get-tuple-element.161.refs_0_, bf16[4,64,1024]{2,1,0:T(8,128)(2,1)} %get-tuple-element.162.refs_1_, ...), custom_call_target="tpu_custom_call" | custom-call | tf_op jit(solution)/shard_map/space_backward/pallas_call | solution.py:380
  513.0 25.7 %time_grad.1 = bf16[8,512,1024]{2,1,0:T(8,128)(2,1)} custom-call(f32[1,1024]{1,0:T(1,128)} %get-tuple-element.173.refs_0_, bf16[4,256,1024]{2,1,0:T(8,128)(2,1)} %get-tuple-element.174.refs_1_, bf16[4,256,1024]{2,1,0:T(8,128)(2,1)} %get-tuple-element.175.refs_2_, bf16[4,256,3072]{2,1,0:T(8,128)(2,1)} %get-tuple-element.176.refs_3_, ...), custom_call_target="tpu_custom_call" | custom-call | tf_op jit(solution)/shard_map/time_grad/pallas_call | solution.py:380
  546.2 3.0 collective-permute-start.23
  549.2 34.3 %space_backward.3 = (bf16[4,256,3072]{2,1,0:T(8,128)(2,1)}, bf16[4,256,1024]{2,1,0:T(8,128)(2,1)}, f32[2,4,256,1024]{3,2,1,0:T(8,128)}, f32[1,1024]{1,0:T(1,128)...) custom-call(bf16[8,128]{1,0:T(8,128)(2,1)} %slice.244.refs_0_, ...), custom_call_target="tpu_custom_call", output_to_operand_aliasing={{2}: (17, {})} | custom-call | tf_op jit(solution)/shard_map/space_backward/pallas_call | solution.py:380
  589.5 27.2 %space_grad.1 = bf16[8,544,1024]{2,1,0:T(8,128)(2,1)} custom-call(bf16[8,128]{1,0:T(8,128)(2,1)} %slice.243.refs_0_, bf16[4,256,1024]{2,1,0:T(8,128)(2,1)} %get-tuple-element.170.refs_1_, bf16[4,256,1024]{2,1,0:T(8,128)(2,1)} %get-tuple-element.171.refs_2_, bf16[4,256,3072]{2,1,0:T(8,128)(2,1)} %get-tuple-element.172.refs_3_, ...), custom_call_target="tpu_custom_call" | custom-call | tf_op jit(solution)/shard_map/space_grad/pallas_call | solution.py:380
  620.2 3.5 collective-permute-start.28
  623.7 6.7 collective-permute-done.27
  630.4 7.1 collective-permute-done.28
  639.5 6.1 collective-permute-start.30
  645.6 4.8 assemble.1
  650.7 2.6 collective-permute-start.34
  653.3 2.9 collective-permute-start.32
  657.6 26.0 %collective-permute-done.31 = bf16[128,1024]{1,0:T(8,128)(2,1)S(1)} collective-permute-done((bf16[128,1024]{1,0:T(8,128)(2,1)}, bf16[128,1024]{1,0:T(8,128)(2,1)S(1)}, u32[]{:S(2)}, u32[]{:S(2)}) %collective-permute-start.31) | collective-permute-done | bytes 262176 | tf_op jit(solution)/shard_map/ppermute | solution.py:721
  683.6 2.8 collective-permute-done.32
  688.7 6.1 collective-permute-done.34
  694.8 5.1 collective-permute-done.35
  704.3 13.9 %collective-permute-start.36 = (bf16[136,1024]{1,0:T(8,128)(2,1)S(1)}, bf16[136,1024]{1,0:T(8,128)(2,1)S(1)}, u32[]{:S(2)}, u32[]{:S(2)}) collective-permute-start(bf16[136,1024]{1,0:T(8,128)(2,1)S(1)} %get-tuple-element.246), channel_id=1, source_target_pairs={{0,1},{1,2},{2,3},{3,0},{4,5},{5,6},{6,7},{7,4},{8,9},{9,10},{10,1... | collective-permute-start | bytes 835592 | tf_op jit(solution)/shard_map/ppermute | solution.py:721
  718.2 3.4 collective-permute-start.37
  721.5 7.1 collective-permute-done.36
  728.7 10.7 %collective-permute-done.37 = bf16[136,1024]{1,0:T(8,128)(2,1)S(1)} collective-permute-done((bf16[136,1024]{1,0:T(8,128)(2,1)S(1)}, bf16[136,1024]{1,0:T(8,128)(2,1)S(1)}, u32[]{:S(2)}, u32[]{:S(2)}) %collective-permute-start.37) | collective-permute-done | bytes 278560 | tf_op jit(solution)/shard_map/ppermute | solution.py:721
  740.7 6.5 collective-permute-start.39
  749.6 4.6 collective-permute-done.39
  754.2 9.6 %collective-permute-done.40 = bf16[136,1024]{1,0:T(8,128)(2,1)S(1)} collective-permute-done((bf16[136,1024]{1,0:T(8,128)(2,1)S(1)}, bf16[136,1024]{1,0:T(8,128)(2,1)S(1)}, u32[]{:S(2)}, u32[]{:S(2)}) %collective-permute-start.40) | collective-permute-done | bytes 278560 | tf_op jit(solution)/shard_map/ppermute | solution.py:721
  (247 shorter events, 77.6 us)
Async XLA Ops:
  7.2 60.8 %all-gather.9.cloned.1.call-start = ((), (), s32[]{:S(2)}) async-start(), calls=%async_computation.6 | async-start | bytes 9437184 | tf_op jit(solution)/shard_map/all_gather | solution.py:712
  10.5 118.4 %all-gather.11.cloned.1.call-start = ((), (), s32[]{:S(2)}) async-start(), calls=%async_computation.7 | async-start | bytes 9437184 | tf_op jit(solution)/shard_map/all_gather | solution.py:712
  11.7 205.5 %all-gather.13.cloned.1.call-start = ((), (), s32[]{:S(2)}) async-start(), calls=%async_computation.8 | async-start | bytes 18874368 | tf_op jit(solution)/shard_map/all_gather | solution.py:712
  14.7 527.3 %reduce-scatter.4.cloned.1.call-start = ((), (), s32[]{:S(2)}) async-start(), calls=%async_computation.3 | async-start | bytes 18874368 | tf_op jit(solution)/shard_map/reduce_scatter | solution.py:716
  20.5 73.3 %collective-permute-start = (bf16[4,64,1024]{2,1,0:T(8,128)(2,1)}, bf16[4,64,1024]{2,1,0:T(8,128)(2,1)S(1)}, u32[]{:S(2)}, u32[]{:S(2)}) collective-permute-start(bf16[4,64,1024]{2,1,0:T(8,128)(2,1)} %get-tuple-element.241), channel_id=1, source_target_pairs={{0,1},{1,2},{2,3},{3,0},{4,5},{5,6},{6,7},{7,4},{8,9},{9,10},{10,1... | collective-permute-start | bytes 1572872 | tf_op jit(solution)/shard_map/ppermute | solution.py:802
  23.5 70.9 %collective-permute-start.1 = (bf16[4,64,1024]{2,1,0:T(8,128)(2,1)}, bf16[4,64,1024]{2,1,0:T(8,128)(2,1)S(1)}, u32[]{:S(2)}, u32[]{:S(2)}) collective-permute-start(bf16[4,64,1024]{2,1,0:T(8,128)(2,1)} %get-tuple-element.240), channel_id=1, source_target_pairs={{0,2},{1,3},{2,0},{3,1},{4,6},{5,7},{6,4},{7,5},{8,10},{9,11},{10,... | collective-permute-start | bytes 1572872 | tf_op jit(solution)/shard_map/ppermute | solution.py:802
  26.1 68.9 %collective-permute-start.2 = (bf16[4,64,1024]{2,1,0:T(8,128)(2,1)}, bf16[4,64,1024]{2,1,0:T(8,128)(2,1)}, u32[]{:S(2)}, u32[]{:S(2)}) collective-permute-start(bf16[4,64,1024]{2,1,0:T(8,128)(2,1)} %get-tuple-element.239), channel_id=1, source_target_pairs={{0,3},{1,0},{2,1},{3,2},{4,7},{5,4},{6,5},{7,6},{8,11},{9,8},{10,9... | collective-permute-start | bytes 1572872 | tf_op jit(solution)/shard_map/ppermute | solution.py:802
  90.6 34.7 %collective-permute-start.3 = (bf16[4,64,1024]{2,1,0:T(8,128)(2,1)}, bf16[4,64,1024]{2,1,0:T(8,128)(2,1)S(1)}, u32[]{:S(2)}, u32[]{:S(2)}) collective-permute-start(bf16[4,64,1024]{2,1,0:T(8,128)(2,1)} %get-tuple-element.120), channel_id=1, source_target_pairs={{0,1},{1,2},{2,3},{3,0},{4,5},{5,6},{6,7},{7,4},{8,9},{9,10},{10,1... | collective-permute-start | bytes 1572872 | tf_op jit(solution)/shard_map/ppermute | solution.py:802
  96.2 55.0 %collective-permute-start.4 = (bf16[4,64,1024]{2,1,0:T(8,128)(2,1)}, bf16[4,64,1024]{2,1,0:T(8,128)(2,1)S(1)}, u32[]{:S(2)}, u32[]{:S(2)}) collective-permute-start(bf16[4,64,1024]{2,1,0:T(8,128)(2,1)} %get-tuple-element.121), channel_id=1, source_target_pairs={{0,2},{1,3},{2,0},{3,1},{4,6},{5,7},{6,4},{7,5},{8,10},{9,11},{10,... | collective-permute-start | bytes 1572872 | tf_op jit(solution)/shard_map/ppermute | solution.py:802
  98.7 52.6 %collective-permute-start.5 = (bf16[4,64,1024]{2,1,0:T(8,128)(2,1)}, bf16[4,64,1024]{2,1,0:T(8,128)(2,1)S(1)}, u32[]{:S(2)}, u32[]{:S(2)}) collective-permute-start(bf16[4,64,1024]{2,1,0:T(8,128)(2,1)} %get-tuple-element.122), channel_id=1, source_target_pairs={{0,3},{1,0},{2,1},{3,2},{4,7},{5,4},{6,5},{7,6},{8,11},{9,8},{10,9... | collective-permute-start | bytes 1572872 | tf_op jit(solution)/shard_map/ppermute | solution.py:802
  122.8 51.3 %collective-permute-start.6 = (bf16[4,64,1024]{2,1,0:T(8,128)(2,1)}, bf16[4,64,1024]{2,1,0:T(8,128)(2,1)}, u32[]{:S(2)}, u32[]{:S(2)}) collective-permute-start(bf16[4,64,1024]{2,1,0:T(8,128)(2,1)} %get-tuple-element.125), channel_id=1, source_target_pairs={{0,1},{1,2},{2,3},{3,0},{4,5},{5,6},{6,7},{7,4},{8,9},{9,10},{10,1... | collective-permute-start | bytes 1572872 | tf_op jit(solution)/shard_map/ppermute | solution.py:802
  123.5 51.0 %collective-permute-start.7 = (bf16[4,64,1024]{2,1,0:T(8,128)(2,1)}, bf16[4,64,1024]{2,1,0:T(8,128)(2,1)}, u32[]{:S(2)}, u32[]{:S(2)}) collective-permute-start(bf16[4,64,1024]{2,1,0:T(8,128)(2,1)} %get-tuple-element.126), channel_id=1, source_target_pairs={{0,2},{1,3},{2,0},{3,1},{4,6},{5,7},{6,4},{7,5},{8,10},{9,11},{10,... | collective-permute-start | bytes 1572872 | tf_op jit(solution)/shard_map/ppermute | solution.py:802
  125.3 49.1 %collective-permute-start.8 = (bf16[4,64,1024]{2,1,0:T(8,128)(2,1)}, bf16[4,64,1024]{2,1,0:T(8,128)(2,1)}, u32[]{:S(2)}, u32[]{:S(2)}) collective-permute-start(bf16[4,64,1024]{2,1,0:T(8,128)(2,1)} %get-tuple-element.127), channel_id=1, source_target_pairs={{0,3},{1,0},{2,1},{3,2},{4,7},{5,4},{6,5},{7,6},{8,11},{9,8},{10,9... | collective-permute-start | bytes 1572872 | tf_op jit(solution)/shard_map/ppermute | solution.py:802
  196.4 75.1 %collective-permute-start.10 = (bf16[4,64,1024]{2,1,0:T(8,128)(2,1)}, bf16[4,64,1024]{2,1,0:T(8,128)(2,1)S(1)}, u32[]{:S(2)}, u32[]{:S(2)}) collective-permute-start(bf16[4,64,1024]{2,1,0:T(8,128)(2,1)} %get-tuple-element.135), channel_id=1, source_target_pairs={{0,2},{1,3},{2,0},{3,1},{4,6},{5,7},{6,4},{7,5},{8,10},{9,11},{10,... | collective-permute-start | bytes 1572872 | tf_op jit(solution)/shard_map/ppermute | solution.py:802
  207.8 65.7 %collective-permute-start.11 = (bf16[4,64,1024]{2,1,0:T(8,128)(2,1)}, bf16[4,64,1024]{2,1,0:T(8,128)(2,1)}, u32[]{:S(2)}, u32[]{:S(2)}) collective-permute-start(bf16[4,64,1024]{2,1,0:T(8,128)(2,1)} %get-tuple-element.136), channel_id=1, source_target_pairs={{0,3},{1,0},{2,1},{3,2},{4,7},{5,4},{6,5},{7,6},{8,11},{9,8},{10,9... | collective-permute-start | bytes 1572872 | tf_op jit(solution)/shard_map/ppermute | solution.py:802
  211.2 62.3 %collective-permute-start.9 = (bf16[4,64,1024]{2,1,0:T(8,128)(2,1)}, bf16[4,64,1024]{2,1,0:T(8,128)(2,1)}, u32[]{:S(2)}, u32[]{:S(2)}) collective-permute-start(bf16[4,64,1024]{2,1,0:T(8,128)(2,1)} %get-tuple-element.134), channel_id=1, source_target_pairs={{0,1},{1,2},{2,3},{3,0},{4,5},{5,6},{6,7},{7,4},{8,9},{9,10},{10,1... | collective-permute-start | bytes 1572872 | tf_op jit(solution)/shard_map/ppermute | solution.py:802
  268.0 60.2 %collective-permute-start.12 = (bf16[4,64,1024]{2,1,0:T(8,128)(2,1)}, bf16[4,64,1024]{2,1,0:T(8,128)(2,1)S(1)}, u32[]{:S(2)}, u32[]{:S(2)}) collective-permute-start(bf16[4,64,1024]{2,1,0:T(8,128)(2,1)} %get-tuple-element.142), channel_id=1, source_target_pairs={{0,3},{1,0},{2,1},{3,2},{4,7},{5,4},{6,5},{7,6},{8,11},{9,8},{10,9... | collective-permute-start | bytes 1572872 | tf_op jit(solution)/shard_map/ppermute | solution.py:805
  271.4 57.6 %collective-permute-start.13 = (bf16[4,64,1024]{2,1,0:T(8,128)(2,1)}, bf16[4,64,1024]{2,1,0:T(8,128)(2,1)S(1)}, u32[]{:S(2)}, u32[]{:S(2)}) collective-permute-start(bf16[4,64,1024]{2,1,0:T(8,128)(2,1)} %get-tuple-element.143), channel_id=1, source_target_pairs={{0,2},{1,3},{2,0},{3,1},{4,6},{5,7},{6,4},{7,5},{8,10},{9,11},{10,... | collective-permute-start | bytes 1572872 | tf_op jit(solution)/shard_map/ppermute | solution.py:805
  272.2 57.4 %collective-permute-start.14 = (bf16[4,64,1024]{2,1,0:T(8,128)(2,1)}, bf16[4,64,1024]{2,1,0:T(8,128)(2,1)S(1)}, u32[]{:S(2)}, u32[]{:S(2)}) collective-permute-start(bf16[4,64,1024]{2,1,0:T(8,128)(2,1)} %get-tuple-element.144), channel_id=1, source_target_pairs={{0,1},{1,2},{2,3},{3,0},{4,5},{5,6},{6,7},{7,4},{8,9},{9,10},{10,1... | collective-permute-start | bytes 1572872 | tf_op jit(solution)/shard_map/ppermute | solution.py:805
  324.3 52.1 %collective-permute-start.15 = (bf16[4,64,1024]{2,1,0:T(8,128)(2,1)}, bf16[4,64,1024]{2,1,0:T(8,128)(2,1)}, u32[]{:S(2)}, u32[]{:S(2)}) collective-permute-start(bf16[4,64,1024]{2,1,0:T(8,128)(2,1)} %get-tuple-element.150), channel_id=1, source_target_pairs={{0,3},{1,0},{2,1},{3,2},{4,7},{5,4},{6,5},{7,6},{8,11},{9,8},{10,9... | collective-permute-start | bytes 1572872 | tf_op jit(solution)/shard_map/ppermute | solution.py:805
  327.1 49.4 %collective-permute-start.16 = (bf16[4,64,1024]{2,1,0:T(8,128)(2,1)}, bf16[4,64,1024]{2,1,0:T(8,128)(2,1)}, u32[]{:S(2)}, u32[]{:S(2)}) collective-permute-start(bf16[4,64,1024]{2,1,0:T(8,128)(2,1)} %get-tuple-element.151), channel_id=1, source_target_pairs={{0,2},{1,3},{2,0},{3,1},{4,6},{5,7},{6,4},{7,5},{8,10},{9,11},{10,... | collective-permute-start | bytes 1572872 | tf_op jit(solution)/shard_map/ppermute | solution.py:805
  328.2 48.2 %collective-permute-start.17 = (bf16[4,64,1024]{2,1,0:T(8,128)(2,1)}, bf16[4,64,1024]{2,1,0:T(8,128)(2,1)}, u32[]{:S(2)}, u32[]{:S(2)}) collective-permute-start(bf16[4,64,1024]{2,1,0:T(8,128)(2,1)} %get-tuple-element.152), channel_id=1, source_target_pairs={{0,1},{1,2},{2,3},{3,0},{4,5},{5,6},{6,7},{7,4},{8,9},{9,10},{10,1... | collective-permute-start | bytes 1572872 | tf_op jit(solution)/shard_map/ppermute | solution.py:805
  376.5 240.3 %reduce-scatter.8.cloned.1.call-start = ((), (), s32[]{:S(2)}) async-start(), calls=%async_computation.5 | async-start | bytes 9437184 | tf_op jit(solution)/shard_map/reduce_scatter | solution.py:716
  406.5 39.5 %collective-permute-start.18 = (bf16[4,64,1024]{2,1,0:T(8,128)(2,1)}, bf16[4,64,1024]{2,1,0:T(8,128)(2,1)S(1)}, u32[]{:S(2)}, u32[]{:S(2)}) collective-permute-start(bf16[4,64,1024]{2,1,0:T(8,128)(2,1)} %get-tuple-element.163), channel_id=1, source_target_pairs={{0,3},{1,0},{2,1},{3,2},{4,7},{5,4},{6,5},{7,6},{8,11},{9,8},{10,9... | collective-permute-start | bytes 1572872 | tf_op jit(solution)/shard_map/ppermute | solution.py:805
  410.3 69.3 %collective-permute-start.19 = (bf16[4,64,1024]{2,1,0:T(8,128)(2,1)}, bf16[4,64,1024]{2,1,0:T(8,128)(2,1)}, u32[]{:S(2)}, u32[]{:S(2)}) collective-permute-start(bf16[4,64,1024]{2,1,0:T(8,128)(2,1)} %get-tuple-element.164), channel_id=1, source_target_pairs={{0,2},{1,3},{2,0},{3,1},{4,6},{5,7},{6,4},{7,5},{8,10},{9,11},{10,... | collective-permute-start | bytes 1572872 | tf_op jit(solution)/shard_map/ppermute | solution.py:805
  410.3 69.3 %collective-permute-start.20 = (bf16[4,64,1024]{2,1,0:T(8,128)(2,1)}, bf16[4,64,1024]{2,1,0:T(8,128)(2,1)}, u32[]{:S(2)}, u32[]{:S(2)}) collective-permute-start(bf16[4,64,1024]{2,1,0:T(8,128)(2,1)} %get-tuple-element.165), channel_id=1, source_target_pairs={{0,1},{1,2},{2,3},{3,0},{4,5},{5,6},{6,7},{7,4},{8,9},{9,10},{10,1... | collective-permute-start | bytes 1572872 | tf_op jit(solution)/shard_map/ppermute | solution.py:805
  441.6 97.1 %collective-permute-start.24 = (bf16[4,64,1024]{2,1,0:T(8,128)(2,1)}, bf16[4,64,1024]{2,1,0:T(8,128)(2,1)S(1)}, u32[]{:S(2)}, u32[]{:S(2)}) collective-permute-start(bf16[4,64,1024]{2,1,0:T(8,128)(2,1)} %get-tuple-element.179), channel_id=1, source_target_pairs={{0,3},{1,0},{2,1},{3,2},{4,7},{5,4},{6,5},{7,6},{8,11},{9,8},{10,9... | collective-permute-start | bytes 1572872 | tf_op jit(solution)/shard_map/ppermute | solution.py:805
  444.8 93.9 %collective-permute-start.25 = (bf16[4,64,1024]{2,1,0:T(8,128)(2,1)}, bf16[4,64,1024]{2,1,0:T(8,128)(2,1)S(1)}, u32[]{:S(2)}, u32[]{:S(2)}) collective-permute-start(bf16[4,64,1024]{2,1,0:T(8,128)(2,1)} %get-tuple-element.180), channel_id=1, source_target_pairs={{0,2},{1,3},{2,0},{3,1},{4,6},{5,7},{6,4},{7,5},{8,10},{9,11},{10,... | collective-permute-start | bytes 1572872 | tf_op jit(solution)/shard_map/ppermute | solution.py:805
  446.8 92.0 %collective-permute-start.26 = (bf16[4,64,1024]{2,1,0:T(8,128)(2,1)}, bf16[4,64,1024]{2,1,0:T(8,128)(2,1)S(1)}, u32[]{:S(2)}, u32[]{:S(2)}) collective-permute-start(bf16[4,64,1024]{2,1,0:T(8,128)(2,1)} %get-tuple-element.181), channel_id=1, source_target_pairs={{0,1},{1,2},{2,3},{3,0},{4,5},{5,6},{6,7},{7,4},{8,9},{9,10},{10,1... | collective-permute-start | bytes 1572872 | tf_op jit(solution)/shard_map/ppermute | solution.py:805
  539.9 163.3 %reduce-scatter.6.cloned.1.call-start = ((), (), s32[]{:S(2)}) async-start(), calls=%async_computation.4 | async-start | bytes 10027008 | tf_op jit(solution)/shard_map/reduce_scatter | solution.py:716
  544.8 42.2 %collective-permute-start.21 = (bf16[256,1024]{1,0:T(8,128)(2,1)S(1)}, bf16[256,1024]{1,0:T(8,128)(2,1)}, u32[]{:S(2)}, u32[]{:S(2)}) collective-permute-start(bf16[256,1024]{1,0:T(8,128)(2,1)S(1)} %get-tuple-element.231), channel_id=1, source_target_pairs={{0,1},{1,2},{2,3},{3,0},{4,5},{5,6},{6,7},{7,4},{8,9},{9,10},{10,1... | collective-permute-start | bytes 1572872 | tf_op jit(solution)/shard_map/ppermute | solution.py:721
  544.9 42.1 %collective-permute-start.22 = (bf16[256,1024]{1,0:T(8,128)(2,1)S(1)}, bf16[256,1024]{1,0:T(8,128)(2,1)}, u32[]{:S(2)}, u32[]{:S(2)}) collective-permute-start(bf16[256,1024]{1,0:T(8,128)(2,1)S(1)} %get-tuple-element.233), channel_id=1, source_target_pairs={{0,2},{1,3},{2,0},{3,1},{4,6},{5,7},{6,4},{7,5},{8,10},{9,11},{10,... | collective-permute-start | bytes 1572872 | tf_op jit(solution)/shard_map/ppermute | solution.py:721
  546.2 40.7 %collective-permute-start.23 = (bf16[256,1024]{1,0:T(8,128)(2,1)S(1)}, bf16[256,1024]{1,0:T(8,128)(2,1)}, u32[]{:S(2)}, u32[]{:S(2)}) collective-permute-start(bf16[256,1024]{1,0:T(8,128)(2,1)S(1)} %get-tuple-element.232), channel_id=1, source_target_pairs={{0,3},{1,0},{2,1},{3,2},{4,7},{5,4},{6,5},{7,6},{8,11},{9,8},{10,9... | collective-permute-start | bytes 1572872 | tf_op jit(solution)/shard_map/ppermute | solution.py:721
  618.0 12.4 %collective-permute-start.27 = (bf16[128,1024]{1,0:T(8,128)(2,1)S(1)}, bf16[128,1024]{1,0:T(8,128)(2,1)S(1)}, u32[]{:S(2)}, u32[]{:S(2)}) collective-permute-start(bf16[128,1024]{1,0:T(8,128)(2,1)S(1)} %get-tuple-element.253), channel_id=1, source_target_pairs={{0,1},{1,2},{2,3},{3,0},{4,5},{5,6},{6,7},{7,4},{8,9},{9,10},{10,1... | collective-permute-start | bytes 786440 | tf_op jit(solution)/shard_map/ppermute | solution.py:721
  620.2 17.3 %collective-permute-start.28 = (bf16[128,1024]{1,0:T(8,128)(2,1)S(1)}, bf16[128,1024]{1,0:T(8,128)(2,1)S(1)}, u32[]{:S(2)}, u32[]{:S(2)}) collective-permute-start(bf16[128,1024]{1,0:T(8,128)(2,1)S(1)} %get-tuple-element.255), channel_id=1, source_target_pairs={{0,2},{1,3},{2,0},{3,1},{4,6},{5,7},{6,4},{7,5},{8,10},{9,11},{10,... | collective-permute-start | bytes 786440 | tf_op jit(solution)/shard_map/ppermute | solution.py:721
  623.7 13.8 %collective-permute-start.29 = (bf16[128,1024]{1,0:T(8,128)(2,1)S(1)}, bf16[128,1024]{1,0:T(8,128)(2,1)S(1)}, u32[]{:S(2)}, u32[]{:S(2)}) collective-permute-start(bf16[128,1024]{1,0:T(8,128)(2,1)S(1)} %get-tuple-element.254), channel_id=1, source_target_pairs={{0,3},{1,0},{2,1},{3,2},{4,7},{5,4},{6,5},{7,6},{8,11},{9,8},{10,9... | collective-permute-start | bytes 786440 | tf_op jit(solution)/shard_map/ppermute | solution.py:721
  639.5 17.0 %collective-permute-start.30 = (bf16[128,1024]{1,0:T(8,128)(2,1)}, bf16[128,1024]{1,0:T(8,128)(2,1)}, u32[]{:S(2)}, u32[]{:S(2)}) collective-permute-start(bf16[128,1024]{1,0:T(8,128)(2,1)} %get-tuple-element.224), channel_id=1, source_target_pairs={{0,1},{1,2},{2,3},{3,0},{4,5},{5,6},{6,7},{7,4},{8,9},{9,10},{10,1... | collective-permute-start | bytes 786440 | tf_op jit(solution)/shard_map/ppermute | solution.py:721
  645.6 38.0 %collective-permute-start.31 = (bf16[128,1024]{1,0:T(8,128)(2,1)}, bf16[128,1024]{1,0:T(8,128)(2,1)S(1)}, u32[]{:S(2)}, u32[]{:S(2)}) collective-permute-start(bf16[128,1024]{1,0:T(8,128)(2,1)} %get-tuple-element.224), channel_id=1, source_target_pairs={{0,2},{1,3},{2,0},{3,1},{4,6},{5,7},{6,4},{7,5},{8,10},{9,11},{10,... | collective-permute-start | bytes 786440 | tf_op jit(solution)/shard_map/ppermute | solution.py:721
  650.3 38.3 %collective-permute-start.33 = (bf16[256,1024]{1,0:T(8,128)(2,1)S(1)}, bf16[256,1024]{1,0:T(8,128)(2,1)S(1)}, u32[]{:S(2)}, u32[]{:S(2)}) collective-permute-start(bf16[256,1024]{1,0:T(8,128)(2,1)S(1)} %add_convert_fusion), channel_id=1, source_target_pairs={{0,1},{1,2},{2,3},{3,0},{4,5},{5,6},{6,7},{7,4},{8,9},{9,10},{10,1... | collective-permute-start | bytes 1572872 | tf_op jit(solution)/shard_map/ppermute | solution.py:721
  650.7 44.1 %collective-permute-start.34 = (bf16[256,1024]{1,0:T(8,128)(2,1)S(1)}, bf16[256,1024]{1,0:T(8,128)(2,1)S(1)}, u32[]{:S(2)}, u32[]{:S(2)}) collective-permute-start(bf16[256,1024]{1,0:T(8,128)(2,1)S(1)} %add_convert_fusion), channel_id=1, source_target_pairs={{0,2},{1,3},{2,0},{3,1},{4,6},{5,7},{6,4},{7,5},{8,10},{9,11},{10,... | collective-permute-start | bytes 1572872 | tf_op jit(solution)/shard_map/ppermute | solution.py:721
  653.3 33.0 %collective-permute-start.32 = (bf16[128,1024]{1,0:T(8,128)(2,1)}, bf16[128,1024]{1,0:T(8,128)(2,1)S(1)}, u32[]{:S(2)}, u32[]{:S(2)}) collective-permute-start(bf16[128,1024]{1,0:T(8,128)(2,1)} %get-tuple-element.224), channel_id=1, source_target_pairs={{0,3},{1,0},{2,1},{3,2},{4,7},{5,4},{6,5},{7,6},{8,11},{9,8},{10,9... | collective-permute-start | bytes 786440 | tf_op jit(solution)/shard_map/ppermute | solution.py:721
  656.5 43.4 %collective-permute-start.35 = (bf16[256,1024]{1,0:T(8,128)(2,1)S(1)}, bf16[256,1024]{1,0:T(8,128)(2,1)S(1)}, u32[]{:S(2)}, u32[]{:S(2)}) collective-permute-start(bf16[256,1024]{1,0:T(8,128)(2,1)S(1)} %add_convert_fusion), channel_id=1, source_target_pairs={{0,3},{1,0},{2,1},{3,2},{4,7},{5,4},{6,5},{7,6},{8,11},{9,8},{10,9... | collective-permute-start | bytes 1572872 | tf_op jit(solution)/shard_map/ppermute | solution.py:721
  704.3 24.4 %collective-permute-start.36 = (bf16[136,1024]{1,0:T(8,128)(2,1)S(1)}, bf16[136,1024]{1,0:T(8,128)(2,1)S(1)}, u32[]{:S(2)}, u32[]{:S(2)}) collective-permute-start(bf16[136,1024]{1,0:T(8,128)(2,1)S(1)} %get-tuple-element.246), channel_id=1, source_target_pairs={{0,1},{1,2},{2,3},{3,0},{4,5},{5,6},{6,7},{7,4},{8,9},{9,10},{10,1... | collective-permute-start | bytes 835592 | tf_op jit(solution)/shard_map/ppermute | solution.py:721
  718.2 21.2 %collective-permute-start.37 = (bf16[136,1024]{1,0:T(8,128)(2,1)S(1)}, bf16[136,1024]{1,0:T(8,128)(2,1)S(1)}, u32[]{:S(2)}, u32[]{:S(2)}) collective-permute-start(bf16[136,1024]{1,0:T(8,128)(2,1)S(1)} %get-tuple-element.248), channel_id=1, source_target_pairs={{0,2},{1,3},{2,0},{3,1},{4,6},{5,7},{6,4},{7,5},{8,10},{9,11},{10,... | collective-permute-start | bytes 835592 | tf_op jit(solution)/shard_map/ppermute | solution.py:721
  721.5 17.8 %collective-permute-start.38 = (bf16[136,1024]{1,0:T(8,128)(2,1)S(1)}, bf16[136,1024]{1,0:T(8,128)(2,1)S(1)}, u32[]{:S(2)}, u32[]{:S(2)}) collective-permute-start(bf16[136,1024]{1,0:T(8,128)(2,1)S(1)} %get-tuple-element.247), channel_id=1, source_target_pairs={{0,3},{1,0},{2,1},{3,2},{4,7},{5,4},{6,5},{7,6},{8,11},{9,8},{10,9... | collective-permute-start | bytes 835592 | tf_op jit(solution)/shard_map/ppermute | solution.py:721
  740.7 13.5 %collective-permute-start.39 = (bf16[136,1024]{1,0:T(8,128)(2,1)S(1)}, bf16[136,1024]{1,0:T(8,128)(2,1)S(1)}, u32[]{:S(2)}, u32[]{:S(2)}) collective-permute-start(bf16[136,1024]{1,0:T(8,128)(2,1)S(1)} %get-tuple-element.222), channel_id=1, source_target_pairs={{0,1},{1,2},{2,3},{3,0},{4,5},{5,6},{6,7},{7,4},{8,9},{9,10},{10,1... | collective-permute-start | bytes 835592 | tf_op jit(solution)/shard_map/ppermute | solution.py:721
  747.1 16.7 %collective-permute-start.40 = (bf16[136,1024]{1,0:T(8,128)(2,1)S(1)}, bf16[136,1024]{1,0:T(8,128)(2,1)S(1)}, u32[]{:S(2)}, u32[]{:S(2)}) collective-permute-start(bf16[136,1024]{1,0:T(8,128)(2,1)S(1)} %get-tuple-element.222), channel_id=1, source_target_pairs={{0,2},{1,3},{2,0},{3,1},{4,6},{5,7},{6,4},{7,5},{8,10},{9,11},{10,... | collective-permute-start | bytes 835592 | tf_op jit(solution)/shard_map/ppermute | solution.py:721
  747.2 18.1 %collective-permute-start.41 = (bf16[136,1024]{1,0:T(8,128)(2,1)S(1)}, bf16[136,1024]{1,0:T(8,128)(2,1)S(1)}, u32[]{:S(2)}, u32[]{:S(2)}) collective-permute-start(bf16[136,1024]{1,0:T(8,128)(2,1)S(1)} %get-tuple-element.222), channel_id=1, source_target_pairs={{0,3},{1,0},{2,1},{3,2},{4,7},{5,4},{6,5},{7,6},{8,11},{9,8},{10,9... | collective-permute-start | bytes 835592 | tf_op jit(solution)/shard_map/ppermute | solution.py:721
  (39 other events, 301.2 us)
Sparse Core Ops, SparseCore 0:
  10.7 57.2 all-gather.8
  70.4 54.3 all-gather.10
  127.3 89.8 all-gather.12
  376.6 116.3 reduce-scatter.3
  539.0 68.9 reduce-scatter.7
  616.9 75.5 reduce-scatter.5

commit v4 on v2

--- a/solution.py
+++ b/solution.py
@@ -860,7 +860,7 @@
         grad_buffer = last[m][2]
         behind = []
         if m == 0:
-            (ff_part,), (last[m][3],) = together([ff_part], [last[m][3]])
+            (ff_part,), (last[m][3],), gas[-1] = together([ff_part], [last[m][3]], gas[-1])
             ff_half = sum_half(ff_part)
             behind = [mark(ff_part)]
 
@@ -899,7 +899,7 @@
         ff_sum[4 * own :].astype(f32),
     )
     space_part, *early = lax.optimization_barrier((space_part,) + early)
-    space_sum = share_half(sum_half(space_part))
+    space_sum = lax.psum(space_part, "tm")
     mine = space_sum[4 * own :].reshape(-1)[: small_rows * own].reshape(small_rows, own).astype(f32)
     return (
         early[0],

time: 772 us -> 772 us (level)
  waiting for transfers between devices: 153 us -> 184 us
  starting transfers between devices: 105 us -> 76 us
    psum x0 -> x1, waiting for transfers between devices: none -> 66 us  [local(): space_sum = lax.psum(space_part, 'tm')]
    ppermute x18 -> x12, starting transfers between devices: 54.8 us -> 25.7 us  [shift(): lax.ppermute(values, 'tm', [(k, (k + step) % count) for k in range(count)])]
    ppermute x18 -> x12, waiting for transfers between devices: 73.2 us -> 55.6 us  [shift(): lax.ppermute(values, 'tm', [(k, (k + step) % count) for k in range(count)])]
    ppermute x12, waiting for transfers between devices: 26 us -> 9.37 us  [local(): lax.ppermute(parts[d], 'tm', [(k, (k - d) % pieces) for k in range(pieces)])]
  transfers between devices with their start and end apart: 48 -> 43, of which waited for: 14 -> 11; matrix products, arithmetic and copies ran while one was open for 6% -> 6% of each run, Pallas kernels for 55% -> 55%
where the time goes in v4:
time: 772 us; the launch traced here: 763 us
  Pallas kernels  422 us (55%)
  waiting for transfers between devices  184 us (24%)
  starting transfers between devices  76 us (10%)
  local copies, waits for them, and re-layouts  30.8 us (4%)
  other arithmetic  25.5 us (3%)
  between operations  15.2 us (2%)
  blocking collectives  9.16 us (1%)
    pallas_call x15, Pallas kernels, ordered_call(): return lambda *operands: call(*behind, *operands)  422 us
    psum x1, waiting for transfers between devices, local(): space_sum = lax.psum(space_part, 'tm')  66 us
    ppermute x12, waiting for transfers between devices, shift(): lax.ppermute(values, 'tm', [(k, (k + step) % count) for k in range(count)])  55.6 us
    ppermute x12, starting transfers between devices, local(): lax.ppermute(parts[d], 'tm', [(k, (k + d) % pieces) for k in range(pieces)])  31.6 us
    all_gather x3, waiting for transfers between devices, gather(): lax.all_gather(jnp.concatenate(parts, axis=0), 'clip', axis=0, tiled=False)  30.5 us
    ppermute x12, starting transfers between devices, shift(): lax.ppermute(values, 'tm', [(k, (k + step) % count) for k in range(count)])  25.7 us
    ppermute x12, waiting for transfers between devices, local(): lax.ppermute(parts[d], 'tm', [(k, (k + d) % pieces) for k in range(pieces)])  22.7 us
    ppermute x12, starting transfers between devices, local(): lax.ppermute(parts[d], 'tm', [(k, (k - d) % pieces) for k in range(pieces)])  18.4 us
  transfers between devices with their start and end apart: 43, of which 11 were waited for; matrix products, arithmetic and copies ran while one was open for 6% of the time, Pallas kernels for 55%

profile of v4, /device:TPU:0, one launch (start us, length us, event | category | flops | bytes accessed | tf_op | source)
XLA Modules:
  0.0 763.0 jit_solution(4735796609026034746)
XLA Ops:
  8.5 2.0 pad_maximum_fusion
  14.8 4.1 fusion.26
  20.4 3.0 collective-permute-start
  23.5 2.6 collective-permute-start.1
  27.7 9.2 %all-gather.4 = bf16[8,19,128]{2,1,0:T(8,128)(2,1)S(1)} all-gather(bf16[1,19,128]{2,1,0:T(8,128)(2,1)S(1)} %bitcast.125), channel_id=2, replica_groups=mesh['clip'=8,'tm'=4] {'clip'}, dimensions={0}, use_global_device_ids=true | all-gather | bytes 43776 | tf_op jit(solution)/shard_map/all_gather | solution.py:782
  43.0 24.9 %all-gather.9.cloned.1.call-done = bf16[4096,1024]{1,0:T(8,128)(2,1)} async-done(((bf16[512,1024]{1,0:T(8,128)(2,1)}), bf16[4096,1024]{1,0:T(8,128)(2,1)}) %all-gather.9.cloned.1.call-update) | async-done | bytes 8388624 | tf_op jit(solution)/shard_map/all_gather | solution.py:712
  68.0 22.7 %space_forward.2 = (bf16[4,256,1024]{2,1,0:T(8,128)(2,1)}, bf16[4,256,3072]{2,1,0:T(8,128)(2,1)}, bf16[4,256,1024]{2,1,0:T(8,128)(2,1)}, f32[4,16,256]{2,1,0:T(8...) custom-call(s32[1]{0:T(128)} %bitcast.refs_0_.refs_4_.refs_5_, ...), custom_call_target="tpu_custom_call" | custom-call | tf_op jit(solution)/shard_map/space_forward/pallas_call | solution.py:380
  96.3 2.4 collective-permute-start.4
  100.1 22.7 %space_forward.3 = (bf16[4,256,1024]{2,1,0:T(8,128)(2,1)}, bf16[4,256,3072]{2,1,0:T(8,128)(2,1)}, bf16[4,256,1024]{2,1,0:T(8,128)(2,1)}, f32[4,16,256]{2,1,0:T(8...) custom-call(f32[4,16,256]{2,1,0:T(8,128)} %get-tuple-element.121.ref, ...), custom_call_target="tpu_custom_call" | custom-call | tf_op jit(solution)/shard_map/space_forward/pallas_call | solution.py:380
  125.3 2.1 collective-permute-start.8
  129.0 22.3 %collective-permute-done.4.refs_6_.refs_3_ = bf16[4,64,1024]{2,1,0:T(8,128)(2,1)S(1)} collective-permute-done((bf16[4,64,1024]{2,1,0:T(8,128)(2,1)}, bf16[4,64,1024]{2,1,0:T(8,128)(2,1)S(1)}, u32[]{:S(2)}, u32[]{:S(2)}) %collective-permute-start.4) | collective-permute-done | bytes 524320 | tf_op jit(solution)/shard_map/ppermute | solution.py:802
  152.3 21.8 %time_forward.2 = (bf16[4,256,1024]{2,1,0:T(8,128)(2,1)}, bf16[4,256,3072]{2,1,0:T(8,128)(2,1)}, bf16[4,256,1024]{2,1,0:T(8,128)(2,1)}, f32[4,16,256]{2,1,0:T(8,128)}, f32[4,256,1024]{2,1,0:T(8,128)}) custom-call(f32[4,16,256]{2,1,0:T(8,128)} %get-tuple-element.122.refs_0_.refs_15_, bf16[8,128]{1,0:T(8,128)(2,1)} %slice.227.refs_1_, ...), custom_call_target="tpu_custom_call" | custom-call | tf_op jit(solution)/shard_map/time_forward/pallas_call | solution.py:380
  174.5 21.9 %time_forward.3 = (bf16[4,256,1024]{2,1,0:T(8,128)(2,1)}, bf16[4,256,3072]{2,1,0:T(8,128)(2,1)}, bf16[4,256,1024]{2,1,0:T(8,128)(2,1)}, f32[4,16,256]{2,1,0:T(8,128)}, f32[4,256,1024]{2,1,0:T(8,128)}) custom-call(f32[4,16,256]{2,1,0:T(8,128)} %get-tuple-element.127.refs_0_.refs_12_, bf16[4,64,1024]{2,1,0:T(8,128)(2,1)} %get-tuple-element.128.refs_1_, ...), custom_call_target="tpu_custom_call" | custom-call | tf_op jit(solution)/shard_map/time_forward/pallas_call | solution.py:380
  196.4 10.9 %collective-permute-start.10 = (bf16[4,64,1024]{2,1,0:T(8,128)(2,1)}, bf16[4,64,1024]{2,1,0:T(8,128)(2,1)S(1)}, u32[]{:S(2)}, u32[]{:S(2)}) collective-permute-start(bf16[4,64,1024]{2,1,0:T(8,128)(2,1)} %get-tuple-element.139), channel_id=1, source_target_pairs={{0,2},{1,3},{2,0},{3,1},{4,6},{5,7},{6,4},{7,5},{8,10},{9,11},{10,... | collective-permute-start | bytes 1572872 | tf_op jit(solution)/shard_map/ppermute | solution.py:802
  207.8 3.4 collective-permute-start.11
  211.6 5.6 all-gather.13.cloned.1.call-done
  217.2 50.8 %feed_forward.2 = (bf16[4,256,1024]{2,1,0:T(8,128)(2,1)}, bf16[4,256,4096]{2,1,0:T(8,128)(2,1)}, bf16[4,256,4096]{2,1,0:T(8,128)(2,1)}, bf16[4,256,1024]{2,1,0:T...) custom-call(f32[4,16,256]{2,1,0:T(8,128)} %get-tuple-element.132.ref, ...), custom_call_target="tpu_custom_call" | custom-call | tf_op jit(solution)/shard_map/feed_forward/pallas_call | solution.py:380
  268.0 3.4 collective-permute-start.12
  273.5 50.9 %feed_forward.3 = (bf16[4,256,1024]{2,1,0:T(8,128)(2,1)}, bf16[4,256,4096]{2,1,0:T(8,128)(2,1)}, bf16[4,256,4096]{2,1,0:T(8,128)(2,1)}, bf16[4,256,1024]{2,1,0:T...) custom-call(f32[1,1024]{1,0:T(1,128)} %get-tuple-element.135.refs_0_, ...), custom_call_target="tpu_custom_call" | custom-call | tf_op jit(solution)/shard_map/feed_forward/pallas_call | solution.py:380
  324.3 2.8 collective-permute-start.15
  330.3 22.9 %down_grad.1.refs_4_ = bf16[8,1024,1024]{2,1,0:T(8,128)(2,1)} custom-call(f32[1,1024]{1,0:T(1,128)} %get-tuple-element.145.refs_0_, bf16[8,128]{1,0:T(8,128)(2,1)} %slice.232.refs_1_, bf16[8,128]{1,0:T(8,128)(2,1)} %slice.233.refs_2_, bf16[8,128]{1,0:T(8,128)(2,1)} %slice.234.refs_3_, bf16[4,256,4096]{2,1,0:T(8,128)(2,1)} %get-tuple-element.149.refs_4_, ...), custom_call_target="tpu_custom_call" | custom-call | tf_op jit(solution)/shard_map/down_grad/pallas_call | solution.py:380
  353.2 23.2 %hidden_grad.1.refs_0_ = bf16[8,1024,1024]{2,1,0:T(8,128)(2,1)} custom-call(bf16[4,256,1024]{2,1,0:T(8,128)(2,1)} %get-tuple-element.134.refs_0_, bf16[4,256,1024]{2,1,0:T(8,128)(2,1)} %get-tuple-element.142.refs_1_, bf16[4,256,4096]{2,1,0:T(8,128)(2,1)} %get-tuple-element.143.refs_2_, ...), custom_call_target="tpu_custom_call", output_to_operand_aliasing={{}: (4, {})} | custom-call | tf_op jit(solution)/shard_map/hidden_grad/pallas_call | solution.py:380
  376.6 30.0 %time_backward.2 = (bf16[4,256,3072]{2,1,0:T(8,128)(2,1)}, f32[1,1024]{1,0:T(1,128)}, f32[1,1024]{1,0:T(1,128)}, bf16[4,64,1024]{2,1,0:T(8,128)(2,1)}, bf16[4,64...) custom-call(bf16[8,1024,1024]{2,1,0:T(8,128)(2,1)} %hidden_grad.1.refs_0_, ...), custom_call_target="tpu_custom_call" | custom-call | tf_op jit(solution)/shard_map/time_backward/pallas_call | solution.py:380
  406.5 3.8 collective-permute-start.18
  411.2 30.6 %time_backward.3 = (bf16[4,256,3072]{2,1,0:T(8,128)(2,1)}, f32[1,1024]{1,0:T(1,128)}, f32[1,1024]{1,0:T(1,128)}, bf16[4,64,1024]{2,1,0:T(8,128)(2,1)}, bf16[4,64...) custom-call(f32[1,1024]{1,0:T(1,128)} %get-tuple-element.161.refs_0_, ...), custom_call_target="tpu_custom_call" | custom-call | tf_op jit(solution)/shard_map/time_backward/pallas_call | solution.py:380
  441.9 26.0 %time_grad.1.refs_0_ = bf16[8,512,1024]{2,1,0:T(8,128)(2,1)} custom-call(f32[1,1024]{1,0:T(1,128)} %get-tuple-element.165.refs_0_, bf16[4,256,1024]{2,1,0:T(8,128)(2,1)} %get-tuple-element.166.refs_1_, bf16[4,256,1024]{2,1,0:T(8,128)(2,1)} %get-tuple-element.167.refs_2_, bf16[4,256,3072]{2,1,0:T(8,128)(2,1)} %get-tuple-element.168.refs_3_, ...), custom_call_target="tpu_custom_call" | custom-call | tf_op jit(solution)/shard_map/time_grad/pallas_call | solution.py:380
  469.2 3.3 collective-permute-start.21
  474.3 33.5 %space_backward.2 = (bf16[4,256,3072]{2,1,0:T(8,128)(2,1)}, bf16[4,256,1024]{2,1,0:T(8,128)(2,1)}, f32[2,4,256,1024]{3,2,1,0:T(8,128)}, f32[1,1024]{1,0:T(1,128)...) custom-call(bf16[8,512,1024]{2,1,0:T(8,128)(2,1)} %time_grad.1.refs_0_, bf16[4,64,1024]{2,1,0:T(8,128)(2,1)} %get-tuple-element.175.refs_1_, ...), custom_call_target="tpu_custom_call" | custom-call | tf_op jit(solution)/shard_map/space_backward/pallas_call | solution.py:380
  507.8 9.3 %collective-permute-done.22.refs_3_ = bf16[4,64,1024]{2,1,0:T(8,128)(2,1)S(1)} collective-permute-done((bf16[4,64,1024]{2,1,0:T(8,128)(2,1)}, bf16[4,64,1024]{2,1,0:T(8,128)(2,1)S(1)}, u32[]{:S(2)}, u32[]{:S(2)}) %collective-permute-start.22) | collective-permute-done | bytes 524320 | tf_op jit(solution)/shard_map/ppermute | solution.py:805
  518.5 2.6 constant_dynamic-slice_fusion.5
  521.7 3.4 collective-permute-start.26
  525.1 33.4 %space_backward.3 = (bf16[4,256,3072]{2,1,0:T(8,128)(2,1)}, bf16[4,256,1024]{2,1,0:T(8,128)(2,1)}, f32[2,4,256,1024]{3,2,1,0:T(8,128)}, f32[1,1024]{1,0:T(1,128)...) custom-call(bf16[8,128]{1,0:T(8,128)(2,1)} %slice.201.refs_0_, ...), custom_call_target="tpu_custom_call", output_to_operand_aliasing={{2}: (16, {})} | custom-call | tf_op jit(solution)/shard_map/space_backward/pallas_call | solution.py:380
  561.9 1.9 add_convert_fusion
  564.4 26.7 %space_grad.1 = bf16[8,544,1024]{2,1,0:T(8,128)(2,1)} custom-call(bf16[8,128]{1,0:T(8,128)(2,1)} %slice.235.refs_0_, bf16[4,256,1024]{2,1,0:T(8,128)(2,1)} %get-tuple-element.187.refs_1_, bf16[4,256,1024]{2,1,0:T(8,128)(2,1)} %get-tuple-element.188.refs_2_, bf16[4,256,3072]{2,1,0:T(8,128)(2,1)} %get-tuple-element.189.refs_3_, ...), custom_call_target="tpu_custom_call" | custom-call | tf_op jit(solution)/shard_map/space_grad/pallas_call | solution.py:380
  592.3 6.2 collective-permute-start.27
  598.6 2.1 collective-permute-start.28
  601.0 6.5 collective-permute-done.27
  607.5 8.9 %collective-permute-done.28 = bf16[128,1024]{1,0:T(8,128)(2,1)S(1)} collective-permute-done((bf16[128,1024]{1,0:T(8,128)(2,1)S(1)}, bf16[128,1024]{1,0:T(8,128)(2,1)S(1)}, u32[]{:S(2)}, u32[]{:S(2)}) %collective-permute-start.28) | collective-permute-done | bytes 262176 | tf_op jit(solution)/shard_map/ppermute | solution.py:721
  616.5 1.8 constant_dynamic-update-slice_fusion.12
  618.3 6.2 collective-permute-start.30
  624.5 2.4 collective-permute-start.31
  626.9 4.9 assemble.1
  632.4 3.2 collective-permute-start.32
  637.6 28.7 %collective-permute-done.31 = bf16[128,1024]{1,0:T(8,128)(2,1)S(1)} collective-permute-done((bf16[128,1024]{1,0:T(8,128)(2,1)}, bf16[128,1024]{1,0:T(8,128)(2,1)S(1)}, u32[]{:S(2)}, u32[]{:S(2)}) %collective-permute-start.31) | collective-permute-done | bytes 262176 | tf_op jit(solution)/shard_map/ppermute | solution.py:721
  668.6 8.8 %collective-permute-done.34 = bf16[256,1024]{1,0:T(8,128)(2,1)S(1)} collective-permute-done((bf16[256,1024]{1,0:T(8,128)(2,1)S(1)}, bf16[256,1024]{1,0:T(8,128)(2,1)S(1)}, u32[]{:S(2)}, u32[]{:S(2)}) %collective-permute-start.34) | collective-permute-done | bytes 524320 | tf_op jit(solution)/shard_map/ppermute | solution.py:721
  677.5 2.7 collective-permute-done.35
  683.4 66.0 %all-reduce.4.cloned.1.call-done = bf16[544,1024]{1,0:T(8,128)(2,1)} async-done(((bf16[544,1024]{1,0:T(8,128)(2,1)}), bf16[544,1024]{1,0:T(8,128)(2,1)}) %all-reduce.4.cloned.1.call-update) | async-done | bytes 1114128 | tf_op jit(solution)/shard_map/psum | solution.py:902
  752.6 2.1 slice_convert_fusion.1
  (234 shorter events, 57.1 us)
Async XLA Ops:
  7.2 60.8 %all-gather.9.cloned.1.call-start = ((), (), s32[]{:S(2)}) async-start(), calls=%async_computation.7 | async-start | bytes 9437184 | tf_op jit(solution)/shard_map/all_gather | solution.py:712
  10.5 118.4 %all-gather.11.cloned.1.call-start = ((), (), s32[]{:S(2)}) async-start(), calls=%async_computation.8 | async-start | bytes 9437184 | tf_op jit(solution)/shard_map/all_gather | solution.py:712
  11.7 205.5 %all-gather.13.cloned.1.call-start = ((), (), s32[]{:S(2)}) async-start(), calls=%async_computation.9 | async-start | bytes 18874368 | tf_op jit(solution)/shard_map/all_gather | solution.py:712
  14.7 502.5 %reduce-scatter.4.cloned.1.call-start = ((), (), s32[]{:S(2)}) async-start(), calls=%async_computation.3 | async-start | bytes 18874368 | tf_op jit(solution)/shard_map/reduce_scatter | solution.py:716
  20.4 73.3 %collective-permute-start = (bf16[4,64,1024]{2,1,0:T(8,128)(2,1)}, bf16[4,64,1024]{2,1,0:T(8,128)(2,1)S(1)}, u32[]{:S(2)}, u32[]{:S(2)}) collective-permute-start(bf16[4,64,1024]{2,1,0:T(8,128)(2,1)} %get-tuple-element.247), channel_id=1, source_target_pairs={{0,1},{1,2},{2,3},{3,0},{4,5},{5,6},{6,7},{7,4},{8,9},{9,10},{10,1... | collective-permute-start | bytes 1572872 | tf_op jit(solution)/shard_map/ppermute | solution.py:802
  23.5 70.9 %collective-permute-start.1 = (bf16[4,64,1024]{2,1,0:T(8,128)(2,1)}, bf16[4,64,1024]{2,1,0:T(8,128)(2,1)S(1)}, u32[]{:S(2)}, u32[]{:S(2)}) collective-permute-start(bf16[4,64,1024]{2,1,0:T(8,128)(2,1)} %get-tuple-element.246), channel_id=1, source_target_pairs={{0,2},{1,3},{2,0},{3,1},{4,6},{5,7},{6,4},{7,5},{8,10},{9,11},{10,... | collective-permute-start | bytes 1572872 | tf_op jit(solution)/shard_map/ppermute | solution.py:802
  26.0 69.0 %collective-permute-start.2 = (bf16[4,64,1024]{2,1,0:T(8,128)(2,1)}, bf16[4,64,1024]{2,1,0:T(8,128)(2,1)}, u32[]{:S(2)}, u32[]{:S(2)}) collective-permute-start(bf16[4,64,1024]{2,1,0:T(8,128)(2,1)} %get-tuple-element.245), channel_id=1, source_target_pairs={{0,3},{1,0},{2,1},{3,2},{4,7},{5,4},{6,5},{7,6},{8,11},{9,8},{10,9... | collective-permute-start | bytes 1572872 | tf_op jit(solution)/shard_map/ppermute | solution.py:802
  90.6 34.7 %collective-permute-start.3 = (bf16[4,64,1024]{2,1,0:T(8,128)(2,1)}, bf16[4,64,1024]{2,1,0:T(8,128)(2,1)S(1)}, u32[]{:S(2)}, u32[]{:S(2)}) collective-permute-start(bf16[4,64,1024]{2,1,0:T(8,128)(2,1)} %get-tuple-element.124), channel_id=1, source_target_pairs={{0,1},{1,2},{2,3},{3,0},{4,5},{5,6},{6,7},{7,4},{8,9},{9,10},{10,1... | collective-permute-start | bytes 1572872 | tf_op jit(solution)/shard_map/ppermute | solution.py:802
  96.3 55.0 %collective-permute-start.4 = (bf16[4,64,1024]{2,1,0:T(8,128)(2,1)}, bf16[4,64,1024]{2,1,0:T(8,128)(2,1)S(1)}, u32[]{:S(2)}, u32[]{:S(2)}) collective-permute-start(bf16[4,64,1024]{2,1,0:T(8,128)(2,1)} %get-tuple-element.125), channel_id=1, source_target_pairs={{0,2},{1,3},{2,0},{3,1},{4,6},{5,7},{6,4},{7,5},{8,10},{9,11},{10,... | collective-permute-start | bytes 1572872 | tf_op jit(solution)/shard_map/ppermute | solution.py:802
  98.7 52.6 %collective-permute-start.5 = (bf16[4,64,1024]{2,1,0:T(8,128)(2,1)}, bf16[4,64,1024]{2,1,0:T(8,128)(2,1)S(1)}, u32[]{:S(2)}, u32[]{:S(2)}) collective-permute-start(bf16[4,64,1024]{2,1,0:T(8,128)(2,1)} %get-tuple-element.126), channel_id=1, source_target_pairs={{0,3},{1,0},{2,1},{3,2},{4,7},{5,4},{6,5},{7,6},{8,11},{9,8},{10,9... | collective-permute-start | bytes 1572872 | tf_op jit(solution)/shard_map/ppermute | solution.py:802
  122.8 51.3 %collective-permute-start.6 = (bf16[4,64,1024]{2,1,0:T(8,128)(2,1)}, bf16[4,64,1024]{2,1,0:T(8,128)(2,1)}, u32[]{:S(2)}, u32[]{:S(2)}) collective-permute-start(bf16[4,64,1024]{2,1,0:T(8,128)(2,1)} %get-tuple-element.129), channel_id=1, source_target_pairs={{0,1},{1,2},{2,3},{3,0},{4,5},{5,6},{6,7},{7,4},{8,9},{9,10},{10,1... | collective-permute-start | bytes 1572872 | tf_op jit(solution)/shard_map/ppermute | solution.py:802
  123.5 51.0 %collective-permute-start.7 = (bf16[4,64,1024]{2,1,0:T(8,128)(2,1)}, bf16[4,64,1024]{2,1,0:T(8,128)(2,1)}, u32[]{:S(2)}, u32[]{:S(2)}) collective-permute-start(bf16[4,64,1024]{2,1,0:T(8,128)(2,1)} %get-tuple-element.130), channel_id=1, source_target_pairs={{0,2},{1,3},{2,0},{3,1},{4,6},{5,7},{6,4},{7,5},{8,10},{9,11},{10,... | collective-permute-start | bytes 1572872 | tf_op jit(solution)/shard_map/ppermute | solution.py:802
  125.3 26.0 %copy-start.1 = (bf16[4,64,1024]{2,1,0:T(8,128)(2,1)}, bf16[4,64,1024]{2,1,0:T(8,128)(2,1)S(1)}, u32[]{:S(2)}) copy-start(bf16[4,64,1024]{2,1,0:T(8,128)(2,1)S(1)} %collective-permute-done.3.refs_5_.refs_2_) | copy-start | bytes 1572868
  125.3 49.1 %collective-permute-start.8 = (bf16[4,64,1024]{2,1,0:T(8,128)(2,1)}, bf16[4,64,1024]{2,1,0:T(8,128)(2,1)}, u32[]{:S(2)}, u32[]{:S(2)}) collective-permute-start(bf16[4,64,1024]{2,1,0:T(8,128)(2,1)} %get-tuple-element.131), channel_id=1, source_target_pairs={{0,3},{1,0},{2,1},{3,2},{4,7},{5,4},{6,5},{7,6},{8,11},{9,8},{10,9... | collective-permute-start | bytes 1572872 | tf_op jit(solution)/shard_map/ppermute | solution.py:802
  196.4 75.0 %collective-permute-start.10 = (bf16[4,64,1024]{2,1,0:T(8,128)(2,1)}, bf16[4,64,1024]{2,1,0:T(8,128)(2,1)S(1)}, u32[]{:S(2)}, u32[]{:S(2)}) collective-permute-start(bf16[4,64,1024]{2,1,0:T(8,128)(2,1)} %get-tuple-element.139), channel_id=1, source_target_pairs={{0,2},{1,3},{2,0},{3,1},{4,6},{5,7},{6,4},{7,5},{8,10},{9,11},{10,... | collective-permute-start | bytes 1572872 | tf_op jit(solution)/shard_map/ppermute | solution.py:802
  207.8 65.6 %collective-permute-start.11 = (bf16[4,64,1024]{2,1,0:T(8,128)(2,1)}, bf16[4,64,1024]{2,1,0:T(8,128)(2,1)}, u32[]{:S(2)}, u32[]{:S(2)}) collective-permute-start(bf16[4,64,1024]{2,1,0:T(8,128)(2,1)} %get-tuple-element.140), channel_id=1, source_target_pairs={{0,3},{1,0},{2,1},{3,2},{4,7},{5,4},{6,5},{7,6},{8,11},{9,8},{10,9... | collective-permute-start | bytes 1572872 | tf_op jit(solution)/shard_map/ppermute | solution.py:802
  211.2 62.2 %collective-permute-start.9 = (bf16[4,64,1024]{2,1,0:T(8,128)(2,1)}, bf16[4,64,1024]{2,1,0:T(8,128)(2,1)}, u32[]{:S(2)}, u32[]{:S(2)}) collective-permute-start(bf16[4,64,1024]{2,1,0:T(8,128)(2,1)} %get-tuple-element.138), channel_id=1, source_target_pairs={{0,1},{1,2},{2,3},{3,0},{4,5},{5,6},{6,7},{7,4},{8,9},{9,10},{10,1... | collective-permute-start | bytes 1572872 | tf_op jit(solution)/shard_map/ppermute | solution.py:802
  268.0 60.2 %collective-permute-start.12 = (bf16[4,64,1024]{2,1,0:T(8,128)(2,1)}, bf16[4,64,1024]{2,1,0:T(8,128)(2,1)S(1)}, u32[]{:S(2)}, u32[]{:S(2)}) collective-permute-start(bf16[4,64,1024]{2,1,0:T(8,128)(2,1)} %get-tuple-element.146), channel_id=1, source_target_pairs={{0,3},{1,0},{2,1},{3,2},{4,7},{5,4},{6,5},{7,6},{8,11},{9,8},{10,9... | collective-permute-start | bytes 1572872 | tf_op jit(solution)/shard_map/ppermute | solution.py:805
  271.4 57.7 %collective-permute-start.13 = (bf16[4,64,1024]{2,1,0:T(8,128)(2,1)}, bf16[4,64,1024]{2,1,0:T(8,128)(2,1)S(1)}, u32[]{:S(2)}, u32[]{:S(2)}) collective-permute-start(bf16[4,64,1024]{2,1,0:T(8,128)(2,1)} %get-tuple-element.147), channel_id=1, source_target_pairs={{0,2},{1,3},{2,0},{3,1},{4,6},{5,7},{6,4},{7,5},{8,10},{9,11},{10,... | collective-permute-start | bytes 1572872 | tf_op jit(solution)/shard_map/ppermute | solution.py:805
  272.2 57.5 %collective-permute-start.14 = (bf16[4,64,1024]{2,1,0:T(8,128)(2,1)}, bf16[4,64,1024]{2,1,0:T(8,128)(2,1)S(1)}, u32[]{:S(2)}, u32[]{:S(2)}) collective-permute-start(bf16[4,64,1024]{2,1,0:T(8,128)(2,1)} %get-tuple-element.148), channel_id=1, source_target_pairs={{0,1},{1,2},{2,3},{3,0},{4,5},{5,6},{6,7},{7,4},{8,9},{9,10},{10,1... | collective-permute-start | bytes 1572872 | tf_op jit(solution)/shard_map/ppermute | solution.py:805
  324.3 52.1 %collective-permute-start.15 = (bf16[4,64,1024]{2,1,0:T(8,128)(2,1)}, bf16[4,64,1024]{2,1,0:T(8,128)(2,1)}, u32[]{:S(2)}, u32[]{:S(2)}) collective-permute-start(bf16[4,64,1024]{2,1,0:T(8,128)(2,1)} %get-tuple-element.154), channel_id=1, source_target_pairs={{0,3},{1,0},{2,1},{3,2},{4,7},{5,4},{6,5},{7,6},{8,11},{9,8},{10,9... | collective-permute-start | bytes 1572872 | tf_op jit(solution)/shard_map/ppermute | solution.py:805
  327.1 49.4 %collective-permute-start.16 = (bf16[4,64,1024]{2,1,0:T(8,128)(2,1)}, bf16[4,64,1024]{2,1,0:T(8,128)(2,1)}, u32[]{:S(2)}, u32[]{:S(2)}) collective-permute-start(bf16[4,64,1024]{2,1,0:T(8,128)(2,1)} %get-tuple-element.155), channel_id=1, source_target_pairs={{0,2},{1,3},{2,0},{3,1},{4,6},{5,7},{6,4},{7,5},{8,10},{9,11},{10,... | collective-permute-start | bytes 1572872 | tf_op jit(solution)/shard_map/ppermute | solution.py:805
  328.2 25.0 %copy-start.6 = (bf16[4,64,1024]{2,1,0:T(8,128)(2,1)}, bf16[4,64,1024]{2,1,0:T(8,128)(2,1)S(1)}, u32[]{:S(2)}) copy-start(bf16[4,64,1024]{2,1,0:T(8,128)(2,1)S(1)} %collective-permute-done.12.refs_2_) | copy-start | bytes 1572868
  328.2 48.2 %collective-permute-start.17 = (bf16[4,64,1024]{2,1,0:T(8,128)(2,1)}, bf16[4,64,1024]{2,1,0:T(8,128)(2,1)}, u32[]{:S(2)}, u32[]{:S(2)}) collective-permute-start(bf16[4,64,1024]{2,1,0:T(8,128)(2,1)} %get-tuple-element.156), channel_id=1, source_target_pairs={{0,1},{1,2},{2,3},{3,0},{4,5},{5,6},{6,7},{7,4},{8,9},{9,10},{10,1... | collective-permute-start | bytes 1572872 | tf_op jit(solution)/shard_map/ppermute | solution.py:805
  329.1 24.1 %copy-start.7 = (bf16[4,64,1024]{2,1,0:T(8,128)(2,1)}, bf16[4,64,1024]{2,1,0:T(8,128)(2,1)S(1)}, u32[]{:S(2)}) copy-start(bf16[4,64,1024]{2,1,0:T(8,128)(2,1)S(1)} %collective-permute-done.13.refs_3_) | copy-start | bytes 1572868
  376.5 214.7 %reduce-scatter.8.cloned.1.call-start = ((), (), s32[]{:S(2)}) async-start(), calls=%async_computation.5 | async-start | bytes 9437184 | tf_op jit(solution)/shard_map/reduce_scatter | solution.py:716
  406.5 61.4 %collective-permute-start.18 = (bf16[4,64,1024]{2,1,0:T(8,128)(2,1)}, bf16[4,64,1024]{2,1,0:T(8,128)(2,1)S(1)}, u32[]{:S(2)}, u32[]{:S(2)}) collective-permute-start(bf16[4,64,1024]{2,1,0:T(8,128)(2,1)} %get-tuple-element.171), channel_id=1, source_target_pairs={{0,3},{1,0},{2,1},{3,2},{4,7},{5,4},{6,5},{7,6},{8,11},{9,8},{10,9... | collective-permute-start | bytes 1572872 | tf_op jit(solution)/shard_map/ppermute | solution.py:805
  410.4 57.6 %collective-permute-start.19 = (bf16[4,64,1024]{2,1,0:T(8,128)(2,1)}, bf16[4,64,1024]{2,1,0:T(8,128)(2,1)S(1)}, u32[]{:S(2)}, u32[]{:S(2)}) collective-permute-start(bf16[4,64,1024]{2,1,0:T(8,128)(2,1)} %get-tuple-element.172), channel_id=1, source_target_pairs={{0,2},{1,3},{2,0},{3,1},{4,6},{5,7},{6,4},{7,5},{8,10},{9,11},{10,... | collective-permute-start | bytes 1572872 | tf_op jit(solution)/shard_map/ppermute | solution.py:805
  410.4 57.6 %collective-permute-start.20 = (bf16[4,64,1024]{2,1,0:T(8,128)(2,1)}, bf16[4,64,1024]{2,1,0:T(8,128)(2,1)S(1)}, u32[]{:S(2)}, u32[]{:S(2)}) collective-permute-start(bf16[4,64,1024]{2,1,0:T(8,128)(2,1)} %get-tuple-element.173), channel_id=1, source_target_pairs={{0,1},{1,2},{2,3},{3,0},{4,5},{5,6},{6,7},{7,4},{8,9},{9,10},{10,1... | collective-permute-start | bytes 1572872 | tf_op jit(solution)/shard_map/ppermute | solution.py:805
  469.1 214.3 %reduce-scatter.6.cloned.1.call-start = ((), (), s32[]{:S(2)}) async-start(), calls=%async_computation.4 | async-start | bytes 10027008 | tf_op jit(solution)/shard_map/reduce_scatter | solution.py:716
  469.2 38.6 %collective-permute-start.21 = (bf16[4,64,1024]{2,1,0:T(8,128)(2,1)}, bf16[4,64,1024]{2,1,0:T(8,128)(2,1)S(1)}, u32[]{:S(2)}, u32[]{:S(2)}) collective-permute-start(bf16[4,64,1024]{2,1,0:T(8,128)(2,1)} %get-tuple-element.183), channel_id=1, source_target_pairs={{0,3},{1,0},{2,1},{3,2},{4,7},{5,4},{6,5},{7,6},{8,11},{9,8},{10,9... | collective-permute-start | bytes 1572872 | tf_op jit(solution)/shard_map/ppermute | solution.py:805
  472.5 44.7 %collective-permute-start.22 = (bf16[4,64,1024]{2,1,0:T(8,128)(2,1)}, bf16[4,64,1024]{2,1,0:T(8,128)(2,1)S(1)}, u32[]{:S(2)}, u32[]{:S(2)}) collective-permute-start(bf16[4,64,1024]{2,1,0:T(8,128)(2,1)} %get-tuple-element.184), channel_id=1, source_target_pairs={{0,2},{1,3},{2,0},{3,1},{4,6},{5,7},{6,4},{7,5},{8,10},{9,11},{10,... | collective-permute-start | bytes 1572872 | tf_op jit(solution)/shard_map/ppermute | solution.py:805
  473.7 43.5 %collective-permute-start.23 = (bf16[4,64,1024]{2,1,0:T(8,128)(2,1)}, bf16[4,64,1024]{2,1,0:T(8,128)(2,1)S(1)}, u32[]{:S(2)}, u32[]{:S(2)}) collective-permute-start(bf16[4,64,1024]{2,1,0:T(8,128)(2,1)} %get-tuple-element.185), channel_id=1, source_target_pairs={{0,1},{1,2},{2,3},{3,0},{4,5},{5,6},{6,7},{7,4},{8,9},{9,10},{10,1... | collective-permute-start | bytes 1572872 | tf_op jit(solution)/shard_map/ppermute | solution.py:805
  521.1 40.8 %collective-permute-start.24 = (bf16[256,1024]{1,0:T(8,128)(2,1)}, bf16[256,1024]{1,0:T(8,128)(2,1)}, u32[]{:S(2)}, u32[]{:S(2)}) collective-permute-start(bf16[256,1024]{1,0:T(8,128)(2,1)} %get-tuple-element.237), channel_id=1, source_target_pairs={{0,1},{1,2},{2,3},{3,0},{4,5},{5,6},{6,7},{7,4},{8,9},{9,10},{10,1... | collective-permute-start | bytes 1572872 | tf_op jit(solution)/shard_map/ppermute | solution.py:721
  521.1 40.8 %collective-permute-start.25 = (bf16[256,1024]{1,0:T(8,128)(2,1)}, bf16[256,1024]{1,0:T(8,128)(2,1)}, u32[]{:S(2)}, u32[]{:S(2)}) collective-permute-start(bf16[256,1024]{1,0:T(8,128)(2,1)} %get-tuple-element.239), channel_id=1, source_target_pairs={{0,2},{1,3},{2,0},{3,1},{4,6},{5,7},{6,4},{7,5},{8,10},{9,11},{10,... | collective-permute-start | bytes 1572872 | tf_op jit(solution)/shard_map/ppermute | solution.py:721
  521.7 40.2 %collective-permute-start.26 = (bf16[256,1024]{1,0:T(8,128)(2,1)}, bf16[256,1024]{1,0:T(8,128)(2,1)}, u32[]{:S(2)}, u32[]{:S(2)}) collective-permute-start(bf16[256,1024]{1,0:T(8,128)(2,1)} %get-tuple-element.238), channel_id=1, source_target_pairs={{0,3},{1,0},{2,1},{3,2},{4,7},{5,4},{6,5},{7,6},{8,11},{9,8},{10,9... | collective-permute-start | bytes 1572872 | tf_op jit(solution)/shard_map/ppermute | solution.py:721
  525.1 33.4 %copy-start.30 = (f32[1,1024]{1,0:T(1,128)S(1)}, f32[1,1024]{1,0:T(1,128)}, u32[]{:S(2)}) copy-start(f32[1,1024]{1,0:T(1,128)} %get-tuple-element.202) | copy-start | bytes 12292
  525.1 34.1 %copy-start.29 = (f32[1,1024]{1,0:T(1,128)S(1)}, f32[1,1024]{1,0:T(1,128)}, u32[]{:S(2)}) copy-start(f32[1,1024]{1,0:T(1,128)} %get-tuple-element.200) | copy-start | bytes 12292
  591.1 158.3 %all-reduce.4.cloned.1.call-start = ((), (), s32[]{:S(2)}) async-start(), calls=%async_computation.6 | async-start | bytes 2228224 | tf_op jit(solution)/shard_map/psum | solution.py:902
  592.3 15.2 %collective-permute-start.27 = (bf16[128,1024]{1,0:T(8,128)(2,1)S(1)}, bf16[128,1024]{1,0:T(8,128)(2,1)S(1)}, u32[]{:S(2)}, u32[]{:S(2)}) collective-permute-start(bf16[128,1024]{1,0:T(8,128)(2,1)S(1)} %get-tuple-element.256), channel_id=1, source_target_pairs={{0,1},{1,2},{2,3},{3,0},{4,5},{5,6},{6,7},{7,4},{8,9},{9,10},{10,1... | collective-permute-start | bytes 786440 | tf_op jit(solution)/shard_map/ppermute | solution.py:721
  598.6 17.8 %collective-permute-start.28 = (bf16[128,1024]{1,0:T(8,128)(2,1)S(1)}, bf16[128,1024]{1,0:T(8,128)(2,1)S(1)}, u32[]{:S(2)}, u32[]{:S(2)}) collective-permute-start(bf16[128,1024]{1,0:T(8,128)(2,1)S(1)} %get-tuple-element.258), channel_id=1, source_target_pairs={{0,2},{1,3},{2,0},{3,1},{4,6},{5,7},{6,4},{7,5},{8,10},{9,11},{10,... | collective-permute-start | bytes 786440 | tf_op jit(solution)/shard_map/ppermute | solution.py:721
  600.7 15.6 %collective-permute-start.29 = (bf16[128,1024]{1,0:T(8,128)(2,1)S(1)}, bf16[128,1024]{1,0:T(8,128)(2,1)S(1)}, u32[]{:S(2)}, u32[]{:S(2)}) collective-permute-start(bf16[128,1024]{1,0:T(8,128)(2,1)S(1)} %get-tuple-element.257), channel_id=1, source_target_pairs={{0,3},{1,0},{2,1},{3,2},{4,7},{5,4},{6,5},{7,6},{8,11},{9,8},{10,9... | collective-permute-start | bytes 786440 | tf_op jit(solution)/shard_map/ppermute | solution.py:721
  618.3 17.6 %collective-permute-start.30 = (bf16[128,1024]{1,0:T(8,128)(2,1)}, bf16[128,1024]{1,0:T(8,128)(2,1)}, u32[]{:S(2)}, u32[]{:S(2)}) collective-permute-start(bf16[128,1024]{1,0:T(8,128)(2,1)} %get-tuple-element.230), channel_id=1, source_target_pairs={{0,1},{1,2},{2,3},{3,0},{4,5},{5,6},{6,7},{7,4},{8,9},{9,10},{10,1... | collective-permute-start | bytes 786440 | tf_op jit(solution)/shard_map/ppermute | solution.py:721
  624.5 41.8 %collective-permute-start.31 = (bf16[128,1024]{1,0:T(8,128)(2,1)}, bf16[128,1024]{1,0:T(8,128)(2,1)S(1)}, u32[]{:S(2)}, u32[]{:S(2)}) collective-permute-start(bf16[128,1024]{1,0:T(8,128)(2,1)} %get-tuple-element.230), channel_id=1, source_target_pairs={{0,2},{1,3},{2,0},{3,1},{4,6},{5,7},{6,4},{7,5},{8,10},{9,11},{10,... | collective-permute-start | bytes 786440 | tf_op jit(solution)/shard_map/ppermute | solution.py:721
  631.7 36.8 %collective-permute-start.33 = (bf16[256,1024]{1,0:T(8,128)(2,1)S(1)}, bf16[256,1024]{1,0:T(8,128)(2,1)S(1)}, u32[]{:S(2)}, u32[]{:S(2)}) collective-permute-start(bf16[256,1024]{1,0:T(8,128)(2,1)S(1)} %add_convert_fusion), channel_id=1, source_target_pairs={{0,1},{1,2},{2,3},{3,0},{4,5},{5,6},{6,7},{7,4},{8,9},{9,10},{10,1... | collective-permute-start | bytes 1572872 | tf_op jit(solution)/shard_map/ppermute | solution.py:721
  631.8 45.7 %collective-permute-start.34 = (bf16[256,1024]{1,0:T(8,128)(2,1)S(1)}, bf16[256,1024]{1,0:T(8,128)(2,1)S(1)}, u32[]{:S(2)}, u32[]{:S(2)}) collective-permute-start(bf16[256,1024]{1,0:T(8,128)(2,1)S(1)} %add_convert_fusion), channel_id=1, source_target_pairs={{0,2},{1,3},{2,0},{3,1},{4,6},{5,7},{6,4},{7,5},{8,10},{9,11},{10,... | collective-permute-start | bytes 1572872 | tf_op jit(solution)/shard_map/ppermute | solution.py:721
  632.4 33.9 %collective-permute-start.32 = (bf16[128,1024]{1,0:T(8,128)(2,1)}, bf16[128,1024]{1,0:T(8,128)(2,1)S(1)}, u32[]{:S(2)}, u32[]{:S(2)}) collective-permute-start(bf16[128,1024]{1,0:T(8,128)(2,1)} %get-tuple-element.230), channel_id=1, source_target_pairs={{0,3},{1,0},{2,1},{3,2},{4,7},{5,4},{6,5},{7,6},{8,11},{9,8},{10,9... | collective-permute-start | bytes 786440 | tf_op jit(solution)/shard_map/ppermute | solution.py:721
  635.9 44.3 %collective-permute-start.35 = (bf16[256,1024]{1,0:T(8,128)(2,1)S(1)}, bf16[256,1024]{1,0:T(8,128)(2,1)S(1)}, u32[]{:S(2)}, u32[]{:S(2)}) collective-permute-start(bf16[256,1024]{1,0:T(8,128)(2,1)S(1)} %add_convert_fusion), channel_id=1, source_target_pairs={{0,3},{1,0},{2,1},{3,2},{4,7},{5,4},{6,5},{7,6},{8,11},{9,8},{10,9... | collective-permute-start | bytes 1572872 | tf_op jit(solution)/shard_map/ppermute | solution.py:721
  (36 other events, 218.8 us)
Sparse Core Ops, SparseCore 0:
  10.7 57.2 all-gather.8
  70.4 54.3 all-gather.10
  127.3 89.8 all-gather.12
  376.6 116.3 reduce-scatter.3
  496.4 71.2 reduce-scatter.7
  591.2 78.2 reduce-scatter.5
  683.6 65.8 all-reduce.3

commit v5 on v4

--- a/solution.py
+++ b/solution.py
@@ -732,15 +732,18 @@
     return total.astype(bf16)
 
 
-def share_half(mine):
-    count = lax.axis_size("tm")
-    rows = mine.shape[0]
+def share(mine):
+    return [mine] + [shift(mine, step) for step in range(1, lax.axis_size("tm"))]
+
+
+def joined(held):
+    count = len(held)
+    rows, width = held[0].shape
     me = lax.axis_index("tm")
-    whole_rows = jnp.zeros((count * rows, mine.shape[1]), mine.dtype)
-    for step, held in enumerate([mine] + [shift(mine, step) for step in range(1, count)]):
-        at = lax.rem(me + count - step, count) * rows
-        whole_rows = lax.dynamic_update_slice_in_dim(whole_rows, held, at, axis=0)
-    return whole_rows
+    values = jnp.zeros((count * rows, width), held[0].dtype)
+    for step, piece in enumerate(held):
+        values = lax.dynamic_update_slice_in_dim(values, piece, lax.rem(me + count - step, count) * rows, axis=0)
+    return values
 
 
 def mark(values):
@@ -885,12 +888,11 @@
         clips, 4 * own + extra, "space_grad", small=small_grads,
     )
 
-    ff_sum = lax.psum(ff_part, "tm")
-    (ff_half,), (space_grad,) = together([ff_half], [space_grad])
+    ff_shared = share(ff_half)
+    (space_grad,), (time_part,), ff_shared[1::2] = together([space_grad], [time_part], ff_shared[1::2])
     space_part = reduce_clip(space_grad)
-    ff_sum = share_half(ff_half)
-    (time_part,), (ff_half,) = together([time_part], [ff_half])
-    time_sum = share_half(sum_half(time_part))
+    ff_sum = joined(ff_shared)
+    time_sum = joined(share(sum_half(time_part)))
     early = (
         call_assemble(place, pieces_out),
         columns(time_sum, own, 0, 3),
@@ -899,7 +901,7 @@
         ff_sum[4 * own :].astype(f32),
     )
     space_part, *early = lax.optimization_barrier((space_part,) + early)
-    space_sum = lax.psum(space_part, "tm")
+    space_sum = joined(share(sum_half(space_part)))
     mine = space_sum[4 * own :].reshape(-1)[: small_rows * own].reshape(small_rows, own).astype(f32)
     return (
         early[0],

time: 772 us -> 750 us (0.972)
  waiting for transfers between devices: 184 us -> 136 us
  starting transfers between devices: 76 us -> 90.9 us
    psum x1 -> x0, waiting for transfers between devices: 66 us -> none  [local(): space_sum = lax.psum(space_part, 'tm')]
    ppermute x12 -> x18, starting transfers between devices: 25.7 us -> 40.7 us  [shift(): lax.ppermute(values, 'tm', [(k, (k + step) % count) for k in range(count)])]
    ppermute x12 -> x18, waiting for transfers between devices: 55.6 us -> 69.8 us  [shift(): lax.ppermute(values, 'tm', [(k, (k + step) % count) for k in range(count)])]
  transfers between devices with their start and end apart: 43 -> 48, of which waited for: 11 -> 13; matrix products, arithmetic and copies ran while one was open for 6% -> 6% of each run, Pallas kernels for 55% -> 57%
where the time goes in v5:
time: 750 us; the launch traced here: 737 us
  Pallas kernels  422 us (56%)
  waiting for transfers between devices  136 us (18%)
  starting transfers between devices  90.9 us (12%)
  local copies, waits for them, and re-layouts  37.2 us (5%)
  other arithmetic  25.9 us (3%)
  between operations  15.3 us (2%)
  blocking collectives  9.17 us (1%)
    pallas_call x15, Pallas kernels, ordered_call(): return lambda *operands: call(*behind, *operands)  422 us
    ppermute x18, waiting for transfers between devices, shift(): lax.ppermute(values, 'tm', [(k, (k + step) % count) for k in range(count)])  69.8 us
    ppermute x18, starting transfers between devices, shift(): lax.ppermute(values, 'tm', [(k, (k + step) % count) for k in range(count)])  40.7 us
    ppermute x12, starting transfers between devices, local(): lax.ppermute(parts[d], 'tm', [(k, (k + d) % pieces) for k in range(pieces)])  31.7 us
    all_gather x3, waiting for transfers between devices, gather(): lax.all_gather(jnp.concatenate(parts, axis=0), 'clip', axis=0, tiled=False)  30.5 us
    ppermute x12, waiting for transfers between devices, local(): lax.ppermute(parts[d], 'tm', [(k, (k + d) % pieces) for k in range(pieces)])  22.7 us
    ppermute x12, starting transfers between devices, local(): lax.ppermute(parts[d], 'tm', [(k, (k - d) % pieces) for k in range(pieces)])  18.4 us
  transfers between devices with their start and end apart: 48, of which 13 were waited for; matrix products, arithmetic and copies ran while one was open for 6% of the time, Pallas kernels for 57%

profile of v5, /device:TPU:0, one launch (start us, length us, event | category | flops | bytes accessed | tf_op | source)
XLA Modules:
  0.0 736.6 jit_solution(8807027155016244942)
XLA Ops:
  14.8 4.1 fusion.26
  20.5 3.0 collective-permute-start
  23.5 2.6 collective-permute-start.1
  27.7 9.2 %all-gather.4 = bf16[8,19,128]{2,1,0:T(8,128)(2,1)S(1)} all-gather(bf16[1,19,128]{2,1,0:T(8,128)(2,1)S(1)} %bitcast.126), channel_id=2, replica_groups=mesh['clip'=8,'tm'=4] {'clip'}, dimensions={0}, use_global_device_ids=true | all-gather | bytes 43776 | tf_op jit(solution)/shard_map/all_gather | solution.py:785
  43.0 24.9 %all-gather.9.cloned.1.call-done = bf16[4096,1024]{1,0:T(8,128)(2,1)} async-done(((bf16[512,1024]{1,0:T(8,128)(2,1)}), bf16[4096,1024]{1,0:T(8,128)(2,1)}) %all-gather.9.cloned.1.call-update) | async-done | bytes 8388624 | tf_op jit(solution)/shard_map/all_gather | solution.py:712
  68.0 22.6 %space_forward.2 = (bf16[4,256,1024]{2,1,0:T(8,128)(2,1)}, bf16[4,256,3072]{2,1,0:T(8,128)(2,1)}, bf16[4,256,1024]{2,1,0:T(8,128)(2,1)}, f32[4,16,256]{2,1,0:T(8...) custom-call(s32[1]{0:T(128)} %bitcast.refs_0_.refs_4_.refs_5_, ...), custom_call_target="tpu_custom_call" | custom-call | tf_op jit(solution)/shard_map/space_forward/pallas_call | solution.py:380
  96.2 2.4 collective-permute-start.4
  100.1 22.7 %space_forward.3 = (bf16[4,256,1024]{2,1,0:T(8,128)(2,1)}, bf16[4,256,3072]{2,1,0:T(8,128)(2,1)}, bf16[4,256,1024]{2,1,0:T(8,128)(2,1)}, f32[4,16,256]{2,1,0:T(8...) custom-call(f32[4,16,256]{2,1,0:T(8,128)} %get-tuple-element.122.ref, ...), custom_call_target="tpu_custom_call" | custom-call | tf_op jit(solution)/shard_map/space_forward/pallas_call | solution.py:380
  125.3 2.2 collective-permute-start.8
  129.0 22.3 %collective-permute-done.4.refs_6_.refs_3_ = bf16[4,64,1024]{2,1,0:T(8,128)(2,1)S(1)} collective-permute-done((bf16[4,64,1024]{2,1,0:T(8,128)(2,1)}, bf16[4,64,1024]{2,1,0:T(8,128)(2,1)S(1)}, u32[]{:S(2)}, u32[]{:S(2)}) %collective-permute-start.4) | collective-permute-done | bytes 524320 | tf_op jit(solution)/shard_map/ppermute | solution.py:805
  152.3 21.8 %time_forward.2 = (bf16[4,256,1024]{2,1,0:T(8,128)(2,1)}, bf16[4,256,3072]{2,1,0:T(8,128)(2,1)}, bf16[4,256,1024]{2,1,0:T(8,128)(2,1)}, f32[4,16,256]{2,1,0:T(8,128)}, f32[4,256,1024]{2,1,0:T(8,128)}) custom-call(f32[4,16,256]{2,1,0:T(8,128)} %get-tuple-element.123.refs_0_.refs_15_, bf16[8,128]{1,0:T(8,128)(2,1)} %slice.227.refs_1_, ...), custom_call_target="tpu_custom_call" | custom-call | tf_op jit(solution)/shard_map/time_forward/pallas_call | solution.py:380
  174.4 21.9 %time_forward.3 = (bf16[4,256,1024]{2,1,0:T(8,128)(2,1)}, bf16[4,256,3072]{2,1,0:T(8,128)(2,1)}, bf16[4,256,1024]{2,1,0:T(8,128)(2,1)}, f32[4,16,256]{2,1,0:T(8,128)}, f32[4,256,1024]{2,1,0:T(8,128)}) custom-call(f32[4,16,256]{2,1,0:T(8,128)} %get-tuple-element.128.refs_0_.refs_12_, bf16[4,64,1024]{2,1,0:T(8,128)(2,1)} %get-tuple-element.129.refs_1_, ...), custom_call_target="tpu_custom_call" | custom-call | tf_op jit(solution)/shard_map/time_forward/pallas_call | solution.py:380
  196.4 10.9 %collective-permute-start.10 = (bf16[4,64,1024]{2,1,0:T(8,128)(2,1)}, bf16[4,64,1024]{2,1,0:T(8,128)(2,1)S(1)}, u32[]{:S(2)}, u32[]{:S(2)}) collective-permute-start(bf16[4,64,1024]{2,1,0:T(8,128)(2,1)} %get-tuple-element.140), channel_id=1, source_target_pairs={{0,2},{1,3},{2,0},{3,1},{4,6},{5,7},{6,4},{7,5},{8,10},{9,11},{10,... | collective-permute-start | bytes 1572872 | tf_op jit(solution)/shard_map/ppermute | solution.py:805
  207.9 3.4 collective-permute-start.11
  211.6 5.6 all-gather.13.cloned.1.call-done
  217.2 50.8 %feed_forward.2 = (bf16[4,256,1024]{2,1,0:T(8,128)(2,1)}, bf16[4,256,4096]{2,1,0:T(8,128)(2,1)}, bf16[4,256,4096]{2,1,0:T(8,128)(2,1)}, bf16[4,256,1024]{2,1,0:T...) custom-call(f32[4,16,256]{2,1,0:T(8,128)} %get-tuple-element.133.ref, ...), custom_call_target="tpu_custom_call" | custom-call | tf_op jit(solution)/shard_map/feed_forward/pallas_call | solution.py:380
  268.0 3.4 collective-permute-start.12
  273.5 50.8 %feed_forward.3 = (bf16[4,256,1024]{2,1,0:T(8,128)(2,1)}, bf16[4,256,4096]{2,1,0:T(8,128)(2,1)}, bf16[4,256,4096]{2,1,0:T(8,128)(2,1)}, bf16[4,256,1024]{2,1,0:T...) custom-call(f32[1,1024]{1,0:T(1,128)} %get-tuple-element.136.refs_0_, ...), custom_call_target="tpu_custom_call" | custom-call | tf_op jit(solution)/shard_map/feed_forward/pallas_call | solution.py:380
  324.3 2.8 collective-permute-start.15
  330.2 22.9 %down_grad.1.refs_4_ = bf16[8,1024,1024]{2,1,0:T(8,128)(2,1)} custom-call(f32[1,1024]{1,0:T(1,128)} %get-tuple-element.146.refs_0_, bf16[8,128]{1,0:T(8,128)(2,1)} %slice.232.refs_1_, bf16[8,128]{1,0:T(8,128)(2,1)} %slice.233.refs_2_, bf16[8,128]{1,0:T(8,128)(2,1)} %slice.234.refs_3_, bf16[4,256,4096]{2,1,0:T(8,128)(2,1)} %get-tuple-element.150.refs_4_, ...), custom_call_target="tpu_custom_call" | custom-call | tf_op jit(solution)/shard_map/down_grad/pallas_call | solution.py:380
  353.2 23.3 %hidden_grad.1.refs_0_ = bf16[8,1024,1024]{2,1,0:T(8,128)(2,1)} custom-call(bf16[4,256,1024]{2,1,0:T(8,128)(2,1)} %get-tuple-element.135.refs_0_, bf16[4,256,1024]{2,1,0:T(8,128)(2,1)} %get-tuple-element.143.refs_1_, bf16[4,256,4096]{2,1,0:T(8,128)(2,1)} %get-tuple-element.144.refs_2_, ...), custom_call_target="tpu_custom_call", output_to_operand_aliasing={{}: (4, {})} | custom-call | tf_op jit(solution)/shard_map/hidden_grad/pallas_call | solution.py:380
  376.5 30.0 %time_backward.2 = (bf16[4,256,3072]{2,1,0:T(8,128)(2,1)}, f32[1,1024]{1,0:T(1,128)}, f32[1,1024]{1,0:T(1,128)}, bf16[4,64,1024]{2,1,0:T(8,128)(2,1)}, bf16[4,64...) custom-call(bf16[8,1024,1024]{2,1,0:T(8,128)(2,1)} %hidden_grad.1.refs_0_, ...), custom_call_target="tpu_custom_call" | custom-call | tf_op jit(solution)/shard_map/time_backward/pallas_call | solution.py:380
  406.5 3.8 collective-permute-start.18
  411.2 30.6 %time_backward.3 = (bf16[4,256,3072]{2,1,0:T(8,128)(2,1)}, f32[1,1024]{1,0:T(1,128)}, f32[1,1024]{1,0:T(1,128)}, bf16[4,64,1024]{2,1,0:T(8,128)(2,1)}, bf16[4,64...) custom-call(f32[1,1024]{1,0:T(1,128)} %get-tuple-element.162.refs_0_, ...), custom_call_target="tpu_custom_call" | custom-call | tf_op jit(solution)/shard_map/time_backward/pallas_call | solution.py:380
  441.8 26.0 %time_grad.1.refs_0_ = bf16[8,512,1024]{2,1,0:T(8,128)(2,1)} custom-call(f32[1,1024]{1,0:T(1,128)} %get-tuple-element.166.refs_0_, bf16[4,256,1024]{2,1,0:T(8,128)(2,1)} %get-tuple-element.167.refs_1_, bf16[4,256,1024]{2,1,0:T(8,128)(2,1)} %get-tuple-element.168.refs_2_, bf16[4,256,3072]{2,1,0:T(8,128)(2,1)} %get-tuple-element.169.refs_3_, ...), custom_call_target="tpu_custom_call" | custom-call | tf_op jit(solution)/shard_map/time_grad/pallas_call | solution.py:380
  469.1 3.3 collective-permute-start.21
  474.1 33.5 %space_backward.2 = (bf16[4,256,3072]{2,1,0:T(8,128)(2,1)}, bf16[4,256,1024]{2,1,0:T(8,128)(2,1)}, f32[2,4,256,1024]{3,2,1,0:T(8,128)}, f32[1,1024]{1,0:T(1,128)...) custom-call(bf16[8,512,1024]{2,1,0:T(8,128)(2,1)} %time_grad.1.refs_0_, bf16[4,64,1024]{2,1,0:T(8,128)(2,1)} %get-tuple-element.176.refs_1_, ...), custom_call_target="tpu_custom_call" | custom-call | tf_op jit(solution)/shard_map/space_backward/pallas_call | solution.py:380
  507.7 9.4 %collective-permute-done.22.refs_3_ = bf16[4,64,1024]{2,1,0:T(8,128)(2,1)S(1)} collective-permute-done((bf16[4,64,1024]{2,1,0:T(8,128)(2,1)}, bf16[4,64,1024]{2,1,0:T(8,128)(2,1)S(1)}, u32[]{:S(2)}, u32[]{:S(2)}) %collective-permute-start.22) | collective-permute-done | bytes 524320 | tf_op jit(solution)/shard_map/ppermute | solution.py:808
  518.4 2.5 constant_dynamic-slice_fusion.8
  521.5 3.4 collective-permute-start.26
  524.9 33.4 %space_backward.3 = (bf16[4,256,3072]{2,1,0:T(8,128)(2,1)}, bf16[4,256,1024]{2,1,0:T(8,128)(2,1)}, f32[2,4,256,1024]{3,2,1,0:T(8,128)}, f32[1,1024]{1,0:T(1,128)...) custom-call(bf16[8,128]{1,0:T(8,128)(2,1)} %slice.201.refs_0_, ...), custom_call_target="tpu_custom_call", output_to_operand_aliasing={{2}: (16, {})} | custom-call | tf_op jit(solution)/shard_map/space_backward/pallas_call | solution.py:380
  562.2 2.7 constant_dynamic-update-slice_fusion.12
  564.9 7.4 %collective-permute-start.27 = (bf16[256,1024]{1,0:T(8,128)(2,1)S(1)}, bf16[256,1024]{1,0:T(8,128)(2,1)S(1)}, u32[]{:S(2)}, u32[]{:S(2)}) collective-permute-start(bf16[256,1024]{1,0:T(8,128)(2,1)S(1)} %get-tuple-element.234), channel_id=1, source_target_pairs={{0,1},{1,2},{2,3},{3,0},{4,5},{5,6},{6,7},{7,4},{8,9},{9,10},{10,1... | collective-permute-start | bytes 1572872 | tf_op jit(solution)/shard_map/ppermute | solution.py:721
  575.6 26.5 %space_grad.1 = bf16[8,544,1024]{2,1,0:T(8,128)(2,1)} custom-call(bf16[8,128]{1,0:T(8,128)(2,1)} %slice.235.refs_0_, bf16[4,256,1024]{2,1,0:T(8,128)(2,1)} %get-tuple-element.188.refs_1_, bf16[4,256,1024]{2,1,0:T(8,128)(2,1)} %get-tuple-element.189.refs_2_, bf16[4,256,3072]{2,1,0:T(8,128)(2,1)} %get-tuple-element.190.refs_3_, ...), custom_call_target="tpu_custom_call" | custom-call | tf_op jit(solution)/shard_map/space_grad/pallas_call | solution.py:380
  603.6 5.2 assemble.1
  611.4 3.0 collective-permute-start.31
  616.4 23.4 %collective-permute-done.35 = bf16[256,1024]{1,0:T(8,128)(2,1)} collective-permute-done((bf16[256,1024]{1,0:T(8,128)(2,1)S(1)}, bf16[256,1024]{1,0:T(8,128)(2,1)}, u32[]{:S(2)}, u32[]{:S(2)}) %collective-permute-start.35) | collective-permute-done | bytes 524320 | tf_op jit(solution)/shard_map/ppermute | solution.py:721
  645.7 4.9 collective-permute-start.32
  653.1 2.8 slice_convert_fusion
  655.9 3.2 collective-permute-done.32
  659.1 9.9 %collective-permute-done.33 = bf16[128,1024]{1,0:T(8,128)(2,1)S(1)} collective-permute-done((bf16[128,1024]{1,0:T(8,128)(2,1)S(1)}, bf16[128,1024]{1,0:T(8,128)(2,1)S(1)}, u32[]{:S(2)}, u32[]{:S(2)}) %collective-permute-start.33) | collective-permute-done | bytes 262176 | tf_op jit(solution)/shard_map/ppermute | solution.py:721
  671.3 3.6 reduce-scatter.8.cloned.1.call-done
  676.1 2.5 collective-permute-start.36
  681.4 6.2 collective-permute-done.36
  687.6 10.8 %collective-permute-done.37 = bf16[136,1024]{1,0:T(8,128)(2,1)S(1)} collective-permute-done((bf16[136,1024]{1,0:T(8,128)(2,1)S(1)}, bf16[136,1024]{1,0:T(8,128)(2,1)S(1)}, u32[]{:S(2)}, u32[]{:S(2)}) %collective-permute-start.37) | collective-permute-done | bytes 278560 | tf_op jit(solution)/shard_map/ppermute | solution.py:721
  699.7 6.5 collective-permute-start.39
  708.6 6.2 collective-permute-done.39
  714.8 10.1 %collective-permute-done.40 = bf16[136,1024]{1,0:T(8,128)(2,1)S(1)} collective-permute-done((bf16[136,1024]{1,0:T(8,128)(2,1)S(1)}, bf16[136,1024]{1,0:T(8,128)(2,1)S(1)}, u32[]{:S(2)}, u32[]{:S(2)}) %collective-permute-start.40) | collective-permute-done | bytes 278560 | tf_op jit(solution)/shard_map/ppermute | solution.py:721
  (256 shorter events, 76.9 us)
Async XLA Ops:
  7.2 60.8 %all-gather.9.cloned.1.call-start = ((), (), s32[]{:S(2)}) async-start(), calls=%async_computation.6 | async-start | bytes 9437184 | tf_op jit(solution)/shard_map/all_gather | solution.py:712
  10.5 118.5 %all-gather.11.cloned.1.call-start = ((), (), s32[]{:S(2)}) async-start(), calls=%async_computation.7 | async-start | bytes 9437184 | tf_op jit(solution)/shard_map/all_gather | solution.py:712
  11.7 205.5 %all-gather.13.cloned.1.call-start = ((), (), s32[]{:S(2)}) async-start(), calls=%async_computation.8 | async-start | bytes 18874368 | tf_op jit(solution)/shard_map/all_gather | solution.py:712
  14.7 502.4 %reduce-scatter.4.cloned.1.call-start = ((), (), s32[]{:S(2)}) async-start(), calls=%async_computation.3 | async-start | bytes 18874368 | tf_op jit(solution)/shard_map/reduce_scatter | solution.py:716
  20.5 73.3 %collective-permute-start = (bf16[4,64,1024]{2,1,0:T(8,128)(2,1)}, bf16[4,64,1024]{2,1,0:T(8,128)(2,1)S(1)}, u32[]{:S(2)}, u32[]{:S(2)}) collective-permute-start(bf16[4,64,1024]{2,1,0:T(8,128)(2,1)} %get-tuple-element.253), channel_id=1, source_target_pairs={{0,1},{1,2},{2,3},{3,0},{4,5},{5,6},{6,7},{7,4},{8,9},{9,10},{10,1... | collective-permute-start | bytes 1572872 | tf_op jit(solution)/shard_map/ppermute | solution.py:805
  23.5 70.9 %collective-permute-start.1 = (bf16[4,64,1024]{2,1,0:T(8,128)(2,1)}, bf16[4,64,1024]{2,1,0:T(8,128)(2,1)S(1)}, u32[]{:S(2)}, u32[]{:S(2)}) collective-permute-start(bf16[4,64,1024]{2,1,0:T(8,128)(2,1)} %get-tuple-element.252), channel_id=1, source_target_pairs={{0,2},{1,3},{2,0},{3,1},{4,6},{5,7},{6,4},{7,5},{8,10},{9,11},{10,... | collective-permute-start | bytes 1572872 | tf_op jit(solution)/shard_map/ppermute | solution.py:805
  26.1 68.9 %collective-permute-start.2 = (bf16[4,64,1024]{2,1,0:T(8,128)(2,1)}, bf16[4,64,1024]{2,1,0:T(8,128)(2,1)}, u32[]{:S(2)}, u32[]{:S(2)}) collective-permute-start(bf16[4,64,1024]{2,1,0:T(8,128)(2,1)} %get-tuple-element.251), channel_id=1, source_target_pairs={{0,3},{1,0},{2,1},{3,2},{4,7},{5,4},{6,5},{7,6},{8,11},{9,8},{10,9... | collective-permute-start | bytes 1572872 | tf_op jit(solution)/shard_map/ppermute | solution.py:805
  90.6 34.7 %collective-permute-start.3 = (bf16[4,64,1024]{2,1,0:T(8,128)(2,1)}, bf16[4,64,1024]{2,1,0:T(8,128)(2,1)S(1)}, u32[]{:S(2)}, u32[]{:S(2)}) collective-permute-start(bf16[4,64,1024]{2,1,0:T(8,128)(2,1)} %get-tuple-element.125), channel_id=1, source_target_pairs={{0,1},{1,2},{2,3},{3,0},{4,5},{5,6},{6,7},{7,4},{8,9},{9,10},{10,1... | collective-permute-start | bytes 1572872 | tf_op jit(solution)/shard_map/ppermute | solution.py:805
  96.2 55.1 %collective-permute-start.4 = (bf16[4,64,1024]{2,1,0:T(8,128)(2,1)}, bf16[4,64,1024]{2,1,0:T(8,128)(2,1)S(1)}, u32[]{:S(2)}, u32[]{:S(2)}) collective-permute-start(bf16[4,64,1024]{2,1,0:T(8,128)(2,1)} %get-tuple-element.126), channel_id=1, source_target_pairs={{0,2},{1,3},{2,0},{3,1},{4,6},{5,7},{6,4},{7,5},{8,10},{9,11},{10,... | collective-permute-start | bytes 1572872 | tf_op jit(solution)/shard_map/ppermute | solution.py:805
  98.7 52.6 %collective-permute-start.5 = (bf16[4,64,1024]{2,1,0:T(8,128)(2,1)}, bf16[4,64,1024]{2,1,0:T(8,128)(2,1)S(1)}, u32[]{:S(2)}, u32[]{:S(2)}) collective-permute-start(bf16[4,64,1024]{2,1,0:T(8,128)(2,1)} %get-tuple-element.127), channel_id=1, source_target_pairs={{0,3},{1,0},{2,1},{3,2},{4,7},{5,4},{6,5},{7,6},{8,11},{9,8},{10,9... | collective-permute-start | bytes 1572872 | tf_op jit(solution)/shard_map/ppermute | solution.py:805
  122.8 51.3 %collective-permute-start.6 = (bf16[4,64,1024]{2,1,0:T(8,128)(2,1)}, bf16[4,64,1024]{2,1,0:T(8,128)(2,1)}, u32[]{:S(2)}, u32[]{:S(2)}) collective-permute-start(bf16[4,64,1024]{2,1,0:T(8,128)(2,1)} %get-tuple-element.130), channel_id=1, source_target_pairs={{0,1},{1,2},{2,3},{3,0},{4,5},{5,6},{6,7},{7,4},{8,9},{9,10},{10,1... | collective-permute-start | bytes 1572872 | tf_op jit(solution)/shard_map/ppermute | solution.py:805
  123.5 51.0 %collective-permute-start.7 = (bf16[4,64,1024]{2,1,0:T(8,128)(2,1)}, bf16[4,64,1024]{2,1,0:T(8,128)(2,1)}, u32[]{:S(2)}, u32[]{:S(2)}) collective-permute-start(bf16[4,64,1024]{2,1,0:T(8,128)(2,1)} %get-tuple-element.131), channel_id=1, source_target_pairs={{0,2},{1,3},{2,0},{3,1},{4,6},{5,7},{6,4},{7,5},{8,10},{9,11},{10,... | collective-permute-start | bytes 1572872 | tf_op jit(solution)/shard_map/ppermute | solution.py:805
  125.3 49.1 %collective-permute-start.8 = (bf16[4,64,1024]{2,1,0:T(8,128)(2,1)}, bf16[4,64,1024]{2,1,0:T(8,128)(2,1)}, u32[]{:S(2)}, u32[]{:S(2)}) collective-permute-start(bf16[4,64,1024]{2,1,0:T(8,128)(2,1)} %get-tuple-element.132), channel_id=1, source_target_pairs={{0,3},{1,0},{2,1},{3,2},{4,7},{5,4},{6,5},{7,6},{8,11},{9,8},{10,9... | collective-permute-start | bytes 1572872 | tf_op jit(solution)/shard_map/ppermute | solution.py:805
  196.4 75.0 %collective-permute-start.10 = (bf16[4,64,1024]{2,1,0:T(8,128)(2,1)}, bf16[4,64,1024]{2,1,0:T(8,128)(2,1)S(1)}, u32[]{:S(2)}, u32[]{:S(2)}) collective-permute-start(bf16[4,64,1024]{2,1,0:T(8,128)(2,1)} %get-tuple-element.140), channel_id=1, source_target_pairs={{0,2},{1,3},{2,0},{3,1},{4,6},{5,7},{6,4},{7,5},{8,10},{9,11},{10,... | collective-permute-start | bytes 1572872 | tf_op jit(solution)/shard_map/ppermute | solution.py:805
  207.9 65.6 %collective-permute-start.11 = (bf16[4,64,1024]{2,1,0:T(8,128)(2,1)}, bf16[4,64,1024]{2,1,0:T(8,128)(2,1)}, u32[]{:S(2)}, u32[]{:S(2)}) collective-permute-start(bf16[4,64,1024]{2,1,0:T(8,128)(2,1)} %get-tuple-element.141), channel_id=1, source_target_pairs={{0,3},{1,0},{2,1},{3,2},{4,7},{5,4},{6,5},{7,6},{8,11},{9,8},{10,9... | collective-permute-start | bytes 1572872 | tf_op jit(solution)/shard_map/ppermute | solution.py:805
  211.2 62.2 %collective-permute-start.9 = (bf16[4,64,1024]{2,1,0:T(8,128)(2,1)}, bf16[4,64,1024]{2,1,0:T(8,128)(2,1)}, u32[]{:S(2)}, u32[]{:S(2)}) collective-permute-start(bf16[4,64,1024]{2,1,0:T(8,128)(2,1)} %get-tuple-element.139), channel_id=1, source_target_pairs={{0,1},{1,2},{2,3},{3,0},{4,5},{5,6},{6,7},{7,4},{8,9},{9,10},{10,1... | collective-permute-start | bytes 1572872 | tf_op jit(solution)/shard_map/ppermute | solution.py:805
  268.0 60.2 %collective-permute-start.12 = (bf16[4,64,1024]{2,1,0:T(8,128)(2,1)}, bf16[4,64,1024]{2,1,0:T(8,128)(2,1)S(1)}, u32[]{:S(2)}, u32[]{:S(2)}) collective-permute-start(bf16[4,64,1024]{2,1,0:T(8,128)(2,1)} %get-tuple-element.147), channel_id=1, source_target_pairs={{0,3},{1,0},{2,1},{3,2},{4,7},{5,4},{6,5},{7,6},{8,11},{9,8},{10,9... | collective-permute-start | bytes 1572872 | tf_op jit(solution)/shard_map/ppermute | solution.py:808
  271.4 57.6 %collective-permute-start.13 = (bf16[4,64,1024]{2,1,0:T(8,128)(2,1)}, bf16[4,64,1024]{2,1,0:T(8,128)(2,1)S(1)}, u32[]{:S(2)}, u32[]{:S(2)}) collective-permute-start(bf16[4,64,1024]{2,1,0:T(8,128)(2,1)} %get-tuple-element.148), channel_id=1, source_target_pairs={{0,2},{1,3},{2,0},{3,1},{4,6},{5,7},{6,4},{7,5},{8,10},{9,11},{10,... | collective-permute-start | bytes 1572872 | tf_op jit(solution)/shard_map/ppermute | solution.py:808
  272.2 57.4 %collective-permute-start.14 = (bf16[4,64,1024]{2,1,0:T(8,128)(2,1)}, bf16[4,64,1024]{2,1,0:T(8,128)(2,1)S(1)}, u32[]{:S(2)}, u32[]{:S(2)}) collective-permute-start(bf16[4,64,1024]{2,1,0:T(8,128)(2,1)} %get-tuple-element.149), channel_id=1, source_target_pairs={{0,1},{1,2},{2,3},{3,0},{4,5},{5,6},{6,7},{7,4},{8,9},{9,10},{10,1... | collective-permute-start | bytes 1572872 | tf_op jit(solution)/shard_map/ppermute | solution.py:808
  324.3 52.2 %collective-permute-start.15 = (bf16[4,64,1024]{2,1,0:T(8,128)(2,1)}, bf16[4,64,1024]{2,1,0:T(8,128)(2,1)}, u32[]{:S(2)}, u32[]{:S(2)}) collective-permute-start(bf16[4,64,1024]{2,1,0:T(8,128)(2,1)} %get-tuple-element.155), channel_id=1, source_target_pairs={{0,3},{1,0},{2,1},{3,2},{4,7},{5,4},{6,5},{7,6},{8,11},{9,8},{10,9... | collective-permute-start | bytes 1572872 | tf_op jit(solution)/shard_map/ppermute | solution.py:808
  327.1 49.4 %collective-permute-start.16 = (bf16[4,64,1024]{2,1,0:T(8,128)(2,1)}, bf16[4,64,1024]{2,1,0:T(8,128)(2,1)}, u32[]{:S(2)}, u32[]{:S(2)}) collective-permute-start(bf16[4,64,1024]{2,1,0:T(8,128)(2,1)} %get-tuple-element.156), channel_id=1, source_target_pairs={{0,2},{1,3},{2,0},{3,1},{4,6},{5,7},{6,4},{7,5},{8,10},{9,11},{10,... | collective-permute-start | bytes 1572872 | tf_op jit(solution)/shard_map/ppermute | solution.py:808
  328.2 48.3 %collective-permute-start.17 = (bf16[4,64,1024]{2,1,0:T(8,128)(2,1)}, bf16[4,64,1024]{2,1,0:T(8,128)(2,1)}, u32[]{:S(2)}, u32[]{:S(2)}) collective-permute-start(bf16[4,64,1024]{2,1,0:T(8,128)(2,1)} %get-tuple-element.157), channel_id=1, source_target_pairs={{0,1},{1,2},{2,3},{3,0},{4,5},{5,6},{6,7},{7,4},{8,9},{9,10},{10,1... | collective-permute-start | bytes 1572872 | tf_op jit(solution)/shard_map/ppermute | solution.py:808
  376.5 225.7 %reduce-scatter.6.cloned.1.call-start = ((), (), s32[]{:S(2)}) async-start(), calls=%async_computation.4 | async-start | bytes 9437184 | tf_op jit(solution)/shard_map/reduce_scatter | solution.py:716
  406.5 61.3 %collective-permute-start.18 = (bf16[4,64,1024]{2,1,0:T(8,128)(2,1)}, bf16[4,64,1024]{2,1,0:T(8,128)(2,1)S(1)}, u32[]{:S(2)}, u32[]{:S(2)}) collective-permute-start(bf16[4,64,1024]{2,1,0:T(8,128)(2,1)} %get-tuple-element.172), channel_id=1, source_target_pairs={{0,3},{1,0},{2,1},{3,2},{4,7},{5,4},{6,5},{7,6},{8,11},{9,8},{10,9... | collective-permute-start | bytes 1572872 | tf_op jit(solution)/shard_map/ppermute | solution.py:808
  410.3 57.5 %collective-permute-start.19 = (bf16[4,64,1024]{2,1,0:T(8,128)(2,1)}, bf16[4,64,1024]{2,1,0:T(8,128)(2,1)S(1)}, u32[]{:S(2)}, u32[]{:S(2)}) collective-permute-start(bf16[4,64,1024]{2,1,0:T(8,128)(2,1)} %get-tuple-element.173), channel_id=1, source_target_pairs={{0,2},{1,3},{2,0},{3,1},{4,6},{5,7},{6,4},{7,5},{8,10},{9,11},{10,... | collective-permute-start | bytes 1572872 | tf_op jit(solution)/shard_map/ppermute | solution.py:808
  410.3 57.5 %collective-permute-start.20 = (bf16[4,64,1024]{2,1,0:T(8,128)(2,1)}, bf16[4,64,1024]{2,1,0:T(8,128)(2,1)S(1)}, u32[]{:S(2)}, u32[]{:S(2)}) collective-permute-start(bf16[4,64,1024]{2,1,0:T(8,128)(2,1)} %get-tuple-element.174), channel_id=1, source_target_pairs={{0,1},{1,2},{2,3},{3,0},{4,5},{5,6},{6,7},{7,4},{8,9},{9,10},{10,1... | collective-permute-start | bytes 1572872 | tf_op jit(solution)/shard_map/ppermute | solution.py:808
  469.0 205.9 %reduce-scatter.8.cloned.1.call-start = ((), (), s32[]{:S(2)}) async-start(), calls=%async_computation.5 | async-start | bytes 10027008 | tf_op jit(solution)/shard_map/reduce_scatter | solution.py:716
  469.1 38.5 %collective-permute-start.21 = (bf16[4,64,1024]{2,1,0:T(8,128)(2,1)}, bf16[4,64,1024]{2,1,0:T(8,128)(2,1)S(1)}, u32[]{:S(2)}, u32[]{:S(2)}) collective-permute-start(bf16[4,64,1024]{2,1,0:T(8,128)(2,1)} %get-tuple-element.184), channel_id=1, source_target_pairs={{0,3},{1,0},{2,1},{3,2},{4,7},{5,4},{6,5},{7,6},{8,11},{9,8},{10,9... | collective-permute-start | bytes 1572872 | tf_op jit(solution)/shard_map/ppermute | solution.py:808
  472.4 44.6 %collective-permute-start.22 = (bf16[4,64,1024]{2,1,0:T(8,128)(2,1)}, bf16[4,64,1024]{2,1,0:T(8,128)(2,1)S(1)}, u32[]{:S(2)}, u32[]{:S(2)}) collective-permute-start(bf16[4,64,1024]{2,1,0:T(8,128)(2,1)} %get-tuple-element.185), channel_id=1, source_target_pairs={{0,2},{1,3},{2,0},{3,1},{4,6},{5,7},{6,4},{7,5},{8,10},{9,11},{10,... | collective-permute-start | bytes 1572872 | tf_op jit(solution)/shard_map/ppermute | solution.py:808
  473.6 43.5 %collective-permute-start.23 = (bf16[4,64,1024]{2,1,0:T(8,128)(2,1)}, bf16[4,64,1024]{2,1,0:T(8,128)(2,1)S(1)}, u32[]{:S(2)}, u32[]{:S(2)}) collective-permute-start(bf16[4,64,1024]{2,1,0:T(8,128)(2,1)} %get-tuple-element.186), channel_id=1, source_target_pairs={{0,1},{1,2},{2,3},{3,0},{4,5},{5,6},{6,7},{7,4},{8,9},{9,10},{10,1... | collective-permute-start | bytes 1572872 | tf_op jit(solution)/shard_map/ppermute | solution.py:808
  520.9 39.6 %collective-permute-start.24 = (bf16[256,1024]{1,0:T(8,128)(2,1)}, bf16[256,1024]{1,0:T(8,128)(2,1)}, u32[]{:S(2)}, u32[]{:S(2)}) collective-permute-start(bf16[256,1024]{1,0:T(8,128)(2,1)} %get-tuple-element.243), channel_id=1, source_target_pairs={{0,1},{1,2},{2,3},{3,0},{4,5},{5,6},{6,7},{7,4},{8,9},{9,10},{10,1... | collective-permute-start | bytes 1572872 | tf_op jit(solution)/shard_map/ppermute | solution.py:721
  520.9 39.6 %collective-permute-start.25 = (bf16[256,1024]{1,0:T(8,128)(2,1)}, bf16[256,1024]{1,0:T(8,128)(2,1)}, u32[]{:S(2)}, u32[]{:S(2)}) collective-permute-start(bf16[256,1024]{1,0:T(8,128)(2,1)} %get-tuple-element.245), channel_id=1, source_target_pairs={{0,2},{1,3},{2,0},{3,1},{4,6},{5,7},{6,4},{7,5},{8,10},{9,11},{10,... | collective-permute-start | bytes 1572872 | tf_op jit(solution)/shard_map/ppermute | solution.py:721
  521.5 39.1 %collective-permute-start.26 = (bf16[256,1024]{1,0:T(8,128)(2,1)}, bf16[256,1024]{1,0:T(8,128)(2,1)}, u32[]{:S(2)}, u32[]{:S(2)}) collective-permute-start(bf16[256,1024]{1,0:T(8,128)(2,1)} %get-tuple-element.244), channel_id=1, source_target_pairs={{0,3},{1,0},{2,1},{3,2},{4,7},{5,4},{6,5},{7,6},{8,11},{9,8},{10,9... | collective-permute-start | bytes 1572872 | tf_op jit(solution)/shard_map/ppermute | solution.py:721
  564.9 37.3 %collective-permute-start.27 = (bf16[256,1024]{1,0:T(8,128)(2,1)S(1)}, bf16[256,1024]{1,0:T(8,128)(2,1)S(1)}, u32[]{:S(2)}, u32[]{:S(2)}) collective-permute-start(bf16[256,1024]{1,0:T(8,128)(2,1)S(1)} %get-tuple-element.234), channel_id=1, source_target_pairs={{0,1},{1,2},{2,3},{3,0},{4,5},{5,6},{6,7},{7,4},{8,9},{9,10},{10,1... | collective-permute-start | bytes 1572872 | tf_op jit(solution)/shard_map/ppermute | solution.py:721
  572.3 29.8 %collective-permute-start.28 = (bf16[256,1024]{1,0:T(8,128)(2,1)S(1)}, bf16[256,1024]{1,0:T(8,128)(2,1)S(1)}, u32[]{:S(2)}, u32[]{:S(2)}) collective-permute-start(bf16[256,1024]{1,0:T(8,128)(2,1)S(1)} %get-tuple-element.234), channel_id=1, source_target_pairs={{0,3},{1,0},{2,1},{3,2},{4,7},{5,4},{6,5},{7,6},{8,11},{9,8},{10,9... | collective-permute-start | bytes 1572872 | tf_op jit(solution)/shard_map/ppermute | solution.py:721
  603.0 36.8 %collective-permute-start.35 = (bf16[256,1024]{1,0:T(8,128)(2,1)S(1)}, bf16[256,1024]{1,0:T(8,128)(2,1)}, u32[]{:S(2)}, u32[]{:S(2)}) collective-permute-start(bf16[256,1024]{1,0:T(8,128)(2,1)S(1)} %get-tuple-element.234), channel_id=1, source_target_pairs={{0,2},{1,3},{2,0},{3,1},{4,6},{5,7},{6,4},{7,5},{8,10},{9,11},{10,... | collective-permute-start | bytes 1572872 | tf_op jit(solution)/shard_map/ppermute | solution.py:721
  608.9 36.6 %collective-permute-start.29 = (bf16[128,1024]{1,0:T(8,128)(2,1)S(1)}, bf16[128,1024]{1,0:T(8,128)(2,1)S(1)}, u32[]{:S(2)}, u32[]{:S(2)}) collective-permute-start(bf16[128,1024]{1,0:T(8,128)(2,1)S(1)} %get-tuple-element.265), channel_id=1, source_target_pairs={{0,1},{1,2},{2,3},{3,0},{4,5},{5,6},{6,7},{7,4},{8,9},{9,10},{10,1... | collective-permute-start | bytes 786440 | tf_op jit(solution)/shard_map/ppermute | solution.py:721
  610.9 34.5 %collective-permute-start.30 = (bf16[128,1024]{1,0:T(8,128)(2,1)S(1)}, bf16[128,1024]{1,0:T(8,128)(2,1)S(1)}, u32[]{:S(2)}, u32[]{:S(2)}) collective-permute-start(bf16[128,1024]{1,0:T(8,128)(2,1)S(1)} %get-tuple-element.267), channel_id=1, source_target_pairs={{0,2},{1,3},{2,0},{3,1},{4,6},{5,7},{6,4},{7,5},{8,10},{9,11},{10,... | collective-permute-start | bytes 786440 | tf_op jit(solution)/shard_map/ppermute | solution.py:721
  611.4 34.1 %collective-permute-start.31 = (bf16[128,1024]{1,0:T(8,128)(2,1)S(1)}, bf16[128,1024]{1,0:T(8,128)(2,1)S(1)}, u32[]{:S(2)}, u32[]{:S(2)}) collective-permute-start(bf16[128,1024]{1,0:T(8,128)(2,1)S(1)} %get-tuple-element.266), channel_id=1, source_target_pairs={{0,3},{1,0},{2,1},{3,2},{4,7},{5,4},{6,5},{7,6},{8,11},{9,8},{10,9... | collective-permute-start | bytes 786440 | tf_op jit(solution)/shard_map/ppermute | solution.py:721
  645.7 13.4 %collective-permute-start.32 = (bf16[128,1024]{1,0:T(8,128)(2,1)S(1)}, bf16[128,1024]{1,0:T(8,128)(2,1)S(1)}, u32[]{:S(2)}, u32[]{:S(2)}) collective-permute-start(bf16[128,1024]{1,0:T(8,128)(2,1)S(1)} %get-tuple-element.236), channel_id=1, source_target_pairs={{0,1},{1,2},{2,3},{3,0},{4,5},{5,6},{6,7},{7,4},{8,9},{9,10},{10,1... | collective-permute-start | bytes 786440 | tf_op jit(solution)/shard_map/ppermute | solution.py:721
  650.6 18.4 %collective-permute-start.33 = (bf16[128,1024]{1,0:T(8,128)(2,1)S(1)}, bf16[128,1024]{1,0:T(8,128)(2,1)S(1)}, u32[]{:S(2)}, u32[]{:S(2)}) collective-permute-start(bf16[128,1024]{1,0:T(8,128)(2,1)S(1)} %get-tuple-element.236), channel_id=1, source_target_pairs={{0,2},{1,3},{2,0},{3,1},{4,6},{5,7},{6,4},{7,5},{8,10},{9,11},{10,... | collective-permute-start | bytes 786440 | tf_op jit(solution)/shard_map/ppermute | solution.py:721
  652.3 16.7 %collective-permute-start.34 = (bf16[128,1024]{1,0:T(8,128)(2,1)S(1)}, bf16[128,1024]{1,0:T(8,128)(2,1)S(1)}, u32[]{:S(2)}, u32[]{:S(2)}) collective-permute-start(bf16[128,1024]{1,0:T(8,128)(2,1)S(1)} %get-tuple-element.236), channel_id=1, source_target_pairs={{0,3},{1,0},{2,1},{3,2},{4,7},{5,4},{6,5},{7,6},{8,11},{9,8},{10,9... | collective-permute-start | bytes 786440 | tf_op jit(solution)/shard_map/ppermute | solution.py:721
  676.1 11.5 %collective-permute-start.36 = (bf16[136,1024]{1,0:T(8,128)(2,1)S(1)}, bf16[136,1024]{1,0:T(8,128)(2,1)S(1)}, u32[]{:S(2)}, u32[]{:S(2)}) collective-permute-start(bf16[136,1024]{1,0:T(8,128)(2,1)S(1)} %get-tuple-element.258), channel_id=1, source_target_pairs={{0,1},{1,2},{2,3},{3,0},{4,5},{5,6},{6,7},{7,4},{8,9},{9,10},{10,1... | collective-permute-start | bytes 835592 | tf_op jit(solution)/shard_map/ppermute | solution.py:721
  678.6 19.8 %collective-permute-start.37 = (bf16[136,1024]{1,0:T(8,128)(2,1)S(1)}, bf16[136,1024]{1,0:T(8,128)(2,1)S(1)}, u32[]{:S(2)}, u32[]{:S(2)}) collective-permute-start(bf16[136,1024]{1,0:T(8,128)(2,1)S(1)} %get-tuple-element.260), channel_id=1, source_target_pairs={{0,2},{1,3},{2,0},{3,1},{4,6},{5,7},{6,4},{7,5},{8,10},{9,11},{10,... | collective-permute-start | bytes 835592 | tf_op jit(solution)/shard_map/ppermute | solution.py:721
  680.0 18.4 %collective-permute-start.38 = (bf16[136,1024]{1,0:T(8,128)(2,1)S(1)}, bf16[136,1024]{1,0:T(8,128)(2,1)S(1)}, u32[]{:S(2)}, u32[]{:S(2)}) collective-permute-start(bf16[136,1024]{1,0:T(8,128)(2,1)S(1)} %get-tuple-element.259), channel_id=1, source_target_pairs={{0,3},{1,0},{2,1},{3,2},{4,7},{5,4},{6,5},{7,6},{8,11},{9,8},{10,9... | collective-permute-start | bytes 835592 | tf_op jit(solution)/shard_map/ppermute | solution.py:721
  699.7 15.1 %collective-permute-start.39 = (bf16[136,1024]{1,0:T(8,128)(2,1)S(1)}, bf16[136,1024]{1,0:T(8,128)(2,1)S(1)}, u32[]{:S(2)}, u32[]{:S(2)}) collective-permute-start(bf16[136,1024]{1,0:T(8,128)(2,1)S(1)} %get-tuple-element.232), channel_id=1, source_target_pairs={{0,1},{1,2},{2,3},{3,0},{4,5},{5,6},{6,7},{7,4},{8,9},{9,10},{10,1... | collective-permute-start | bytes 835592 | tf_op jit(solution)/shard_map/ppermute | solution.py:721
  706.2 18.7 %collective-permute-start.40 = (bf16[136,1024]{1,0:T(8,128)(2,1)S(1)}, bf16[136,1024]{1,0:T(8,128)(2,1)S(1)}, u32[]{:S(2)}, u32[]{:S(2)}) collective-permute-start(bf16[136,1024]{1,0:T(8,128)(2,1)S(1)} %get-tuple-element.232), channel_id=1, source_target_pairs={{0,2},{1,3},{2,0},{3,1},{4,6},{5,7},{6,4},{7,5},{8,10},{9,11},{10,... | collective-permute-start | bytes 835592 | tf_op jit(solution)/shard_map/ppermute | solution.py:721
  707.6 17.3 %collective-permute-start.41 = (bf16[136,1024]{1,0:T(8,128)(2,1)S(1)}, bf16[136,1024]{1,0:T(8,128)(2,1)S(1)}, u32[]{:S(2)}, u32[]{:S(2)}) collective-permute-start(bf16[136,1024]{1,0:T(8,128)(2,1)S(1)} %get-tuple-element.232), channel_id=1, source_target_pairs={{0,3},{1,0},{2,1},{3,2},{4,7},{5,4},{6,5},{7,6},{8,11},{9,8},{10,9... | collective-permute-start | bytes 835592 | tf_op jit(solution)/shard_map/ppermute | solution.py:721
  (45 other events, 401.9 us)
Sparse Core Ops, SparseCore 0:
  10.7 57.2 all-gather.8
  70.4 54.3 all-gather.10
  127.3 89.8 all-gather.12
  376.6 116.4 reduce-scatter.3
  496.4 71.2 reduce-scatter.5
  602.3 72.5 reduce-scatter.7

commit v6 on v5

--- a/solution.py
+++ b/solution.py
@@ -12,6 +12,7 @@
 EPS = 1e-05
 MASKED = -1e30
 ROWS = 256
+RAISED = (HEADS // 2, ROWS, 2 * ROWS)
 FF_CHUNK = 1024
 FF_GROUPS = 1
 VMEM_LIMIT = 62 * 1024 * 1024
@@ -62,7 +63,7 @@
     return slice(lane, lane + 128), slice(1024 + lane, 1024 + lane + 128), slice(2048 + lane, 2048 + lane + 128)
 
 
-def attend(qkv_ref, key_mask, query_mask, mixed_t, lse_ref):
+def attend(qkv_ref, key_mask, query_mask, mixed_t, raised_ref, rate_ref):
     blank = jnp.zeros((HEAD, ROWS), bf16)
     scale = jnp.asarray(HEAD**-0.5, bf16)
 
@@ -80,14 +81,14 @@
         raised = jnp.exp(scores - top)
         total = jnp.sum(raised, axis=0, keepdims=True)
         weights = raised.astype(bf16)
-        lse = top + jnp.log(total)
         rate = 1.0 / total
+        raised_ref[pair] = weights
         for part in range(2):
             head = pair * 2 + part
             at = slice(part * ROWS, (part + 1) * ROWS)
             mixed = dot(v_t[part * HEAD : (part + 1) * HEAD], weights[:, at])
             mixed_t[head * HEAD : (head + 1) * HEAD, :] = (mixed * rate[:, at]).astype(bf16)
-            lse_ref[head : head + 1, :] = lse[:, at]
+            rate_ref[head : head + 1, :] = rate[:, at]
 
     queue = [scores_of(0), scores_of(1)]
     for pair in range(HEADS // 2):
@@ -96,36 +97,32 @@
         finish(pair, queue.pop(0))
 
 
-def attend_back(qkv_ref, key_mask, query_mask, lse_ref, grad_ref, grad_t, mixed_t, out_ref, query_t):
+def attend_back(qkv_ref, raised_ref, rate_ref, grad_ref, grad_t, mixed_t, out_ref, query_t):
     blank = jnp.zeros((HEAD, ROWS), bf16)
     scale = jnp.asarray(HEAD**-0.5, bf16)
     low_half = lax.broadcasted_iota(jnp.int32, (ROWS, 128), 1) < HEAD
     zero = jnp.zeros((ROWS, 128), bf16)
 
-    def both(top, bottom, extra):
-        first = jnp.concatenate([top, blank] + extra, axis=0)
-        second = jnp.concatenate([blank, bottom] + extra, axis=0)
+    def both(top, bottom):
+        first = jnp.concatenate([top, blank], axis=0)
+        second = jnp.concatenate([blank, bottom], axis=0)
         return jnp.concatenate([first, second], axis=1)
 
     def halves(values):
         return jnp.concatenate([jnp.where(low_half, values, zero), jnp.where(low_half, zero, values)], axis=0)
 
     def start(pair):
-        q_at, k_at, v_at = pair_slices(pair)
-        q_t = (qkv_ref[:, q_at] * scale).T
-        keys = jnp.concatenate([qkv_ref[:, k_at], key_mask], axis=1)
-        scores = dot(keys, both(q_t[:HEAD], q_t[HEAD:], [query_mask]))
+        q_at, _, v_at = pair_slices(pair)
         pair_t = grad_t[q_at, :]
-        grad_probs = dot(qkv_ref[:, v_at], both(pair_t[:HEAD], pair_t[HEAD:], []))
-        return scores, grad_probs
-
-    def finish(pair, scores, grad_probs):
+        return dot(qkv_ref[:, v_at], both(pair_t[:HEAD], pair_t[HEAD:]))
+
+    def finish(pair, grad_probs):
         q_at, k_at, v_at = pair_slices(pair)
         head = pair * 2
-        lse = jnp.concatenate([lse_ref[head : head + 1, :], lse_ref[head + 1 : head + 2, :]], axis=1)
+        rate = jnp.concatenate([rate_ref[head : head + 1, :], rate_ref[head + 1 : head + 2, :]], axis=1)
         product = grad_t[q_at, :].astype(f32) * mixed_t[q_at, :].astype(f32)
         along = jnp.concatenate([column_sum(product[:HEAD]), column_sum(product[HEAD:])], axis=1)
-        probs = jnp.exp(scores - lse)
+        probs = raised_ref[pair].astype(f32) * rate
         grad_scores = (probs * (grad_probs - along)).astype(bf16)
         out_ref[:, v_at] = dot(probs.astype(bf16), halves(grad_ref[:, q_at])).astype(bf16)
         out_ref[:, k_at] = dot(grad_scores, halves(qkv_ref[:, q_at] * scale)).astype(bf16)
@@ -140,7 +137,7 @@
         held = ahead
         if pair + 1 < HEADS // 2:
             ahead = start(pair + 1)
-        finish(pair, *held)
+        finish(pair, held)
     for quarter in range(4):
         at = slice(quarter * 256, (quarter + 1) * 256)
         out_ref[:, at] = query_t[at, :].T
@@ -173,7 +170,7 @@
 
 def space_forward(
     place, tok, hot, kmask, qmask, gain, bias, table, weights,
-    norm_out, qkv_out, mix_out, lse_out, *rest,
+    norm_out, qkv_out, mix_out, lse_out, raised_out, *rest,
 ):
     after_out, (mixed_t, after) = rest[:-2], rest[-2:]
     embedded = tok[...].astype(f32) + dot(hot[...], table[...])
@@ -182,7 +179,7 @@
     norm_out[...] = normed
     for part in range(3):
         qkv_out[:, part * 1024 : (part + 1) * 1024] = dot(normed, block_of(weights, part)).astype(bf16)
-    attend(qkv_out, kmask[...], qmask[...], mixed_t, lse_out)
+    attend(qkv_out, kmask[...], qmask[...], mixed_t, raised_out, lse_out)
     mixed = mixed_t[...].T
     mix_out[...] = mixed
     after[...] = (embedded + dot(mixed, block_of(weights, 3))).astype(bf16)
@@ -202,7 +199,7 @@
 def space_backward(count, *refs):
     grads, refs = refs[:count], refs[count:]
     (
-        place, tok, hot, kmask, qmask, gain, table, weights, qkv, mix, lse,
+        place, tok, hot, raised, gain, table, weights, qkv, mix, lse,
         gqkv_out, gas_out, tok_out, gain_out, bias_out, table_out, grad_t, mixed_t, query_t, grad_rows,
     ) = refs
     first = pl.program_id(0) == 0
@@ -212,7 +209,7 @@
     mixed_t[...] = mix[...].T
     grad_rows[...] = dot(upstream, block_of(weights, 3), NT).astype(bf16)
     grad_t[...] = grad_rows[...].T
-    attend_back(qkv, kmask[...], qmask[...], lse, grad_rows, grad_t, mixed_t, gqkv_out, query_t)
+    attend_back(qkv, raised, lse, grad_rows, grad_t, mixed_t, gqkv_out, query_t)
     grad_norm = grad_into_norm(gqkv_out, weights)
     embedded = tok[...].astype(f32) + dot(hot[...], table[...])
     hat, rate = standardize(embedded)
@@ -225,14 +222,14 @@
 
 def time_forward(count, *refs):
     x, refs = refs[:count], refs[count:]
-    kmask, qmask, gain, bias, weights, norm_out, qkv_out, mix_out, lse_out, after_out, mixed_t = refs
+    kmask, qmask, gain, bias, weights, norm_out, qkv_out, mix_out, lse_out, raised_out, after_out, mixed_t = refs
     after_space = stacked(x).astype(f32)
     hat, _ = standardize(after_space)
     normed = (hat * gain[1:2, :] + bias[1:2, :]).astype(bf16)
     norm_out[...] = normed
     for part in range(3):
         qkv_out[:, part * 1024 : (part + 1) * 1024] = dot(normed, block_of(weights, part)).astype(bf16)
-    attend(qkv_out, kmask[...], qmask[...], mixed_t, lse_out)
+    attend(qkv_out, kmask[...], qmask[...], mixed_t, raised_out, lse_out)
     mixed = mixed_t[...].T
     mix_out[...] = mixed
     after_out[...] = after_space + dot(mixed, block_of(weights, 3))
@@ -307,15 +304,15 @@
 
 def time_backward(count, *refs):
     x, refs = refs[:count], refs[count:]
-    gat, kmask, qmask, gain, weights, qkv, mix, lse, gqkv_out, gain_out, bias_out = refs[:11]
-    gas_out = refs[11 : 11 + count]
-    grad_t, mixed_t, query_t, grad_rows = refs[11 + count :]
+    gat, raised, gain, weights, qkv, mix, lse, gqkv_out, gain_out, bias_out = refs[:10]
+    gas_out = refs[10 : 10 + count]
+    grad_t, mixed_t, query_t, grad_rows = refs[10 + count :]
     first = pl.program_id(0) == 0
     upstream = gat[...]
     mixed_t[...] = mix[...].T
     grad_rows[...] = dot(upstream, block_of(weights, 3), NT).astype(bf16)
     grad_t[...] = grad_rows[...].T
-    attend_back(qkv, kmask[...], qmask[...], lse, grad_rows, grad_t, mixed_t, gqkv_out, query_t)
+    attend_back(qkv, raised, lse, grad_rows, grad_t, mixed_t, gqkv_out, query_t)
     grad_norm = grad_into_norm(gqkv_out, weights)
     hat, rate = standardize(stacked(x).astype(f32))
     add_row(gain_out, column_sum(grad_norm * hat), first)
@@ -419,12 +416,13 @@
         + [whole(a.shape) for a in (kmask, qmask, gain, bias, table, weights)],
         out_specs=[
             step_spec((slots, width)), step_spec((slots, 3 * width)), step_spec((slots, width)),
-            step_spec((HEADS, slots)),
+            step_spec((HEADS, slots)), step_spec(RAISED),
         ]
         + [step_spec((per, width))] * count,
         out_shape=[
             shape_of((frames, slots, width), bf16), shape_of((frames, slots, 3 * width), bf16),
             shape_of((frames, slots, width), bf16), shape_of((frames, HEADS, slots), f32),
+            shape_of((frames,) + RAISED, bf16),
         ]
         + [shape_of((frames, per, width), bf16)] * count,
         scratch_shapes=[pltpu.VMEM((width, ROWS), bf16), pltpu.VMEM((ROWS, width), bf16)],
@@ -440,16 +438,16 @@
 
 
 def call_space_backward(
-    behind, micro, grads, place, tok, hot, kmask, qmask, gain, table, weights, qkv, mix, lse, buffer
+    behind, micro, grads, place, tok, hot, raised, gain, table, weights, qkv, mix, lse, buffer
 ):
     micros, frames, slots, width = tok.shape
     count = len(grads)
     row = shape_of((1, width), f32)
-    operands = list(grads) + [place, tok, hot, kmask, qmask, gain, table, weights, qkv, mix, lse]
+    operands = list(grads) + [place, tok, hot, raised, gain, table, weights, qkv, mix, lse]
     specs = (
         [step_spec((slots // count, width))] * count
-        + [smem(), micro_spec(micro, (slots, width)), step_spec(hot.shape[1:])]
-        + [whole(a.shape) for a in (kmask, qmask, gain, table, weights)]
+        + [smem(), micro_spec(micro, (slots, width)), step_spec(hot.shape[1:]), step_spec(RAISED)]
+        + [whole(a.shape) for a in (gain, table, weights)]
         + [step_spec((slots, 3 * width)), step_spec((slots, width)), step_spec((HEADS, slots))]
     )
     before = len(operands)
@@ -495,12 +493,12 @@
         in_specs=[group_spec(a, count) for a in x] + [whole(a.shape) for a in (kmask, qmask, gain, bias, weights)],
         out_specs=[
             step_spec((ROWS, width)), step_spec((ROWS, 3 * width)), step_spec((ROWS, width)),
-            step_spec((HEADS, ROWS)), step_spec((ROWS, width)),
+            step_spec((HEADS, ROWS)), step_spec(RAISED), step_spec((ROWS, width)),
         ],
         out_shape=[
             shape_of((groups, ROWS, width), bf16), shape_of((groups, ROWS, 3 * width), bf16),
             shape_of((groups, ROWS, width), bf16), shape_of((groups, HEADS, ROWS), f32),
-            shape_of((groups, ROWS, width), f32),
+            shape_of((groups,) + RAISED, bf16), shape_of((groups, ROWS, width), f32),
         ],
         scratch_shapes=[pltpu.VMEM((width, ROWS), bf16)],
         name="time_forward",
@@ -536,7 +534,7 @@
     )(*grad, x, gain, bias, hidden_bias, out_bias, weights)
 
 
-def call_time_backward(behind, x, gat, kmask, qmask, gain, weights, qkv, mix, lse):
+def call_time_backward(behind, x, gat, raised, gain, weights, qkv, mix, lse):
     count = len(x)
     groups, _, width = gat.shape
     row = shape_of((1, width), f32)
@@ -545,15 +543,15 @@
         behind,
         grid=(groups,),
         in_specs=[group_spec(a, count) for a in x]
-        + [step_spec((ROWS, width))]
-        + [whole(a.shape) for a in (kmask, qmask, gain, weights)]
+        + [step_spec((ROWS, width)), step_spec(RAISED)]
+        + [whole(a.shape) for a in (gain, weights)]
         + [step_spec((ROWS, 3 * width)), step_spec((ROWS, width)), step_spec((HEADS, ROWS))],
         out_specs=[step_spec((ROWS, 3 * width)), total_spec((1, width)), total_spec((1, width))]
         + [group_spec(a, count) for a in x],
         out_shape=[shape_of((groups, ROWS, 3 * width), bf16), row, row] + [shape_of(a.shape, bf16) for a in x],
         scratch_shapes=back_scratch(width),
         name="time_backward",
-    )(*x, gat, kmask, qmask, gain, weights, qkv, mix, lse)
+    )(*x, gat, raised, gain, weights, qkv, mix, lse)
 
 
 def call_assemble(place, parts):
@@ -818,16 +816,16 @@
         forward.append(
             call_space_forward(behind, m, place, tokens, hots[m], *smasks[m], gain, bias, table, w_space, pieces)
         )
-        after.append(outward(forward[m][4:]))
+        after.append(outward(forward[m][5:]))
         behind = [forward[m][3]] + marks(branch[0])
     for m in micro:
         middle.append(list(call_time_forward(behind, after[m], *tmasks, gain, bias, w_time)))
         behind = [middle[m][3]]
     for m in micro[1:]:
-        late, (middle[-1][4],) = together(sent[m], [middle[-1][4]])
+        late, (middle[-1][5],) = together(sent[m], [middle[-1][5]])
         branch.append(outward(late))
     for m in micro:
-        ahead.append(call_feed_forward(behind, branch[m], middle[m][4], gain, bias, hb_all, ob_all, w_ff))
+        ahead.append(call_feed_forward(behind, branch[m], middle[m][5], gain, bias, hb_all, ob_all, w_ff))
         pieces_out.append(inward(ahead[m][9:]))
         behind = [ahead[m][5]]
     behind += marks(pieces_out[0])
@@ -839,7 +837,7 @@
     for m in micro:
         back.append(
             call_time_backward(
-                behind, after[m], ahead[m][3], *tmasks, gain, w_time, middle[m][1], middle[m][2], middle[m][3]
+                behind, after[m], ahead[m][3], middle[m][4], gain, w_time, middle[m][1], middle[m][2], middle[m][3]
             )
         )
         gas.append(inward(back[m][3:]))
@@ -855,7 +853,7 @@
         last.append(
             list(
                 call_space_backward(
-                    behind, m, gas[m], place, tokens, hots[m], *smasks[m], gain, table, w_space,
+                    behind, m, gas[m], place, tokens, hots[m], forward[m][4], gain, table, w_space,
                     forward[m][1], forward[m][2], forward[m][3], grad_buffer,
                 )
             )

time: 750 us -> 744 us (level)
  transfers between devices with their start and end apart: 48 -> 48, of which waited for: 13 -> 13; matrix products, arithmetic and copies ran while one was open for 6% -> 7% of each run, Pallas kernels for 57% -> 57%
where the time goes in v6:
time: 744 us; the launch traced here: 732 us
  Pallas kernels  416 us (56%)
  waiting for transfers between devices  132 us (18%)
  starting transfers between devices  95.3 us (13%)
  local copies, waits for them, and re-layouts  37.2 us (5%)
  other arithmetic  25.9 us (3%)
  between operations  15.3 us (2%)
  blocking collectives  9.16 us (1%)
    pallas_call x15, Pallas kernels, ordered_call(): return lambda *operands: call(*behind, *operands)  416 us
    ppermute x18, waiting for transfers between devices, shift(): lax.ppermute(values, 'tm', [(k, (k + step) % count) for k in range(count)])  70.3 us
    ppermute x18, starting transfers between devices, shift(): lax.ppermute(values, 'tm', [(k, (k + step) % count) for k in range(count)])  44.6 us
    ppermute x12, starting transfers between devices, local(): lax.ppermute(parts[d], 'tm', [(k, (k + d) % pieces) for k in range(pieces)])  31.8 us
    all_gather x3, waiting for transfers between devices, gather(): lax.all_gather(jnp.concatenate(parts, axis=0), 'clip', axis=0, tiled=False)  26.6 us
    ppermute x12, waiting for transfers between devices, local(): lax.ppermute(parts[d], 'tm', [(k, (k + d) % pieces) for k in range(pieces)])  20.8 us
    ppermute x12, starting transfers between devices, local(): lax.ppermute(parts[d], 'tm', [(k, (k - d) % pieces) for k in range(pieces)])  18.7 us
  transfers between devices with their start and end apart: 48, of which 13 were waited for; matrix products, arithmetic and copies ran while one was open for 7% of the time, Pallas kernels for 57%

profile of v6, /device:TPU:0, one launch (start us, length us, event | category | flops | bytes accessed | tf_op | source)
XLA Modules:
  0.0 731.5 jit_solution(5657303526138390504)
XLA Ops:
  14.8 4.1 fusion.26
  20.4 3.0 collective-permute-start
  23.4 2.6 collective-permute-start.1
  27.6 9.2 %all-gather.4 = bf16[8,19,128]{2,1,0:T(8,128)(2,1)S(1)} all-gather(bf16[1,19,128]{2,1,0:T(8,128)(2,1)S(1)} %bitcast.126), channel_id=2, replica_groups=mesh['clip'=8,'tm'=4] {'clip'}, dimensions={0}, use_global_device_ids=true | all-gather | bytes 43776 | tf_op jit(solution)/shard_map/all_gather | solution.py:783
  43.0 25.0 %all-gather.9.cloned.1.call-done = bf16[4096,1024]{1,0:T(8,128)(2,1)} async-done(((bf16[512,1024]{1,0:T(8,128)(2,1)}), bf16[4096,1024]{1,0:T(8,128)(2,1)}) %all-gather.9.cloned.1.call-update) | async-done | bytes 8388624 | tf_op jit(solution)/shard_map/all_gather | solution.py:710
  68.0 23.7 %space_forward.2 = (bf16[4,256,1024]{2,1,0:T(8,128)(2,1)}, bf16[4,256,3072]{2,1,0:T(8,128)(2,1)}, bf16[4,256,1024]{2,1,0:T(8,128)(2,1)}, f32[4,16,256]{2,1,0:T(8...) custom-call(s32[1]{0:T(128)} %bitcast.refs_0_.refs_4_.refs_5_, ...), custom_call_target="tpu_custom_call" | custom-call | tf_op jit(solution)/shard_map/space_forward/pallas_call | solution.py:377
  97.3 2.4 collective-permute-start.4
  101.2 23.8 %space_forward.3 = (bf16[4,256,1024]{2,1,0:T(8,128)(2,1)}, bf16[4,256,3072]{2,1,0:T(8,128)(2,1)}, bf16[4,256,1024]{2,1,0:T(8,128)(2,1)}, f32[4,16,256]{2,1,0:T(8...) custom-call(f32[4,16,256]{2,1,0:T(8,128)} %get-tuple-element.126.ref, ...), custom_call_target="tpu_custom_call" | custom-call | tf_op jit(solution)/shard_map/space_forward/pallas_call | solution.py:377
  126.9 2.2 collective-permute-start.8
  131.2 24.0 %time_forward.2 = (bf16[4,256,1024]{2,1,0:T(8,128)(2,1)}, bf16[4,256,3072]{2,1,0:T(8,128)(2,1)}, bf16[4,256,1024]{2,1,0:T(8,128)(2,1)}, f32[4,16,256]{2,1,0:T(8,...) custom-call(f32[4,16,256]{2,1,0:T(8,128)} %get-tuple-element.127.refs_0_.refs_14_, ...), custom_call_target="tpu_custom_call" | custom-call | tf_op jit(solution)/shard_map/time_forward/pallas_call | solution.py:377
  155.2 20.2 %collective-permute-done.7.refs_3_ = bf16[4,64,1024]{2,1,0:T(8,128)(2,1)S(1)} collective-permute-done((bf16[4,64,1024]{2,1,0:T(8,128)(2,1)}, bf16[4,64,1024]{2,1,0:T(8,128)(2,1)S(1)}, u32[]{:S(2)}, u32[]{:S(2)}) %collective-permute-start.7) | collective-permute-done | bytes 524320 | tf_op jit(solution)/shard_map/ppermute | solution.py:803
  176.2 22.9 %time_forward.3 = (bf16[4,256,1024]{2,1,0:T(8,128)(2,1)}, bf16[4,256,3072]{2,1,0:T(8,128)(2,1)}, bf16[4,256,1024]{2,1,0:T(8,128)(2,1)}, f32[4,16,256]{2,1,0:T(8,...) custom-call(f32[4,16,256]{2,1,0:T(8,128)} %get-tuple-element.132.refs_0_.refs_11_, ...), custom_call_target="tpu_custom_call" | custom-call | tf_op jit(solution)/shard_map/time_forward/pallas_call | solution.py:377
  199.1 11.6 %collective-permute-start.10 = (bf16[4,64,1024]{2,1,0:T(8,128)(2,1)}, bf16[4,64,1024]{2,1,0:T(8,128)(2,1)S(1)}, u32[]{:S(2)}, u32[]{:S(2)}) collective-permute-start(bf16[4,64,1024]{2,1,0:T(8,128)(2,1)} %get-tuple-element.144), channel_id=1, source_target_pairs={{0,2},{1,3},{2,0},{3,1},{4,6},{5,7},{6,4},{7,5},{8,10},{9,11},{10,... | collective-permute-start | bytes 1572872 | tf_op jit(solution)/shard_map/ppermute | solution.py:803
  211.3 3.3 collective-permute-start.11
  216.6 50.8 %feed_forward.2 = (bf16[4,256,1024]{2,1,0:T(8,128)(2,1)}, bf16[4,256,4096]{2,1,0:T(8,128)(2,1)}, bf16[4,256,4096]{2,1,0:T(8,128)(2,1)}, bf16[4,256,1024]{2,1,0:T...) custom-call(f32[4,16,256]{2,1,0:T(8,128)} %get-tuple-element.137.ref, ...), custom_call_target="tpu_custom_call" | custom-call | tf_op jit(solution)/shard_map/feed_forward/pallas_call | solution.py:377
  267.4 3.4 collective-permute-start.12
  272.9 50.8 %feed_forward.3 = (bf16[4,256,1024]{2,1,0:T(8,128)(2,1)}, bf16[4,256,4096]{2,1,0:T(8,128)(2,1)}, bf16[4,256,4096]{2,1,0:T(8,128)(2,1)}, bf16[4,256,1024]{2,1,0:T...) custom-call(f32[1,1024]{1,0:T(1,128)} %get-tuple-element.140.refs_0_, ...), custom_call_target="tpu_custom_call" | custom-call | tf_op jit(solution)/shard_map/feed_forward/pallas_call | solution.py:377
  323.7 2.8 collective-permute-start.15
  329.6 22.9 %down_grad.1.refs_4_ = bf16[8,1024,1024]{2,1,0:T(8,128)(2,1)} custom-call(f32[1,1024]{1,0:T(1,128)} %get-tuple-element.150.refs_0_, bf16[8,128]{1,0:T(8,128)(2,1)} %slice.232.refs_1_, bf16[8,128]{1,0:T(8,128)(2,1)} %slice.233.refs_2_, bf16[8,128]{1,0:T(8,128)(2,1)} %slice.234.refs_3_, bf16[4,256,4096]{2,1,0:T(8,128)(2,1)} %get-tuple-element.154.refs_4_, ...), custom_call_target="tpu_custom_call" | custom-call | tf_op jit(solution)/shard_map/down_grad/pallas_call | solution.py:377
  352.6 23.3 %hidden_grad.1.refs_0_ = bf16[8,1024,1024]{2,1,0:T(8,128)(2,1)} custom-call(bf16[4,256,1024]{2,1,0:T(8,128)(2,1)} %get-tuple-element.139.refs_0_, bf16[4,256,1024]{2,1,0:T(8,128)(2,1)} %get-tuple-element.147.refs_1_, bf16[4,256,4096]{2,1,0:T(8,128)(2,1)} %get-tuple-element.148.refs_2_, ...), custom_call_target="tpu_custom_call", output_to_operand_aliasing={{}: (4, {})} | custom-call | tf_op jit(solution)/shard_map/hidden_grad/pallas_call | solution.py:377
  376.0 27.0 %time_backward.2 = (bf16[4,256,3072]{2,1,0:T(8,128)(2,1)}, f32[1,1024]{1,0:T(1,128)}, f32[1,1024]{1,0:T(1,128)}, bf16[4,64,1024]{2,1,0:T(8,128)(2,1)}, bf16[4,64...) custom-call(bf16[8,1024,1024]{2,1,0:T(8,128)(2,1)} %hidden_grad.1.refs_0_, ...), custom_call_target="tpu_custom_call" | custom-call | tf_op jit(solution)/shard_map/time_backward/pallas_call | solution.py:377
  402.9 3.8 collective-permute-start.18
  407.6 27.0 %time_backward.3 = (bf16[4,256,3072]{2,1,0:T(8,128)(2,1)}, f32[1,1024]{1,0:T(1,128)}, f32[1,1024]{1,0:T(1,128)}, bf16[4,64,1024]{2,1,0:T(8,128)(2,1)}, bf16[4,64...) custom-call(f32[1,1024]{1,0:T(1,128)} %get-tuple-element.167.refs_0_, ...), custom_call_target="tpu_custom_call" | custom-call | tf_op jit(solution)/shard_map/time_backward/pallas_call | solution.py:377
  434.7 26.2 %time_grad.1.refs_0_ = bf16[8,512,1024]{2,1,0:T(8,128)(2,1)} custom-call(f32[1,1024]{1,0:T(1,128)} %get-tuple-element.172.refs_0_, bf16[4,256,1024]{2,1,0:T(8,128)(2,1)} %get-tuple-element.173.refs_1_, bf16[4,256,1024]{2,1,0:T(8,128)(2,1)} %get-tuple-element.174.refs_2_, bf16[4,256,3072]{2,1,0:T(8,128)(2,1)} %get-tuple-element.175.refs_3_, ...), custom_call_target="tpu_custom_call" | custom-call | tf_op jit(solution)/shard_map/time_grad/pallas_call | solution.py:377
  462.2 3.2 collective-permute-start.21
  467.5 30.8 %space_backward.2 = (bf16[4,256,3072]{2,1,0:T(8,128)(2,1)}, bf16[4,256,1024]{2,1,0:T(8,128)(2,1)}, f32[2,4,256,1024]{3,2,1,0:T(8,128)}, f32[1,1024]{1,0:T(1,128)...) custom-call(bf16[8,512,1024]{2,1,0:T(8,128)(2,1)} %time_grad.1.refs_0_, bf16[4,64,1024]{2,1,0:T(8,128)(2,1)} %get-tuple-element.182.refs_1_, ...), custom_call_target="tpu_custom_call" | custom-call | tf_op jit(solution)/shard_map/space_backward/pallas_call | solution.py:377
  498.3 11.5 %collective-permute-done.22.refs_3_ = bf16[4,64,1024]{2,1,0:T(8,128)(2,1)S(1)} collective-permute-done((bf16[4,64,1024]{2,1,0:T(8,128)(2,1)}, bf16[4,64,1024]{2,1,0:T(8,128)(2,1)S(1)}, u32[]{:S(2)}, u32[]{:S(2)}) %collective-permute-start.22) | collective-permute-done | bytes 524320 | tf_op jit(solution)/shard_map/ppermute | solution.py:806
  511.2 2.6 constant_dynamic-slice_fusion.8
  515.3 3.1 collective-permute-start.26
  518.4 31.4 %space_backward.3 = (bf16[4,256,3072]{2,1,0:T(8,128)(2,1)}, bf16[4,256,1024]{2,1,0:T(8,128)(2,1)}, f32[2,4,256,1024]{3,2,1,0:T(8,128)}, f32[1,1024]{1,0:T(1,128)...) custom-call(bf16[8,128]{1,0:T(8,128)(2,1)} %slice.201.refs_0_, ...), custom_call_target="tpu_custom_call", output_to_operand_aliasing={{2}: (15, {})} | custom-call | tf_op jit(solution)/shard_map/space_backward/pallas_call | solution.py:377
  553.7 2.7 constant_dynamic-update-slice_fusion.12
  556.4 8.6 %collective-permute-start.27 = (bf16[256,1024]{1,0:T(8,128)(2,1)S(1)}, bf16[256,1024]{1,0:T(8,128)(2,1)S(1)}, u32[]{:S(2)}, u32[]{:S(2)}) collective-permute-start(bf16[256,1024]{1,0:T(8,128)(2,1)S(1)} %get-tuple-element.242), channel_id=1, source_target_pairs={{0,1},{1,2},{2,3},{3,0},{4,5},{5,6},{6,7},{7,4},{8,9},{9,10},{10,1... | collective-permute-start | bytes 1572872 | tf_op jit(solution)/shard_map/ppermute | solution.py:719
  565.1 2.7 collective-permute-start.28
  569.5 26.5 %space_grad.1 = bf16[8,544,1024]{2,1,0:T(8,128)(2,1)} custom-call(bf16[8,128]{1,0:T(8,128)(2,1)} %slice.235.refs_0_, bf16[4,256,1024]{2,1,0:T(8,128)(2,1)} %get-tuple-element.195.refs_1_, bf16[4,256,1024]{2,1,0:T(8,128)(2,1)} %get-tuple-element.196.refs_2_, bf16[4,256,3072]{2,1,0:T(8,128)(2,1)} %get-tuple-element.197.refs_3_, ...), custom_call_target="tpu_custom_call" | custom-call | tf_op jit(solution)/shard_map/space_grad/pallas_call | solution.py:377
  597.5 5.2 assemble.1
  605.2 2.8 collective-permute-start.31
  610.0 22.4 %collective-permute-done.35 = bf16[256,1024]{1,0:T(8,128)(2,1)} collective-permute-done((bf16[256,1024]{1,0:T(8,128)(2,1)S(1)}, bf16[256,1024]{1,0:T(8,128)(2,1)}, u32[]{:S(2)}, u32[]{:S(2)}) %collective-permute-start.35) | collective-permute-done | bytes 524320 | tf_op jit(solution)/shard_map/ppermute | solution.py:719
  638.4 5.9 collective-permute-start.32
  646.8 2.8 slice_convert_fusion
  649.6 3.2 collective-permute-done.32
  652.8 10.6 %collective-permute-done.33 = bf16[128,1024]{1,0:T(8,128)(2,1)S(1)} collective-permute-done((bf16[128,1024]{1,0:T(8,128)(2,1)S(1)}, bf16[128,1024]{1,0:T(8,128)(2,1)S(1)}, u32[]{:S(2)}, u32[]{:S(2)}) %collective-permute-start.33) | collective-permute-done | bytes 262176 | tf_op jit(solution)/shard_map/ppermute | solution.py:719
  665.7 3.1 reduce-scatter.8.cloned.1.call-done
  670.0 3.0 collective-permute-start.36
  675.5 6.1 collective-permute-done.36
  681.5 10.8 %collective-permute-done.37 = bf16[136,1024]{1,0:T(8,128)(2,1)S(1)} collective-permute-done((bf16[136,1024]{1,0:T(8,128)(2,1)S(1)}, bf16[136,1024]{1,0:T(8,128)(2,1)S(1)}, u32[]{:S(2)}, u32[]{:S(2)}) %collective-permute-start.37) | collective-permute-done | bytes 278560 | tf_op jit(solution)/shard_map/ppermute | solution.py:719
  693.6 6.5 collective-permute-start.39
  702.5 6.6 collective-permute-done.39
  709.2 10.7 %collective-permute-done.40 = bf16[136,1024]{1,0:T(8,128)(2,1)S(1)} collective-permute-done((bf16[136,1024]{1,0:T(8,128)(2,1)S(1)}, bf16[136,1024]{1,0:T(8,128)(2,1)S(1)}, u32[]{:S(2)}, u32[]{:S(2)}) %collective-permute-start.40) | collective-permute-done | bytes 278560 | tf_op jit(solution)/shard_map/ppermute | solution.py:719
  (256 shorter events, 77.4 us)
Async XLA Ops:
  7.2 60.8 %all-gather.9.cloned.1.call-start = ((), (), s32[]{:S(2)}) async-start(), calls=%async_computation.6 | async-start | bytes 9437184 | tf_op jit(solution)/shard_map/all_gather | solution.py:710
  10.5 120.1 %all-gather.11.cloned.1.call-start = ((), (), s32[]{:S(2)}) async-start(), calls=%async_computation.7 | async-start | bytes 9437184 | tf_op jit(solution)/shard_map/all_gather | solution.py:710
  11.7 204.9 %all-gather.13.cloned.1.call-start = ((), (), s32[]{:S(2)}) async-start(), calls=%async_computation.8 | async-start | bytes 18874368 | tf_op jit(solution)/shard_map/all_gather | solution.py:710
  14.7 495.2 %reduce-scatter.4.cloned.1.call-start = ((), (), s32[]{:S(2)}) async-start(), calls=%async_computation.3 | async-start | bytes 18874368 | tf_op jit(solution)/shard_map/reduce_scatter | solution.py:714
  20.4 74.4 %collective-permute-start = (bf16[4,64,1024]{2,1,0:T(8,128)(2,1)}, bf16[4,64,1024]{2,1,0:T(8,128)(2,1)S(1)}, u32[]{:S(2)}, u32[]{:S(2)}) collective-permute-start(bf16[4,64,1024]{2,1,0:T(8,128)(2,1)} %get-tuple-element.261), channel_id=1, source_target_pairs={{0,1},{1,2},{2,3},{3,0},{4,5},{5,6},{6,7},{7,4},{8,9},{9,10},{10,1... | collective-permute-start | bytes 1572872 | tf_op jit(solution)/shard_map/ppermute | solution.py:803
  23.4 72.0 %collective-permute-start.1 = (bf16[4,64,1024]{2,1,0:T(8,128)(2,1)}, bf16[4,64,1024]{2,1,0:T(8,128)(2,1)S(1)}, u32[]{:S(2)}, u32[]{:S(2)}) collective-permute-start(bf16[4,64,1024]{2,1,0:T(8,128)(2,1)} %get-tuple-element.260), channel_id=1, source_target_pairs={{0,2},{1,3},{2,0},{3,1},{4,6},{5,7},{6,4},{7,5},{8,10},{9,11},{10,... | collective-permute-start | bytes 1572872 | tf_op jit(solution)/shard_map/ppermute | solution.py:803
  26.0 70.0 %collective-permute-start.2 = (bf16[4,64,1024]{2,1,0:T(8,128)(2,1)}, bf16[4,64,1024]{2,1,0:T(8,128)(2,1)}, u32[]{:S(2)}, u32[]{:S(2)}) collective-permute-start(bf16[4,64,1024]{2,1,0:T(8,128)(2,1)} %get-tuple-element.259), channel_id=1, source_target_pairs={{0,3},{1,0},{2,1},{3,2},{4,7},{5,4},{6,5},{7,6},{8,11},{9,8},{10,9... | collective-permute-start | bytes 1572872 | tf_op jit(solution)/shard_map/ppermute | solution.py:803
  91.7 35.2 %collective-permute-start.3 = (bf16[4,64,1024]{2,1,0:T(8,128)(2,1)}, bf16[4,64,1024]{2,1,0:T(8,128)(2,1)S(1)}, u32[]{:S(2)}, u32[]{:S(2)}) collective-permute-start(bf16[4,64,1024]{2,1,0:T(8,128)(2,1)} %get-tuple-element.129), channel_id=1, source_target_pairs={{0,1},{1,2},{2,3},{3,0},{4,5},{5,6},{6,7},{7,4},{8,9},{9,10},{10,1... | collective-permute-start | bytes 1572872 | tf_op jit(solution)/shard_map/ppermute | solution.py:803
  97.3 33.9 %collective-permute-start.4 = (bf16[4,64,1024]{2,1,0:T(8,128)(2,1)}, bf16[4,64,1024]{2,1,0:T(8,128)(2,1)}, u32[]{:S(2)}, u32[]{:S(2)}) collective-permute-start(bf16[4,64,1024]{2,1,0:T(8,128)(2,1)} %get-tuple-element.130), channel_id=1, source_target_pairs={{0,2},{1,3},{2,0},{3,1},{4,6},{5,7},{6,4},{7,5},{8,10},{9,11},{10,... | collective-permute-start | bytes 1572872 | tf_op jit(solution)/shard_map/ppermute | solution.py:803
  99.7 31.5 %collective-permute-start.5 = (bf16[4,64,1024]{2,1,0:T(8,128)(2,1)}, bf16[4,64,1024]{2,1,0:T(8,128)(2,1)}, u32[]{:S(2)}, u32[]{:S(2)}) collective-permute-start(bf16[4,64,1024]{2,1,0:T(8,128)(2,1)} %get-tuple-element.131), channel_id=1, source_target_pairs={{0,3},{1,0},{2,1},{3,2},{4,7},{5,4},{6,5},{7,6},{8,11},{9,8},{10,9... | collective-permute-start | bytes 1572872 | tf_op jit(solution)/shard_map/ppermute | solution.py:803
  125.0 30.2 %collective-permute-start.6 = (bf16[4,64,1024]{2,1,0:T(8,128)(2,1)}, bf16[4,64,1024]{2,1,0:T(8,128)(2,1)S(1)}, u32[]{:S(2)}, u32[]{:S(2)}) collective-permute-start(bf16[4,64,1024]{2,1,0:T(8,128)(2,1)} %get-tuple-element.134), channel_id=1, source_target_pairs={{0,1},{1,2},{2,3},{3,0},{4,5},{5,6},{6,7},{7,4},{8,9},{9,10},{10,1... | collective-permute-start | bytes 1572872 | tf_op jit(solution)/shard_map/ppermute | solution.py:803
  125.6 49.8 %collective-permute-start.7 = (bf16[4,64,1024]{2,1,0:T(8,128)(2,1)}, bf16[4,64,1024]{2,1,0:T(8,128)(2,1)S(1)}, u32[]{:S(2)}, u32[]{:S(2)}) collective-permute-start(bf16[4,64,1024]{2,1,0:T(8,128)(2,1)} %get-tuple-element.135), channel_id=1, source_target_pairs={{0,2},{1,3},{2,0},{3,1},{4,6},{5,7},{6,4},{7,5},{8,10},{9,11},{10,... | collective-permute-start | bytes 1572872 | tf_op jit(solution)/shard_map/ppermute | solution.py:803
  126.9 48.5 %collective-permute-start.8 = (bf16[4,64,1024]{2,1,0:T(8,128)(2,1)}, bf16[4,64,1024]{2,1,0:T(8,128)(2,1)}, u32[]{:S(2)}, u32[]{:S(2)}) collective-permute-start(bf16[4,64,1024]{2,1,0:T(8,128)(2,1)} %get-tuple-element.136), channel_id=1, source_target_pairs={{0,3},{1,0},{2,1},{3,2},{4,7},{5,4},{6,5},{7,6},{8,11},{9,8},{10,9... | collective-permute-start | bytes 1572872 | tf_op jit(solution)/shard_map/ppermute | solution.py:803
  199.1 71.7 %collective-permute-start.10 = (bf16[4,64,1024]{2,1,0:T(8,128)(2,1)}, bf16[4,64,1024]{2,1,0:T(8,128)(2,1)S(1)}, u32[]{:S(2)}, u32[]{:S(2)}) collective-permute-start(bf16[4,64,1024]{2,1,0:T(8,128)(2,1)} %get-tuple-element.144), channel_id=1, source_target_pairs={{0,2},{1,3},{2,0},{3,1},{4,6},{5,7},{6,4},{7,5},{8,10},{9,11},{10,... | collective-permute-start | bytes 1572872 | tf_op jit(solution)/shard_map/ppermute | solution.py:803
  211.3 61.6 %collective-permute-start.11 = (bf16[4,64,1024]{2,1,0:T(8,128)(2,1)}, bf16[4,64,1024]{2,1,0:T(8,128)(2,1)}, u32[]{:S(2)}, u32[]{:S(2)}) collective-permute-start(bf16[4,64,1024]{2,1,0:T(8,128)(2,1)} %get-tuple-element.145), channel_id=1, source_target_pairs={{0,3},{1,0},{2,1},{3,2},{4,7},{5,4},{6,5},{7,6},{8,11},{9,8},{10,9... | collective-permute-start | bytes 1572872 | tf_op jit(solution)/shard_map/ppermute | solution.py:803
  214.6 58.3 %collective-permute-start.9 = (bf16[4,64,1024]{2,1,0:T(8,128)(2,1)}, bf16[4,64,1024]{2,1,0:T(8,128)(2,1)}, u32[]{:S(2)}, u32[]{:S(2)}) collective-permute-start(bf16[4,64,1024]{2,1,0:T(8,128)(2,1)} %get-tuple-element.143), channel_id=1, source_target_pairs={{0,1},{1,2},{2,3},{3,0},{4,5},{5,6},{6,7},{7,4},{8,9},{9,10},{10,1... | collective-permute-start | bytes 1572872 | tf_op jit(solution)/shard_map/ppermute | solution.py:803
  267.4 60.2 %collective-permute-start.12 = (bf16[4,64,1024]{2,1,0:T(8,128)(2,1)}, bf16[4,64,1024]{2,1,0:T(8,128)(2,1)S(1)}, u32[]{:S(2)}, u32[]{:S(2)}) collective-permute-start(bf16[4,64,1024]{2,1,0:T(8,128)(2,1)} %get-tuple-element.151), channel_id=1, source_target_pairs={{0,3},{1,0},{2,1},{3,2},{4,7},{5,4},{6,5},{7,6},{8,11},{9,8},{10,9... | collective-permute-start | bytes 1572872 | tf_op jit(solution)/shard_map/ppermute | solution.py:806
  270.8 57.6 %collective-permute-start.13 = (bf16[4,64,1024]{2,1,0:T(8,128)(2,1)}, bf16[4,64,1024]{2,1,0:T(8,128)(2,1)S(1)}, u32[]{:S(2)}, u32[]{:S(2)}) collective-permute-start(bf16[4,64,1024]{2,1,0:T(8,128)(2,1)} %get-tuple-element.152), channel_id=1, source_target_pairs={{0,2},{1,3},{2,0},{3,1},{4,6},{5,7},{6,4},{7,5},{8,10},{9,11},{10,... | collective-permute-start | bytes 1572872 | tf_op jit(solution)/shard_map/ppermute | solution.py:806
  271.6 57.4 %collective-permute-start.14 = (bf16[4,64,1024]{2,1,0:T(8,128)(2,1)}, bf16[4,64,1024]{2,1,0:T(8,128)(2,1)S(1)}, u32[]{:S(2)}, u32[]{:S(2)}) collective-permute-start(bf16[4,64,1024]{2,1,0:T(8,128)(2,1)} %get-tuple-element.153), channel_id=1, source_target_pairs={{0,1},{1,2},{2,3},{3,0},{4,5},{5,6},{6,7},{7,4},{8,9},{9,10},{10,1... | collective-permute-start | bytes 1572872 | tf_op jit(solution)/shard_map/ppermute | solution.py:806
  323.7 52.2 %collective-permute-start.15 = (bf16[4,64,1024]{2,1,0:T(8,128)(2,1)}, bf16[4,64,1024]{2,1,0:T(8,128)(2,1)}, u32[]{:S(2)}, u32[]{:S(2)}) collective-permute-start(bf16[4,64,1024]{2,1,0:T(8,128)(2,1)} %get-tuple-element.159), channel_id=1, source_target_pairs={{0,3},{1,0},{2,1},{3,2},{4,7},{5,4},{6,5},{7,6},{8,11},{9,8},{10,9... | collective-permute-start | bytes 1572872 | tf_op jit(solution)/shard_map/ppermute | solution.py:806
  326.5 49.4 %collective-permute-start.16 = (bf16[4,64,1024]{2,1,0:T(8,128)(2,1)}, bf16[4,64,1024]{2,1,0:T(8,128)(2,1)}, u32[]{:S(2)}, u32[]{:S(2)}) collective-permute-start(bf16[4,64,1024]{2,1,0:T(8,128)(2,1)} %get-tuple-element.160), channel_id=1, source_target_pairs={{0,2},{1,3},{2,0},{3,1},{4,6},{5,7},{6,4},{7,5},{8,10},{9,11},{10,... | collective-permute-start | bytes 1572872 | tf_op jit(solution)/shard_map/ppermute | solution.py:806
  327.6 48.3 %collective-permute-start.17 = (bf16[4,64,1024]{2,1,0:T(8,128)(2,1)}, bf16[4,64,1024]{2,1,0:T(8,128)(2,1)}, u32[]{:S(2)}, u32[]{:S(2)}) collective-permute-start(bf16[4,64,1024]{2,1,0:T(8,128)(2,1)} %get-tuple-element.161), channel_id=1, source_target_pairs={{0,1},{1,2},{2,3},{3,0},{4,5},{5,6},{6,7},{7,4},{8,9},{9,10},{10,1... | collective-permute-start | bytes 1572872 | tf_op jit(solution)/shard_map/ppermute | solution.py:806
  375.9 220.1 %reduce-scatter.6.cloned.1.call-start = ((), (), s32[]{:S(2)}) async-start(), calls=%async_computation.4 | async-start | bytes 9437184 | tf_op jit(solution)/shard_map/reduce_scatter | solution.py:714
  402.9 57.9 %collective-permute-start.18 = (bf16[4,64,1024]{2,1,0:T(8,128)(2,1)}, bf16[4,64,1024]{2,1,0:T(8,128)(2,1)S(1)}, u32[]{:S(2)}, u32[]{:S(2)}) collective-permute-start(bf16[4,64,1024]{2,1,0:T(8,128)(2,1)} %get-tuple-element.178), channel_id=1, source_target_pairs={{0,3},{1,0},{2,1},{3,2},{4,7},{5,4},{6,5},{7,6},{8,11},{9,8},{10,9... | collective-permute-start | bytes 1572872 | tf_op jit(solution)/shard_map/ppermute | solution.py:806
  406.8 54.2 %collective-permute-start.19 = (bf16[4,64,1024]{2,1,0:T(8,128)(2,1)}, bf16[4,64,1024]{2,1,0:T(8,128)(2,1)S(1)}, u32[]{:S(2)}, u32[]{:S(2)}) collective-permute-start(bf16[4,64,1024]{2,1,0:T(8,128)(2,1)} %get-tuple-element.179), channel_id=1, source_target_pairs={{0,2},{1,3},{2,0},{3,1},{4,6},{5,7},{6,4},{7,5},{8,10},{9,11},{10,... | collective-permute-start | bytes 1572872 | tf_op jit(solution)/shard_map/ppermute | solution.py:806
  406.8 54.2 %collective-permute-start.20 = (bf16[4,64,1024]{2,1,0:T(8,128)(2,1)}, bf16[4,64,1024]{2,1,0:T(8,128)(2,1)S(1)}, u32[]{:S(2)}, u32[]{:S(2)}) collective-permute-start(bf16[4,64,1024]{2,1,0:T(8,128)(2,1)} %get-tuple-element.180), channel_id=1, source_target_pairs={{0,1},{1,2},{2,3},{3,0},{4,5},{5,6},{6,7},{7,4},{8,9},{9,10},{10,1... | collective-permute-start | bytes 1572872 | tf_op jit(solution)/shard_map/ppermute | solution.py:806
  462.0 206.7 %reduce-scatter.8.cloned.1.call-start = ((), (), s32[]{:S(2)}) async-start(), calls=%async_computation.5 | async-start | bytes 10027008 | tf_op jit(solution)/shard_map/reduce_scatter | solution.py:714
  462.2 36.1 %collective-permute-start.21 = (bf16[4,64,1024]{2,1,0:T(8,128)(2,1)}, bf16[4,64,1024]{2,1,0:T(8,128)(2,1)S(1)}, u32[]{:S(2)}, u32[]{:S(2)}) collective-permute-start(bf16[4,64,1024]{2,1,0:T(8,128)(2,1)} %get-tuple-element.191), channel_id=1, source_target_pairs={{0,3},{1,0},{2,1},{3,2},{4,7},{5,4},{6,5},{7,6},{8,11},{9,8},{10,9... | collective-permute-start | bytes 1572872 | tf_op jit(solution)/shard_map/ppermute | solution.py:806
  465.3 44.5 %collective-permute-start.22 = (bf16[4,64,1024]{2,1,0:T(8,128)(2,1)}, bf16[4,64,1024]{2,1,0:T(8,128)(2,1)S(1)}, u32[]{:S(2)}, u32[]{:S(2)}) collective-permute-start(bf16[4,64,1024]{2,1,0:T(8,128)(2,1)} %get-tuple-element.192), channel_id=1, source_target_pairs={{0,2},{1,3},{2,0},{3,1},{4,6},{5,7},{6,4},{7,5},{8,10},{9,11},{10,... | collective-permute-start | bytes 1572872 | tf_op jit(solution)/shard_map/ppermute | solution.py:806
  467.0 42.9 %collective-permute-start.23 = (bf16[4,64,1024]{2,1,0:T(8,128)(2,1)}, bf16[4,64,1024]{2,1,0:T(8,128)(2,1)S(1)}, u32[]{:S(2)}, u32[]{:S(2)}) collective-permute-start(bf16[4,64,1024]{2,1,0:T(8,128)(2,1)} %get-tuple-element.193), channel_id=1, source_target_pairs={{0,1},{1,2},{2,3},{3,0},{4,5},{5,6},{6,7},{7,4},{8,9},{9,10},{10,1... | collective-permute-start | bytes 1572872 | tf_op jit(solution)/shard_map/ppermute | solution.py:806
  513.8 38.3 %collective-permute-start.24 = (bf16[256,1024]{1,0:T(8,128)(2,1)}, bf16[256,1024]{1,0:T(8,128)(2,1)}, u32[]{:S(2)}, u32[]{:S(2)}) collective-permute-start(bf16[256,1024]{1,0:T(8,128)(2,1)} %get-tuple-element.251), channel_id=1, source_target_pairs={{0,1},{1,2},{2,3},{3,0},{4,5},{5,6},{6,7},{7,4},{8,9},{9,10},{10,1... | collective-permute-start | bytes 1572872 | tf_op jit(solution)/shard_map/ppermute | solution.py:719
  513.8 38.3 %collective-permute-start.25 = (bf16[256,1024]{1,0:T(8,128)(2,1)}, bf16[256,1024]{1,0:T(8,128)(2,1)}, u32[]{:S(2)}, u32[]{:S(2)}) collective-permute-start(bf16[256,1024]{1,0:T(8,128)(2,1)} %get-tuple-element.253), channel_id=1, source_target_pairs={{0,2},{1,3},{2,0},{3,1},{4,6},{5,7},{6,4},{7,5},{8,10},{9,11},{10,... | collective-permute-start | bytes 1572872 | tf_op jit(solution)/shard_map/ppermute | solution.py:719
  515.3 36.8 %collective-permute-start.26 = (bf16[256,1024]{1,0:T(8,128)(2,1)}, bf16[256,1024]{1,0:T(8,128)(2,1)}, u32[]{:S(2)}, u32[]{:S(2)}) collective-permute-start(bf16[256,1024]{1,0:T(8,128)(2,1)} %get-tuple-element.252), channel_id=1, source_target_pairs={{0,3},{1,0},{2,1},{3,2},{4,7},{5,4},{6,5},{7,6},{8,11},{9,8},{10,9... | collective-permute-start | bytes 1572872 | tf_op jit(solution)/shard_map/ppermute | solution.py:719
  556.4 39.6 %collective-permute-start.27 = (bf16[256,1024]{1,0:T(8,128)(2,1)S(1)}, bf16[256,1024]{1,0:T(8,128)(2,1)S(1)}, u32[]{:S(2)}, u32[]{:S(2)}) collective-permute-start(bf16[256,1024]{1,0:T(8,128)(2,1)S(1)} %get-tuple-element.242), channel_id=1, source_target_pairs={{0,1},{1,2},{2,3},{3,0},{4,5},{5,6},{6,7},{7,4},{8,9},{9,10},{10,1... | collective-permute-start | bytes 1572872 | tf_op jit(solution)/shard_map/ppermute | solution.py:719
  565.1 31.0 %collective-permute-start.28 = (bf16[256,1024]{1,0:T(8,128)(2,1)S(1)}, bf16[256,1024]{1,0:T(8,128)(2,1)S(1)}, u32[]{:S(2)}, u32[]{:S(2)}) collective-permute-start(bf16[256,1024]{1,0:T(8,128)(2,1)S(1)} %get-tuple-element.242), channel_id=1, source_target_pairs={{0,3},{1,0},{2,1},{3,2},{4,7},{5,4},{6,5},{7,6},{8,11},{9,8},{10,9... | collective-permute-start | bytes 1572872 | tf_op jit(solution)/shard_map/ppermute | solution.py:719
  596.9 35.5 %collective-permute-start.35 = (bf16[256,1024]{1,0:T(8,128)(2,1)S(1)}, bf16[256,1024]{1,0:T(8,128)(2,1)}, u32[]{:S(2)}, u32[]{:S(2)}) collective-permute-start(bf16[256,1024]{1,0:T(8,128)(2,1)S(1)} %get-tuple-element.242), channel_id=1, source_target_pairs={{0,2},{1,3},{2,0},{3,1},{4,6},{5,7},{6,4},{7,5},{8,10},{9,11},{10,... | collective-permute-start | bytes 1572872 | tf_op jit(solution)/shard_map/ppermute | solution.py:719
  602.8 35.3 %collective-permute-start.29 = (bf16[128,1024]{1,0:T(8,128)(2,1)S(1)}, bf16[128,1024]{1,0:T(8,128)(2,1)S(1)}, u32[]{:S(2)}, u32[]{:S(2)}) collective-permute-start(bf16[128,1024]{1,0:T(8,128)(2,1)S(1)} %get-tuple-element.273), channel_id=1, source_target_pairs={{0,1},{1,2},{2,3},{3,0},{4,5},{5,6},{6,7},{7,4},{8,9},{9,10},{10,1... | collective-permute-start | bytes 786440 | tf_op jit(solution)/shard_map/ppermute | solution.py:719
  604.8 33.3 %collective-permute-start.30 = (bf16[128,1024]{1,0:T(8,128)(2,1)S(1)}, bf16[128,1024]{1,0:T(8,128)(2,1)S(1)}, u32[]{:S(2)}, u32[]{:S(2)}) collective-permute-start(bf16[128,1024]{1,0:T(8,128)(2,1)S(1)} %get-tuple-element.275), channel_id=1, source_target_pairs={{0,2},{1,3},{2,0},{3,1},{4,6},{5,7},{6,4},{7,5},{8,10},{9,11},{10,... | collective-permute-start | bytes 786440 | tf_op jit(solution)/shard_map/ppermute | solution.py:719
  605.2 32.9 %collective-permute-start.31 = (bf16[128,1024]{1,0:T(8,128)(2,1)S(1)}, bf16[128,1024]{1,0:T(8,128)(2,1)S(1)}, u32[]{:S(2)}, u32[]{:S(2)}) collective-permute-start(bf16[128,1024]{1,0:T(8,128)(2,1)S(1)} %get-tuple-element.274), channel_id=1, source_target_pairs={{0,3},{1,0},{2,1},{3,2},{4,7},{5,4},{6,5},{7,6},{8,11},{9,8},{10,9... | collective-permute-start | bytes 786440 | tf_op jit(solution)/shard_map/ppermute | solution.py:719
  638.4 14.4 %collective-permute-start.32 = (bf16[128,1024]{1,0:T(8,128)(2,1)S(1)}, bf16[128,1024]{1,0:T(8,128)(2,1)S(1)}, u32[]{:S(2)}, u32[]{:S(2)}) collective-permute-start(bf16[128,1024]{1,0:T(8,128)(2,1)S(1)} %get-tuple-element.244), channel_id=1, source_target_pairs={{0,1},{1,2},{2,3},{3,0},{4,5},{5,6},{6,7},{7,4},{8,9},{9,10},{10,1... | collective-permute-start | bytes 786440 | tf_op jit(solution)/shard_map/ppermute | solution.py:719
  644.4 19.0 %collective-permute-start.33 = (bf16[128,1024]{1,0:T(8,128)(2,1)S(1)}, bf16[128,1024]{1,0:T(8,128)(2,1)S(1)}, u32[]{:S(2)}, u32[]{:S(2)}) collective-permute-start(bf16[128,1024]{1,0:T(8,128)(2,1)S(1)} %get-tuple-element.244), channel_id=1, source_target_pairs={{0,2},{1,3},{2,0},{3,1},{4,6},{5,7},{6,4},{7,5},{8,10},{9,11},{10,... | collective-permute-start | bytes 786440 | tf_op jit(solution)/shard_map/ppermute | solution.py:719
  646.1 17.3 %collective-permute-start.34 = (bf16[128,1024]{1,0:T(8,128)(2,1)S(1)}, bf16[128,1024]{1,0:T(8,128)(2,1)S(1)}, u32[]{:S(2)}, u32[]{:S(2)}) collective-permute-start(bf16[128,1024]{1,0:T(8,128)(2,1)S(1)} %get-tuple-element.244), channel_id=1, source_target_pairs={{0,3},{1,0},{2,1},{3,2},{4,7},{5,4},{6,5},{7,6},{8,11},{9,8},{10,9... | collective-permute-start | bytes 786440 | tf_op jit(solution)/shard_map/ppermute | solution.py:719
  670.0 11.5 %collective-permute-start.36 = (bf16[136,1024]{1,0:T(8,128)(2,1)S(1)}, bf16[136,1024]{1,0:T(8,128)(2,1)S(1)}, u32[]{:S(2)}, u32[]{:S(2)}) collective-permute-start(bf16[136,1024]{1,0:T(8,128)(2,1)S(1)} %get-tuple-element.266), channel_id=1, source_target_pairs={{0,1},{1,2},{2,3},{3,0},{4,5},{5,6},{6,7},{7,4},{8,9},{9,10},{10,1... | collective-permute-start | bytes 835592 | tf_op jit(solution)/shard_map/ppermute | solution.py:719
  673.0 19.3 %collective-permute-start.37 = (bf16[136,1024]{1,0:T(8,128)(2,1)S(1)}, bf16[136,1024]{1,0:T(8,128)(2,1)S(1)}, u32[]{:S(2)}, u32[]{:S(2)}) collective-permute-start(bf16[136,1024]{1,0:T(8,128)(2,1)S(1)} %get-tuple-element.268), channel_id=1, source_target_pairs={{0,2},{1,3},{2,0},{3,1},{4,6},{5,7},{6,4},{7,5},{8,10},{9,11},{10,... | collective-permute-start | bytes 835592 | tf_op jit(solution)/shard_map/ppermute | solution.py:719
  674.3 18.0 %collective-permute-start.38 = (bf16[136,1024]{1,0:T(8,128)(2,1)S(1)}, bf16[136,1024]{1,0:T(8,128)(2,1)S(1)}, u32[]{:S(2)}, u32[]{:S(2)}) collective-permute-start(bf16[136,1024]{1,0:T(8,128)(2,1)S(1)} %get-tuple-element.267), channel_id=1, source_target_pairs={{0,3},{1,0},{2,1},{3,2},{4,7},{5,4},{6,5},{7,6},{8,11},{9,8},{10,9... | collective-permute-start | bytes 835592 | tf_op jit(solution)/shard_map/ppermute | solution.py:719
  693.6 15.5 %collective-permute-start.39 = (bf16[136,1024]{1,0:T(8,128)(2,1)S(1)}, bf16[136,1024]{1,0:T(8,128)(2,1)S(1)}, u32[]{:S(2)}, u32[]{:S(2)}) collective-permute-start(bf16[136,1024]{1,0:T(8,128)(2,1)S(1)} %get-tuple-element.240), channel_id=1, source_target_pairs={{0,1},{1,2},{2,3},{3,0},{4,5},{5,6},{6,7},{7,4},{8,9},{9,10},{10,1... | collective-permute-start | bytes 835592 | tf_op jit(solution)/shard_map/ppermute | solution.py:719
  700.1 19.8 %collective-permute-start.40 = (bf16[136,1024]{1,0:T(8,128)(2,1)S(1)}, bf16[136,1024]{1,0:T(8,128)(2,1)S(1)}, u32[]{:S(2)}, u32[]{:S(2)}) collective-permute-start(bf16[136,1024]{1,0:T(8,128)(2,1)S(1)} %get-tuple-element.240), channel_id=1, source_target_pairs={{0,2},{1,3},{2,0},{3,1},{4,6},{5,7},{6,4},{7,5},{8,10},{9,11},{10,... | collective-permute-start | bytes 835592 | tf_op jit(solution)/shard_map/ppermute | solution.py:719
  702.0 17.9 %collective-permute-start.41 = (bf16[136,1024]{1,0:T(8,128)(2,1)S(1)}, bf16[136,1024]{1,0:T(8,128)(2,1)S(1)}, u32[]{:S(2)}, u32[]{:S(2)}) collective-permute-start(bf16[136,1024]{1,0:T(8,128)(2,1)S(1)} %get-tuple-element.240), channel_id=1, source_target_pairs={{0,3},{1,0},{2,1},{3,2},{4,7},{5,4},{6,5},{7,6},{8,11},{9,8},{10,9... | collective-permute-start | bytes 835592 | tf_op jit(solution)/shard_map/ppermute | solution.py:719
  (45 other events, 452.9 us)
Sparse Core Ops, SparseCore 0:
  10.7 57.2 all-gather.8
  70.4 54.3 all-gather.10
  126.7 89.8 all-gather.12
  376.0 116.3 reduce-scatter.3
  495.8 71.2 reduce-scatter.5
  596.2 72.5 reduce-scatter.7

commit v7 on v6

--- a/solution.py
+++ b/solution.py
@@ -744,10 +744,6 @@
     return values
 
 
-def mark(values):
-    return values.reshape(-1, values.shape[-1])[:8, :128]
-
-
 def together(*lists):
     flat = lax.optimization_barrier([a for arrays in lists for a in arrays])
     out = []
@@ -805,7 +801,7 @@
     inward = lambda parts: [parts[0]] + [
         lax.ppermute(parts[d], "tm", [(k, (k - d) % pieces) for k in range(pieces)]) for d in range(1, pieces)
     ]
-    marks = lambda parts: [mark(a) for a in parts[1:]]
+    marks = lambda parts: parts[1:]
     rounded = lambda values, d: lax.dynamic_slice_in_dim(values, (me + d) % pieces * per, per, axis=1).astype(bf16)
     sent = [[rounded(out_grad[m], d) for d in range(pieces)] for m in micro]
 
@@ -863,7 +859,7 @@
         if m == 0:
             (ff_part,), (last[m][3],), gas[-1] = together([ff_part], [last[m][3]], gas[-1])
             ff_half = sum_half(ff_part)
-            behind = [mark(ff_part)]
+            behind = [ff_part]
 
     total = lambda values: functools.reduce(jnp.add, values)
     gain_grad = jnp.concatenate([total(pick(last, 3)), total(pick(back, 1)), total(pick(ahead, 5))])
@@ -882,7 +878,7 @@
     extra = 8 * pieces - 4 * own % (8 * pieces)
     small_grads = jnp.pad(small_grads, ((0, 0), (0, extra * 1024 - small_grads.shape[1]))).reshape(clips, extra, 1024)
     space_grad = weight_grad(
-        [mark(ff_half)], [(pick(forward, 0), pick(last, 0)), (pick(forward, 2), pick(last, 1))],
+        [ff_half], [(pick(forward, 0), pick(last, 0)), (pick(forward, 2), pick(last, 1))],
         clips, 4 * own + extra, "space_grad", small=small_grads,
     )
 

time: 744 us -> 742 us (level)
  transfers between devices with their start and end apart: 48 -> 48, of which waited for: 13 -> 12; matrix products, arithmetic and copies ran while one was open for 7% -> 6% of each run, Pallas kernels for 57% -> 57%
where the time goes in v7:
time: 742 us; the launch traced here: 729 us
  Pallas kernels  415 us (56%)
  waiting for transfers between devices  134 us (18%)
  starting transfers between devices  96.3 us (13%)
  local copies, waits for them, and re-layouts  33.3 us (4%)
  other arithmetic  26 us (4%)
  between operations  15.3 us (2%)
  blocking collectives  9.16 us (1%)
    pallas_call x15, Pallas kernels, ordered_call(): return lambda *operands: call(*behind, *operands)  415 us
    ppermute x18, waiting for transfers between devices, shift(): lax.ppermute(values, 'tm', [(k, (k + step) % count) for k in range(count)])  70.2 us
    ppermute x18, starting transfers between devices, shift(): lax.ppermute(values, 'tm', [(k, (k + step) % count) for k in range(count)])  44.8 us
    ppermute x12, starting transfers between devices, local(): lax.ppermute(parts[d], 'tm', [(k, (k + d) % pieces) for k in range(pieces)])  32.6 us
    all_gather x3, waiting for transfers between devices, gather(): lax.all_gather(jnp.concatenate(parts, axis=0), 'clip', axis=0, tiled=False)  26.6 us
    ppermute x12, waiting for transfers between devices, local(): lax.ppermute(parts[d], 'tm', [(k, (k + d) % pieces) for k in range(pieces)])  22.7 us
    ppermute x12, starting transfers between devices, local(): lax.ppermute(parts[d], 'tm', [(k, (k - d) % pieces) for k in range(pieces)])  18.7 us
  transfers between devices with their start and end apart: 48, of which 12 were waited for; matrix products, arithmetic and copies ran while one was open for 6% of the time, Pallas kernels for 57%

profile of v7, /device:TPU:0, one launch (start us, length us, event | category | flops | bytes accessed | tf_op | source)
XLA Modules:
  0.0 728.9 jit_solution(13413514211485670338)
XLA Ops:
  8.5 2.0 pad_maximum_fusion
  14.8 4.1 fusion.26
  20.4 3.0 collective-permute-start
  23.4 2.6 collective-permute-start.1
  27.6 9.2 %all-gather.4 = bf16[8,19,128]{2,1,0:T(8,128)(2,1)S(1)} all-gather(bf16[1,19,128]{2,1,0:T(8,128)(2,1)S(1)} %bitcast.115), channel_id=2, replica_groups=mesh['clip'=8,'tm'=4] {'clip'}, dimensions={0}, use_global_device_ids=true | all-gather | bytes 43776 | tf_op jit(solution)/shard_map/all_gather | solution.py:779
  42.9 25.0 %all-gather.9.cloned.1.call-done = bf16[4096,1024]{1,0:T(8,128)(2,1)} async-done(((bf16[512,1024]{1,0:T(8,128)(2,1)}), bf16[4096,1024]{1,0:T(8,128)(2,1)}) %all-gather.9.cloned.1.call-update) | async-done | bytes 8388624 | tf_op jit(solution)/shard_map/all_gather | solution.py:710
  68.0 23.7 %space_forward.2 = (bf16[4,256,1024]{2,1,0:T(8,128)(2,1)}, bf16[4,256,3072]{2,1,0:T(8,128)(2,1)}, bf16[4,256,1024]{2,1,0:T(8,128)(2,1)}, f32[4,16,256]{2,1,0:T(8...) custom-call(s32[1]{0:T(128)} %bitcast.refs_0_.refs_4_.refs_5_, ...), custom_call_target="tpu_custom_call" | custom-call | tf_op jit(solution)/shard_map/space_forward/pallas_call | solution.py:377
  94.8 2.4 collective-permute-start.4
  99.5 23.7 %space_forward.3 = (bf16[4,256,1024]{2,1,0:T(8,128)(2,1)}, bf16[4,256,3072]{2,1,0:T(8,128)(2,1)}, bf16[4,256,1024]{2,1,0:T(8,128)(2,1)}, f32[4,16,256]{2,1,0:T(8...) custom-call(f32[4,16,256]{2,1,0:T(8,128)} %get-tuple-element.126.ref, ...), custom_call_target="tpu_custom_call" | custom-call | tf_op jit(solution)/shard_map/space_forward/pallas_call | solution.py:377
  125.8 2.5 collective-permute-start.8
  129.8 22.7 %collective-permute-done.4.refs_6_.refs_3_ = bf16[4,64,1024]{2,1,0:T(8,128)(2,1)} collective-permute-done((bf16[4,64,1024]{2,1,0:T(8,128)(2,1)}, bf16[4,64,1024]{2,1,0:T(8,128)(2,1)}, u32[]{:S(2)}, u32[]{:S(2)}) %collective-permute-start.4) | collective-permute-done | bytes 524320 | tf_op jit(solution)/shard_map/ppermute | solution.py:799
  152.5 22.9 %time_forward.2 = (bf16[4,256,1024]{2,1,0:T(8,128)(2,1)}, bf16[4,256,3072]{2,1,0:T(8,128)(2,1)}, bf16[4,256,1024]{2,1,0:T(8,128)(2,1)}, f32[4,16,256]{2,1,0:T(8,...) custom-call(f32[4,16,256]{2,1,0:T(8,128)} %get-tuple-element.127.refs_0_.refs_14_, ...), custom_call_target="tpu_custom_call" | custom-call | tf_op jit(solution)/shard_map/time_forward/pallas_call | solution.py:377
  176.3 22.9 %time_forward.3 = (bf16[4,256,1024]{2,1,0:T(8,128)(2,1)}, bf16[4,256,3072]{2,1,0:T(8,128)(2,1)}, bf16[4,256,1024]{2,1,0:T(8,128)(2,1)}, f32[4,16,256]{2,1,0:T(8,...) custom-call(f32[4,16,256]{2,1,0:T(8,128)} %get-tuple-element.132.refs_0_.refs_11_, ...), custom_call_target="tpu_custom_call" | custom-call | tf_op jit(solution)/shard_map/time_forward/pallas_call | solution.py:377
  199.2 11.5 %collective-permute-start.10 = (bf16[4,64,1024]{2,1,0:T(8,128)(2,1)}, bf16[4,64,1024]{2,1,0:T(8,128)(2,1)S(1)}, u32[]{:S(2)}, u32[]{:S(2)}) collective-permute-start(bf16[4,64,1024]{2,1,0:T(8,128)(2,1)} %get-tuple-element.144), channel_id=1, source_target_pairs={{0,2},{1,3},{2,0},{3,1},{4,6},{5,7},{6,4},{7,5},{8,10},{9,11},{10,... | collective-permute-start | bytes 1572872 | tf_op jit(solution)/shard_map/ppermute | solution.py:799
  211.3 3.3 collective-permute-start.11
  216.6 50.9 %feed_forward.2 = (bf16[4,256,1024]{2,1,0:T(8,128)(2,1)}, bf16[4,256,4096]{2,1,0:T(8,128)(2,1)}, bf16[4,256,4096]{2,1,0:T(8,128)(2,1)}, bf16[4,256,1024]{2,1,0:T...) custom-call(f32[4,16,256]{2,1,0:T(8,128)} %get-tuple-element.137.ref, ...), custom_call_target="tpu_custom_call" | custom-call | tf_op jit(solution)/shard_map/feed_forward/pallas_call | solution.py:377
  267.5 3.4 collective-permute-start.12
  272.9 50.8 %feed_forward.3 = (bf16[4,256,1024]{2,1,0:T(8,128)(2,1)}, bf16[4,256,4096]{2,1,0:T(8,128)(2,1)}, bf16[4,256,4096]{2,1,0:T(8,128)(2,1)}, bf16[4,256,1024]{2,1,0:T...) custom-call(f32[1,1024]{1,0:T(1,128)} %get-tuple-element.140.refs_0_, ...), custom_call_target="tpu_custom_call" | custom-call | tf_op jit(solution)/shard_map/feed_forward/pallas_call | solution.py:377
  323.7 2.8 collective-permute-start.15
  328.9 22.9 %down_grad.1.refs_4_ = bf16[8,1024,1024]{2,1,0:T(8,128)(2,1)} custom-call(f32[1,1024]{1,0:T(1,128)} %get-tuple-element.150.refs_0_, bf16[4,64,1024]{2,1,0:T(8,128)(2,1)} %copy-done.3, bf16[4,64,1024]{2,1,0:T(8,128)(2,1)} %copy-done.4, bf16[4,64,1024]{2,1,0:T(8,128)(2,1)} %copy-done.5, bf16[4,256,4096]{2,1,0:T(8,128)(2,1)} %get-tuple-element.154.refs_4_, ...), custom_call_target="tpu_custom_call" | custom-call | tf_op jit(solution)/shard_map/down_grad/pallas_call | solution.py:377
  351.8 23.2 %hidden_grad.1.refs_0_ = bf16[8,1024,1024]{2,1,0:T(8,128)(2,1)} custom-call(bf16[4,256,1024]{2,1,0:T(8,128)(2,1)} %get-tuple-element.139.refs_0_, bf16[4,256,1024]{2,1,0:T(8,128)(2,1)} %get-tuple-element.147.refs_1_, bf16[4,256,4096]{2,1,0:T(8,128)(2,1)} %get-tuple-element.148.refs_2_, ...), custom_call_target="tpu_custom_call", output_to_operand_aliasing={{}: (4, {})} | custom-call | tf_op jit(solution)/shard_map/hidden_grad/pallas_call | solution.py:377
  375.1 27.0 %time_backward.2 = (bf16[4,256,3072]{2,1,0:T(8,128)(2,1)}, f32[1,1024]{1,0:T(1,128)}, f32[1,1024]{1,0:T(1,128)}, bf16[4,64,1024]{2,1,0:T(8,128)(2,1)}, bf16[4,64...) custom-call(bf16[8,1024,1024]{2,1,0:T(8,128)(2,1)} %hidden_grad.1.refs_0_, ...), custom_call_target="tpu_custom_call" | custom-call | tf_op jit(solution)/shard_map/time_backward/pallas_call | solution.py:377
  402.1 3.8 collective-permute-start.18
  406.8 27.1 %time_backward.3 = (bf16[4,256,3072]{2,1,0:T(8,128)(2,1)}, f32[1,1024]{1,0:T(1,128)}, f32[1,1024]{1,0:T(1,128)}, bf16[4,64,1024]{2,1,0:T(8,128)(2,1)}, bf16[4,64...) custom-call(f32[1,1024]{1,0:T(1,128)} %get-tuple-element.167.refs_0_, ...), custom_call_target="tpu_custom_call" | custom-call | tf_op jit(solution)/shard_map/time_backward/pallas_call | solution.py:377
  433.9 26.2 %time_grad.1.refs_0_ = bf16[8,512,1024]{2,1,0:T(8,128)(2,1)} custom-call(f32[1,1024]{1,0:T(1,128)} %get-tuple-element.172.refs_0_, bf16[4,256,1024]{2,1,0:T(8,128)(2,1)} %get-tuple-element.173.refs_1_, bf16[4,256,1024]{2,1,0:T(8,128)(2,1)} %get-tuple-element.174.refs_2_, bf16[4,256,3072]{2,1,0:T(8,128)(2,1)} %get-tuple-element.175.refs_3_, ...), custom_call_target="tpu_custom_call" | custom-call | tf_op jit(solution)/shard_map/time_grad/pallas_call | solution.py:377
  461.4 3.1 collective-permute-start.21
  466.7 30.8 %space_backward.2 = (bf16[4,256,3072]{2,1,0:T(8,128)(2,1)}, bf16[4,256,1024]{2,1,0:T(8,128)(2,1)}, f32[2,4,256,1024]{3,2,1,0:T(8,128)}, f32[1,1024]{1,0:T(1,128)...) custom-call(bf16[8,512,1024]{2,1,0:T(8,128)(2,1)} %time_grad.1.refs_0_, bf16[4,64,1024]{2,1,0:T(8,128)(2,1)} %get-tuple-element.182.refs_1_, ...), custom_call_target="tpu_custom_call" | custom-call | tf_op jit(solution)/shard_map/space_backward/pallas_call | solution.py:377
  497.6 11.5 %collective-permute-done.22.refs_3_ = bf16[4,64,1024]{2,1,0:T(8,128)(2,1)S(1)} collective-permute-done((bf16[4,64,1024]{2,1,0:T(8,128)(2,1)}, bf16[4,64,1024]{2,1,0:T(8,128)(2,1)S(1)}, u32[]{:S(2)}, u32[]{:S(2)}) %collective-permute-start.22) | collective-permute-done | bytes 524320 | tf_op jit(solution)/shard_map/ppermute | solution.py:802
  513.1 3.0 collective-permute-start.26
  516.1 31.4 %space_backward.3 = (bf16[4,256,3072]{2,1,0:T(8,128)(2,1)}, bf16[4,256,1024]{2,1,0:T(8,128)(2,1)}, f32[2,4,256,1024]{3,2,1,0:T(8,128)}, f32[1,1024]{1,0:T(1,128)...) custom-call(bf16[1024,1024]{1,0:T(8,128)(2,1)} %bitcast.103, ...), custom_call_target="tpu_custom_call", output_to_operand_aliasing={{2}: (15, {})} | custom-call | tf_op jit(solution)/shard_map/space_backward/pallas_call | solution.py:377
  551.3 2.8 constant_dynamic-update-slice_fusion.12
  554.2 8.3 %collective-permute-start.27 = (bf16[256,1024]{1,0:T(8,128)(2,1)S(1)}, bf16[256,1024]{1,0:T(8,128)(2,1)S(1)}, u32[]{:S(2)}, u32[]{:S(2)}) collective-permute-start(bf16[256,1024]{1,0:T(8,128)(2,1)S(1)} %get-tuple-element.242.refs_0_), channel_id=1, source_target_pairs={{0,1},{1,2},{2,3},{3,0},{4,5},{5,6},{6,7},{7,4},{8,9},{9,10},{10,1... | collective-permute-start | bytes 1572872 | tf_op jit(solution)/shard_map/ppermute | solution.py:719
  562.4 2.8 collective-permute-start.28
  566.4 26.5 %space_grad.1 = bf16[8,544,1024]{2,1,0:T(8,128)(2,1)} custom-call(bf16[256,1024]{1,0:T(8,128)(2,1)} %copy-done.7, bf16[4,256,1024]{2,1,0:T(8,128)(2,1)} %get-tuple-element.195.refs_1_, bf16[4,256,1024]{2,1,0:T(8,128)(2,1)} %get-tuple-element.196.refs_2_, bf16[4,256,3072]{2,1,0:T(8,128)(2,1)} %get-tuple-element.197.refs_3_, ...), custom_call_target="tpu_custom_call" | custom-call | tf_op jit(solution)/shard_map/space_grad/pallas_call | solution.py:377
  595.0 5.0 assemble.1
  602.7 2.8 collective-permute-start.31
  607.5 22.5 %collective-permute-done.35 = bf16[256,1024]{1,0:T(8,128)(2,1)} collective-permute-done((bf16[256,1024]{1,0:T(8,128)(2,1)S(1)}, bf16[256,1024]{1,0:T(8,128)(2,1)}, u32[]{:S(2)}, u32[]{:S(2)}) %collective-permute-start.35) | collective-permute-done | bytes 524320 | tf_op jit(solution)/shard_map/ppermute | solution.py:719
  636.1 5.9 collective-permute-start.32
  644.4 2.8 slice_convert_fusion
  647.2 2.9 collective-permute-done.32
  650.2 10.6 %collective-permute-done.33 = bf16[128,1024]{1,0:T(8,128)(2,1)S(1)} collective-permute-done((bf16[128,1024]{1,0:T(8,128)(2,1)S(1)}, bf16[128,1024]{1,0:T(8,128)(2,1)S(1)}, u32[]{:S(2)}, u32[]{:S(2)}) %collective-permute-start.33) | collective-permute-done | bytes 262176 | tf_op jit(solution)/shard_map/ppermute | solution.py:719
  663.1 2.7 reduce-scatter.8.cloned.1.call-done
  667.0 3.4 collective-permute-start.36
  672.8 6.2 collective-permute-done.36
  679.0 10.8 %collective-permute-done.37 = bf16[136,1024]{1,0:T(8,128)(2,1)S(1)} collective-permute-done((bf16[136,1024]{1,0:T(8,128)(2,1)S(1)}, bf16[136,1024]{1,0:T(8,128)(2,1)S(1)}, u32[]{:S(2)}, u32[]{:S(2)}) %collective-permute-start.37) | collective-permute-done | bytes 278560 | tf_op jit(solution)/shard_map/ppermute | solution.py:719
  691.1 6.5 collective-permute-start.39
  700.1 6.4 collective-permute-done.39
  706.5 10.7 %collective-permute-done.40 = bf16[136,1024]{1,0:T(8,128)(2,1)S(1)} collective-permute-done((bf16[136,1024]{1,0:T(8,128)(2,1)S(1)}, bf16[136,1024]{1,0:T(8,128)(2,1)S(1)}, u32[]{:S(2)}, u32[]{:S(2)}) %collective-permute-start.40) | collective-permute-done | bytes 278560 | tf_op jit(solution)/shard_map/ppermute | solution.py:719
  (252 shorter events, 74.5 us)
Async XLA Ops:
  7.2 60.8 %all-gather.9.cloned.1.call-start = ((), (), s32[]{:S(2)}) async-start(), calls=%async_computation.6 | async-start | bytes 9437184 | tf_op jit(solution)/shard_map/all_gather | solution.py:710
  10.5 119.3 %all-gather.11.cloned.1.call-start = ((), (), s32[]{:S(2)}) async-start(), calls=%async_computation.7 | async-start | bytes 9437184 | tf_op jit(solution)/shard_map/all_gather | solution.py:710
  11.7 204.9 %all-gather.13.cloned.1.call-start = ((), (), s32[]{:S(2)}) async-start(), calls=%async_computation.8 | async-start | bytes 18874368 | tf_op jit(solution)/shard_map/all_gather | solution.py:710
  14.7 494.4 %reduce-scatter.4.cloned.1.call-start = ((), (), s32[]{:S(2)}) async-start(), calls=%async_computation.3 | async-start | bytes 18874368 | tf_op jit(solution)/shard_map/reduce_scatter | solution.py:714
  20.4 76.8 %collective-permute-start = (bf16[4,64,1024]{2,1,0:T(8,128)(2,1)}, bf16[4,64,1024]{2,1,0:T(8,128)(2,1)S(1)}, u32[]{:S(2)}, u32[]{:S(2)}) collective-permute-start(bf16[4,64,1024]{2,1,0:T(8,128)(2,1)} %get-tuple-element.261), channel_id=1, source_target_pairs={{0,1},{1,2},{2,3},{3,0},{4,5},{5,6},{6,7},{7,4},{8,9},{9,10},{10,1... | collective-permute-start | bytes 1572872 | tf_op jit(solution)/shard_map/ppermute | solution.py:799
  23.4 75.2 %collective-permute-start.1 = (bf16[4,64,1024]{2,1,0:T(8,128)(2,1)}, bf16[4,64,1024]{2,1,0:T(8,128)(2,1)S(1)}, u32[]{:S(2)}, u32[]{:S(2)}) collective-permute-start(bf16[4,64,1024]{2,1,0:T(8,128)(2,1)} %get-tuple-element.260), channel_id=1, source_target_pairs={{0,2},{1,3},{2,0},{3,1},{4,6},{5,7},{6,4},{7,5},{8,10},{9,11},{10,... | collective-permute-start | bytes 1572872 | tf_op jit(solution)/shard_map/ppermute | solution.py:799
  26.0 72.7 %collective-permute-start.2 = (bf16[4,64,1024]{2,1,0:T(8,128)(2,1)}, bf16[4,64,1024]{2,1,0:T(8,128)(2,1)}, u32[]{:S(2)}, u32[]{:S(2)}) collective-permute-start(bf16[4,64,1024]{2,1,0:T(8,128)(2,1)} %get-tuple-element.259), channel_id=1, source_target_pairs={{0,3},{1,0},{2,1},{3,2},{4,7},{5,4},{6,5},{7,6},{8,11},{9,8},{10,9... | collective-permute-start | bytes 1572872 | tf_op jit(solution)/shard_map/ppermute | solution.py:799
  91.7 34.1 %collective-permute-start.3 = (bf16[4,64,1024]{2,1,0:T(8,128)(2,1)}, bf16[4,64,1024]{2,1,0:T(8,128)(2,1)S(1)}, u32[]{:S(2)}, u32[]{:S(2)}) collective-permute-start(bf16[4,64,1024]{2,1,0:T(8,128)(2,1)} %get-tuple-element.129), channel_id=1, source_target_pairs={{0,1},{1,2},{2,3},{3,0},{4,5},{5,6},{6,7},{7,4},{8,9},{9,10},{10,1... | collective-permute-start | bytes 1572872 | tf_op jit(solution)/shard_map/ppermute | solution.py:799
  94.8 57.6 %collective-permute-start.4 = (bf16[4,64,1024]{2,1,0:T(8,128)(2,1)}, bf16[4,64,1024]{2,1,0:T(8,128)(2,1)}, u32[]{:S(2)}, u32[]{:S(2)}) collective-permute-start(bf16[4,64,1024]{2,1,0:T(8,128)(2,1)} %get-tuple-element.130), channel_id=1, source_target_pairs={{0,2},{1,3},{2,0},{3,1},{4,6},{5,7},{6,4},{7,5},{8,10},{9,11},{10,... | collective-permute-start | bytes 1572872 | tf_op jit(solution)/shard_map/ppermute | solution.py:799
  97.2 55.2 %collective-permute-start.5 = (bf16[4,64,1024]{2,1,0:T(8,128)(2,1)}, bf16[4,64,1024]{2,1,0:T(8,128)(2,1)}, u32[]{:S(2)}, u32[]{:S(2)}) collective-permute-start(bf16[4,64,1024]{2,1,0:T(8,128)(2,1)} %get-tuple-element.131), channel_id=1, source_target_pairs={{0,3},{1,0},{2,1},{3,2},{4,7},{5,4},{6,5},{7,6},{8,11},{9,8},{10,9... | collective-permute-start | bytes 1572872 | tf_op jit(solution)/shard_map/ppermute | solution.py:799
  123.2 52.1 %collective-permute-start.6 = (bf16[4,64,1024]{2,1,0:T(8,128)(2,1)}, bf16[4,64,1024]{2,1,0:T(8,128)(2,1)S(1)}, u32[]{:S(2)}, u32[]{:S(2)}) collective-permute-start(bf16[4,64,1024]{2,1,0:T(8,128)(2,1)} %get-tuple-element.134), channel_id=1, source_target_pairs={{0,1},{1,2},{2,3},{3,0},{4,5},{5,6},{6,7},{7,4},{8,9},{9,10},{10,1... | collective-permute-start | bytes 1572872 | tf_op jit(solution)/shard_map/ppermute | solution.py:799
  124.6 50.9 %collective-permute-start.7 = (bf16[4,64,1024]{2,1,0:T(8,128)(2,1)}, bf16[4,64,1024]{2,1,0:T(8,128)(2,1)S(1)}, u32[]{:S(2)}, u32[]{:S(2)}) collective-permute-start(bf16[4,64,1024]{2,1,0:T(8,128)(2,1)} %get-tuple-element.135), channel_id=1, source_target_pairs={{0,2},{1,3},{2,0},{3,1},{4,6},{5,7},{6,4},{7,5},{8,10},{9,11},{10,... | collective-permute-start | bytes 1572872 | tf_op jit(solution)/shard_map/ppermute | solution.py:799
  125.8 49.6 %collective-permute-start.8 = (bf16[4,64,1024]{2,1,0:T(8,128)(2,1)}, bf16[4,64,1024]{2,1,0:T(8,128)(2,1)}, u32[]{:S(2)}, u32[]{:S(2)}) collective-permute-start(bf16[4,64,1024]{2,1,0:T(8,128)(2,1)} %get-tuple-element.136), channel_id=1, source_target_pairs={{0,3},{1,0},{2,1},{3,2},{4,7},{5,4},{6,5},{7,6},{8,11},{9,8},{10,9... | collective-permute-start | bytes 1572872 | tf_op jit(solution)/shard_map/ppermute | solution.py:799
  199.2 71.6 %collective-permute-start.10 = (bf16[4,64,1024]{2,1,0:T(8,128)(2,1)}, bf16[4,64,1024]{2,1,0:T(8,128)(2,1)S(1)}, u32[]{:S(2)}, u32[]{:S(2)}) collective-permute-start(bf16[4,64,1024]{2,1,0:T(8,128)(2,1)} %get-tuple-element.144), channel_id=1, source_target_pairs={{0,2},{1,3},{2,0},{3,1},{4,6},{5,7},{6,4},{7,5},{8,10},{9,11},{10,... | collective-permute-start | bytes 1572872 | tf_op jit(solution)/shard_map/ppermute | solution.py:799
  211.3 61.6 %collective-permute-start.11 = (bf16[4,64,1024]{2,1,0:T(8,128)(2,1)}, bf16[4,64,1024]{2,1,0:T(8,128)(2,1)}, u32[]{:S(2)}, u32[]{:S(2)}) collective-permute-start(bf16[4,64,1024]{2,1,0:T(8,128)(2,1)} %get-tuple-element.145), channel_id=1, source_target_pairs={{0,3},{1,0},{2,1},{3,2},{4,7},{5,4},{6,5},{7,6},{8,11},{9,8},{10,9... | collective-permute-start | bytes 1572872 | tf_op jit(solution)/shard_map/ppermute | solution.py:799
  214.6 58.3 %collective-permute-start.9 = (bf16[4,64,1024]{2,1,0:T(8,128)(2,1)}, bf16[4,64,1024]{2,1,0:T(8,128)(2,1)}, u32[]{:S(2)}, u32[]{:S(2)}) collective-permute-start(bf16[4,64,1024]{2,1,0:T(8,128)(2,1)} %get-tuple-element.143), channel_id=1, source_target_pairs={{0,1},{1,2},{2,3},{3,0},{4,5},{5,6},{6,7},{7,4},{8,9},{9,10},{10,1... | collective-permute-start | bytes 1572872 | tf_op jit(solution)/shard_map/ppermute | solution.py:799
  267.5 60.2 %collective-permute-start.12 = (bf16[4,64,1024]{2,1,0:T(8,128)(2,1)}, bf16[4,64,1024]{2,1,0:T(8,128)(2,1)S(1)}, u32[]{:S(2)}, u32[]{:S(2)}) collective-permute-start(bf16[4,64,1024]{2,1,0:T(8,128)(2,1)} %get-tuple-element.151), channel_id=1, source_target_pairs={{0,3},{1,0},{2,1},{3,2},{4,7},{5,4},{6,5},{7,6},{8,11},{9,8},{10,9... | collective-permute-start | bytes 1572872 | tf_op jit(solution)/shard_map/ppermute | solution.py:802
  270.9 57.0 %collective-permute-start.13 = (bf16[4,64,1024]{2,1,0:T(8,128)(2,1)}, bf16[4,64,1024]{2,1,0:T(8,128)(2,1)S(1)}, u32[]{:S(2)}, u32[]{:S(2)}) collective-permute-start(bf16[4,64,1024]{2,1,0:T(8,128)(2,1)} %get-tuple-element.152), channel_id=1, source_target_pairs={{0,2},{1,3},{2,0},{3,1},{4,6},{5,7},{6,4},{7,5},{8,10},{9,11},{10,... | collective-permute-start | bytes 1572872 | tf_op jit(solution)/shard_map/ppermute | solution.py:802
  271.7 56.2 %collective-permute-start.14 = (bf16[4,64,1024]{2,1,0:T(8,128)(2,1)}, bf16[4,64,1024]{2,1,0:T(8,128)(2,1)S(1)}, u32[]{:S(2)}, u32[]{:S(2)}) collective-permute-start(bf16[4,64,1024]{2,1,0:T(8,128)(2,1)} %get-tuple-element.153), channel_id=1, source_target_pairs={{0,1},{1,2},{2,3},{3,0},{4,5},{5,6},{6,7},{7,4},{8,9},{9,10},{10,1... | collective-permute-start | bytes 1572872 | tf_op jit(solution)/shard_map/ppermute | solution.py:802
  323.7 51.3 %collective-permute-start.15 = (bf16[4,64,1024]{2,1,0:T(8,128)(2,1)}, bf16[4,64,1024]{2,1,0:T(8,128)(2,1)}, u32[]{:S(2)}, u32[]{:S(2)}) collective-permute-start(bf16[4,64,1024]{2,1,0:T(8,128)(2,1)} %get-tuple-element.159), channel_id=1, source_target_pairs={{0,3},{1,0},{2,1},{3,2},{4,7},{5,4},{6,5},{7,6},{8,11},{9,8},{10,9... | collective-permute-start | bytes 1572872 | tf_op jit(solution)/shard_map/ppermute | solution.py:802
  326.5 48.5 %collective-permute-start.16 = (bf16[4,64,1024]{2,1,0:T(8,128)(2,1)}, bf16[4,64,1024]{2,1,0:T(8,128)(2,1)}, u32[]{:S(2)}, u32[]{:S(2)}) collective-permute-start(bf16[4,64,1024]{2,1,0:T(8,128)(2,1)} %get-tuple-element.160), channel_id=1, source_target_pairs={{0,2},{1,3},{2,0},{3,1},{4,6},{5,7},{6,4},{7,5},{8,10},{9,11},{10,... | collective-permute-start | bytes 1572872 | tf_op jit(solution)/shard_map/ppermute | solution.py:802
  327.6 47.4 %collective-permute-start.17 = (bf16[4,64,1024]{2,1,0:T(8,128)(2,1)}, bf16[4,64,1024]{2,1,0:T(8,128)(2,1)}, u32[]{:S(2)}, u32[]{:S(2)}) collective-permute-start(bf16[4,64,1024]{2,1,0:T(8,128)(2,1)} %get-tuple-element.161), channel_id=1, source_target_pairs={{0,1},{1,2},{2,3},{3,0},{4,5},{5,6},{6,7},{7,4},{8,9},{9,10},{10,1... | collective-permute-start | bytes 1572872 | tf_op jit(solution)/shard_map/ppermute | solution.py:802
  375.1 217.9 %reduce-scatter.6.cloned.1.call-start = ((), (), s32[]{:S(2)}) async-start(), calls=%async_computation.4 | async-start | bytes 9437184 | tf_op jit(solution)/shard_map/reduce_scatter | solution.py:714
  402.1 58.0 %collective-permute-start.18 = (bf16[4,64,1024]{2,1,0:T(8,128)(2,1)}, bf16[4,64,1024]{2,1,0:T(8,128)(2,1)S(1)}, u32[]{:S(2)}, u32[]{:S(2)}) collective-permute-start(bf16[4,64,1024]{2,1,0:T(8,128)(2,1)} %get-tuple-element.178), channel_id=1, source_target_pairs={{0,3},{1,0},{2,1},{3,2},{4,7},{5,4},{6,5},{7,6},{8,11},{9,8},{10,9... | collective-permute-start | bytes 1572872 | tf_op jit(solution)/shard_map/ppermute | solution.py:802
  405.9 54.2 %collective-permute-start.19 = (bf16[4,64,1024]{2,1,0:T(8,128)(2,1)}, bf16[4,64,1024]{2,1,0:T(8,128)(2,1)S(1)}, u32[]{:S(2)}, u32[]{:S(2)}) collective-permute-start(bf16[4,64,1024]{2,1,0:T(8,128)(2,1)} %get-tuple-element.179), channel_id=1, source_target_pairs={{0,2},{1,3},{2,0},{3,1},{4,6},{5,7},{6,4},{7,5},{8,10},{9,11},{10,... | collective-permute-start | bytes 1572872 | tf_op jit(solution)/shard_map/ppermute | solution.py:802
  405.9 54.2 %collective-permute-start.20 = (bf16[4,64,1024]{2,1,0:T(8,128)(2,1)}, bf16[4,64,1024]{2,1,0:T(8,128)(2,1)S(1)}, u32[]{:S(2)}, u32[]{:S(2)}) collective-permute-start(bf16[4,64,1024]{2,1,0:T(8,128)(2,1)} %get-tuple-element.180), channel_id=1, source_target_pairs={{0,1},{1,2},{2,3},{3,0},{4,5},{5,6},{6,7},{7,4},{8,9},{9,10},{10,1... | collective-permute-start | bytes 1572872 | tf_op jit(solution)/shard_map/ppermute | solution.py:802
  461.3 204.5 %reduce-scatter.8.cloned.1.call-start = ((), (), s32[]{:S(2)}) async-start(), calls=%async_computation.5 | async-start | bytes 10027008 | tf_op jit(solution)/shard_map/reduce_scatter | solution.py:714
  461.4 36.2 %collective-permute-start.21 = (bf16[4,64,1024]{2,1,0:T(8,128)(2,1)}, bf16[4,64,1024]{2,1,0:T(8,128)(2,1)S(1)}, u32[]{:S(2)}, u32[]{:S(2)}) collective-permute-start(bf16[4,64,1024]{2,1,0:T(8,128)(2,1)} %get-tuple-element.191), channel_id=1, source_target_pairs={{0,3},{1,0},{2,1},{3,2},{4,7},{5,4},{6,5},{7,6},{8,11},{9,8},{10,9... | collective-permute-start | bytes 1572872 | tf_op jit(solution)/shard_map/ppermute | solution.py:802
  464.5 44.5 %collective-permute-start.22 = (bf16[4,64,1024]{2,1,0:T(8,128)(2,1)}, bf16[4,64,1024]{2,1,0:T(8,128)(2,1)S(1)}, u32[]{:S(2)}, u32[]{:S(2)}) collective-permute-start(bf16[4,64,1024]{2,1,0:T(8,128)(2,1)} %get-tuple-element.192), channel_id=1, source_target_pairs={{0,2},{1,3},{2,0},{3,1},{4,6},{5,7},{6,4},{7,5},{8,10},{9,11},{10,... | collective-permute-start | bytes 1572872 | tf_op jit(solution)/shard_map/ppermute | solution.py:802
  466.2 42.9 %collective-permute-start.23 = (bf16[4,64,1024]{2,1,0:T(8,128)(2,1)}, bf16[4,64,1024]{2,1,0:T(8,128)(2,1)S(1)}, u32[]{:S(2)}, u32[]{:S(2)}) collective-permute-start(bf16[4,64,1024]{2,1,0:T(8,128)(2,1)} %get-tuple-element.193), channel_id=1, source_target_pairs={{0,1},{1,2},{2,3},{3,0},{4,5},{5,6},{6,7},{7,4},{8,9},{9,10},{10,1... | collective-permute-start | bytes 1572872 | tf_op jit(solution)/shard_map/ppermute | solution.py:802
  511.6 38.1 %collective-permute-start.24 = (bf16[256,1024]{1,0:T(8,128)(2,1)S(1)}, bf16[256,1024]{1,0:T(8,128)(2,1)}, u32[]{:S(2)}, u32[]{:S(2)}) collective-permute-start(bf16[256,1024]{1,0:T(8,128)(2,1)S(1)} %get-tuple-element.251), channel_id=1, source_target_pairs={{0,1},{1,2},{2,3},{3,0},{4,5},{5,6},{6,7},{7,4},{8,9},{9,10},{10,1... | collective-permute-start | bytes 1572872 | tf_op jit(solution)/shard_map/ppermute | solution.py:719
  511.6 38.1 %collective-permute-start.25 = (bf16[256,1024]{1,0:T(8,128)(2,1)S(1)}, bf16[256,1024]{1,0:T(8,128)(2,1)}, u32[]{:S(2)}, u32[]{:S(2)}) collective-permute-start(bf16[256,1024]{1,0:T(8,128)(2,1)S(1)} %get-tuple-element.253), channel_id=1, source_target_pairs={{0,2},{1,3},{2,0},{3,1},{4,6},{5,7},{6,4},{7,5},{8,10},{9,11},{10,... | collective-permute-start | bytes 1572872 | tf_op jit(solution)/shard_map/ppermute | solution.py:719
  513.1 36.6 %collective-permute-start.26 = (bf16[256,1024]{1,0:T(8,128)(2,1)S(1)}, bf16[256,1024]{1,0:T(8,128)(2,1)}, u32[]{:S(2)}, u32[]{:S(2)}) collective-permute-start(bf16[256,1024]{1,0:T(8,128)(2,1)S(1)} %get-tuple-element.252), channel_id=1, source_target_pairs={{0,3},{1,0},{2,1},{3,2},{4,7},{5,4},{6,5},{7,6},{8,11},{9,8},{10,9... | collective-permute-start | bytes 1572872 | tf_op jit(solution)/shard_map/ppermute | solution.py:719
  554.2 38.8 %collective-permute-start.27 = (bf16[256,1024]{1,0:T(8,128)(2,1)S(1)}, bf16[256,1024]{1,0:T(8,128)(2,1)S(1)}, u32[]{:S(2)}, u32[]{:S(2)}) collective-permute-start(bf16[256,1024]{1,0:T(8,128)(2,1)S(1)} %get-tuple-element.242.refs_0_), channel_id=1, source_target_pairs={{0,1},{1,2},{2,3},{3,0},{4,5},{5,6},{6,7},{7,4},{8,9},{9,10},{10,1... | collective-permute-start | bytes 1572872 | tf_op jit(solution)/shard_map/ppermute | solution.py:719
  562.4 30.5 %collective-permute-start.28 = (bf16[256,1024]{1,0:T(8,128)(2,1)S(1)}, bf16[256,1024]{1,0:T(8,128)(2,1)S(1)}, u32[]{:S(2)}, u32[]{:S(2)}) collective-permute-start(bf16[256,1024]{1,0:T(8,128)(2,1)S(1)} %get-tuple-element.242.refs_0_), channel_id=1, source_target_pairs={{0,3},{1,0},{2,1},{3,2},{4,7},{5,4},{6,5},{7,6},{8,11},{9,8},{10,9... | collective-permute-start | bytes 1572872 | tf_op jit(solution)/shard_map/ppermute | solution.py:719
  594.4 35.6 %collective-permute-start.35 = (bf16[256,1024]{1,0:T(8,128)(2,1)S(1)}, bf16[256,1024]{1,0:T(8,128)(2,1)}, u32[]{:S(2)}, u32[]{:S(2)}) collective-permute-start(bf16[256,1024]{1,0:T(8,128)(2,1)S(1)} %copy-done.8), channel_id=1, source_target_pairs={{0,2},{1,3},{2,0},{3,1},{4,6},{5,7},{6,4},{7,5},{8,10},{9,11},{10,... | collective-permute-start | bytes 1572872 | tf_op jit(solution)/shard_map/ppermute | solution.py:719
  600.1 35.6 %collective-permute-start.29 = (bf16[128,1024]{1,0:T(8,128)(2,1)S(1)}, bf16[128,1024]{1,0:T(8,128)(2,1)S(1)}, u32[]{:S(2)}, u32[]{:S(2)}) collective-permute-start(bf16[128,1024]{1,0:T(8,128)(2,1)S(1)} %get-tuple-element.273), channel_id=1, source_target_pairs={{0,1},{1,2},{2,3},{3,0},{4,5},{5,6},{6,7},{7,4},{8,9},{9,10},{10,1... | collective-permute-start | bytes 786440 | tf_op jit(solution)/shard_map/ppermute | solution.py:719
  602.1 33.6 %collective-permute-start.30 = (bf16[128,1024]{1,0:T(8,128)(2,1)S(1)}, bf16[128,1024]{1,0:T(8,128)(2,1)S(1)}, u32[]{:S(2)}, u32[]{:S(2)}) collective-permute-start(bf16[128,1024]{1,0:T(8,128)(2,1)S(1)} %get-tuple-element.275), channel_id=1, source_target_pairs={{0,2},{1,3},{2,0},{3,1},{4,6},{5,7},{6,4},{7,5},{8,10},{9,11},{10,... | collective-permute-start | bytes 786440 | tf_op jit(solution)/shard_map/ppermute | solution.py:719
  602.7 33.0 %collective-permute-start.31 = (bf16[128,1024]{1,0:T(8,128)(2,1)S(1)}, bf16[128,1024]{1,0:T(8,128)(2,1)S(1)}, u32[]{:S(2)}, u32[]{:S(2)}) collective-permute-start(bf16[128,1024]{1,0:T(8,128)(2,1)S(1)} %get-tuple-element.274), channel_id=1, source_target_pairs={{0,3},{1,0},{2,1},{3,2},{4,7},{5,4},{6,5},{7,6},{8,11},{9,8},{10,9... | collective-permute-start | bytes 786440 | tf_op jit(solution)/shard_map/ppermute | solution.py:719
  636.1 14.1 %collective-permute-start.32 = (bf16[128,1024]{1,0:T(8,128)(2,1)S(1)}, bf16[128,1024]{1,0:T(8,128)(2,1)S(1)}, u32[]{:S(2)}, u32[]{:S(2)}) collective-permute-start(bf16[128,1024]{1,0:T(8,128)(2,1)S(1)} %get-tuple-element.244), channel_id=1, source_target_pairs={{0,1},{1,2},{2,3},{3,0},{4,5},{5,6},{6,7},{7,4},{8,9},{9,10},{10,1... | collective-permute-start | bytes 786440 | tf_op jit(solution)/shard_map/ppermute | solution.py:719
  642.0 18.8 %collective-permute-start.33 = (bf16[128,1024]{1,0:T(8,128)(2,1)S(1)}, bf16[128,1024]{1,0:T(8,128)(2,1)S(1)}, u32[]{:S(2)}, u32[]{:S(2)}) collective-permute-start(bf16[128,1024]{1,0:T(8,128)(2,1)S(1)} %get-tuple-element.244), channel_id=1, source_target_pairs={{0,2},{1,3},{2,0},{3,1},{4,6},{5,7},{6,4},{7,5},{8,10},{9,11},{10,... | collective-permute-start | bytes 786440 | tf_op jit(solution)/shard_map/ppermute | solution.py:719
  643.5 17.3 %collective-permute-start.34 = (bf16[128,1024]{1,0:T(8,128)(2,1)S(1)}, bf16[128,1024]{1,0:T(8,128)(2,1)S(1)}, u32[]{:S(2)}, u32[]{:S(2)}) collective-permute-start(bf16[128,1024]{1,0:T(8,128)(2,1)S(1)} %get-tuple-element.244), channel_id=1, source_target_pairs={{0,3},{1,0},{2,1},{3,2},{4,7},{5,4},{6,5},{7,6},{8,11},{9,8},{10,9... | collective-permute-start | bytes 786440 | tf_op jit(solution)/shard_map/ppermute | solution.py:719
  667.0 12.0 %collective-permute-start.36 = (bf16[136,1024]{1,0:T(8,128)(2,1)S(1)}, bf16[136,1024]{1,0:T(8,128)(2,1)S(1)}, u32[]{:S(2)}, u32[]{:S(2)}) collective-permute-start(bf16[136,1024]{1,0:T(8,128)(2,1)S(1)} %get-tuple-element.266), channel_id=1, source_target_pairs={{0,1},{1,2},{2,3},{3,0},{4,5},{5,6},{6,7},{7,4},{8,9},{9,10},{10,1... | collective-permute-start | bytes 835592 | tf_op jit(solution)/shard_map/ppermute | solution.py:719
  670.4 19.5 %collective-permute-start.37 = (bf16[136,1024]{1,0:T(8,128)(2,1)S(1)}, bf16[136,1024]{1,0:T(8,128)(2,1)S(1)}, u32[]{:S(2)}, u32[]{:S(2)}) collective-permute-start(bf16[136,1024]{1,0:T(8,128)(2,1)S(1)} %get-tuple-element.268), channel_id=1, source_target_pairs={{0,2},{1,3},{2,0},{3,1},{4,6},{5,7},{6,4},{7,5},{8,10},{9,11},{10,... | collective-permute-start | bytes 835592 | tf_op jit(solution)/shard_map/ppermute | solution.py:719
  671.9 17.9 %collective-permute-start.38 = (bf16[136,1024]{1,0:T(8,128)(2,1)S(1)}, bf16[136,1024]{1,0:T(8,128)(2,1)S(1)}, u32[]{:S(2)}, u32[]{:S(2)}) collective-permute-start(bf16[136,1024]{1,0:T(8,128)(2,1)S(1)} %get-tuple-element.267), channel_id=1, source_target_pairs={{0,3},{1,0},{2,1},{3,2},{4,7},{5,4},{6,5},{7,6},{8,11},{9,8},{10,9... | collective-permute-start | bytes 835592 | tf_op jit(solution)/shard_map/ppermute | solution.py:719
  691.1 15.4 %collective-permute-start.39 = (bf16[136,1024]{1,0:T(8,128)(2,1)S(1)}, bf16[136,1024]{1,0:T(8,128)(2,1)S(1)}, u32[]{:S(2)}, u32[]{:S(2)}) collective-permute-start(bf16[136,1024]{1,0:T(8,128)(2,1)S(1)} %get-tuple-element.240), channel_id=1, source_target_pairs={{0,1},{1,2},{2,3},{3,0},{4,5},{5,6},{6,7},{7,4},{8,9},{9,10},{10,1... | collective-permute-start | bytes 835592 | tf_op jit(solution)/shard_map/ppermute | solution.py:719
  697.6 19.6 %collective-permute-start.40 = (bf16[136,1024]{1,0:T(8,128)(2,1)S(1)}, bf16[136,1024]{1,0:T(8,128)(2,1)S(1)}, u32[]{:S(2)}, u32[]{:S(2)}) collective-permute-start(bf16[136,1024]{1,0:T(8,128)(2,1)S(1)} %get-tuple-element.240), channel_id=1, source_target_pairs={{0,2},{1,3},{2,0},{3,1},{4,6},{5,7},{6,4},{7,5},{8,10},{9,11},{10,... | collective-permute-start | bytes 835592 | tf_op jit(solution)/shard_map/ppermute | solution.py:719
  699.4 17.9 %collective-permute-start.41 = (bf16[136,1024]{1,0:T(8,128)(2,1)S(1)}, bf16[136,1024]{1,0:T(8,128)(2,1)S(1)}, u32[]{:S(2)}, u32[]{:S(2)}) collective-permute-start(bf16[136,1024]{1,0:T(8,128)(2,1)S(1)} %get-tuple-element.240), channel_id=1, source_target_pairs={{0,3},{1,0},{2,1},{3,2},{4,7},{5,4},{6,5},{7,6},{8,11},{9,8},{10,9... | collective-permute-start | bytes 835592 | tf_op jit(solution)/shard_map/ppermute | solution.py:719
  (47 other events, 318.3 us)
Sparse Core Ops, SparseCore 0:
  10.7 57.2 all-gather.8
  70.4 54.3 all-gather.10
  126.7 89.8 all-gather.12
  375.2 116.3 reduce-scatter.3
  494.9 71.2 reduce-scatter.5
  593.1 72.6 reduce-scatter.7

commit v8 on v7

--- a/solution.py
+++ b/solution.py
@@ -877,8 +877,9 @@
     ).astype(bf16).reshape(clips, -1)
     extra = 8 * pieces - 4 * own % (8 * pieces)
     small_grads = jnp.pad(small_grads, ((0, 0), (0, extra * 1024 - small_grads.shape[1]))).reshape(clips, extra, 1024)
+    block_out = call_assemble(place, pieces_out)
     space_grad = weight_grad(
-        [ff_half], [(pick(forward, 0), pick(last, 0)), (pick(forward, 2), pick(last, 1))],
+        [ff_half, block_out], [(pick(forward, 0), pick(last, 0)), (pick(forward, 2), pick(last, 1))],
         clips, 4 * own + extra, "space_grad", small=small_grads,
     )
 
@@ -888,7 +889,7 @@
     ff_sum = joined(ff_shared)
     time_sum = joined(share(sum_half(time_part)))
     early = (
-        call_assemble(place, pieces_out),
+        block_out,
         columns(time_sum, own, 0, 3),
         columns(time_sum, own, 3, 1),
         columns(ff_sum, own, 0, 4),

time: 742 us -> 741 us (level)
  transfers between devices with their start and end apart: 48 -> 48, of which waited for: 12 -> 12; matrix products, arithmetic and copies ran while one was open for 6% -> 5% of each run, Pallas kernels for 57% -> 57%
where the time goes in v8:
time: 741 us; the launch traced here: 729 us
  Pallas kernels  415 us (56%)
  waiting for transfers between devices  135 us (18%)
  starting transfers between devices  95.7 us (13%)
  local copies, waits for them, and re-layouts  32 us (4%)
  other arithmetic  26.1 us (4%)
  between operations  15.3 us (2%)
  blocking collectives  9.16 us (1%)
    pallas_call x15, Pallas kernels, ordered_call(): return lambda *operands: call(*behind, *operands)  415 us
    ppermute x18, waiting for transfers between devices, shift(): lax.ppermute(values, 'tm', [(k, (k + step) % count) for k in range(count)])  76.6 us
    ppermute x18, starting transfers between devices, shift(): lax.ppermute(values, 'tm', [(k, (k + step) % count) for k in range(count)])  44.2 us
    ppermute x12, starting transfers between devices, local(): lax.ppermute(parts[d], 'tm', [(k, (k + d) % pieces) for k in range(pieces)])  32.6 us
    all_gather x3, waiting for transfers between devices, gather(): lax.all_gather(jnp.concatenate(parts, axis=0), 'clip', axis=0, tiled=False)  26.5 us
    ppermute x12, waiting for transfers between devices, local(): lax.ppermute(parts[d], 'tm', [(k, (k + d) % pieces) for k in range(pieces)])  22.7 us
    ppermute x12, starting transfers between devices, local(): lax.ppermute(parts[d], 'tm', [(k, (k - d) % pieces) for k in range(pieces)])  18.7 us
  transfers between devices with their start and end apart: 48, of which 12 were waited for; matrix products, arithmetic and copies ran while one was open for 5% of the time, Pallas kernels for 57%

profile of v8, /device:TPU:0, one launch (start us, length us, event | category | flops | bytes accessed | tf_op | source)
XLA Modules:
  0.0 728.7 jit_solution(13133573364141677565)
XLA Ops:
  14.8 4.1 fusion.26
  20.4 3.0 collective-permute-start
  23.4 2.6 collective-permute-start.1
  27.6 9.2 %all-gather.4 = bf16[8,19,128]{2,1,0:T(8,128)(2,1)S(1)} all-gather(bf16[1,19,128]{2,1,0:T(8,128)(2,1)S(1)} %bitcast.115), channel_id=2, replica_groups=mesh['clip'=8,'tm'=4] {'clip'}, dimensions={0}, use_global_device_ids=true | all-gather | bytes 43776 | tf_op jit(solution)/shard_map/all_gather | solution.py:779
  43.0 24.9 %all-gather.9.cloned.1.call-done = bf16[4096,1024]{1,0:T(8,128)(2,1)} async-done(((bf16[512,1024]{1,0:T(8,128)(2,1)}), bf16[4096,1024]{1,0:T(8,128)(2,1)}) %all-gather.9.cloned.1.call-update) | async-done | bytes 8388624 | tf_op jit(solution)/shard_map/all_gather | solution.py:710
  68.0 23.7 %space_forward.2 = (bf16[4,256,1024]{2,1,0:T(8,128)(2,1)}, bf16[4,256,3072]{2,1,0:T(8,128)(2,1)}, bf16[4,256,1024]{2,1,0:T(8,128)(2,1)}, f32[4,16,256]{2,1,0:T(8...) custom-call(s32[1]{0:T(128)} %bitcast.refs_0_.refs_4_.refs_5_, ...), custom_call_target="tpu_custom_call" | custom-call | tf_op jit(solution)/shard_map/space_forward/pallas_call | solution.py:377
  94.8 2.4 collective-permute-start.4
  99.5 23.8 %space_forward.3 = (bf16[4,256,1024]{2,1,0:T(8,128)(2,1)}, bf16[4,256,3072]{2,1,0:T(8,128)(2,1)}, bf16[4,256,1024]{2,1,0:T(8,128)(2,1)}, f32[4,16,256]{2,1,0:T(8...) custom-call(f32[4,16,256]{2,1,0:T(8,128)} %get-tuple-element.126.ref, ...), custom_call_target="tpu_custom_call" | custom-call | tf_op jit(solution)/shard_map/space_forward/pallas_call | solution.py:377
  125.8 2.5 collective-permute-start.8
  129.9 22.6 %collective-permute-done.4.refs_6_.refs_3_ = bf16[4,64,1024]{2,1,0:T(8,128)(2,1)} collective-permute-done((bf16[4,64,1024]{2,1,0:T(8,128)(2,1)}, bf16[4,64,1024]{2,1,0:T(8,128)(2,1)}, u32[]{:S(2)}, u32[]{:S(2)}) %collective-permute-start.4) | collective-permute-done | bytes 524320 | tf_op jit(solution)/shard_map/ppermute | solution.py:799
  152.5 22.9 %time_forward.2 = (bf16[4,256,1024]{2,1,0:T(8,128)(2,1)}, bf16[4,256,3072]{2,1,0:T(8,128)(2,1)}, bf16[4,256,1024]{2,1,0:T(8,128)(2,1)}, f32[4,16,256]{2,1,0:T(8,...) custom-call(f32[4,16,256]{2,1,0:T(8,128)} %get-tuple-element.127.refs_0_.refs_14_, ...), custom_call_target="tpu_custom_call" | custom-call | tf_op jit(solution)/shard_map/time_forward/pallas_call | solution.py:377
  176.3 22.9 %time_forward.3 = (bf16[4,256,1024]{2,1,0:T(8,128)(2,1)}, bf16[4,256,3072]{2,1,0:T(8,128)(2,1)}, bf16[4,256,1024]{2,1,0:T(8,128)(2,1)}, f32[4,16,256]{2,1,0:T(8,...) custom-call(f32[4,16,256]{2,1,0:T(8,128)} %get-tuple-element.132.refs_0_.refs_11_, ...), custom_call_target="tpu_custom_call" | custom-call | tf_op jit(solution)/shard_map/time_forward/pallas_call | solution.py:377
  199.3 11.5 %collective-permute-start.10 = (bf16[4,64,1024]{2,1,0:T(8,128)(2,1)}, bf16[4,64,1024]{2,1,0:T(8,128)(2,1)S(1)}, u32[]{:S(2)}, u32[]{:S(2)}) collective-permute-start(bf16[4,64,1024]{2,1,0:T(8,128)(2,1)} %get-tuple-element.144), channel_id=1, source_target_pairs={{0,2},{1,3},{2,0},{3,1},{4,6},{5,7},{6,4},{7,5},{8,10},{9,11},{10,... | collective-permute-start | bytes 1572872 | tf_op jit(solution)/shard_map/ppermute | solution.py:799
  211.4 3.3 collective-permute-start.11
  216.6 50.8 %feed_forward.2 = (bf16[4,256,1024]{2,1,0:T(8,128)(2,1)}, bf16[4,256,4096]{2,1,0:T(8,128)(2,1)}, bf16[4,256,4096]{2,1,0:T(8,128)(2,1)}, bf16[4,256,1024]{2,1,0:T...) custom-call(f32[4,16,256]{2,1,0:T(8,128)} %get-tuple-element.137.ref, ...), custom_call_target="tpu_custom_call" | custom-call | tf_op jit(solution)/shard_map/feed_forward/pallas_call | solution.py:377
  267.5 3.4 collective-permute-start.12
  272.9 50.8 %feed_forward.3 = (bf16[4,256,1024]{2,1,0:T(8,128)(2,1)}, bf16[4,256,4096]{2,1,0:T(8,128)(2,1)}, bf16[4,256,4096]{2,1,0:T(8,128)(2,1)}, bf16[4,256,1024]{2,1,0:T...) custom-call(f32[1,1024]{1,0:T(1,128)} %get-tuple-element.140.refs_0_, ...), custom_call_target="tpu_custom_call" | custom-call | tf_op jit(solution)/shard_map/feed_forward/pallas_call | solution.py:377
  323.8 2.8 collective-permute-start.15
  329.0 22.9 %down_grad.1.refs_4_ = bf16[8,1024,1024]{2,1,0:T(8,128)(2,1)} custom-call(f32[1,1024]{1,0:T(1,128)} %get-tuple-element.150.refs_0_, bf16[4,64,1024]{2,1,0:T(8,128)(2,1)} %copy-done.4, bf16[4,64,1024]{2,1,0:T(8,128)(2,1)} %copy-done.5, bf16[4,64,1024]{2,1,0:T(8,128)(2,1)} %copy-done.6, bf16[4,256,4096]{2,1,0:T(8,128)(2,1)} %get-tuple-element.154.refs_4_, ...), custom_call_target="tpu_custom_call" | custom-call | tf_op jit(solution)/shard_map/down_grad/pallas_call | solution.py:377
  351.9 23.2 %hidden_grad.1.refs_0_ = bf16[8,1024,1024]{2,1,0:T(8,128)(2,1)} custom-call(bf16[4,256,1024]{2,1,0:T(8,128)(2,1)} %get-tuple-element.139.refs_0_, bf16[4,256,1024]{2,1,0:T(8,128)(2,1)} %get-tuple-element.147.refs_1_, bf16[4,256,4096]{2,1,0:T(8,128)(2,1)} %get-tuple-element.148.refs_2_, ...), custom_call_target="tpu_custom_call", output_to_operand_aliasing={{}: (4, {})} | custom-call | tf_op jit(solution)/shard_map/hidden_grad/pallas_call | solution.py:377
  375.2 27.0 %time_backward.2 = (bf16[4,256,3072]{2,1,0:T(8,128)(2,1)}, f32[1,1024]{1,0:T(1,128)}, f32[1,1024]{1,0:T(1,128)}, bf16[4,64,1024]{2,1,0:T(8,128)(2,1)}, bf16[4,64...) custom-call(bf16[8,1024,1024]{2,1,0:T(8,128)(2,1)} %hidden_grad.1.refs_0_, ...), custom_call_target="tpu_custom_call" | custom-call | tf_op jit(solution)/shard_map/time_backward/pallas_call | solution.py:377
  402.3 3.8 collective-permute-start.18
  407.0 27.1 %time_backward.3 = (bf16[4,256,3072]{2,1,0:T(8,128)(2,1)}, f32[1,1024]{1,0:T(1,128)}, f32[1,1024]{1,0:T(1,128)}, bf16[4,64,1024]{2,1,0:T(8,128)(2,1)}, bf16[4,64...) custom-call(f32[1,1024]{1,0:T(1,128)} %get-tuple-element.167.refs_0_, ...), custom_call_target="tpu_custom_call" | custom-call | tf_op jit(solution)/shard_map/time_backward/pallas_call | solution.py:377
  434.1 26.2 %time_grad.1.refs_0_ = bf16[8,512,1024]{2,1,0:T(8,128)(2,1)} custom-call(f32[1,1024]{1,0:T(1,128)} %get-tuple-element.172.refs_0_, bf16[4,256,1024]{2,1,0:T(8,128)(2,1)} %get-tuple-element.173.refs_1_, bf16[4,256,1024]{2,1,0:T(8,128)(2,1)} %get-tuple-element.174.refs_2_, bf16[4,256,3072]{2,1,0:T(8,128)(2,1)} %get-tuple-element.175.refs_3_, ...), custom_call_target="tpu_custom_call" | custom-call | tf_op jit(solution)/shard_map/time_grad/pallas_call | solution.py:377
  461.6 3.1 collective-permute-start.21
  466.9 4.8 assemble.1.refs_1_
  471.8 31.1 %space_backward.2 = (bf16[4,256,3072]{2,1,0:T(8,128)(2,1)}, bf16[4,256,1024]{2,1,0:T(8,128)(2,1)}, f32[2,4,256,1024]{3,2,1,0:T(8,128)}, f32[1,1024]{1,0:T(1,128)...) custom-call(bf16[8,512,1024]{2,1,0:T(8,128)(2,1)} %time_grad.1.refs_0_, bf16[4,64,1024]{2,1,0:T(8,128)(2,1)} %get-tuple-element.182.refs_1_, ...), custom_call_target="tpu_custom_call" | custom-call | tf_op jit(solution)/shard_map/space_backward/pallas_call | solution.py:377
  502.9 6.3 collective-permute-done.22.refs_3_
  513.3 3.0 collective-permute-start.26
  516.3 31.4 %space_backward.3 = (bf16[4,256,3072]{2,1,0:T(8,128)(2,1)}, bf16[4,256,1024]{2,1,0:T(8,128)(2,1)}, f32[2,4,256,1024]{3,2,1,0:T(8,128)}, f32[1,1024]{1,0:T(1,128)...) custom-call(bf16[1024,1024]{1,0:T(8,128)(2,1)} %bitcast.103, ...), custom_call_target="tpu_custom_call", output_to_operand_aliasing={{2}: (15, {})} | custom-call | tf_op jit(solution)/shard_map/space_backward/pallas_call | solution.py:377
  551.5 2.8 constant_dynamic-update-slice_fusion.12
  554.3 8.2 %collective-permute-start.27 = (bf16[256,1024]{1,0:T(8,128)(2,1)S(1)}, bf16[256,1024]{1,0:T(8,128)(2,1)S(1)}, u32[]{:S(2)}, u32[]{:S(2)}) collective-permute-start(bf16[256,1024]{1,0:T(8,128)(2,1)S(1)} %get-tuple-element.242.refs_0_), channel_id=1, source_target_pairs={{0,1},{1,2},{2,3},{3,0},{4,5},{5,6},{6,7},{7,4},{8,9},{9,10},{10,1... | collective-permute-start | bytes 1572872 | tf_op jit(solution)/shard_map/ppermute | solution.py:719
  562.5 2.8 collective-permute-start.28
  566.5 26.5 %space_grad.1 = bf16[8,544,1024]{2,1,0:T(8,128)(2,1)} custom-call(bf16[256,1024]{1,0:T(8,128)(2,1)} %copy-done.7, bf16[2,4,256,1024]{3,2,1,0:T(8,128)(2,1)} %assemble.1.refs_1_, bf16[4,256,1024]{2,1,0:T(8,128)(2,1)} %get-tuple-element.200.refs_2_, bf16[4,256,1024]{2,1,0:T(8,128)(2,1)} %get-tuple-element.201.refs_3_, ...), custom_call_target="tpu_custom_call" | custom-call | tf_op jit(solution)/shard_map/space_grad/pallas_call | solution.py:377
  594.8 2.1 collective-permute-start.29
  597.2 2.8 collective-permute-start.31
  600.9 28.8 %collective-permute-done.35 = bf16[256,1024]{1,0:T(8,128)(2,1)} collective-permute-done((bf16[256,1024]{1,0:T(8,128)(2,1)S(1)}, bf16[256,1024]{1,0:T(8,128)(2,1)}, u32[]{:S(2)}, u32[]{:S(2)}) %collective-permute-start.35) | collective-permute-done | bytes 524320 | tf_op jit(solution)/shard_map/ppermute | solution.py:719
  635.8 5.9 collective-permute-start.32
  644.1 2.8 slice_convert_fusion
  646.9 3.0 collective-permute-done.32
  650.0 10.6 %collective-permute-done.33 = bf16[128,1024]{1,0:T(8,128)(2,1)S(1)} collective-permute-done((bf16[128,1024]{1,0:T(8,128)(2,1)S(1)}, bf16[128,1024]{1,0:T(8,128)(2,1)S(1)}, u32[]{:S(2)}, u32[]{:S(2)}) %collective-permute-start.33) | collective-permute-done | bytes 262176 | tf_op jit(solution)/shard_map/ppermute | solution.py:719
  662.8 3.0 reduce-scatter.8.cloned.1.call-done
  667.0 3.1 collective-permute-start.36
  672.6 6.1 collective-permute-done.36
  678.7 10.8 %collective-permute-done.37 = bf16[136,1024]{1,0:T(8,128)(2,1)S(1)} collective-permute-done((bf16[136,1024]{1,0:T(8,128)(2,1)S(1)}, bf16[136,1024]{1,0:T(8,128)(2,1)S(1)}, u32[]{:S(2)}, u32[]{:S(2)}) %collective-permute-start.37) | collective-permute-done | bytes 278560 | tf_op jit(solution)/shard_map/ppermute | solution.py:719
  690.8 6.5 collective-permute-start.39
  699.7 6.5 collective-permute-done.39
  706.3 10.7 %collective-permute-done.40 = bf16[136,1024]{1,0:T(8,128)(2,1)S(1)} collective-permute-done((bf16[136,1024]{1,0:T(8,128)(2,1)S(1)}, bf16[136,1024]{1,0:T(8,128)(2,1)S(1)}, u32[]{:S(2)}, u32[]{:S(2)}) %collective-permute-start.40) | collective-permute-done | bytes 278560 | tf_op jit(solution)/shard_map/ppermute | solution.py:719
  (246 shorter events, 73.0 us)
Async XLA Ops:
  7.2 60.8 %all-gather.9.cloned.1.call-start = ((), (), s32[]{:S(2)}) async-start(), calls=%async_computation.6 | async-start | bytes 9437184 | tf_op jit(solution)/shard_map/all_gather | solution.py:710
  10.5 119.3 %all-gather.11.cloned.1.call-start = ((), (), s32[]{:S(2)}) async-start(), calls=%async_computation.7 | async-start | bytes 9437184 | tf_op jit(solution)/shard_map/all_gather | solution.py:710
  11.7 204.9 %all-gather.13.cloned.1.call-start = ((), (), s32[]{:S(2)}) async-start(), calls=%async_computation.8 | async-start | bytes 18874368 | tf_op jit(solution)/shard_map/all_gather | solution.py:710
  14.7 494.6 %reduce-scatter.4.cloned.1.call-start = ((), (), s32[]{:S(2)}) async-start(), calls=%async_computation.3 | async-start | bytes 18874368 | tf_op jit(solution)/shard_map/reduce_scatter | solution.py:714
  20.4 76.8 %collective-permute-start = (bf16[4,64,1024]{2,1,0:T(8,128)(2,1)}, bf16[4,64,1024]{2,1,0:T(8,128)(2,1)S(1)}, u32[]{:S(2)}, u32[]{:S(2)}) collective-permute-start(bf16[4,64,1024]{2,1,0:T(8,128)(2,1)} %get-tuple-element.261), channel_id=1, source_target_pairs={{0,1},{1,2},{2,3},{3,0},{4,5},{5,6},{6,7},{7,4},{8,9},{9,10},{10,1... | collective-permute-start | bytes 1572872 | tf_op jit(solution)/shard_map/ppermute | solution.py:799
  23.4 75.3 %collective-permute-start.1 = (bf16[4,64,1024]{2,1,0:T(8,128)(2,1)}, bf16[4,64,1024]{2,1,0:T(8,128)(2,1)S(1)}, u32[]{:S(2)}, u32[]{:S(2)}) collective-permute-start(bf16[4,64,1024]{2,1,0:T(8,128)(2,1)} %get-tuple-element.260), channel_id=1, source_target_pairs={{0,2},{1,3},{2,0},{3,1},{4,6},{5,7},{6,4},{7,5},{8,10},{9,11},{10,... | collective-permute-start | bytes 1572872 | tf_op jit(solution)/shard_map/ppermute | solution.py:799
  26.0 72.7 %collective-permute-start.2 = (bf16[4,64,1024]{2,1,0:T(8,128)(2,1)}, bf16[4,64,1024]{2,1,0:T(8,128)(2,1)}, u32[]{:S(2)}, u32[]{:S(2)}) collective-permute-start(bf16[4,64,1024]{2,1,0:T(8,128)(2,1)} %get-tuple-element.259), channel_id=1, source_target_pairs={{0,3},{1,0},{2,1},{3,2},{4,7},{5,4},{6,5},{7,6},{8,11},{9,8},{10,9... | collective-permute-start | bytes 1572872 | tf_op jit(solution)/shard_map/ppermute | solution.py:799
  91.7 34.2 %collective-permute-start.3 = (bf16[4,64,1024]{2,1,0:T(8,128)(2,1)}, bf16[4,64,1024]{2,1,0:T(8,128)(2,1)S(1)}, u32[]{:S(2)}, u32[]{:S(2)}) collective-permute-start(bf16[4,64,1024]{2,1,0:T(8,128)(2,1)} %get-tuple-element.129), channel_id=1, source_target_pairs={{0,1},{1,2},{2,3},{3,0},{4,5},{5,6},{6,7},{7,4},{8,9},{9,10},{10,1... | collective-permute-start | bytes 1572872 | tf_op jit(solution)/shard_map/ppermute | solution.py:799
  94.8 57.6 %collective-permute-start.4 = (bf16[4,64,1024]{2,1,0:T(8,128)(2,1)}, bf16[4,64,1024]{2,1,0:T(8,128)(2,1)}, u32[]{:S(2)}, u32[]{:S(2)}) collective-permute-start(bf16[4,64,1024]{2,1,0:T(8,128)(2,1)} %get-tuple-element.130), channel_id=1, source_target_pairs={{0,2},{1,3},{2,0},{3,1},{4,6},{5,7},{6,4},{7,5},{8,10},{9,11},{10,... | collective-permute-start | bytes 1572872 | tf_op jit(solution)/shard_map/ppermute | solution.py:799
  97.3 55.2 %collective-permute-start.5 = (bf16[4,64,1024]{2,1,0:T(8,128)(2,1)}, bf16[4,64,1024]{2,1,0:T(8,128)(2,1)}, u32[]{:S(2)}, u32[]{:S(2)}) collective-permute-start(bf16[4,64,1024]{2,1,0:T(8,128)(2,1)} %get-tuple-element.131), channel_id=1, source_target_pairs={{0,3},{1,0},{2,1},{3,2},{4,7},{5,4},{6,5},{7,6},{8,11},{9,8},{10,9... | collective-permute-start | bytes 1572872 | tf_op jit(solution)/shard_map/ppermute | solution.py:799
  123.3 52.1 %collective-permute-start.6 = (bf16[4,64,1024]{2,1,0:T(8,128)(2,1)}, bf16[4,64,1024]{2,1,0:T(8,128)(2,1)S(1)}, u32[]{:S(2)}, u32[]{:S(2)}) collective-permute-start(bf16[4,64,1024]{2,1,0:T(8,128)(2,1)} %get-tuple-element.134), channel_id=1, source_target_pairs={{0,1},{1,2},{2,3},{3,0},{4,5},{5,6},{6,7},{7,4},{8,9},{9,10},{10,1... | collective-permute-start | bytes 1572872 | tf_op jit(solution)/shard_map/ppermute | solution.py:799
  124.6 50.8 %collective-permute-start.7 = (bf16[4,64,1024]{2,1,0:T(8,128)(2,1)}, bf16[4,64,1024]{2,1,0:T(8,128)(2,1)S(1)}, u32[]{:S(2)}, u32[]{:S(2)}) collective-permute-start(bf16[4,64,1024]{2,1,0:T(8,128)(2,1)} %get-tuple-element.135), channel_id=1, source_target_pairs={{0,2},{1,3},{2,0},{3,1},{4,6},{5,7},{6,4},{7,5},{8,10},{9,11},{10,... | collective-permute-start | bytes 1572872 | tf_op jit(solution)/shard_map/ppermute | solution.py:799
  125.8 49.6 %collective-permute-start.8 = (bf16[4,64,1024]{2,1,0:T(8,128)(2,1)}, bf16[4,64,1024]{2,1,0:T(8,128)(2,1)}, u32[]{:S(2)}, u32[]{:S(2)}) collective-permute-start(bf16[4,64,1024]{2,1,0:T(8,128)(2,1)} %get-tuple-element.136), channel_id=1, source_target_pairs={{0,3},{1,0},{2,1},{3,2},{4,7},{5,4},{6,5},{7,6},{8,11},{9,8},{10,9... | collective-permute-start | bytes 1572872 | tf_op jit(solution)/shard_map/ppermute | solution.py:799
  199.3 71.6 %collective-permute-start.10 = (bf16[4,64,1024]{2,1,0:T(8,128)(2,1)}, bf16[4,64,1024]{2,1,0:T(8,128)(2,1)S(1)}, u32[]{:S(2)}, u32[]{:S(2)}) collective-permute-start(bf16[4,64,1024]{2,1,0:T(8,128)(2,1)} %get-tuple-element.144), channel_id=1, source_target_pairs={{0,2},{1,3},{2,0},{3,1},{4,6},{5,7},{6,4},{7,5},{8,10},{9,11},{10,... | collective-permute-start | bytes 1572872 | tf_op jit(solution)/shard_map/ppermute | solution.py:799
  211.4 61.5 %collective-permute-start.11 = (bf16[4,64,1024]{2,1,0:T(8,128)(2,1)}, bf16[4,64,1024]{2,1,0:T(8,128)(2,1)}, u32[]{:S(2)}, u32[]{:S(2)}) collective-permute-start(bf16[4,64,1024]{2,1,0:T(8,128)(2,1)} %get-tuple-element.145), channel_id=1, source_target_pairs={{0,3},{1,0},{2,1},{3,2},{4,7},{5,4},{6,5},{7,6},{8,11},{9,8},{10,9... | collective-permute-start | bytes 1572872 | tf_op jit(solution)/shard_map/ppermute | solution.py:799
  214.7 58.2 %collective-permute-start.9 = (bf16[4,64,1024]{2,1,0:T(8,128)(2,1)}, bf16[4,64,1024]{2,1,0:T(8,128)(2,1)}, u32[]{:S(2)}, u32[]{:S(2)}) collective-permute-start(bf16[4,64,1024]{2,1,0:T(8,128)(2,1)} %get-tuple-element.143), channel_id=1, source_target_pairs={{0,1},{1,2},{2,3},{3,0},{4,5},{5,6},{6,7},{7,4},{8,9},{9,10},{10,1... | collective-permute-start | bytes 1572872 | tf_op jit(solution)/shard_map/ppermute | solution.py:799
  267.5 60.2 %collective-permute-start.12 = (bf16[4,64,1024]{2,1,0:T(8,128)(2,1)}, bf16[4,64,1024]{2,1,0:T(8,128)(2,1)S(1)}, u32[]{:S(2)}, u32[]{:S(2)}) collective-permute-start(bf16[4,64,1024]{2,1,0:T(8,128)(2,1)} %get-tuple-element.151), channel_id=1, source_target_pairs={{0,3},{1,0},{2,1},{3,2},{4,7},{5,4},{6,5},{7,6},{8,11},{9,8},{10,9... | collective-permute-start | bytes 1572872 | tf_op jit(solution)/shard_map/ppermute | solution.py:802
  270.8 57.1 %collective-permute-start.13 = (bf16[4,64,1024]{2,1,0:T(8,128)(2,1)}, bf16[4,64,1024]{2,1,0:T(8,128)(2,1)S(1)}, u32[]{:S(2)}, u32[]{:S(2)}) collective-permute-start(bf16[4,64,1024]{2,1,0:T(8,128)(2,1)} %get-tuple-element.152), channel_id=1, source_target_pairs={{0,2},{1,3},{2,0},{3,1},{4,6},{5,7},{6,4},{7,5},{8,10},{9,11},{10,... | collective-permute-start | bytes 1572872 | tf_op jit(solution)/shard_map/ppermute | solution.py:802
  271.7 56.3 %collective-permute-start.14 = (bf16[4,64,1024]{2,1,0:T(8,128)(2,1)}, bf16[4,64,1024]{2,1,0:T(8,128)(2,1)S(1)}, u32[]{:S(2)}, u32[]{:S(2)}) collective-permute-start(bf16[4,64,1024]{2,1,0:T(8,128)(2,1)} %get-tuple-element.153), channel_id=1, source_target_pairs={{0,1},{1,2},{2,3},{3,0},{4,5},{5,6},{6,7},{7,4},{8,9},{9,10},{10,1... | collective-permute-start | bytes 1572872 | tf_op jit(solution)/shard_map/ppermute | solution.py:802
  323.8 51.4 %collective-permute-start.15 = (bf16[4,64,1024]{2,1,0:T(8,128)(2,1)}, bf16[4,64,1024]{2,1,0:T(8,128)(2,1)}, u32[]{:S(2)}, u32[]{:S(2)}) collective-permute-start(bf16[4,64,1024]{2,1,0:T(8,128)(2,1)} %get-tuple-element.159), channel_id=1, source_target_pairs={{0,3},{1,0},{2,1},{3,2},{4,7},{5,4},{6,5},{7,6},{8,11},{9,8},{10,9... | collective-permute-start | bytes 1572872 | tf_op jit(solution)/shard_map/ppermute | solution.py:802
  326.5 48.6 %collective-permute-start.16 = (bf16[4,64,1024]{2,1,0:T(8,128)(2,1)}, bf16[4,64,1024]{2,1,0:T(8,128)(2,1)}, u32[]{:S(2)}, u32[]{:S(2)}) collective-permute-start(bf16[4,64,1024]{2,1,0:T(8,128)(2,1)} %get-tuple-element.160), channel_id=1, source_target_pairs={{0,2},{1,3},{2,0},{3,1},{4,6},{5,7},{6,4},{7,5},{8,10},{9,11},{10,... | collective-permute-start | bytes 1572872 | tf_op jit(solution)/shard_map/ppermute | solution.py:802
  327.7 47.5 %collective-permute-start.17 = (bf16[4,64,1024]{2,1,0:T(8,128)(2,1)}, bf16[4,64,1024]{2,1,0:T(8,128)(2,1)}, u32[]{:S(2)}, u32[]{:S(2)}) collective-permute-start(bf16[4,64,1024]{2,1,0:T(8,128)(2,1)} %get-tuple-element.161), channel_id=1, source_target_pairs={{0,1},{1,2},{2,3},{3,0},{4,5},{5,6},{6,7},{7,4},{8,9},{9,10},{10,1... | collective-permute-start | bytes 1572872 | tf_op jit(solution)/shard_map/ppermute | solution.py:802
  375.2 217.8 %reduce-scatter.6.cloned.1.call-start = ((), (), s32[]{:S(2)}) async-start(), calls=%async_computation.4 | async-start | bytes 9437184 | tf_op jit(solution)/shard_map/reduce_scatter | solution.py:714
  402.3 58.0 %collective-permute-start.18 = (bf16[4,64,1024]{2,1,0:T(8,128)(2,1)}, bf16[4,64,1024]{2,1,0:T(8,128)(2,1)S(1)}, u32[]{:S(2)}, u32[]{:S(2)}) collective-permute-start(bf16[4,64,1024]{2,1,0:T(8,128)(2,1)} %get-tuple-element.178), channel_id=1, source_target_pairs={{0,3},{1,0},{2,1},{3,2},{4,7},{5,4},{6,5},{7,6},{8,11},{9,8},{10,9... | collective-permute-start | bytes 1572872 | tf_op jit(solution)/shard_map/ppermute | solution.py:802
  406.1 54.2 %collective-permute-start.19 = (bf16[4,64,1024]{2,1,0:T(8,128)(2,1)}, bf16[4,64,1024]{2,1,0:T(8,128)(2,1)S(1)}, u32[]{:S(2)}, u32[]{:S(2)}) collective-permute-start(bf16[4,64,1024]{2,1,0:T(8,128)(2,1)} %get-tuple-element.179), channel_id=1, source_target_pairs={{0,2},{1,3},{2,0},{3,1},{4,6},{5,7},{6,4},{7,5},{8,10},{9,11},{10,... | collective-permute-start | bytes 1572872 | tf_op jit(solution)/shard_map/ppermute | solution.py:802
  406.1 54.2 %collective-permute-start.20 = (bf16[4,64,1024]{2,1,0:T(8,128)(2,1)}, bf16[4,64,1024]{2,1,0:T(8,128)(2,1)S(1)}, u32[]{:S(2)}, u32[]{:S(2)}) collective-permute-start(bf16[4,64,1024]{2,1,0:T(8,128)(2,1)} %get-tuple-element.180), channel_id=1, source_target_pairs={{0,1},{1,2},{2,3},{3,0},{4,5},{5,6},{6,7},{7,4},{8,9},{9,10},{10,1... | collective-permute-start | bytes 1572872 | tf_op jit(solution)/shard_map/ppermute | solution.py:802
  461.5 204.4 %reduce-scatter.8.cloned.1.call-start = ((), (), s32[]{:S(2)}) async-start(), calls=%async_computation.5 | async-start | bytes 10027008 | tf_op jit(solution)/shard_map/reduce_scatter | solution.py:714
  461.6 41.3 %collective-permute-start.21 = (bf16[4,64,1024]{2,1,0:T(8,128)(2,1)}, bf16[4,64,1024]{2,1,0:T(8,128)(2,1)S(1)}, u32[]{:S(2)}, u32[]{:S(2)}) collective-permute-start(bf16[4,64,1024]{2,1,0:T(8,128)(2,1)} %get-tuple-element.191), channel_id=1, source_target_pairs={{0,3},{1,0},{2,1},{3,2},{4,7},{5,4},{6,5},{7,6},{8,11},{9,8},{10,9... | collective-permute-start | bytes 1572872 | tf_op jit(solution)/shard_map/ppermute | solution.py:802
  464.7 44.5 %collective-permute-start.22 = (bf16[4,64,1024]{2,1,0:T(8,128)(2,1)}, bf16[4,64,1024]{2,1,0:T(8,128)(2,1)S(1)}, u32[]{:S(2)}, u32[]{:S(2)}) collective-permute-start(bf16[4,64,1024]{2,1,0:T(8,128)(2,1)} %get-tuple-element.192), channel_id=1, source_target_pairs={{0,2},{1,3},{2,0},{3,1},{4,6},{5,7},{6,4},{7,5},{8,10},{9,11},{10,... | collective-permute-start | bytes 1572872 | tf_op jit(solution)/shard_map/ppermute | solution.py:802
  466.4 42.9 %collective-permute-start.23 = (bf16[4,64,1024]{2,1,0:T(8,128)(2,1)}, bf16[4,64,1024]{2,1,0:T(8,128)(2,1)S(1)}, u32[]{:S(2)}, u32[]{:S(2)}) collective-permute-start(bf16[4,64,1024]{2,1,0:T(8,128)(2,1)} %get-tuple-element.193), channel_id=1, source_target_pairs={{0,1},{1,2},{2,3},{3,0},{4,5},{5,6},{6,7},{7,4},{8,9},{9,10},{10,1... | collective-permute-start | bytes 1572872 | tf_op jit(solution)/shard_map/ppermute | solution.py:802
  511.8 38.1 %collective-permute-start.24 = (bf16[256,1024]{1,0:T(8,128)(2,1)S(1)}, bf16[256,1024]{1,0:T(8,128)(2,1)}, u32[]{:S(2)}, u32[]{:S(2)}) collective-permute-start(bf16[256,1024]{1,0:T(8,128)(2,1)S(1)} %get-tuple-element.251), channel_id=1, source_target_pairs={{0,1},{1,2},{2,3},{3,0},{4,5},{5,6},{6,7},{7,4},{8,9},{9,10},{10,1... | collective-permute-start | bytes 1572872 | tf_op jit(solution)/shard_map/ppermute | solution.py:719
  511.8 38.1 %collective-permute-start.25 = (bf16[256,1024]{1,0:T(8,128)(2,1)S(1)}, bf16[256,1024]{1,0:T(8,128)(2,1)}, u32[]{:S(2)}, u32[]{:S(2)}) collective-permute-start(bf16[256,1024]{1,0:T(8,128)(2,1)S(1)} %get-tuple-element.253), channel_id=1, source_target_pairs={{0,2},{1,3},{2,0},{3,1},{4,6},{5,7},{6,4},{7,5},{8,10},{9,11},{10,... | collective-permute-start | bytes 1572872 | tf_op jit(solution)/shard_map/ppermute | solution.py:719
  513.3 36.7 %collective-permute-start.26 = (bf16[256,1024]{1,0:T(8,128)(2,1)S(1)}, bf16[256,1024]{1,0:T(8,128)(2,1)}, u32[]{:S(2)}, u32[]{:S(2)}) collective-permute-start(bf16[256,1024]{1,0:T(8,128)(2,1)S(1)} %get-tuple-element.252), channel_id=1, source_target_pairs={{0,3},{1,0},{2,1},{3,2},{4,7},{5,4},{6,5},{7,6},{8,11},{9,8},{10,9... | collective-permute-start | bytes 1572872 | tf_op jit(solution)/shard_map/ppermute | solution.py:719
  554.3 38.7 %collective-permute-start.27 = (bf16[256,1024]{1,0:T(8,128)(2,1)S(1)}, bf16[256,1024]{1,0:T(8,128)(2,1)S(1)}, u32[]{:S(2)}, u32[]{:S(2)}) collective-permute-start(bf16[256,1024]{1,0:T(8,128)(2,1)S(1)} %get-tuple-element.242.refs_0_), channel_id=1, source_target_pairs={{0,1},{1,2},{2,3},{3,0},{4,5},{5,6},{6,7},{7,4},{8,9},{9,10},{10,1... | collective-permute-start | bytes 1572872 | tf_op jit(solution)/shard_map/ppermute | solution.py:719
  562.5 30.5 %collective-permute-start.28 = (bf16[256,1024]{1,0:T(8,128)(2,1)S(1)}, bf16[256,1024]{1,0:T(8,128)(2,1)S(1)}, u32[]{:S(2)}, u32[]{:S(2)}) collective-permute-start(bf16[256,1024]{1,0:T(8,128)(2,1)S(1)} %get-tuple-element.242.refs_0_), channel_id=1, source_target_pairs={{0,3},{1,0},{2,1},{3,2},{4,7},{5,4},{6,5},{7,6},{8,11},{9,8},{10,9... | collective-permute-start | bytes 1572872 | tf_op jit(solution)/shard_map/ppermute | solution.py:719
  594.1 35.6 %collective-permute-start.35 = (bf16[256,1024]{1,0:T(8,128)(2,1)S(1)}, bf16[256,1024]{1,0:T(8,128)(2,1)}, u32[]{:S(2)}, u32[]{:S(2)}) collective-permute-start(bf16[256,1024]{1,0:T(8,128)(2,1)S(1)} %copy-done.8), channel_id=1, source_target_pairs={{0,2},{1,3},{2,0},{3,1},{4,6},{5,7},{6,4},{7,5},{8,10},{9,11},{10,... | collective-permute-start | bytes 1572872 | tf_op jit(solution)/shard_map/ppermute | solution.py:719
  594.8 40.6 %collective-permute-start.29 = (bf16[128,1024]{1,0:T(8,128)(2,1)S(1)}, bf16[128,1024]{1,0:T(8,128)(2,1)S(1)}, u32[]{:S(2)}, u32[]{:S(2)}) collective-permute-start(bf16[128,1024]{1,0:T(8,128)(2,1)S(1)} %get-tuple-element.273), channel_id=1, source_target_pairs={{0,1},{1,2},{2,3},{3,0},{4,5},{5,6},{6,7},{7,4},{8,9},{9,10},{10,1... | collective-permute-start | bytes 786440 | tf_op jit(solution)/shard_map/ppermute | solution.py:719
  596.9 38.6 %collective-permute-start.30 = (bf16[128,1024]{1,0:T(8,128)(2,1)S(1)}, bf16[128,1024]{1,0:T(8,128)(2,1)S(1)}, u32[]{:S(2)}, u32[]{:S(2)}) collective-permute-start(bf16[128,1024]{1,0:T(8,128)(2,1)S(1)} %get-tuple-element.275), channel_id=1, source_target_pairs={{0,2},{1,3},{2,0},{3,1},{4,6},{5,7},{6,4},{7,5},{8,10},{9,11},{10,... | collective-permute-start | bytes 786440 | tf_op jit(solution)/shard_map/ppermute | solution.py:719
  597.2 38.2 %collective-permute-start.31 = (bf16[128,1024]{1,0:T(8,128)(2,1)S(1)}, bf16[128,1024]{1,0:T(8,128)(2,1)S(1)}, u32[]{:S(2)}, u32[]{:S(2)}) collective-permute-start(bf16[128,1024]{1,0:T(8,128)(2,1)S(1)} %get-tuple-element.274), channel_id=1, source_target_pairs={{0,3},{1,0},{2,1},{3,2},{4,7},{5,4},{6,5},{7,6},{8,11},{9,8},{10,9... | collective-permute-start | bytes 786440 | tf_op jit(solution)/shard_map/ppermute | solution.py:719
  635.8 14.1 %collective-permute-start.32 = (bf16[128,1024]{1,0:T(8,128)(2,1)S(1)}, bf16[128,1024]{1,0:T(8,128)(2,1)S(1)}, u32[]{:S(2)}, u32[]{:S(2)}) collective-permute-start(bf16[128,1024]{1,0:T(8,128)(2,1)S(1)} %get-tuple-element.244), channel_id=1, source_target_pairs={{0,1},{1,2},{2,3},{3,0},{4,5},{5,6},{6,7},{7,4},{8,9},{9,10},{10,1... | collective-permute-start | bytes 786440 | tf_op jit(solution)/shard_map/ppermute | solution.py:719
  641.7 18.9 %collective-permute-start.33 = (bf16[128,1024]{1,0:T(8,128)(2,1)S(1)}, bf16[128,1024]{1,0:T(8,128)(2,1)S(1)}, u32[]{:S(2)}, u32[]{:S(2)}) collective-permute-start(bf16[128,1024]{1,0:T(8,128)(2,1)S(1)} %get-tuple-element.244), channel_id=1, source_target_pairs={{0,2},{1,3},{2,0},{3,1},{4,6},{5,7},{6,4},{7,5},{8,10},{9,11},{10,... | collective-permute-start | bytes 786440 | tf_op jit(solution)/shard_map/ppermute | solution.py:719
  643.2 17.3 %collective-permute-start.34 = (bf16[128,1024]{1,0:T(8,128)(2,1)S(1)}, bf16[128,1024]{1,0:T(8,128)(2,1)S(1)}, u32[]{:S(2)}, u32[]{:S(2)}) collective-permute-start(bf16[128,1024]{1,0:T(8,128)(2,1)S(1)} %get-tuple-element.244), channel_id=1, source_target_pairs={{0,3},{1,0},{2,1},{3,2},{4,7},{5,4},{6,5},{7,6},{8,11},{9,8},{10,9... | collective-permute-start | bytes 786440 | tf_op jit(solution)/shard_map/ppermute | solution.py:719
  667.0 11.6 %collective-permute-start.36 = (bf16[136,1024]{1,0:T(8,128)(2,1)S(1)}, bf16[136,1024]{1,0:T(8,128)(2,1)S(1)}, u32[]{:S(2)}, u32[]{:S(2)}) collective-permute-start(bf16[136,1024]{1,0:T(8,128)(2,1)S(1)} %get-tuple-element.266), channel_id=1, source_target_pairs={{0,1},{1,2},{2,3},{3,0},{4,5},{5,6},{6,7},{7,4},{8,9},{9,10},{10,1... | collective-permute-start | bytes 835592 | tf_op jit(solution)/shard_map/ppermute | solution.py:719
  670.1 19.4 %collective-permute-start.37 = (bf16[136,1024]{1,0:T(8,128)(2,1)S(1)}, bf16[136,1024]{1,0:T(8,128)(2,1)S(1)}, u32[]{:S(2)}, u32[]{:S(2)}) collective-permute-start(bf16[136,1024]{1,0:T(8,128)(2,1)S(1)} %get-tuple-element.268), channel_id=1, source_target_pairs={{0,2},{1,3},{2,0},{3,1},{4,6},{5,7},{6,4},{7,5},{8,10},{9,11},{10,... | collective-permute-start | bytes 835592 | tf_op jit(solution)/shard_map/ppermute | solution.py:719
  671.6 17.9 %collective-permute-start.38 = (bf16[136,1024]{1,0:T(8,128)(2,1)S(1)}, bf16[136,1024]{1,0:T(8,128)(2,1)S(1)}, u32[]{:S(2)}, u32[]{:S(2)}) collective-permute-start(bf16[136,1024]{1,0:T(8,128)(2,1)S(1)} %get-tuple-element.267), channel_id=1, source_target_pairs={{0,3},{1,0},{2,1},{3,2},{4,7},{5,4},{6,5},{7,6},{8,11},{9,8},{10,9... | collective-permute-start | bytes 835592 | tf_op jit(solution)/shard_map/ppermute | solution.py:719
  690.8 15.5 %collective-permute-start.39 = (bf16[136,1024]{1,0:T(8,128)(2,1)S(1)}, bf16[136,1024]{1,0:T(8,128)(2,1)S(1)}, u32[]{:S(2)}, u32[]{:S(2)}) collective-permute-start(bf16[136,1024]{1,0:T(8,128)(2,1)S(1)} %get-tuple-element.240), channel_id=1, source_target_pairs={{0,1},{1,2},{2,3},{3,0},{4,5},{5,6},{6,7},{7,4},{8,9},{9,10},{10,1... | collective-permute-start | bytes 835592 | tf_op jit(solution)/shard_map/ppermute | solution.py:719
  697.3 19.7 %collective-permute-start.40 = (bf16[136,1024]{1,0:T(8,128)(2,1)S(1)}, bf16[136,1024]{1,0:T(8,128)(2,1)S(1)}, u32[]{:S(2)}, u32[]{:S(2)}) collective-permute-start(bf16[136,1024]{1,0:T(8,128)(2,1)S(1)} %get-tuple-element.240), channel_id=1, source_target_pairs={{0,2},{1,3},{2,0},{3,1},{4,6},{5,7},{6,4},{7,5},{8,10},{9,11},{10,... | collective-permute-start | bytes 835592 | tf_op jit(solution)/shard_map/ppermute | solution.py:719
  699.2 17.9 %collective-permute-start.41 = (bf16[136,1024]{1,0:T(8,128)(2,1)S(1)}, bf16[136,1024]{1,0:T(8,128)(2,1)S(1)}, u32[]{:S(2)}, u32[]{:S(2)}) collective-permute-start(bf16[136,1024]{1,0:T(8,128)(2,1)S(1)} %get-tuple-element.240), channel_id=1, source_target_pairs={{0,3},{1,0},{2,1},{3,2},{4,7},{5,4},{6,5},{7,6},{8,11},{9,8},{10,9... | collective-permute-start | bytes 835592 | tf_op jit(solution)/shard_map/ppermute | solution.py:719
  (44 other events, 268.8 us)
Sparse Core Ops, SparseCore 0:
  10.7 57.2 all-gather.8
  70.4 54.3 all-gather.10
  126.7 89.8 all-gather.12
  375.3 116.4 reduce-scatter.3
  495.1 71.2 reduce-scatter.5
  593.2 72.6 reduce-scatter.7

commit v9 on v8

--- a/solution.py
+++ b/solution.py
@@ -13,8 +13,6 @@
 MASKED = -1e30
 ROWS = 256
 RAISED = (HEADS // 2, ROWS, 2 * ROWS)
-FF_CHUNK = 1024
-FF_GROUPS = 1
 VMEM_LIMIT = 62 * 1024 * 1024
 
 bf16 = jnp.bfloat16
@@ -237,69 +235,83 @@
 
 def feed_forward(count, *refs):
     grad, refs = refs[:count], refs[count:]
-    x, gain, bias, hidden_bias, out_bias, weights = refs[:6]
+    x, gain, bias, hidden_bias, out_bias, weights_hbm = refs[:6]
     norm_out, act_out, gpre_out, gat_out, branch_out, gain_out, bias_out, hb_out, ob_out = refs[6:15]
-    block_out = refs[15:]
-    first = pl.program_id(0) == 0
+    block_out = refs[15 : 15 + count]
+    weights, arrived = refs[15 + count :]
     clips = weights.shape[0]
     own = 1024 // clips
-    groups = x.shape[0]
-    width = x.shape[2]
-    size = FF_CHUNK
-    chunks = 4096 // size
-    half = 1024 // size
-    share = size * clips // 4096
-    branch = stacked(grad, groups)
-    branch_out[...] = branch.reshape(branch_out.shape)
-
-    def down_of(chunk):
-        if share:
-            return weights[chunk * share : (chunk + 1) * share, 4 * own :, :].reshape(size, 1024)
-        return None
-
-    def hidden_of(chunk):
-        block, column = chunk // half, chunk % half
-        return weights[:, block * own : (block + 1) * own, column * size : (column + 1) * size].reshape(1024, size)
-
-    part_at = lambda chunk: slice(chunk * size, (chunk + 1) * size)
-    back_act = dot(branch, down_of(0), NT)
-    after_time = x[...].reshape(groups * ROWS, width)
-    hat, rate = standardize(after_time)
-    normed = (hat * gain[2:3, :] + bias[2:3, :]).astype(bf16)
-    norm_out[...] = normed.reshape(norm_out.shape)
-    pre = dot(normed, hidden_of(0)) + hidden_bias[0:1, part_at(0)]
-    result = None
-    grad_norm = None
-    bias_sums = []
-    for chunk in range(chunks):
-        at = part_at(chunk)
-        u, grad_act = pre, back_act
-        if chunk + 1 < chunks:
-            pre = dot(normed, hidden_of(chunk + 1)) + hidden_bias[0:1, part_at(chunk + 1)]
-            back_act = dot(branch, down_of(chunk + 1), NT)
-        c0 = 0.7978845608028654
-        square = u * u
-        t = jnp.tanh(u * (c0 + (c0 * 0.044715) * square))
-        half_plus = 0.5 + 0.5 * t
-        act = (u * half_plus).astype(bf16)
-        act_out[:, :, at] = act.reshape(groups, ROWS, size)
-        slope = half_plus + (0.5 * u) * (1.0 - t * t) * (c0 + (3.0 * c0 * 0.044715) * square)
-        gpre = (grad_act * slope).astype(bf16)
-        gpre_out[:, :, at] = gpre.reshape(groups, ROWS, size)
-        bias_sums.append(column_sum(gpre.astype(f32)))
-        down = dot(act, down_of(chunk))
-        result = down if result is None else result + down
-        back = dot(gpre, hidden_of(chunk), NT)
-        grad_norm = back if grad_norm is None else grad_norm + back
-    block = (after_time + result + out_bias[0:1, :]).astype(bf16)
-    unstack(block_out, block, groups)
-    upstream = branch.astype(f32)
-    gat = (upstream + norm_back(hat, rate, gain[2:3, :], grad_norm)).astype(bf16)
-    gat_out[...] = gat.reshape(gat_out.shape)
-    add_row(gain_out, column_sum(grad_norm * hat), first)
-    add_row(bias_out, column_sum(grad_norm), first)
-    add_row(ob_out, column_sum(upstream), first)
-    add_row(hb_out, jnp.concatenate(bias_sums, axis=1), first)
+    share = clips // 4
+
+    def part_of(ref, index):
+        if index < 4:
+            return ref.at[:, index * own : (index + 1) * own, :]
+        return ref.at[(index - 4) * share : (index - 3) * share, 4 * own :, :]
+
+    def load(index):
+        return pltpu.make_async_copy(part_of(weights_hbm, index), part_of(weights, index), arrived.at[index])
+
+    def run(fresh):
+        def part(index):
+            if fresh and index not in here:
+                load(index).wait()
+                here.add(index)
+            return part_of(weights, index)[...].reshape(1024, 1024)
+
+        def note(ref, row):
+            if fresh:
+                ref[...] = row
+            else:
+                ref[...] += row
+
+        here = set()
+        if fresh:
+            for index in (4, 0, 1, 5, 2, 6, 3, 7):
+                load(index).start()
+        part_at = lambda chunk: slice(chunk * 1024, (chunk + 1) * 1024)
+        branch = stacked(grad)
+        branch_out[...] = branch
+        after_time = x[...]
+        hat, rate = standardize(after_time)
+        normed = (hat * gain[2:3, :] + bias[2:3, :]).astype(bf16)
+        norm_out[...] = normed
+        back_act = dot(branch, part(4), NT)
+        pre = dot(normed, part(0)) + hidden_bias[0:1, part_at(0)]
+        result = None
+        grad_norm = None
+        for chunk in range(4):
+            at = part_at(chunk)
+            u, grad_act = pre, back_act
+            if chunk < 3:
+                pre = dot(normed, part(chunk + 1)) + hidden_bias[0:1, part_at(chunk + 1)]
+                back_act = dot(branch, part(chunk + 5), NT)
+            c0 = 0.7978845608028654
+            square = u * u
+            t = jnp.tanh(u * (c0 + (c0 * 0.044715) * square))
+            half_plus = 0.5 + 0.5 * t
+            act = (u * half_plus).astype(bf16)
+            act_out[:, at] = act
+            slope = half_plus + (0.5 * u) * (1.0 - t * t) * (c0 + (3.0 * c0 * 0.044715) * square)
+            gpre = (grad_act * slope).astype(bf16)
+            gpre_out[:, at] = gpre
+            if fresh:
+                hb_out[0:1, at] = column_sum(gpre.astype(f32))
+            else:
+                hb_out[0:1, at] += column_sum(gpre.astype(f32))
+            down = dot(act, part(chunk + 4))
+            result = down if result is None else result + down
+            back = dot(gpre, part(chunk), NT)
+            grad_norm = back if grad_norm is None else grad_norm + back
+        unstack(block_out, (after_time + result + out_bias[0:1, :]).astype(bf16))
+        upstream = branch.astype(f32)
+        gat_out[...] = (upstream + norm_back(hat, rate, gain[2:3, :], grad_norm)).astype(bf16)
+        note(gain_out, column_sum(grad_norm * hat))
+        note(bias_out, column_sum(grad_norm))
+        note(ob_out, column_sum(upstream))
+
+    first = pl.program_id(0) == 0
+    pl.when(first)(lambda: run(True))
+    pl.when(jnp.logical_not(first))(lambda: run(False))
 
 
 def time_backward(count, *refs):
@@ -509,27 +521,25 @@
     count = len(grad)
     groups, _, width = x.shape
     ff = hidden_bias.shape[1]
-    each = FF_GROUPS if groups % FF_GROUPS == 0 else 1
     row = shape_of((1, width), f32)
     rows = lambda cols: shape_of((groups, ROWS, cols), bf16)
-    spec = lambda cols: pl.BlockSpec((each, ROWS, cols), lambda i: (i, 0, 0))
-    grad_spec = lambda a: pl.BlockSpec(
-        (a.shape[0], each * ROWS // (a.shape[0] * count), width), lambda i: (0, i, 0)
-    )
     return ordered_call(
         functools.partial(feed_forward, count),
         behind,
-        grid=(groups // each,),
-        in_specs=[grad_spec(a) for a in grad]
-        + [spec(width)]
-        + [whole(a.shape) for a in (gain, bias, hidden_bias, out_bias, weights)],
+        grid=(groups,),
+        in_specs=[group_spec(a, count) for a in grad]
+        + [step_spec((ROWS, width))]
+        + [whole(a.shape) for a in (gain, bias, hidden_bias, out_bias)]
+        + [pl.BlockSpec(memory_space=pl.ANY)],
         out_specs=[
-            spec(width), spec(ff), spec(ff), spec(width), spec(width),
+            step_spec((ROWS, width)), step_spec((ROWS, ff)), step_spec((ROWS, ff)),
+            step_spec((ROWS, width)), step_spec((ROWS, width)),
             total_spec((1, width)), total_spec((1, width)), total_spec((1, ff)), total_spec((1, width)),
         ]
-        + [grad_spec(a) for a in grad],
+        + [group_spec(a, count) for a in grad],
         out_shape=[rows(width), rows(ff), rows(ff), rows(width), rows(width), row, row, shape_of((1, ff), f32), row]
         + [shape_of(a.shape, bf16) for a in grad],
+        scratch_shapes=[pltpu.VMEM(weights.shape, bf16), pltpu.SemaphoreType.DMA((8,))],
         name="feed_forward",
     )(*grad, x, gain, bias, hidden_bias, out_bias, weights)
 

time: 741 us -> 768 us (1.036)
  Pallas kernels: 415 us -> 443 us
    pallas_call x15, Pallas kernels: 415 us -> 443 us  [ordered_call(): return lambda *operands: call(*behind, *operands)]
  transfers between devices with their start and end apart: 48 -> 48, of which waited for: 12 -> 12; matrix products, arithmetic and copies ran while one was open for 5% -> 5% of each run, Pallas kernels for 57% -> 59%
where the time goes in v9:
time: 768 us; the launch traced here: 756 us
  Pallas kernels  443 us (58%)
  waiting for transfers between devices  136 us (18%)
  starting transfers between devices  93.8 us (12%)
  local copies, waits for them, and re-layouts  32.1 us (4%)
  other arithmetic  26.1 us (3%)
  between operations  15.5 us (2%)
  blocking collectives  9.16 us (1%)
    pallas_call x15, Pallas kernels, ordered_call(): return lambda *operands: call(*behind, *operands)  443 us
    ppermute x18, waiting for transfers between devices, shift(): lax.ppermute(values, 'tm', [(k, (k + step) % count) for k in range(count)])  76.6 us
    ppermute x18, starting transfers between devices, shift(): lax.ppermute(values, 'tm', [(k, (k + step) % count) for k in range(count)])  43.7 us
    ppermute x12, starting transfers between devices, local(): lax.ppermute(parts[d], 'tm', [(k, (k + d) % pieces) for k in range(pieces)])  32.3 us
    all_gather x3, waiting for transfers between devices, gather(): lax.all_gather(jnp.concatenate(parts, axis=0), 'clip', axis=0, tiled=False)  26.9 us
    ppermute x12, waiting for transfers between devices, local(): lax.ppermute(parts[d], 'tm', [(k, (k + d) % pieces) for k in range(pieces)])  22.6 us
    ppermute x12, starting transfers between devices, local(): lax.ppermute(parts[d], 'tm', [(k, (k - d) % pieces) for k in range(pieces)])  17.6 us
  transfers between devices with their start and end apart: 48, of which 12 were waited for; matrix products, arithmetic and copies ran while one was open for 5% of the time, Pallas kernels for 59%

profile of v9, /device:TPU:0, one launch (start us, length us, event | category | flops | bytes accessed | tf_op | source)
XLA Modules:
  0.0 755.5 jit_solution(5795016483245207032)
XLA Ops:
  14.8 4.1 fusion.26
  20.4 3.0 collective-permute-start
  23.4 2.6 collective-permute-start.1
  27.6 9.2 %all-gather.4 = bf16[8,19,128]{2,1,0:T(8,128)(2,1)S(1)} all-gather(bf16[1,19,128]{2,1,0:T(8,128)(2,1)S(1)} %bitcast.115), channel_id=2, replica_groups=mesh['clip'=8,'tm'=4] {'clip'}, dimensions={0}, use_global_device_ids=true | all-gather | bytes 43776 | tf_op jit(solution)/shard_map/all_gather | solution.py:789
  43.0 24.9 %all-gather.9.cloned.1.call-done = bf16[4096,1024]{1,0:T(8,128)(2,1)} async-done(((bf16[512,1024]{1,0:T(8,128)(2,1)}), bf16[4096,1024]{1,0:T(8,128)(2,1)}) %all-gather.9.cloned.1.call-update) | async-done | bytes 8388624 | tf_op jit(solution)/shard_map/all_gather | solution.py:720
  68.0 23.7 %space_forward.2 = (bf16[4,256,1024]{2,1,0:T(8,128)(2,1)}, bf16[4,256,3072]{2,1,0:T(8,128)(2,1)}, bf16[4,256,1024]{2,1,0:T(8,128)(2,1)}, f32[4,16,256]{2,1,0:T(8...) custom-call(s32[1]{0:T(128)} %bitcast.refs_0_.refs_4_.refs_5_, ...), custom_call_target="tpu_custom_call" | custom-call | tf_op jit(solution)/shard_map/space_forward/pallas_call | solution.py:389
  94.8 2.4 collective-permute-start.4
  99.5 23.8 %space_forward.3 = (bf16[4,256,1024]{2,1,0:T(8,128)(2,1)}, bf16[4,256,3072]{2,1,0:T(8,128)(2,1)}, bf16[4,256,1024]{2,1,0:T(8,128)(2,1)}, f32[4,16,256]{2,1,0:T(8...) custom-call(f32[4,16,256]{2,1,0:T(8,128)} %get-tuple-element.126.ref, ...), custom_call_target="tpu_custom_call" | custom-call | tf_op jit(solution)/shard_map/space_forward/pallas_call | solution.py:389
  125.8 2.6 collective-permute-start.8
  129.9 22.5 %collective-permute-done.4.refs_6_.refs_3_ = bf16[4,64,1024]{2,1,0:T(8,128)(2,1)} collective-permute-done((bf16[4,64,1024]{2,1,0:T(8,128)(2,1)}, bf16[4,64,1024]{2,1,0:T(8,128)(2,1)}, u32[]{:S(2)}, u32[]{:S(2)}) %collective-permute-start.4) | collective-permute-done | bytes 524320 | tf_op jit(solution)/shard_map/ppermute | solution.py:809
  152.5 22.9 %time_forward.2 = (bf16[4,256,1024]{2,1,0:T(8,128)(2,1)}, bf16[4,256,3072]{2,1,0:T(8,128)(2,1)}, bf16[4,256,1024]{2,1,0:T(8,128)(2,1)}, f32[4,16,256]{2,1,0:T(8,...) custom-call(f32[4,16,256]{2,1,0:T(8,128)} %get-tuple-element.127.refs_0_.refs_14_, ...), custom_call_target="tpu_custom_call" | custom-call | tf_op jit(solution)/shard_map/time_forward/pallas_call | solution.py:389
  176.3 22.9 %time_forward.3 = (bf16[4,256,1024]{2,1,0:T(8,128)(2,1)}, bf16[4,256,3072]{2,1,0:T(8,128)(2,1)}, bf16[4,256,1024]{2,1,0:T(8,128)(2,1)}, f32[4,16,256]{2,1,0:T(8,...) custom-call(f32[4,16,256]{2,1,0:T(8,128)} %get-tuple-element.132.refs_0_.refs_11_, ...), custom_call_target="tpu_custom_call" | custom-call | tf_op jit(solution)/shard_map/time_forward/pallas_call | solution.py:389
  199.3 11.5 %collective-permute-start.10 = (bf16[4,64,1024]{2,1,0:T(8,128)(2,1)}, bf16[4,64,1024]{2,1,0:T(8,128)(2,1)S(1)}, u32[]{:S(2)}, u32[]{:S(2)}) collective-permute-start(bf16[4,64,1024]{2,1,0:T(8,128)(2,1)} %get-tuple-element.144), channel_id=1, source_target_pairs={{0,2},{1,3},{2,0},{3,1},{4,6},{5,7},{6,4},{7,5},{8,10},{9,11},{10,... | collective-permute-start | bytes 1572872 | tf_op jit(solution)/shard_map/ppermute | solution.py:809
  211.4 3.3 collective-permute-start.11
  216.6 64.4 %feed_forward.2 = (bf16[4,256,1024]{2,1,0:T(8,128)(2,1)}, bf16[4,256,4096]{2,1,0:T(8,128)(2,1)}, bf16[4,256,4096]{2,1,0:T(8,128)(2,1)}, bf16[4,256,1024]{2,1,0:T...) custom-call(f32[4,16,256]{2,1,0:T(8,128)} %get-tuple-element.137.ref, ...), custom_call_target="tpu_custom_call" | custom-call | tf_op jit(solution)/shard_map/feed_forward/pallas_call | solution.py:389
  281.0 3.4 collective-permute-start.12
  286.3 64.4 %feed_forward.3 = (bf16[4,256,1024]{2,1,0:T(8,128)(2,1)}, bf16[4,256,4096]{2,1,0:T(8,128)(2,1)}, bf16[4,256,4096]{2,1,0:T(8,128)(2,1)}, bf16[4,256,1024]{2,1,0:T...) custom-call(f32[1,1024]{1,0:T(1,128)} %get-tuple-element.140.refs_0_, ...), custom_call_target="tpu_custom_call" | custom-call | tf_op jit(solution)/shard_map/feed_forward/pallas_call | solution.py:389
  350.8 2.8 collective-permute-start.15
  355.9 22.9 %down_grad.1.refs_4_ = bf16[8,1024,1024]{2,1,0:T(8,128)(2,1)} custom-call(f32[1,1024]{1,0:T(1,128)} %get-tuple-element.150.refs_0_, bf16[4,64,1024]{2,1,0:T(8,128)(2,1)} %copy-done.4, bf16[4,64,1024]{2,1,0:T(8,128)(2,1)} %copy-done.5, bf16[4,64,1024]{2,1,0:T(8,128)(2,1)} %copy-done.6, bf16[4,256,4096]{2,1,0:T(8,128)(2,1)} %get-tuple-element.154.refs_4_, ...), custom_call_target="tpu_custom_call" | custom-call | tf_op jit(solution)/shard_map/down_grad/pallas_call | solution.py:389
  378.8 23.2 %hidden_grad.1.refs_0_ = bf16[8,1024,1024]{2,1,0:T(8,128)(2,1)} custom-call(bf16[4,256,1024]{2,1,0:T(8,128)(2,1)} %get-tuple-element.139.refs_0_, bf16[4,256,1024]{2,1,0:T(8,128)(2,1)} %get-tuple-element.147.refs_1_, bf16[4,256,4096]{2,1,0:T(8,128)(2,1)} %get-tuple-element.148.refs_2_, ...), custom_call_target="tpu_custom_call", output_to_operand_aliasing={{}: (4, {})} | custom-call | tf_op jit(solution)/shard_map/hidden_grad/pallas_call | solution.py:389
  402.2 27.0 %time_backward.2 = (bf16[4,256,3072]{2,1,0:T(8,128)(2,1)}, f32[1,1024]{1,0:T(1,128)}, f32[1,1024]{1,0:T(1,128)}, bf16[4,64,1024]{2,1,0:T(8,128)(2,1)}, bf16[4,64...) custom-call(bf16[8,1024,1024]{2,1,0:T(8,128)(2,1)} %hidden_grad.1.refs_0_, ...), custom_call_target="tpu_custom_call" | custom-call | tf_op jit(solution)/shard_map/time_backward/pallas_call | solution.py:389
  429.2 3.7 collective-permute-start.18
  433.5 27.2 %time_backward.3 = (bf16[4,256,3072]{2,1,0:T(8,128)(2,1)}, f32[1,1024]{1,0:T(1,128)}, f32[1,1024]{1,0:T(1,128)}, bf16[4,64,1024]{2,1,0:T(8,128)(2,1)}, bf16[4,64...) custom-call(f32[1,1024]{1,0:T(1,128)} %get-tuple-element.167.refs_0_, ...), custom_call_target="tpu_custom_call" | custom-call | tf_op jit(solution)/shard_map/time_backward/pallas_call | solution.py:389
  460.8 26.2 %time_grad.1.refs_0_ = bf16[8,512,1024]{2,1,0:T(8,128)(2,1)} custom-call(f32[1,1024]{1,0:T(1,128)} %get-tuple-element.172.refs_0_, bf16[4,256,1024]{2,1,0:T(8,128)(2,1)} %get-tuple-element.173.refs_1_, bf16[4,256,1024]{2,1,0:T(8,128)(2,1)} %get-tuple-element.174.refs_2_, bf16[4,256,3072]{2,1,0:T(8,128)(2,1)} %get-tuple-element.175.refs_3_, ...), custom_call_target="tpu_custom_call" | custom-call | tf_op jit(solution)/shard_map/time_grad/pallas_call | solution.py:389
  488.3 3.2 collective-permute-start.21
  493.1 5.0 assemble.1.refs_1_
  498.2 31.2 %space_backward.2 = (bf16[4,256,3072]{2,1,0:T(8,128)(2,1)}, bf16[4,256,1024]{2,1,0:T(8,128)(2,1)}, f32[2,4,256,1024]{3,2,1,0:T(8,128)}, f32[1,1024]{1,0:T(1,128)...) custom-call(bf16[8,512,1024]{2,1,0:T(8,128)(2,1)} %time_grad.1.refs_0_, bf16[4,64,1024]{2,1,0:T(8,128)(2,1)} %get-tuple-element.182.refs_1_, ...), custom_call_target="tpu_custom_call" | custom-call | tf_op jit(solution)/shard_map/space_backward/pallas_call | solution.py:389
  529.5 6.5 collective-permute-done.22.refs_3_
  540.0 2.8 collective-permute-start.26
  542.8 31.6 %space_backward.3 = (bf16[4,256,3072]{2,1,0:T(8,128)(2,1)}, bf16[4,256,1024]{2,1,0:T(8,128)(2,1)}, f32[2,4,256,1024]{3,2,1,0:T(8,128)}, f32[1,1024]{1,0:T(1,128)...) custom-call(bf16[1024,1024]{1,0:T(8,128)(2,1)} %bitcast.103, ...), custom_call_target="tpu_custom_call", output_to_operand_aliasing={{2}: (15, {})} | custom-call | tf_op jit(solution)/shard_map/space_backward/pallas_call | solution.py:389
  578.3 2.8 constant_dynamic-update-slice_fusion.12
  581.1 8.2 %collective-permute-start.27 = (bf16[256,1024]{1,0:T(8,128)(2,1)S(1)}, bf16[256,1024]{1,0:T(8,128)(2,1)S(1)}, u32[]{:S(2)}, u32[]{:S(2)}) collective-permute-start(bf16[256,1024]{1,0:T(8,128)(2,1)S(1)} %get-tuple-element.242.refs_0_), channel_id=1, source_target_pairs={{0,1},{1,2},{2,3},{3,0},{4,5},{5,6},{6,7},{7,4},{8,9},{9,10},{10,1... | collective-permute-start | bytes 1572872 | tf_op jit(solution)/shard_map/ppermute | solution.py:729
  589.3 2.7 collective-permute-start.28
  593.2 26.5 %space_grad.1 = bf16[8,544,1024]{2,1,0:T(8,128)(2,1)} custom-call(bf16[256,1024]{1,0:T(8,128)(2,1)} %copy-done.7, bf16[2,4,256,1024]{3,2,1,0:T(8,128)(2,1)} %assemble.1.refs_1_, bf16[4,256,1024]{2,1,0:T(8,128)(2,1)} %get-tuple-element.200.refs_2_, bf16[4,256,1024]{2,1,0:T(8,128)(2,1)} %get-tuple-element.201.refs_3_, ...), custom_call_target="tpu_custom_call" | custom-call | tf_op jit(solution)/shard_map/space_grad/pallas_call | solution.py:389
  621.5 2.1 collective-permute-start.29
  623.9 2.8 collective-permute-start.31
  627.6 28.9 %collective-permute-done.35 = bf16[256,1024]{1,0:T(8,128)(2,1)} collective-permute-done((bf16[256,1024]{1,0:T(8,128)(2,1)S(1)}, bf16[256,1024]{1,0:T(8,128)(2,1)}, u32[]{:S(2)}, u32[]{:S(2)}) %collective-permute-start.35) | collective-permute-done | bytes 524320 | tf_op jit(solution)/shard_map/ppermute | solution.py:729
  662.6 5.8 collective-permute-start.32
  670.8 2.8 slice_convert_fusion
  673.7 2.9 collective-permute-done.32
  676.6 10.6 %collective-permute-done.33 = bf16[128,1024]{1,0:T(8,128)(2,1)S(1)} collective-permute-done((bf16[128,1024]{1,0:T(8,128)(2,1)S(1)}, bf16[128,1024]{1,0:T(8,128)(2,1)S(1)}, u32[]{:S(2)}, u32[]{:S(2)}) %collective-permute-start.33) | collective-permute-done | bytes 262176 | tf_op jit(solution)/shard_map/ppermute | solution.py:729
  689.5 3.1 reduce-scatter.8.cloned.1.call-done
  693.8 3.0 collective-permute-start.36
  699.2 6.1 collective-permute-done.36
  705.3 10.8 %collective-permute-done.37 = bf16[136,1024]{1,0:T(8,128)(2,1)S(1)} collective-permute-done((bf16[136,1024]{1,0:T(8,128)(2,1)S(1)}, bf16[136,1024]{1,0:T(8,128)(2,1)S(1)}, u32[]{:S(2)}, u32[]{:S(2)}) %collective-permute-start.37) | collective-permute-done | bytes 278560 | tf_op jit(solution)/shard_map/ppermute | solution.py:729
  717.4 6.5 collective-permute-start.39
  726.4 6.6 collective-permute-done.39
  733.0 10.6 %collective-permute-done.40 = bf16[136,1024]{1,0:T(8,128)(2,1)S(1)} collective-permute-done((bf16[136,1024]{1,0:T(8,128)(2,1)S(1)}, bf16[136,1024]{1,0:T(8,128)(2,1)S(1)}, u32[]{:S(2)}, u32[]{:S(2)}) %collective-permute-start.40) | collective-permute-done | bytes 278560 | tf_op jit(solution)/shard_map/ppermute | solution.py:729
  (246 shorter events, 72.1 us)
Async XLA Ops:
  7.2 60.8 %all-gather.9.cloned.1.call-start = ((), (), s32[]{:S(2)}) async-start(), calls=%async_computation.6 | async-start | bytes 9437184 | tf_op jit(solution)/shard_map/all_gather | solution.py:720
  10.5 119.4 %all-gather.11.cloned.1.call-start = ((), (), s32[]{:S(2)}) async-start(), calls=%async_computation.7 | async-start | bytes 9437184 | tf_op jit(solution)/shard_map/all_gather | solution.py:720
  11.7 204.9 %all-gather.13.cloned.1.call-start = ((), (), s32[]{:S(2)}) async-start(), calls=%async_computation.8 | async-start | bytes 18874368 | tf_op jit(solution)/shard_map/all_gather | solution.py:720
  14.7 521.3 %reduce-scatter.4.cloned.1.call-start = ((), (), s32[]{:S(2)}) async-start(), calls=%async_computation.3 | async-start | bytes 18874368 | tf_op jit(solution)/shard_map/reduce_scatter | solution.py:724
  20.4 76.8 %collective-permute-start = (bf16[4,64,1024]{2,1,0:T(8,128)(2,1)}, bf16[4,64,1024]{2,1,0:T(8,128)(2,1)S(1)}, u32[]{:S(2)}, u32[]{:S(2)}) collective-permute-start(bf16[4,64,1024]{2,1,0:T(8,128)(2,1)} %get-tuple-element.261), channel_id=1, source_target_pairs={{0,1},{1,2},{2,3},{3,0},{4,5},{5,6},{6,7},{7,4},{8,9},{9,10},{10,1... | collective-permute-start | bytes 1572872 | tf_op jit(solution)/shard_map/ppermute | solution.py:809
  23.4 75.3 %collective-permute-start.1 = (bf16[4,64,1024]{2,1,0:T(8,128)(2,1)}, bf16[4,64,1024]{2,1,0:T(8,128)(2,1)S(1)}, u32[]{:S(2)}, u32[]{:S(2)}) collective-permute-start(bf16[4,64,1024]{2,1,0:T(8,128)(2,1)} %get-tuple-element.260), channel_id=1, source_target_pairs={{0,2},{1,3},{2,0},{3,1},{4,6},{5,7},{6,4},{7,5},{8,10},{9,11},{10,... | collective-permute-start | bytes 1572872 | tf_op jit(solution)/shard_map/ppermute | solution.py:809
  26.0 72.7 %collective-permute-start.2 = (bf16[4,64,1024]{2,1,0:T(8,128)(2,1)}, bf16[4,64,1024]{2,1,0:T(8,128)(2,1)}, u32[]{:S(2)}, u32[]{:S(2)}) collective-permute-start(bf16[4,64,1024]{2,1,0:T(8,128)(2,1)} %get-tuple-element.259), channel_id=1, source_target_pairs={{0,3},{1,0},{2,1},{3,2},{4,7},{5,4},{6,5},{7,6},{8,11},{9,8},{10,9... | collective-permute-start | bytes 1572872 | tf_op jit(solution)/shard_map/ppermute | solution.py:809
  91.7 34.2 %collective-permute-start.3 = (bf16[4,64,1024]{2,1,0:T(8,128)(2,1)}, bf16[4,64,1024]{2,1,0:T(8,128)(2,1)S(1)}, u32[]{:S(2)}, u32[]{:S(2)}) collective-permute-start(bf16[4,64,1024]{2,1,0:T(8,128)(2,1)} %get-tuple-element.129), channel_id=1, source_target_pairs={{0,1},{1,2},{2,3},{3,0},{4,5},{5,6},{6,7},{7,4},{8,9},{9,10},{10,1... | collective-permute-start | bytes 1572872 | tf_op jit(solution)/shard_map/ppermute | solution.py:809
  94.8 57.6 %collective-permute-start.4 = (bf16[4,64,1024]{2,1,0:T(8,128)(2,1)}, bf16[4,64,1024]{2,1,0:T(8,128)(2,1)}, u32[]{:S(2)}, u32[]{:S(2)}) collective-permute-start(bf16[4,64,1024]{2,1,0:T(8,128)(2,1)} %get-tuple-element.130), channel_id=1, source_target_pairs={{0,2},{1,3},{2,0},{3,1},{4,6},{5,7},{6,4},{7,5},{8,10},{9,11},{10,... | collective-permute-start | bytes 1572872 | tf_op jit(solution)/shard_map/ppermute | solution.py:809
  97.3 55.2 %collective-permute-start.5 = (bf16[4,64,1024]{2,1,0:T(8,128)(2,1)}, bf16[4,64,1024]{2,1,0:T(8,128)(2,1)}, u32[]{:S(2)}, u32[]{:S(2)}) collective-permute-start(bf16[4,64,1024]{2,1,0:T(8,128)(2,1)} %get-tuple-element.131), channel_id=1, source_target_pairs={{0,3},{1,0},{2,1},{3,2},{4,7},{5,4},{6,5},{7,6},{8,11},{9,8},{10,9... | collective-permute-start | bytes 1572872 | tf_op jit(solution)/shard_map/ppermute | solution.py:809
  123.3 52.1 %collective-permute-start.6 = (bf16[4,64,1024]{2,1,0:T(8,128)(2,1)}, bf16[4,64,1024]{2,1,0:T(8,128)(2,1)S(1)}, u32[]{:S(2)}, u32[]{:S(2)}) collective-permute-start(bf16[4,64,1024]{2,1,0:T(8,128)(2,1)} %get-tuple-element.134), channel_id=1, source_target_pairs={{0,1},{1,2},{2,3},{3,0},{4,5},{5,6},{6,7},{7,4},{8,9},{9,10},{10,1... | collective-permute-start | bytes 1572872 | tf_op jit(solution)/shard_map/ppermute | solution.py:809
  124.6 50.8 %collective-permute-start.7 = (bf16[4,64,1024]{2,1,0:T(8,128)(2,1)}, bf16[4,64,1024]{2,1,0:T(8,128)(2,1)S(1)}, u32[]{:S(2)}, u32[]{:S(2)}) collective-permute-start(bf16[4,64,1024]{2,1,0:T(8,128)(2,1)} %get-tuple-element.135), channel_id=1, source_target_pairs={{0,2},{1,3},{2,0},{3,1},{4,6},{5,7},{6,4},{7,5},{8,10},{9,11},{10,... | collective-permute-start | bytes 1572872 | tf_op jit(solution)/shard_map/ppermute | solution.py:809
  125.8 49.6 %collective-permute-start.8 = (bf16[4,64,1024]{2,1,0:T(8,128)(2,1)}, bf16[4,64,1024]{2,1,0:T(8,128)(2,1)}, u32[]{:S(2)}, u32[]{:S(2)}) collective-permute-start(bf16[4,64,1024]{2,1,0:T(8,128)(2,1)} %get-tuple-element.136), channel_id=1, source_target_pairs={{0,3},{1,0},{2,1},{3,2},{4,7},{5,4},{6,5},{7,6},{8,11},{9,8},{10,9... | collective-permute-start | bytes 1572872 | tf_op jit(solution)/shard_map/ppermute | solution.py:809
  199.3 85.1 %collective-permute-start.10 = (bf16[4,64,1024]{2,1,0:T(8,128)(2,1)}, bf16[4,64,1024]{2,1,0:T(8,128)(2,1)S(1)}, u32[]{:S(2)}, u32[]{:S(2)}) collective-permute-start(bf16[4,64,1024]{2,1,0:T(8,128)(2,1)} %get-tuple-element.144), channel_id=1, source_target_pairs={{0,2},{1,3},{2,0},{3,1},{4,6},{5,7},{6,4},{7,5},{8,10},{9,11},{10,... | collective-permute-start | bytes 1572872 | tf_op jit(solution)/shard_map/ppermute | solution.py:809
  211.4 74.9 %collective-permute-start.11 = (bf16[4,64,1024]{2,1,0:T(8,128)(2,1)}, bf16[4,64,1024]{2,1,0:T(8,128)(2,1)}, u32[]{:S(2)}, u32[]{:S(2)}) collective-permute-start(bf16[4,64,1024]{2,1,0:T(8,128)(2,1)} %get-tuple-element.145), channel_id=1, source_target_pairs={{0,3},{1,0},{2,1},{3,2},{4,7},{5,4},{6,5},{7,6},{8,11},{9,8},{10,9... | collective-permute-start | bytes 1572872 | tf_op jit(solution)/shard_map/ppermute | solution.py:809
  214.7 71.6 %collective-permute-start.9 = (bf16[4,64,1024]{2,1,0:T(8,128)(2,1)}, bf16[4,64,1024]{2,1,0:T(8,128)(2,1)}, u32[]{:S(2)}, u32[]{:S(2)}) collective-permute-start(bf16[4,64,1024]{2,1,0:T(8,128)(2,1)} %get-tuple-element.143), channel_id=1, source_target_pairs={{0,1},{1,2},{2,3},{3,0},{4,5},{5,6},{6,7},{7,4},{8,9},{9,10},{10,1... | collective-permute-start | bytes 1572872 | tf_op jit(solution)/shard_map/ppermute | solution.py:809
  281.0 73.7 %collective-permute-start.12 = (bf16[4,64,1024]{2,1,0:T(8,128)(2,1)}, bf16[4,64,1024]{2,1,0:T(8,128)(2,1)S(1)}, u32[]{:S(2)}, u32[]{:S(2)}) collective-permute-start(bf16[4,64,1024]{2,1,0:T(8,128)(2,1)} %get-tuple-element.151), channel_id=1, source_target_pairs={{0,3},{1,0},{2,1},{3,2},{4,7},{5,4},{6,5},{7,6},{8,11},{9,8},{10,9... | collective-permute-start | bytes 1572872 | tf_op jit(solution)/shard_map/ppermute | solution.py:812
  284.4 70.3 %collective-permute-start.13 = (bf16[4,64,1024]{2,1,0:T(8,128)(2,1)}, bf16[4,64,1024]{2,1,0:T(8,128)(2,1)S(1)}, u32[]{:S(2)}, u32[]{:S(2)}) collective-permute-start(bf16[4,64,1024]{2,1,0:T(8,128)(2,1)} %get-tuple-element.152), channel_id=1, source_target_pairs={{0,2},{1,3},{2,0},{3,1},{4,6},{5,7},{6,4},{7,5},{8,10},{9,11},{10,... | collective-permute-start | bytes 1572872 | tf_op jit(solution)/shard_map/ppermute | solution.py:812
  285.2 69.5 %collective-permute-start.14 = (bf16[4,64,1024]{2,1,0:T(8,128)(2,1)}, bf16[4,64,1024]{2,1,0:T(8,128)(2,1)S(1)}, u32[]{:S(2)}, u32[]{:S(2)}) collective-permute-start(bf16[4,64,1024]{2,1,0:T(8,128)(2,1)} %get-tuple-element.153), channel_id=1, source_target_pairs={{0,1},{1,2},{2,3},{3,0},{4,5},{5,6},{6,7},{7,4},{8,9},{9,10},{10,1... | collective-permute-start | bytes 1572872 | tf_op jit(solution)/shard_map/ppermute | solution.py:812
  350.8 51.3 %collective-permute-start.15 = (bf16[4,64,1024]{2,1,0:T(8,128)(2,1)}, bf16[4,64,1024]{2,1,0:T(8,128)(2,1)}, u32[]{:S(2)}, u32[]{:S(2)}) collective-permute-start(bf16[4,64,1024]{2,1,0:T(8,128)(2,1)} %get-tuple-element.159), channel_id=1, source_target_pairs={{0,3},{1,0},{2,1},{3,2},{4,7},{5,4},{6,5},{7,6},{8,11},{9,8},{10,9... | collective-permute-start | bytes 1572872 | tf_op jit(solution)/shard_map/ppermute | solution.py:812
  353.5 48.5 %collective-permute-start.16 = (bf16[4,64,1024]{2,1,0:T(8,128)(2,1)}, bf16[4,64,1024]{2,1,0:T(8,128)(2,1)}, u32[]{:S(2)}, u32[]{:S(2)}) collective-permute-start(bf16[4,64,1024]{2,1,0:T(8,128)(2,1)} %get-tuple-element.160), channel_id=1, source_target_pairs={{0,2},{1,3},{2,0},{3,1},{4,6},{5,7},{6,4},{7,5},{8,10},{9,11},{10,... | collective-permute-start | bytes 1572872 | tf_op jit(solution)/shard_map/ppermute | solution.py:812
  354.7 47.4 %collective-permute-start.17 = (bf16[4,64,1024]{2,1,0:T(8,128)(2,1)}, bf16[4,64,1024]{2,1,0:T(8,128)(2,1)}, u32[]{:S(2)}, u32[]{:S(2)}) collective-permute-start(bf16[4,64,1024]{2,1,0:T(8,128)(2,1)} %get-tuple-element.161), channel_id=1, source_target_pairs={{0,1},{1,2},{2,3},{3,0},{4,5},{5,6},{6,7},{7,4},{8,9},{9,10},{10,1... | collective-permute-start | bytes 1572872 | tf_op jit(solution)/shard_map/ppermute | solution.py:812
  402.1 217.6 %reduce-scatter.6.cloned.1.call-start = ((), (), s32[]{:S(2)}) async-start(), calls=%async_computation.4 | async-start | bytes 9437184 | tf_op jit(solution)/shard_map/reduce_scatter | solution.py:724
  429.2 57.8 %collective-permute-start.18 = (bf16[4,64,1024]{2,1,0:T(8,128)(2,1)}, bf16[4,64,1024]{2,1,0:T(8,128)(2,1)S(1)}, u32[]{:S(2)}, u32[]{:S(2)}) collective-permute-start(bf16[4,64,1024]{2,1,0:T(8,128)(2,1)} %get-tuple-element.178), channel_id=1, source_target_pairs={{0,3},{1,0},{2,1},{3,2},{4,7},{5,4},{6,5},{7,6},{8,11},{9,8},{10,9... | collective-permute-start | bytes 1572872 | tf_op jit(solution)/shard_map/ppermute | solution.py:812
  432.9 54.1 %collective-permute-start.19 = (bf16[4,64,1024]{2,1,0:T(8,128)(2,1)}, bf16[4,64,1024]{2,1,0:T(8,128)(2,1)S(1)}, u32[]{:S(2)}, u32[]{:S(2)}) collective-permute-start(bf16[4,64,1024]{2,1,0:T(8,128)(2,1)} %get-tuple-element.179), channel_id=1, source_target_pairs={{0,2},{1,3},{2,0},{3,1},{4,6},{5,7},{6,4},{7,5},{8,10},{9,11},{10,... | collective-permute-start | bytes 1572872 | tf_op jit(solution)/shard_map/ppermute | solution.py:812
  432.9 54.1 %collective-permute-start.20 = (bf16[4,64,1024]{2,1,0:T(8,128)(2,1)}, bf16[4,64,1024]{2,1,0:T(8,128)(2,1)S(1)}, u32[]{:S(2)}, u32[]{:S(2)}) collective-permute-start(bf16[4,64,1024]{2,1,0:T(8,128)(2,1)} %get-tuple-element.180), channel_id=1, source_target_pairs={{0,1},{1,2},{2,3},{3,0},{4,5},{5,6},{6,7},{7,4},{8,9},{9,10},{10,1... | collective-permute-start | bytes 1572872 | tf_op jit(solution)/shard_map/ppermute | solution.py:812
  488.1 204.5 %reduce-scatter.8.cloned.1.call-start = ((), (), s32[]{:S(2)}) async-start(), calls=%async_computation.5 | async-start | bytes 10027008 | tf_op jit(solution)/shard_map/reduce_scatter | solution.py:724
  488.3 41.2 %collective-permute-start.21 = (bf16[4,64,1024]{2,1,0:T(8,128)(2,1)}, bf16[4,64,1024]{2,1,0:T(8,128)(2,1)S(1)}, u32[]{:S(2)}, u32[]{:S(2)}) collective-permute-start(bf16[4,64,1024]{2,1,0:T(8,128)(2,1)} %get-tuple-element.191), channel_id=1, source_target_pairs={{0,3},{1,0},{2,1},{3,2},{4,7},{5,4},{6,5},{7,6},{8,11},{9,8},{10,9... | collective-permute-start | bytes 1572872 | tf_op jit(solution)/shard_map/ppermute | solution.py:812
  491.5 44.5 %collective-permute-start.22 = (bf16[4,64,1024]{2,1,0:T(8,128)(2,1)}, bf16[4,64,1024]{2,1,0:T(8,128)(2,1)S(1)}, u32[]{:S(2)}, u32[]{:S(2)}) collective-permute-start(bf16[4,64,1024]{2,1,0:T(8,128)(2,1)} %get-tuple-element.192), channel_id=1, source_target_pairs={{0,2},{1,3},{2,0},{3,1},{4,6},{5,7},{6,4},{7,5},{8,10},{9,11},{10,... | collective-permute-start | bytes 1572872 | tf_op jit(solution)/shard_map/ppermute | solution.py:812
  493.1 42.9 %collective-permute-start.23 = (bf16[4,64,1024]{2,1,0:T(8,128)(2,1)}, bf16[4,64,1024]{2,1,0:T(8,128)(2,1)S(1)}, u32[]{:S(2)}, u32[]{:S(2)}) collective-permute-start(bf16[4,64,1024]{2,1,0:T(8,128)(2,1)} %get-tuple-element.193), channel_id=1, source_target_pairs={{0,1},{1,2},{2,3},{3,0},{4,5},{5,6},{6,7},{7,4},{8,9},{9,10},{10,1... | collective-permute-start | bytes 1572872 | tf_op jit(solution)/shard_map/ppermute | solution.py:812
  538.5 38.3 %collective-permute-start.24 = (bf16[256,1024]{1,0:T(8,128)(2,1)S(1)}, bf16[256,1024]{1,0:T(8,128)(2,1)}, u32[]{:S(2)}, u32[]{:S(2)}) collective-permute-start(bf16[256,1024]{1,0:T(8,128)(2,1)S(1)} %get-tuple-element.251), channel_id=1, source_target_pairs={{0,1},{1,2},{2,3},{3,0},{4,5},{5,6},{6,7},{7,4},{8,9},{9,10},{10,1... | collective-permute-start | bytes 1572872 | tf_op jit(solution)/shard_map/ppermute | solution.py:729
  538.5 38.2 %collective-permute-start.25 = (bf16[256,1024]{1,0:T(8,128)(2,1)S(1)}, bf16[256,1024]{1,0:T(8,128)(2,1)}, u32[]{:S(2)}, u32[]{:S(2)}) collective-permute-start(bf16[256,1024]{1,0:T(8,128)(2,1)S(1)} %get-tuple-element.253), channel_id=1, source_target_pairs={{0,2},{1,3},{2,0},{3,1},{4,6},{5,7},{6,4},{7,5},{8,10},{9,11},{10,... | collective-permute-start | bytes 1572872 | tf_op jit(solution)/shard_map/ppermute | solution.py:729
  540.0 36.8 %collective-permute-start.26 = (bf16[256,1024]{1,0:T(8,128)(2,1)S(1)}, bf16[256,1024]{1,0:T(8,128)(2,1)}, u32[]{:S(2)}, u32[]{:S(2)}) collective-permute-start(bf16[256,1024]{1,0:T(8,128)(2,1)S(1)} %get-tuple-element.252), channel_id=1, source_target_pairs={{0,3},{1,0},{2,1},{3,2},{4,7},{5,4},{6,5},{7,6},{8,11},{9,8},{10,9... | collective-permute-start | bytes 1572872 | tf_op jit(solution)/shard_map/ppermute | solution.py:729
  581.1 38.6 %collective-permute-start.27 = (bf16[256,1024]{1,0:T(8,128)(2,1)S(1)}, bf16[256,1024]{1,0:T(8,128)(2,1)S(1)}, u32[]{:S(2)}, u32[]{:S(2)}) collective-permute-start(bf16[256,1024]{1,0:T(8,128)(2,1)S(1)} %get-tuple-element.242.refs_0_), channel_id=1, source_target_pairs={{0,1},{1,2},{2,3},{3,0},{4,5},{5,6},{6,7},{7,4},{8,9},{9,10},{10,1... | collective-permute-start | bytes 1572872 | tf_op jit(solution)/shard_map/ppermute | solution.py:729
  589.3 30.4 %collective-permute-start.28 = (bf16[256,1024]{1,0:T(8,128)(2,1)S(1)}, bf16[256,1024]{1,0:T(8,128)(2,1)S(1)}, u32[]{:S(2)}, u32[]{:S(2)}) collective-permute-start(bf16[256,1024]{1,0:T(8,128)(2,1)S(1)} %get-tuple-element.242.refs_0_), channel_id=1, source_target_pairs={{0,3},{1,0},{2,1},{3,2},{4,7},{5,4},{6,5},{7,6},{8,11},{9,8},{10,9... | collective-permute-start | bytes 1572872 | tf_op jit(solution)/shard_map/ppermute | solution.py:729
  620.8 35.7 %collective-permute-start.35 = (bf16[256,1024]{1,0:T(8,128)(2,1)S(1)}, bf16[256,1024]{1,0:T(8,128)(2,1)}, u32[]{:S(2)}, u32[]{:S(2)}) collective-permute-start(bf16[256,1024]{1,0:T(8,128)(2,1)S(1)} %copy-done.8), channel_id=1, source_target_pairs={{0,2},{1,3},{2,0},{3,1},{4,6},{5,7},{6,4},{7,5},{8,10},{9,11},{10,... | collective-permute-start | bytes 1572872 | tf_op jit(solution)/shard_map/ppermute | solution.py:729
  621.5 40.8 %collective-permute-start.29 = (bf16[128,1024]{1,0:T(8,128)(2,1)S(1)}, bf16[128,1024]{1,0:T(8,128)(2,1)S(1)}, u32[]{:S(2)}, u32[]{:S(2)}) collective-permute-start(bf16[128,1024]{1,0:T(8,128)(2,1)S(1)} %get-tuple-element.273), channel_id=1, source_target_pairs={{0,1},{1,2},{2,3},{3,0},{4,5},{5,6},{6,7},{7,4},{8,9},{9,10},{10,1... | collective-permute-start | bytes 786440 | tf_op jit(solution)/shard_map/ppermute | solution.py:729
  623.6 38.7 %collective-permute-start.30 = (bf16[128,1024]{1,0:T(8,128)(2,1)S(1)}, bf16[128,1024]{1,0:T(8,128)(2,1)S(1)}, u32[]{:S(2)}, u32[]{:S(2)}) collective-permute-start(bf16[128,1024]{1,0:T(8,128)(2,1)S(1)} %get-tuple-element.275), channel_id=1, source_target_pairs={{0,2},{1,3},{2,0},{3,1},{4,6},{5,7},{6,4},{7,5},{8,10},{9,11},{10,... | collective-permute-start | bytes 786440 | tf_op jit(solution)/shard_map/ppermute | solution.py:729
  623.9 38.3 %collective-permute-start.31 = (bf16[128,1024]{1,0:T(8,128)(2,1)S(1)}, bf16[128,1024]{1,0:T(8,128)(2,1)S(1)}, u32[]{:S(2)}, u32[]{:S(2)}) collective-permute-start(bf16[128,1024]{1,0:T(8,128)(2,1)S(1)} %get-tuple-element.274), channel_id=1, source_target_pairs={{0,3},{1,0},{2,1},{3,2},{4,7},{5,4},{6,5},{7,6},{8,11},{9,8},{10,9... | collective-permute-start | bytes 786440 | tf_op jit(solution)/shard_map/ppermute | solution.py:729
  662.6 14.0 %collective-permute-start.32 = (bf16[128,1024]{1,0:T(8,128)(2,1)S(1)}, bf16[128,1024]{1,0:T(8,128)(2,1)S(1)}, u32[]{:S(2)}, u32[]{:S(2)}) collective-permute-start(bf16[128,1024]{1,0:T(8,128)(2,1)S(1)} %get-tuple-element.244), channel_id=1, source_target_pairs={{0,1},{1,2},{2,3},{3,0},{4,5},{5,6},{6,7},{7,4},{8,9},{9,10},{10,1... | collective-permute-start | bytes 786440 | tf_op jit(solution)/shard_map/ppermute | solution.py:729
  668.4 18.8 %collective-permute-start.33 = (bf16[128,1024]{1,0:T(8,128)(2,1)S(1)}, bf16[128,1024]{1,0:T(8,128)(2,1)S(1)}, u32[]{:S(2)}, u32[]{:S(2)}) collective-permute-start(bf16[128,1024]{1,0:T(8,128)(2,1)S(1)} %get-tuple-element.244), channel_id=1, source_target_pairs={{0,2},{1,3},{2,0},{3,1},{4,6},{5,7},{6,4},{7,5},{8,10},{9,11},{10,... | collective-permute-start | bytes 786440 | tf_op jit(solution)/shard_map/ppermute | solution.py:729
  669.9 17.3 %collective-permute-start.34 = (bf16[128,1024]{1,0:T(8,128)(2,1)S(1)}, bf16[128,1024]{1,0:T(8,128)(2,1)S(1)}, u32[]{:S(2)}, u32[]{:S(2)}) collective-permute-start(bf16[128,1024]{1,0:T(8,128)(2,1)S(1)} %get-tuple-element.244), channel_id=1, source_target_pairs={{0,3},{1,0},{2,1},{3,2},{4,7},{5,4},{6,5},{7,6},{8,11},{9,8},{10,9... | collective-permute-start | bytes 786440 | tf_op jit(solution)/shard_map/ppermute | solution.py:729
  693.8 11.5 %collective-permute-start.36 = (bf16[136,1024]{1,0:T(8,128)(2,1)S(1)}, bf16[136,1024]{1,0:T(8,128)(2,1)S(1)}, u32[]{:S(2)}, u32[]{:S(2)}) collective-permute-start(bf16[136,1024]{1,0:T(8,128)(2,1)S(1)} %get-tuple-element.266), channel_id=1, source_target_pairs={{0,1},{1,2},{2,3},{3,0},{4,5},{5,6},{6,7},{7,4},{8,9},{9,10},{10,1... | collective-permute-start | bytes 835592 | tf_op jit(solution)/shard_map/ppermute | solution.py:729
  696.8 19.3 %collective-permute-start.37 = (bf16[136,1024]{1,0:T(8,128)(2,1)S(1)}, bf16[136,1024]{1,0:T(8,128)(2,1)S(1)}, u32[]{:S(2)}, u32[]{:S(2)}) collective-permute-start(bf16[136,1024]{1,0:T(8,128)(2,1)S(1)} %get-tuple-element.268), channel_id=1, source_target_pairs={{0,2},{1,3},{2,0},{3,1},{4,6},{5,7},{6,4},{7,5},{8,10},{9,11},{10,... | collective-permute-start | bytes 835592 | tf_op jit(solution)/shard_map/ppermute | solution.py:729
  698.2 17.9 %collective-permute-start.38 = (bf16[136,1024]{1,0:T(8,128)(2,1)S(1)}, bf16[136,1024]{1,0:T(8,128)(2,1)S(1)}, u32[]{:S(2)}, u32[]{:S(2)}) collective-permute-start(bf16[136,1024]{1,0:T(8,128)(2,1)S(1)} %get-tuple-element.267), channel_id=1, source_target_pairs={{0,3},{1,0},{2,1},{3,2},{4,7},{5,4},{6,5},{7,6},{8,11},{9,8},{10,9... | collective-permute-start | bytes 835592 | tf_op jit(solution)/shard_map/ppermute | solution.py:729
  717.4 15.5 %collective-permute-start.39 = (bf16[136,1024]{1,0:T(8,128)(2,1)S(1)}, bf16[136,1024]{1,0:T(8,128)(2,1)S(1)}, u32[]{:S(2)}, u32[]{:S(2)}) collective-permute-start(bf16[136,1024]{1,0:T(8,128)(2,1)S(1)} %get-tuple-element.240), channel_id=1, source_target_pairs={{0,1},{1,2},{2,3},{3,0},{4,5},{5,6},{6,7},{7,4},{8,9},{9,10},{10,1... | collective-permute-start | bytes 835592 | tf_op jit(solution)/shard_map/ppermute | solution.py:729
  723.9 19.7 %collective-permute-start.40 = (bf16[136,1024]{1,0:T(8,128)(2,1)S(1)}, bf16[136,1024]{1,0:T(8,128)(2,1)S(1)}, u32[]{:S(2)}, u32[]{:S(2)}) collective-permute-start(bf16[136,1024]{1,0:T(8,128)(2,1)S(1)} %get-tuple-element.240), channel_id=1, source_target_pairs={{0,2},{1,3},{2,0},{3,1},{4,6},{5,7},{6,4},{7,5},{8,10},{9,11},{10,... | collective-permute-start | bytes 835592 | tf_op jit(solution)/shard_map/ppermute | solution.py:729
  725.8 17.8 %collective-permute-start.41 = (bf16[136,1024]{1,0:T(8,128)(2,1)S(1)}, bf16[136,1024]{1,0:T(8,128)(2,1)S(1)}, u32[]{:S(2)}, u32[]{:S(2)}) collective-permute-start(bf16[136,1024]{1,0:T(8,128)(2,1)S(1)} %get-tuple-element.240), channel_id=1, source_target_pairs={{0,3},{1,0},{2,1},{3,2},{4,7},{5,4},{6,5},{7,6},{8,11},{9,8},{10,9... | collective-permute-start | bytes 835592 | tf_op jit(solution)/shard_map/ppermute | solution.py:729
  (44 other events, 269.6 us)
Sparse Core Ops, SparseCore 0:
  10.7 57.2 all-gather.8
  70.4 54.3 all-gather.10
  126.7 89.8 all-gather.12
  402.2 116.3 reduce-scatter.3
  521.9 71.2 reduce-scatter.5
  619.9 72.6 reduce-scatter.7
